TPU v7x, 32 devices: a whole 2x2x4 slice. The times are simulated.
32 devices in a mesh: section: 2 (over y), dp: 4 (over z), head: 4 (over x, core).
Axes of the slice: x: 2, y: 2, z: 4, core: 2. Of those that a mesh axis runs over, the one named last changes fastest.
Arguments:
- tokens: bfloat16 [8, 384, 2048], P('dp'), may hold values from -6 to 6
- lengths: int32 [8, 3], P('dp'), may hold values from 1 to 288, 384 in all within a row
- cotangent: bfloat16 [8, 384, 2048], P('dp'), may hold values from -6 to 6
- attn_in: bfloat16 [2, 3, 2048, 2048], P('section', None, None, 'head'), may hold values from -0.125 to 0.125
- beta_weight: bfloat16 [2, 2048, 16], P('section', None, 'head'), may hold values from -0.125 to 0.125
- conv_weight: float32 [2, 3, 4, 2048], P('section', None, None, 'head'), may hold values from -3 to 3
- o_gain: float32 [2, 128], P('section'), may hold values from 0.5 to 1.5
- attn_out: bfloat16 [2, 2048, 2048], P('section', 'head'), may hold values from -0.125 to 0.125
- mlp_in: bfloat16 [2, 2, 2048, 5632], P('section', None, None, 'head'), may hold values from -0.125 to 0.125
- mlp_out: bfloat16 [2, 5632, 2048], P('section', 'head'), may hold values from -0.078125 to 0.078125
- norm_gains: float32 [2, 2, 2048], P('section'), may hold values from 0.5 to 1.5
Outputs:
- grad_tokens: float32 [8, 384, 2048], P('dp', 'head', 'section')
- grad_attn_in: float32 [2, 3, 2048, 2048], P('section', None, 'dp', 'head')
- grad_beta_weight: float32 [2, 2048, 16], P('section', 'dp', 'head')
- grad_conv_weight: float32 [2, 3, 4, 2048], P('section', None, None, 'head')
- grad_o_gain: float32 [2, 128], P('section')
- grad_attn_out: float32 [2, 2048, 2048], P('section', 'head', 'dp')
- grad_mlp_in: float32 [2, 2, 2048, 5632], P('section', None, 'dp', 'head')
- grad_mlp_out: float32 [2, 5632, 2048], P('section', 'head', 'dp')
- grad_norm_gains: float32 [2, 2, 2048], P('section')
Inputs may be any that keep to these rules, and one draw needn't show every extreme that they name: Each row holds the lengths of the 3 sequences packed into one micro-batch; they sum to 384.
All inputs are finite; a program needn't handle non-finite values.
Results may differ from a plain program's by a relative error of at most 0.038.
Values may be sent and summed in bfloat16 or wider, within the bound.
No kernel may reach another device: no remote copies, remote signals or barrier semaphores. Data moves between devices by JAX's collectives and lax.ppermute only.
A program may use at most 320 MiB of HBM per device.

v0:
```python
import jax
import jax.numpy as jnp
from jax import lax
from jax.sharding import PartitionSpec as P

HEAD_DIM = 128
CONV = 4
SPAN = 64
TOK_MB = 384


HIGHEST = lax.Precision.HIGHEST
EPS = 1e-06
OUT_FLOOR = 0.0001


def shifted(block, axis, distance):
    devices = range(lax.axis_size(axis))
    route = [(i - distance, i) for i in devices if i - distance in devices]
    return lax.ppermute(block, axis, route)


def narrow(values):
    return values.astype(jnp.bfloat16)


def product(left, right):
    return jnp.dot(left, right, preferred_element_type=jnp.float32)


def product_left(left, right):
    return lax.dot_general(
        left, right, (((0,), (0,)), ((), ())), preferred_element_type=jnp.float32
    )


def product_right(left, right):
    return lax.dot_general(
        left, right, (((1,), (1,)), ((), ())), preferred_element_type=jnp.float32
    )


def rms_parts(values):
    scale = lax.rsqrt(jnp.mean(values * values, axis=-1, keepdims=True) + EPS)
    return (values * scale, scale)


def norm_back(grad_normed, normed, scale, gain):
    grad_scaled = grad_normed * gain
    return scale * (grad_scaled - normed * jnp.mean(grad_scaled * normed, axis=-1, keepdims=True))


def record(store, values, index, valid):
    current = lax.dynamic_index_in_dim(store, index, 0, keepdims=False)
    return lax.dynamic_update_index_in_dim(store, jnp.where(valid, values, current), index, 0)


def segment_ids(lengths, count):
    ends = jnp.cumsum(lengths)
    places = jnp.arange(count, dtype=jnp.int32)
    return jnp.sum((places[:, None] >= ends[None, :]).astype(jnp.int32), axis=1, dtype=jnp.int32)


def delayed(values, tap):
    if tap == 0:
        return values
    padding = jnp.zeros((tap,) + values.shape[1:], values.dtype)
    return jnp.concatenate([padding, values[: values.shape[0] - tap]], axis=0)


def tap_masks(segment):
    masks = []
    for tap in range(CONV):
        if tap == 0:
            masks.append(jnp.ones((segment.shape[0], 1), jnp.float32))
        else:
            earlier = jnp.concatenate(
                [jnp.full((tap,), -1, jnp.int32), segment[: segment.shape[0] - tap]], axis=0
            )
            masks.append((earlier == segment).astype(jnp.float32)[:, None])
    return masks


def delta_block(state, inputs):
    query, key, value, gate, segment, previous = inputs
    size = segment.shape[0]
    same = (segment[:, None] == segment[None, :]).astype(jnp.float32)
    carry = (segment == previous).astype(jnp.float32)
    identity = jnp.eye(size, dtype=jnp.float32)
    strict = jnp.tril(jnp.ones((size, size), jnp.float32), -1)
    inner = jnp.einsum("hik,hjk->hij", key, key, precision=HIGHEST)
    system = identity + gate[:, :, None] * inner * (same * strict)
    recalled = jnp.einsum("hvk,hik->hiv", state, key, precision=HIGHEST)
    target = gate[:, :, None] * (value - carry[None, :, None] * recalled)
    fresh = jax.scipy.linalg.solve_triangular(system, target, lower=True)
    scores = jnp.einsum("hik,hjk->hij", query, key, precision=HIGHEST) * (
        same * (strict + identity)
    )
    output = carry[None, :, None] * jnp.einsum("hvk,hik->hiv", state, query, precision=HIGHEST)
    output = output + jnp.einsum("hij,hjv->hiv", scores, fresh, precision=HIGHEST)
    keep = (segment == segment[size - 1]).astype(jnp.float32)
    state = carry[size - 1] * state + jnp.einsum(
        "hiv,hik->hvk", fresh * keep[None, :, None], key, precision=HIGHEST
    )
    return (state, output)


def mixer(query_in, key_in, value_in, logit, conv_taps, head_gain, segment):
    count = query_in.shape[0]
    heads = query_in.shape[1] // HEAD_DIM
    masks = tap_masks(segment)

    def convolve(values, which):
        total = jnp.zeros_like(values)
        for tap in range(CONV):
            total = total + conv_taps[which, tap][None, :] * delayed(values, tap) * masks[tap]
        return jax.nn.silu(total).reshape(count, heads, HEAD_DIM)

    query = convolve(query_in, 0)
    key = convolve(key_in, 1)
    value = convolve(value_in, 2)
    query = (
        query * lax.rsqrt(jnp.sum(query * query, axis=-1, keepdims=True) + EPS) * HEAD_DIM ** (-0.5)
    )
    key = key * lax.rsqrt(jnp.sum(key * key, axis=-1, keepdims=True) + EPS)
    gate = jax.nn.sigmoid(logit)
    blocks = count // SPAN

    def blocked(values):
        return values.reshape(blocks, SPAN, heads, HEAD_DIM).transpose(0, 2, 1, 3)

    gates = gate.reshape(blocks, SPAN, heads).transpose(0, 2, 1)
    seg_blocks = segment.reshape(blocks, SPAN)
    previous = jnp.concatenate(
        [jnp.full((1,), -1, jnp.int32), seg_blocks[: blocks - 1, SPAN - 1]], axis=0
    )
    initial = jnp.zeros((heads, HEAD_DIM, HEAD_DIM), jnp.float32)
    final_state, outputs = lax.scan(
        jax.checkpoint(delta_block),
        initial,
        (blocked(query), blocked(key), blocked(value), gates, seg_blocks, previous),
    )
    mixed = outputs.transpose(0, 2, 1, 3).reshape(count, heads, HEAD_DIM)
    mixed = (
        mixed
        * lax.rsqrt(jnp.maximum(jnp.mean(mixed * mixed, axis=-1, keepdims=True), OUT_FLOOR))
        * head_gain
    )
    return mixed.reshape(count, heads * HEAD_DIM)


def per_device(
    tokens,
    lengths,
    cotangent,
    attn_in,
    beta_weight,
    conv_weight,
    o_gain,
    attn_out,
    mlp_in,
    mlp_out,
    norm_gains,
):
    section = lax.axis_index("section")
    member = lax.axis_index("head")
    groups = lax.axis_size("head")
    micro = tokens.shape[0]
    width = tokens.shape[2]
    share = TOK_MB // groups
    projections = attn_in[0]
    gate_proj = beta_weight[0]
    taps = conv_weight[0]
    head_gain = o_gain[0]
    merge_weight = attn_out[0]
    expand = mlp_in[0]
    contract_weight = mlp_out[0]
    gains = norm_gains[0]
    segments = jax.vmap(lambda row: segment_ids(row, TOK_MB))(lengths)

    def own_share(values, axis):
        return lax.dynamic_slice_in_dim(values, member * share, share, axis)

    def settle(values):
        return lax.psum(values, "head")

    def settle_back(values):
        return lax.psum(values.astype(jnp.bfloat16), "head").astype(jnp.float32)

    def gain_rows(values):
        return own_share(values, 0)

    local = TOK_MB

    def backward(incoming, inputs, middle, normed_in, normed_mid, segment):
        query_in = product(normed_in, projections[0])
        key_in = product(normed_in, projections[1])
        value_in = product(normed_in, projections[2])
        logit = product(normed_in, gate_proj)

        def mix_local(query_now, key_now, value_now, logit_now, taps_now, gain_now):
            return mixer(query_now, key_now, value_now, logit_now, taps_now, gain_now, segment)

        mixed_full, mix_pull = jax.vjp(
            mix_local, query_in, key_in, value_in, logit, taps, head_gain
        )
        mixed = narrow(mixed_full)
        gate_in = product(normed_mid, expand[0])
        up_in = product(normed_mid, expand[1])
        sigmoid_gate = jax.nn.sigmoid(gate_in)
        silu_gate = jax.nn.silu(gate_in)
        hidden = narrow(silu_gate * up_in)
        grad_out = narrow(incoming)
        grad_contract = product_left(hidden, grad_out)
        grad_hidden = product_right(grad_out, contract_weight)
        grad_gate = narrow(
            grad_hidden * up_in * sigmoid_gate * (1.0 + gate_in * (1.0 - sigmoid_gate))
        )
        grad_up = narrow(grad_hidden * silu_gate)
        grad_expand = jnp.stack(
            [product_left(normed_mid, grad_gate), product_left(normed_mid, grad_up)]
        )
        grad_mid = settle_back(
            product_right(grad_gate, expand[0]) + product_right(grad_up, expand[1])
        )
        normed_two, scale_two = rms_parts(middle)
        grad_middle = incoming + norm_back(grad_mid, normed_two, scale_two, gains[1])
        gain_two = jnp.sum(gain_rows(grad_mid * normed_two), axis=0)
        grad_branch = narrow(grad_middle)
        grad_merge = product_left(mixed, grad_branch)
        grad_mixed = product_right(grad_branch, merge_weight)
        grad_query, grad_key, grad_value, grad_logit, grad_taps, grad_head_gain = mix_pull(
            grad_mixed
        )
        grad_query = narrow(grad_query)
        grad_key = narrow(grad_key)
        grad_value = narrow(grad_value)
        grad_logit = narrow(grad_logit)
        grad_project = jnp.stack(
            [
                product_left(normed_in, grad_query),
                product_left(normed_in, grad_key),
                product_left(normed_in, grad_value),
            ]
        )
        grad_beta = product_left(normed_in, grad_logit)
        grad_norm = product_right(grad_query, projections[0]) + product_right(
            grad_key, projections[1]
        )
        grad_norm = settle_back(
            grad_norm
            + product_right(grad_value, projections[2])
            + product_right(grad_logit, gate_proj)
        )
        normed, scale = rms_parts(inputs)
        grad_inputs = grad_middle + norm_back(grad_norm, normed, scale, gains[0])
        gain_one = jnp.sum(gain_rows(grad_norm * normed), axis=0)
        terms = (
            grad_project,
            grad_beta,
            grad_taps,
            grad_head_gain,
            grad_merge,
            grad_expand,
            grad_contract,
            jnp.stack([gain_one, gain_two]),
        )
        return (grad_inputs, terms)

    stash_in = jnp.zeros((micro, local, width), jnp.float32)
    stash_mid = jnp.zeros((micro, local, width), jnp.float32)
    stash_norm = jnp.zeros((micro, TOK_MB, width), jnp.bfloat16)
    stash_norm_mid = jnp.zeros((micro, TOK_MB, width), jnp.bfloat16)
    arrived = jnp.zeros((local, width), jnp.float32)
    for step in range(micro + 1):
        index = jnp.clip(step - section, 0, micro - 1)
        valid = (step - section >= 0) & (step - section < micro)
        first = tokens[min(step, micro - 1)].astype(jnp.float32)
        inputs = jnp.where(section == 0, first, arrived)
        segment = lax.dynamic_index_in_dim(segments, index, 0, keepdims=False)
        forward_normed, forward_scale = rms_parts(inputs)
        forward_normed_in = narrow(forward_normed * gains[0])
        forward_query_in = product(forward_normed_in, projections[0])
        forward_key_in = product(forward_normed_in, projections[1])
        forward_value_in = product(forward_normed_in, projections[2])
        forward_logit = product(forward_normed_in, gate_proj)
        forward_mixed = narrow(
            mixer(
                forward_query_in,
                forward_key_in,
                forward_value_in,
                forward_logit,
                taps,
                head_gain,
                segment,
            )
        )
        forward_middle = inputs + settle(product(forward_mixed, merge_weight))
        forward_normed_two, forward_scale_two = rms_parts(forward_middle)
        forward_normed_mid = narrow(forward_normed_two * gains[1])
        forward_gate_in = product(forward_normed_mid, expand[0])
        forward_up_in = product(forward_normed_mid, expand[1])
        forward_hidden = narrow(jax.nn.silu(forward_gate_in) * forward_up_in)
        result = forward_middle + settle(product(forward_hidden, contract_weight))
        result, middle, normed_in, normed_mid = (
            result,
            forward_middle,
            forward_normed_in,
            forward_normed_mid,
        )
        stash_in = record(stash_in, inputs, index, valid)
        stash_mid = record(stash_mid, middle, index, valid)
        stash_norm = record(stash_norm, normed_in, index, valid)
        stash_norm_mid = record(stash_norm_mid, normed_mid, index, valid)
        if step < micro:
            arrived = shifted(narrow(result), "section", 1).astype(jnp.float32)
    totals = (
        jnp.zeros(projections.shape, jnp.float32),
        jnp.zeros(gate_proj.shape, jnp.float32),
        jnp.zeros(taps.shape, jnp.float32),
        jnp.zeros(head_gain.shape, jnp.float32),
        jnp.zeros(merge_weight.shape, jnp.float32),
        jnp.zeros(expand.shape, jnp.float32),
        jnp.zeros(contract_weight.shape, jnp.float32),
        jnp.zeros(gains.shape, jnp.float32),
    )
    kept = jnp.zeros((micro, local, width), jnp.float32)
    arrived = jnp.zeros((local, width), jnp.float32)
    for step in range(micro + 1):
        index = jnp.clip(step - 1 + section, 0, micro - 1)
        valid = (step - 1 + section >= 0) & (step - 1 + section < micro)
        last = cotangent[min(step, micro - 1)].astype(jnp.float32)
        incoming = jnp.where(section == 1, last, arrived)
        segment = lax.dynamic_index_in_dim(segments, index, 0, keepdims=False)
        inputs = lax.dynamic_index_in_dim(stash_in, index, 0, keepdims=False)
        middle = lax.dynamic_index_in_dim(stash_mid, index, 0, keepdims=False)
        normed_in = lax.dynamic_index_in_dim(stash_norm, index, 0, keepdims=False)
        normed_mid = lax.dynamic_index_in_dim(stash_norm_mid, index, 0, keepdims=False)
        grad_inputs, terms = backward(incoming, inputs, middle, normed_in, normed_mid, segment)
        totals = jax.tree.map(
            lambda total, term: total + jnp.where(valid, term, 0.0), totals, terms
        )
        kept = record(kept, grad_inputs, index, valid)
        if step < micro:
            arrived = shifted(narrow(grad_inputs), "section", -1).astype(jnp.float32)
    rows_out = own_share(kept, 1)
    half = width // 2
    moved = shifted(rows_out[:, :, half:].astype(jnp.bfloat16), "section", 1).astype(jnp.float32)
    grad_tokens = jnp.where(section == 0, rows_out[:, :, :half], moved)
    (
        grad_project,
        grad_beta,
        grad_taps,
        grad_head_gain,
        grad_merge,
        grad_expand,
        grad_contract,
        grad_gains,
    ) = totals
    grad_project, grad_expand, grad_merge, grad_contract, grad_beta = (
        lax.psum_scatter(
            grad_project.astype(jnp.bfloat16), "dp", scatter_dimension=1, tiled=True
        ).astype(jnp.float32),
        lax.psum_scatter(
            grad_expand.astype(jnp.bfloat16), "dp", scatter_dimension=1, tiled=True
        ).astype(jnp.float32),
        lax.psum_scatter(
            grad_merge.astype(jnp.bfloat16), "dp", scatter_dimension=1, tiled=True
        ).astype(jnp.float32),
        lax.psum_scatter(
            grad_contract.astype(jnp.bfloat16), "dp", scatter_dimension=1, tiled=True
        ).astype(jnp.float32),
        lax.psum_scatter(
            grad_beta.astype(jnp.bfloat16), "dp", scatter_dimension=0, tiled=True
        ).astype(jnp.float32),
    )
    grad_gains, grad_head_gain = lax.psum((grad_gains, grad_head_gain), ("dp", "head"))
    grad_taps = lax.psum(grad_taps, "dp")
    return (
        grad_tokens,
        grad_project[None],
        grad_beta[None],
        grad_taps[None],
        grad_head_gain[None],
        grad_merge[None],
        grad_expand[None],
        grad_contract[None],
        grad_gains[None],
    )


def solution(mesh):
    return jax.shard_map(
        per_device,
        mesh=mesh,
        in_specs=(
            P("dp", None, None),
            P("dp", None),
            P("dp", None, None),
            P("section", None, None, "head"),
            P("section", None, "head"),
            P("section", None, None, "head"),
            P("section", None),
            P("section", "head", None),
            P("section", None, None, "head"),
            P("section", "head", None),
            P("section", None, None),
        ),
        out_specs=(
            P("dp", "head", "section"),
            P("section", None, "dp", "head"),
            P("section", "dp", "head"),
            P("section", None, None, "head"),
            P("section", None),
            P("section", "head", "dp"),
            P("section", None, "dp", "head"),
            P("section", "head", "dp"),
            P("section", None, None),
        ),
        check_vma=False,
    )
```

profile of v0, /device:TPU:0, one launch (start us, length us, event | category | flops | bytes accessed | tf_op | source)
XLA Modules:
  0.0 3621.2 jit_solution(7871229134423048145)
XLA Ops:
  57.7 186.0 %while.159 = (s32[]{:T(128)}, f32[4,128,128]{2,1,0:T(8,128)S(1)}, f32[6,4,64,128]{3,2,1,0:T(8,128)}, s32[6,64]{1,0:T(8,128)}, s32[6]{0:T(128)S(1)}, /*index=5*/f...) while((s32[]{:T(128)}, f32[4,128,128]{2,1,0:T(8,128)S(1)}, ...), condition=%wide.region_6.8_spmd.clone, body=%wide.region_5.7_spmd.clone.sunk | while | flops 252309824 | bytes 3499751 | solution.py:138
  62.2 19.7 custom-call.48
  249.6 71.2 %all-reduce.142.cloned.1.call-done = f32[384,2048]{1,0:T(8,128)} async-done(((f32[384,2048]{1,0:T(8,128)}), f32[384,2048]{1,0:T(8,128)}) %all-reduce.142.cloned.1.call-update) | async-done | bytes 3145744 | tf_op jit(solution)/shard_map/psum | solution.py:185
  348.4 68.4 %all-reduce.144.cloned.1.call-done = f32[384,2048]{1,0:T(8,128)} async-done(((f32[384,2048]{1,0:T(8,128)}), f32[384,2048]{1,0:T(8,128)}) %all-reduce.144.cloned.1.call-update) | async-done | bytes 3145744 | tf_op jit(solution)/shard_map/psum | solution.py:185
  429.4 30.0 collective-permute-done
  500.5 186.2 %while.160 = (s32[]{:T(128)}, f32[4,128,128]{2,1,0:T(8,128)S(1)}, f32[6,4,64,128]{3,2,1,0:T(8,128)}, s32[6,64]{1,0:T(8,128)}, s32[6]{0:T(128)S(1)}, /*index=5*/f...) while((s32[]{:T(128)}, f32[4,128,128]{2,1,0:T(8,128)S(1)}, ...), condition=%wide.region_15.17_spmd.clone, body=%wide.region_14.16_spmd.clone.sunk | while | flops 252309824 | bytes 3499751 | solution.py:138
  702.2 60.4 %all-reduce.146.cloned.1.call-done = f32[384,2048]{1,0:T(8,128)} async-done(((f32[384,2048]{1,0:T(8,128)}), f32[384,2048]{1,0:T(8,128)}) %all-reduce.146.cloned.1.call-update) | async-done | bytes 3145744 | tf_op jit(solution)/shard_map/psum | solution.py:185
  801.5 55.6 %all-reduce.148.cloned.1.call-done = f32[384,2048]{1,0:T(8,128)} async-done(((f32[384,2048]{1,0:T(8,128)}), f32[384,2048]{1,0:T(8,128)}) %all-reduce.148.cloned.1.call-update) | async-done | bytes 3145744 | tf_op jit(solution)/shard_map/psum | solution.py:185
  1016.3 191.7 %while.161 = (s32[]{:T(128)}, f32[4,128,128]{2,1,0:T(8,128)S(1)}, f32[6,4,64,128]{3,2,1,0:T(8,128)}, s32[6,64]{1,0:T(8,128)S(1)}, s32[6]{0:T(128)S(1)}, /*index=...) while((s32[]{:T(128)}, f32[4,128,128]{2,1,0:T(8,128)S(1)}, ...), condition=%wide.region_24.26_spmd.clone, body=%wide.region_23.25_spmd.clone.sunk | while | flops 252309824 | bytes 3394995 | solution.py:138
  1242.8 220.2 %while.165 = (s32[]{:T(128)}, f32[4,128,128]{2,1,0:T(8,128)S(1)}, f32[6,4,64,128]{3,2,1,0:T(8,128)}, f32[6,4,128,128]{3,2,1,0:T(8,128)}, s32[6,64]{1,0:T(8,128)}...) while((s32[]{:T(128)}, f32[4,128,128]{2,1,0:T(8,128)S(1)}, ...), condition=%wide.region_35.37_spmd.clone.clone.clone, body=%wide.region_34.36_spmd.clone.clone.clone.sunk | while | flops 252375296 | bytes 3975144 | solution.py:138
  1250.8 20.4 custom-call.54
  1287.5 20.4 custom-call.54
  1324.1 20.4 custom-call.54
  1360.8 20.4 custom-call.54
  1397.5 20.4 custom-call.54
  1434.2 20.4 custom-call.54
  1470.2 202.1 %while.166 = (s32[]{:T(128)}, f32[4,128,128]{2,1,0:T(8,128)S(1)}, f32[6,4,64,128]{3,2,1,0:T(8,128)}, f32[6,4,128,128]{3,2,1,0:T(8,128)}, s32[6,64]{1,0:T(8,128)}...) while((s32[]{:T(128)}, f32[4,128,128]{2,1,0:T(8,128)S(1)}, ...), condition=%wide.region_53.56_spmd.clone.clone.clone, body=%wide.region_52.55_spmd.clone.clone.clone.sunk | while | flops 252375296 | bytes 3974348 | solution.py:138
  1733.8 34.8 all-reduce.152.cloned.1.call-done
  1779.6 243.0 %while.162 = (s32[]{:T(128)}, f32[4,128,128]{2,1,0:T(8,128)S(1)}, f32[6,4,64,128]{3,2,1,0:T(8,128)}, f32[6,4,64,128]{3,2,1,0:T(8,128)}, f32[6,4,64,128]{3,2,1,0:...) while((s32[]{:T(128)}, f32[4,128,128]{2,1,0:T(8,128)S(1)}, ...), condition=%wide.region_41.44_spmd.clone, body=%wide.region_38.43_spmd.clone.sunk | while | flops 642969664 | bytes 11633671 | solution.py:138
  1789.9 20.4 custom-call.51
  1830.3 20.4 custom-call.51
  1870.8 20.4 custom-call.51
  1911.3 20.4 custom-call.51
  1951.8 20.4 custom-call.51
  1992.2 20.4 custom-call.51
  2059.3 37.2 %all-reduce.154.cloned.1.call-done = bf16[384,2048]{1,0:T(8,128)(2,1)} async-done(((bf16[384,2048]{1,0:T(8,128)(2,1)}), bf16[384,2048]{1,0:T(8,128)(2,1)}) %all-reduce.154.cloned.1.call-update) | async-done | bytes 1572880 | tf_op jit(solution)/shard_map/psum | solution.py:188
  2157.7 38.6 %all-reduce.156.cloned.1.call-done = bf16[384,2048]{1,0:T(8,128)(2,1)} async-done(((bf16[384,2048]{1,0:T(8,128)(2,1)}), bf16[384,2048]{1,0:T(8,128)(2,1)}) %all-reduce.156.cloned.1.call-update) | async-done | bytes 1572880 | tf_op jit(solution)/shard_map/psum | solution.py:188
  2209.9 261.5 %while.163 = (s32[]{:T(128)}, f32[4,128,128]{2,1,0:T(8,128)}, f32[6,4,64,128]{3,2,1,0:T(8,128)}, f32[6,4,64,128]{3,2,1,0:T(8,128)}, f32[6,4,64,128]{3,2,1,0:T(8,...) while((s32[]{:T(128)}, f32[4,128,128]{2,1,0:T(8,128)}, ...), condition=%wide.region_59.62_spmd.clone, body=%wide.region_56.61_spmd.clone.sunk | while | flops 642969664 | bytes 11632675 | solution.py:138
  2220.5 20.4 custom-call.52
  2264.2 20.4 custom-call.52
  2307.9 20.4 custom-call.52
  2351.7 20.4 custom-call.52
  2395.4 20.4 custom-call.52
  2439.1 20.4 custom-call.52
  2507.5 205.7 %while.167 = (s32[]{:T(128)}, f32[4,128,128]{2,1,0:T(8,128)S(1)}, f32[6,4,64,128]{3,2,1,0:T(8,128)S(1)}, f32[6,4,128,128]{3,2,1,0:T(8,128)}, s32[6,64]{1,0:T(8,1...) while((s32[]{:T(128)}, f32[4,128,128]{2,1,0:T(8,128)S(1)}, ...), condition=%wide.region_71.74_spmd.clone.clone.clone, body=%wide.region_70.73_spmd.clone.clone.clone.sunk | while | flops 252375296 | bytes 3919304 | solution.py:138
  2778.3 34.0 all-reduce.160.cloned.1.call-done
  2825.3 246.5 %while.164 = (s32[]{:T(128)}, f32[4,128,128]{2,1,0:T(8,128)}, f32[6,4,64,128]{3,2,1,0:T(8,128)}, f32[6,4,64,128]{3,2,1,0:T(8,128)}, f32[6,4,64,128]{3,2,1,0:T(8,...) while((s32[]{:T(128)}, f32[4,128,128]{2,1,0:T(8,128)}, ...), condition=%wide.region_77.80_spmd.clone, body=%wide.region_74.79_spmd.clone.sunk | while | flops 642969664 | bytes 11633919 | solution.py:138
  2834.8 20.4 custom-call.53
  2876.0 20.4 custom-call.53
  2917.1 20.4 custom-call.53
  2958.3 20.4 custom-call.53
  2999.5 20.4 custom-call.53
  3040.7 20.4 custom-call.53
  3213.0 20.2 fusion.359
  3252.9 21.9 psum.109
  3294.2 60.0 %all-reduce.129 = (f32[1,128]{1,0:T(1,128)}, f32[1,2,2048]{2,1,0:T(2,128)}) all-reduce(f32[1,128]{1,0:T(1,128)S(1)} %fusion.912, f32[1,2,2048]{2,1,0:T(2,128)S(1)} %fusion.845), channel_id=1, replica_groups=mesh['section'=2,'dp'=4,'head'=4] {'dp','head'}, use_global_device_ids=true, to_apply=%region_124.127 | all-reduce | flops 4224 | bytes 33792 | tf_op jit(solution)/shard_map/psum | solution.py:377
  3361.8 50.0 %reduce-scatter.8.cloned.1.call-done = bf16[3,512,512]{2,1,0:T(8,128)(2,1)} async-done(((bf16[3,2048,512]{2,1,0:T(8,128)(2,1)}), bf16[3,512,512]{2,1,0:T(8,128)(2,1)}) %reduce-scatter.8.cloned.1.call-update) | async-done | bytes 1572880 | tf_op jit(solution)/shard_map/reduce_scatter | solution.py:361
  3415.3 194.3 %reduce-scatter.12.cloned.1.call-done = bf16[2,512,1408]{2,1,0:T(8,128)(2,1)} async-done(((bf16[2,2048,1408]{2,1,0:T(8,128)(2,1)}), bf16[2,512,1408]{2,1,0:T(8,128)(2,1)}) %reduce-scatter.12.cloned.1.call-update) | async-done | bytes 2883600 | tf_op jit(solution)/shard_map/reduce_scatter | solution.py:364
  (2657 shorter events, 2308.0 us)
Async XLA Ops:
  7.2 239.7 %copy-start = (bf16[1,512,2048]{2,1,0:T(8,128)(2,1)S(1)}, bf16[1,512,2048]{2,1,0:T(8,128)(2,1)}, u32[]{:S(2)}) copy-start(bf16[1,512,2048]{2,1,0:T(8,128)(2,1)} %param.42) | copy-start | bytes 6291460
  7.2 313.7 %all-reduce.142.cloned.1.call-start = ((), (), s32[]{:S(2)}) async-start(), calls=%async_computation.5 | async-start | bytes 6291456 | tf_op jit(solution)/shard_map/psum | solution.py:185
  13.7 887.1 %copy-start.135 = (f32[1,1,2048]{2,1,0:T(1,128)}, f32[1,1,2048]{2,1,0:T(1,128)S(1)}, u32[]{:S(2)}) copy-start(f32[1,1,2048]{2,1,0:T(1,128)S(1)} %get-tuple-element.2804) | copy-start | bytes 24580
  25.3 947.3 %copy-start.162 = (f32[1,1,512]{2,1,0:T(1,128)}, f32[1,1,512]{2,1,0:T(1,128)S(1)}, u32[]{:S(2)}) copy-start(f32[1,1,512]{2,1,0:T(1,128)S(1)} %get-tuple-element.2801) | copy-start | bytes 6148
  25.3 947.3 %copy-start.164 = (f32[1,1,512]{2,1,0:T(1,128)}, f32[1,1,512]{2,1,0:T(1,128)S(1)}, u32[]{:S(2)}) copy-start(f32[1,1,512]{2,1,0:T(1,128)S(1)} %get-tuple-element.2802) | copy-start | bytes 6148
  25.3 947.3 %copy-start.167 = (f32[1,1,512]{2,1,0:T(1,128)}, f32[1,1,512]{2,1,0:T(1,128)S(1)}, u32[]{:S(2)}) copy-start(f32[1,1,512]{2,1,0:T(1,128)S(1)} %get-tuple-element.2800) | copy-start | bytes 6148
  25.3 966.0 %copy-start.160 = (f32[1,1,512]{2,1,0:T(1,128)}, f32[1,1,512]{2,1,0:T(1,128)S(1)}, u32[]{:S(2)}) copy-start(f32[1,1,512]{2,1,0:T(1,128)S(1)} %get-tuple-element.2792) | copy-start | bytes 6148
  25.3 966.0 %copy-start.174 = (f32[1,1,512]{2,1,0:T(1,128)}, f32[1,1,512]{2,1,0:T(1,128)S(1)}, u32[]{:S(2)}) copy-start(f32[1,1,512]{2,1,0:T(1,128)S(1)} %get-tuple-element.2794) | copy-start | bytes 6148
  25.3 966.0 %copy-start.178 = (f32[1,1,512]{2,1,0:T(1,128)}, f32[1,1,512]{2,1,0:T(1,128)S(1)}, u32[]{:S(2)}) copy-start(f32[1,1,512]{2,1,0:T(1,128)S(1)} %get-tuple-element.2795) | copy-start | bytes 6148
  25.3 966.0 %copy-start.182 = (f32[1,1,512]{2,1,0:T(1,128)}, f32[1,1,512]{2,1,0:T(1,128)S(1)}, u32[]{:S(2)}) copy-start(f32[1,1,512]{2,1,0:T(1,128)S(1)} %get-tuple-element.2793) | copy-start | bytes 6148
  25.3 1196.7 %copy-start.170 = (f32[1,1,512]{2,1,0:T(1,128)}, f32[1,1,512]{2,1,0:T(1,128)S(1)}, u32[]{:S(2)}) copy-start(f32[1,1,512]{2,1,0:T(1,128)S(1)} %get-tuple-element.2799) | copy-start | bytes 6148
  25.4 1196.7 %copy-start.186 = (f32[1,1,512]{2,1,0:T(1,128)}, f32[1,1,512]{2,1,0:T(1,128)S(1)}, u32[]{:S(2)}) copy-start(f32[1,1,512]{2,1,0:T(1,128)S(1)} %get-tuple-element.2798) | copy-start | bytes 6148
  25.4 1196.7 %copy-start.190 = (f32[1,1,512]{2,1,0:T(1,128)}, f32[1,1,512]{2,1,0:T(1,128)S(1)}, u32[]{:S(2)}) copy-start(f32[1,1,512]{2,1,0:T(1,128)S(1)} %get-tuple-element.2797) | copy-start | bytes 6148
  25.4 1196.7 %copy-start.194 = (f32[1,1,512]{2,1,0:T(1,128)}, f32[1,1,512]{2,1,0:T(1,128)S(1)}, u32[]{:S(2)}) copy-start(f32[1,1,512]{2,1,0:T(1,128)S(1)} %get-tuple-element.2796) | copy-start | bytes 6148
  57.7 187.4 %copy-start.200 = (f32[1,128]{1,0:T(1,128)S(1)}, f32[1,128]{1,0:T(1,128)}, u32[]{:S(2)}) copy-start(f32[1,128]{1,0:T(1,128)} %param.41) | copy-start | bytes 1540
  249.6 167.2 %all-reduce.144.cloned.1.call-start = ((), (), s32[]{:S(2)}) async-start(), calls=%async_computation.6 | async-start | bytes 6291456 | tf_op jit(solution)/shard_map/psum | solution.py:185
  348.1 414.5 %all-reduce.146.cloned.1.call-start = ((), (), s32[]{:S(2)}) async-start(), calls=%async_computation.7 | async-start | bytes 6291456 | tf_op jit(solution)/shard_map/psum | solution.py:185
  422.0 37.3 %collective-permute-start = (bf16[384,2048]{1,0:T(8,128)(2,1)}, bf16[384,2048]{1,0:T(8,128)(2,1)}, u32[]{:S(2)}, u32[]{:S(2)}) collective-permute-start(bf16[384,2048]{1,0:T(8,128)(2,1)} %add_convert_fusion.9), channel_id=1, source_target_pairs={{0,16},{1,17},{2,18},{3,19},{4,20},{5,21},{6,22},{7,23},{8,24},{9,... | collective-permute-start | bytes 4718600 | tf_op jit(solution)/shard_map/ppermute | solution.py:20
  692.7 164.4 %all-reduce.148.cloned.1.call-start = ((), (), s32[]{:S(2)}) async-start(), calls=%async_computation.8 | async-start | bytes 6291456 | tf_op jit(solution)/shard_map/psum | solution.py:185
  699.0 292.3 %copy-start.238 = (f32[384]{0:T(512)}, f32[384]{0:T(512)S(1)}, u32[]{:S(2)}) copy-start(f32[384]{0:T(512)S(1)} %get-tuple-element.2861) | copy-start | bytes 4612
  699.0 292.3 %copy-start.240 = (f32[384]{0:T(512)}, f32[384]{0:T(512)S(1)}, u32[]{:S(2)}) copy-start(f32[384]{0:T(512)S(1)} %get-tuple-element.2863) | copy-start | bytes 4612
  699.1 292.3 %copy-start.242 = (f32[384]{0:T(512)}, f32[384]{0:T(512)S(1)}, u32[]{:S(2)}) copy-start(f32[384]{0:T(512)S(1)} %get-tuple-element.2862) | copy-start | bytes 4612
  699.1 523.0 %copy-start.226 = (f32[384]{0:T(512)}, f32[384]{0:T(512)S(1)}, u32[]{:S(2)}) copy-start(f32[384]{0:T(512)S(1)} %get-tuple-element.2901) | copy-start | bytes 4612
  699.1 523.0 %copy-start.228 = (f32[384]{0:T(512)}, f32[384]{0:T(512)S(1)}, u32[]{:S(2)}) copy-start(f32[384]{0:T(512)S(1)} %get-tuple-element.2903) | copy-start | bytes 4612
  699.1 523.0 %copy-start.230 = (f32[384]{0:T(512)}, f32[384]{0:T(512)S(1)}, u32[]{:S(2)}) copy-start(f32[384]{0:T(512)S(1)} %get-tuple-element.2902) | copy-start | bytes 4612
  699.2 522.9 %copy-start.232 = (f32[384]{0:T(512)}, f32[384]{0:T(512)S(1)}, u32[]{:S(2)}) copy-start(f32[384]{0:T(512)S(1)} %get-tuple-element.2879) | copy-start | bytes 4612
  699.2 522.9 %copy-start.234 = (f32[384]{0:T(512)}, f32[384]{0:T(512)S(1)}, u32[]{:S(2)}) copy-start(f32[384]{0:T(512)S(1)} %get-tuple-element.2881) | copy-start | bytes 4612
  699.2 522.9 %copy-start.236 = (f32[384]{0:T(512)}, f32[384]{0:T(512)S(1)}, u32[]{:S(2)}) copy-start(f32[384]{0:T(512)S(1)} %get-tuple-element.2880) | copy-start | bytes 4612
  788.4 910.0 %all-reduce.150.cloned.1.call-start = ((), (), s32[]{:S(2)}) async-start(), calls=%async_computation.9 | async-start | bytes 6291456 | tf_op jit(solution)/shard_map/psum | solution.py:185
  861.5 37.2 %collective-permute-start.1 = (bf16[384,2048]{1,0:T(8,128)(2,1)}, bf16[384,2048]{1,0:T(8,128)(2,1)}, u32[]{:S(2)}, u32[]{:S(2)}) collective-permute-start(bf16[384,2048]{1,0:T(8,128)(2,1)} %add_convert_fusion.8), channel_id=1, source_target_pairs={{0,16},{1,17},{2,18},{3,19},{4,20},{5,21},{6,22},{7,23},{8,24},{9,... | collective-permute-start | bytes 4718600 | tf_op jit(solution)/shard_map/ppermute | solution.py:20
  1213.9 554.7 %all-reduce.152.cloned.1.call-start = ((), (), s32[]{:S(2)}) async-start(), calls=%async_computation.10 | async-start | bytes 3145728 | tf_op jit(solution)/shard_map/psum | solution.py:188
  1686.2 89.0 %copy-start.157 = (f32[384,4]{0,1:T(4,128)}, f32[384,4]{0,1:T(4,128)S(1)}, u32[]{:S(2)}) copy-start(f32[384,4]{0,1:T(4,128)S(1)} %rsqrt.327) | copy-start | bytes 18436
  1724.3 372.3 %all-reduce.154.cloned.1.call-start = ((), (), s32[]{:S(2)}) async-start(), calls=%async_computation.11 | async-start | bytes 3145728 | tf_op jit(solution)/shard_map/psum | solution.py:188
  1779.6 245.7 %copy-start.207 = (f32[384,4]{0,1:T(4,128)S(1)}, f32[384,4]{0,1:T(4,128)}, u32[]{:S(2)}) copy-start(f32[384,4]{0,1:T(4,128)} %copy-done.206) | copy-start | bytes 18436
  2053.4 142.9 %all-reduce.156.cloned.1.call-start = ((), (), s32[]{:S(2)}) async-start(), calls=%async_computation.12 | async-start | bytes 3145728 | tf_op jit(solution)/shard_map/psum | solution.py:188
  2103.2 38.3 %collective-permute-start.2 = (bf16[384,2048]{1,0:T(8,128)(2,1)}, bf16[384,2048]{1,0:T(8,128)(2,1)}, u32[]{:S(2)}, u32[]{:S(2)}) collective-permute-start(bf16[384,2048]{1,0:T(8,128)(2,1)} %fusion.926), channel_id=1, source_target_pairs={{16,0},{17,1},{18,2},{19,3},{20,4},{21,5},{22,6},{23,7},{24,8},{25... | collective-permute-start | bytes 4718600 | tf_op jit(solution)/shard_map/ppermute | solution.py:20
  2153.9 559.7 %all-reduce.158.cloned.1.call-start = ((), (), s32[]{:S(2)}) async-start(), calls=%async_computation.13 | async-start | bytes 3145728 | tf_op jit(solution)/shard_map/psum | solution.py:188
  2506.0 306.4 %all-reduce.160.cloned.1.call-start = ((), (), s32[]{:S(2)}) async-start(), calls=%async_computation.14 | async-start | bytes 3145728 | tf_op jit(solution)/shard_map/psum | solution.py:188
  2507.5 206.0 %copy-start.314 = (f32[384]{0:T(512)S(1)}, f32[384]{0:T(512)}, u32[]{:S(2)}) copy-start(f32[384]{0:T(512)} %get-tuple-element.2318) | copy-start | bytes 4612
  2719.2 38.3 %collective-permute-start.3 = (bf16[384,2048]{1,0:T(8,128)(2,1)}, bf16[384,2048]{1,0:T(8,128)(2,1)}, u32[]{:S(2)}, u32[]{:S(2)}) collective-permute-start(bf16[384,2048]{1,0:T(8,128)(2,1)} %fusion.927), channel_id=1, source_target_pairs={{16,0},{17,1},{18,2},{19,3},{20,4},{21,5},{22,6},{23,7},{24,8},{25... | collective-permute-start | bytes 4718600 | tf_op jit(solution)/shard_map/ppermute | solution.py:20
  2769.9 504.9 %reduce-scatter.16.cloned.1.call-start = ((), (), s32[]{:S(2)}) async-start(), calls=%async_computation.20 | async-start | bytes 655360
  2825.3 249.9 %copy-start.205 = (f32[384,4]{0,1:T(4,128)S(1)}, f32[384,4]{0,1:T(4,128)}, u32[]{:S(2)}) copy-start(f32[384,4]{0,1:T(4,128)} %copy-done.204) | copy-start | bytes 18436
  3078.0 197.8 %all-reduce.162.cloned.1.call-start = ((), (), s32[]{:S(2)}) async-start(), calls=%async_computation.15 | async-start | bytes 3145728 | tf_op jit(solution)/shard_map/psum | solution.py:188
  3103.0 253.3 %reduce-scatter.10.cloned.1.call-start = ((), (), s32[]{:S(2)}) async-start(), calls=%async_computation.17 | async-start | bytes 2621440 | tf_op jit(solution)/shard_map/reduce_scatter | solution.py:367
  3110.9 247.5 %reduce-scatter.14.cloned.1.call-start = ((), (), s32[]{:S(2)}) async-start(), calls=%async_computation.19 | async-start | bytes 7208960 | tf_op jit(solution)/shard_map/reduce_scatter | solution.py:370
  3144.0 267.8 %reduce-scatter.8.cloned.1.call-start = ((), (), s32[]{:S(2)}) async-start(), calls=%async_computation.16 | async-start | bytes 7864320 | tf_op jit(solution)/shard_map/reduce_scatter | solution.py:361
  3171.3 438.4 %reduce-scatter.12.cloned.1.call-start = ((), (), s32[]{:S(2)}) async-start(), calls=%async_computation.18 | async-start | bytes 14417920 | tf_op jit(solution)/shard_map/reduce_scatter | solution.py:364
  3284.3 69.9 %collective-permute-start.4 = (bf16[2,96,1024]{2,1,0:T(8,128)(2,1)S(1)}, bf16[2,96,1024]{2,1,0:T(8,128)(2,1)S(1)}, u32[]{:S(2)}, u32[]{:S(2)}) collective-permute-start(bf16[2,96,1024]{2,1,0:T(8,128)(2,1)S(1)} %dynamic-slice_convert_fusion), channel_id=1, source_target_pairs={{0,16},{1,17},{2,18},{3,19},{4,20},{5,21},{6,22},{7,23},{8,24},{9,... | collective-permute-start | bytes 1179656 | tf_op jit(solution)/shard_map/ppermute | solution.py:20
  (389 other events, 2494.4 us)
Sparse Core Ops, SparseCore 0:
  249.7 71.1 all-reduce.141
  348.2 68.5 all-reduce.143
  692.8 69.7 all-reduce.145
  788.5 68.5 all-reduce.147
  1214.1 69.9 all-reduce.149
  1724.4 44.2 all-reduce.151
  2053.6 42.8 all-reduce.153
  2154.0 42.2 all-reduce.155
  2506.1 43.5 all-reduce.157
  2770.0 42.2 all-reduce.159
  3078.2 21.6 reduce-scatter.15
  3103.1 42.9 all-reduce.161
  3148.4 43.9 reduce-scatter.9
  3195.2 102.6 reduce-scatter.13
  3300.1 111.6 reduce-scatter.7
  3414.1 195.4 reduce-scatter.11
where the time goes:
time: 3640 us; the launch traced here: 3620 us
  other arithmetic  1540 us (42%)
  matrix products  781 us (21%)
  waiting for transfers between devices  716 us (20%)
  local copies, waits for them, and re-layouts  451 us (12%)
  blocking collectives  81.8 us (2%)
    another operation x126, other arithmetic, delta_block(): fresh = jax.scipy.linalg.solve_triangular(system, target, lower=True)  1090 us
    psum x5, waiting for transfers between devices, settle(): return lax.psum(values, 'head')  256 us
    reduce_scatter x1, waiting for transfers between devices, per_device(): lax.psum_scatter(grad_expand.astype(jnp.bfloat16), 'dp', scatter_dimensio...  194 us
    psum x6, waiting for transfers between devices, settle_back(): return lax.psum(values.astype(jnp.bfloat16), 'head').astype(jnp.float32)  145 us
    dot_general x37, matrix products, product(): return jnp.dot(left, right, preferred_element_type=jnp.float32)  125 us
    dot_general x72, matrix products, delta_block(): jnp.einsum('hvk,hik->hiv', state, query, precision=HIGHEST)  117 us
    dot_general x24, matrix products, product_left(): lax.dot_general(left, right, (((0,), (0,)), ((), ())), preferred_element_...  107 us
    dot_general x90, matrix products, delta_block(): recalled = jnp.einsum('hvk,hik->hiv', state, key, precision=HIGHEST)  106 us
  transfers between devices with their start and end apart: 21, of which 14 were waited for; matrix products, arithmetic and copies ran while one was open for 27% of the time, Pallas kernels for 0%

commit v1 on v0

v1 whole, which is shorter than its diff:
```python
import functools

import jax
import jax.numpy as jnp
from jax import lax
from jax.experimental import pallas as pl
from jax.experimental.pallas import tpu as pltpu
from jax.sharding import PartitionSpec as P

HEAD_DIM = 128
CONV = 4
TOK_MB = 384
BLOCK = 128
BLOCKS = TOK_MB // BLOCK
EPS = 1e-06
OUT_FLOOR = 0.0001
F32 = jnp.float32
BF16 = jnp.bfloat16
BASE = 4


def mm(left, right):
    return lax.dot_general(
        left.astype(BF16), right.astype(BF16), (((1,), (0,)), ((), ())), preferred_element_type=F32
    )


def mm_t(left, right):
    return lax.dot_general(
        left.astype(BF16), right.astype(BF16), (((1,), (1,)), ((), ())), preferred_element_type=F32
    )


def t_mm(left, right):
    return lax.dot_general(
        left.astype(BF16), right.astype(BF16), (((0,), (0,)), ((), ())), preferred_element_type=F32
    )


def rows_of(b):
    return slice(b * BLOCK, (b + 1) * BLOCK)


def stream(x, taps, masks):
    pre = taps[0:1] * x
    for tap in range(1, CONV):
        pre = pre + taps[tap : tap + 1] * (pltpu.roll(x, tap, 0) * masks[tap - 1])
    gate = jax.nn.sigmoid(pre)
    return pre, gate, pre * gate


def unit_inverses(systems):
    size = systems[0].shape[0]
    row = lax.broadcasted_iota(jnp.int32, (size, size), 0)
    col = lax.broadcasted_iota(jnp.int32, (size, size), 1)
    eye = (row == col).astype(F32)
    near = (row // BASE == col // BASE).astype(F32)
    first = [-a * near for a in systems]
    power = 1
    total = [eye + n for n in first]
    second = [mm(n, n) for n in first]
    third = [mm(n, s) for n, s in zip(first, second)]
    total = [t + s + r for t, s, r in zip(total, second, third)]
    step = BASE
    while step < size:
        span = 2 * step
        off = ((row // span == col // span) & (row // step != col // step)).astype(F32)
        inner = [mm(a * off, t) for a, t in zip(systems, total)]
        outer = [mm(t, i) for t, i in zip(total, inner)]
        total = [t - o for t, o in zip(total, outer)]
        step = span
    return total


def forward_kernel(heads_here, save, qkv_ref, logit_ref, taps_ref, gain_ref, masks_ref, seg_col_ref, seg_row_ref, mixed_ref, *saved):
    step = pl.program_id(0)
    masks = [masks_ref[i] for i in range(CONV - 1)]
    logits = logit_ref[...]
    lane = lax.broadcasted_iota(jnp.int32, logits.shape, 1)
    row = lax.broadcasted_iota(jnp.int32, (BLOCK, BLOCK), 0)
    col = lax.broadcasted_iota(jnp.int32, (BLOCK, BLOCK), 1)
    strict = col < row
    lower = col <= row
    same = {}
    for b in range(BLOCKS):
        for c in range(b + 1):
            same[b, c] = seg_col_ref[rows_of(b), :] == seg_row_ref[:, rows_of(c)]
    queries, keys, values, betas = [], [], [], []
    for h in range(heads_here):
        cols = slice(h * HEAD_DIM, (h + 1) * HEAD_DIM)
        taps = [taps_ref[j, :, cols] for j in range(3)]
        _, _, query = stream(qkv_ref[0, :, cols], taps[0], masks)
        _, _, key = stream(qkv_ref[1, :, cols], taps[1], masks)
        _, _, value = stream(qkv_ref[2, :, cols], taps[2], masks)
        query = query * lax.rsqrt(jnp.sum(query * query, axis=-1, keepdims=True) + EPS) * HEAD_DIM**-0.5
        key = key * lax.rsqrt(jnp.sum(key * key, axis=-1, keepdims=True) + EPS)
        logit = jnp.sum(jnp.where(lane == step * heads_here + h, logits, 0.0), axis=1, keepdims=True)
        beta = jax.nn.sigmoid(logit)
        queries.append(query.astype(BF16))
        keys.append(key.astype(BF16))
        values.append(value * beta)
        betas.append(beta)
    attend, system = {}, {}
    for h in range(heads_here):
        for b in range(BLOCKS):
            for c in range(b + 1):
                inner = mm_t(keys[h][rows_of(b)], keys[h][rows_of(c)])
                keep = same[b, c] & strict if b == c else same[b, c]
                system[h, b, c] = jnp.where(keep, inner * betas[h][rows_of(b)], 0.0)
                scores = mm_t(queries[h][rows_of(b)], keys[h][rows_of(c)])
                keep = same[b, c] & lower if b == c else same[b, c]
                attend[h, b, c] = jnp.where(keep, scores, 0.0).astype(BF16)
    index = [(h, b) for h in range(heads_here) for b in range(BLOCKS)]
    inverse = dict(zip(index, unit_inverses([system[h, b, b] for h, b in index])))
    inverse = {k: v.astype(BF16) for k, v in inverse.items()}
    system = {k: v.astype(BF16) for k, v in system.items()}
    fresh = {}
    for b in range(BLOCKS):
        for h in range(heads_here):
            target = values[h][rows_of(b)]
            for c in range(b):
                target = target - mm(system[h, b, c], fresh[h, c])
            fresh[h, b] = mm(inverse[h, b], target).astype(BF16)
    for h in range(heads_here):
        cols = slice(h * HEAD_DIM, (h + 1) * HEAD_DIM)
        for b in range(BLOCKS):
            out = mm(attend[h, b, 0], fresh[h, 0])
            for c in range(1, b + 1):
                out = out + mm(attend[h, b, c], fresh[h, c])
            mean = jnp.mean(out * out, axis=-1, keepdims=True)
            mixed_ref[rows_of(b), cols] = (
                out * lax.rsqrt(jnp.maximum(mean, OUT_FLOOR)) * gain_ref[...]
            ).astype(BF16)
            if save:
                system_ref, attend_ref, inverse_ref, fresh_ref, out_ref = saved
                out_ref[rows_of(b), cols] = out
                fresh_ref[rows_of(b), cols] = fresh[h, b]
                inverse_ref[h, b] = inverse[h, b]
                for c in range(b + 1):
                    attend_ref[h, rows_of(b), rows_of(c)] = attend[h, b, c]
                    if c < b:
                        system_ref[h, rows_of(b), rows_of(c)] = system[h, b, c]


def mix_forward(qkv, logit, taps, gain, masks, seg_col, seg_row, save, per=1):
    heads = logit.shape[1]
    width = per * HEAD_DIM
    full = lambda shape: pl.BlockSpec(shape, lambda h: (0,) * len(shape))
    out_shape = [jax.ShapeDtypeStruct((TOK_MB, heads * HEAD_DIM), BF16)]
    out_specs = [pl.BlockSpec((TOK_MB, width), lambda h: (0, h))]
    if save:
        out_shape += [
            jax.ShapeDtypeStruct((heads, TOK_MB, TOK_MB), BF16),
            jax.ShapeDtypeStruct((heads, TOK_MB, TOK_MB), BF16),
            jax.ShapeDtypeStruct((heads, BLOCKS, BLOCK, BLOCK), BF16),
            jax.ShapeDtypeStruct((TOK_MB, heads * HEAD_DIM), BF16),
            jax.ShapeDtypeStruct((TOK_MB, heads * HEAD_DIM), F32),
        ]
        out_specs += [
            pl.BlockSpec((per, TOK_MB, TOK_MB), lambda h: (h, 0, 0)),
            pl.BlockSpec((per, TOK_MB, TOK_MB), lambda h: (h, 0, 0)),
            pl.BlockSpec((per, BLOCKS, BLOCK, BLOCK), lambda h: (h, 0, 0, 0)),
            pl.BlockSpec((TOK_MB, width), lambda h: (0, h)),
            pl.BlockSpec((TOK_MB, width), lambda h: (0, h)),
        ]
    return pl.pallas_call(
        functools.partial(forward_kernel, per, save),
        grid=(heads // per,),
        in_specs=[
            pl.BlockSpec((3, TOK_MB, width), lambda h: (0, 0, h)),
            full(logit.shape),
            pl.BlockSpec((3, CONV, width), lambda h: (0, 0, h)),
            full(gain.shape),
            full(masks.shape),
            full(seg_col.shape),
            full(seg_row.shape),
        ],
        out_specs=out_specs,
        out_shape=out_shape,
        compiler_params=pltpu.CompilerParams(vmem_limit_bytes=48 * 1024 * 1024),
        cost_estimate=pl.CostEstimate(flops=heads * 10**9, bytes_accessed=heads * 10**6, transcendentals=0),
    )(qkv, logit, taps, gain, masks, seg_col, seg_row)


def stream_back(grad, x, pre, gate, taps, masks, taps_out, j, cols):
    grad_pre = grad * gate * (1.0 + pre * (1.0 - gate))
    grad_x = taps[0:1] * grad_pre
    taps_out[j, 0:1, cols] = jnp.sum(grad_pre * x, axis=0, keepdims=True)
    for tap in range(1, CONV):
        masked = grad_pre * masks[tap - 1]
        grad_x = grad_x + taps[tap : tap + 1] * pltpu.roll(masked, TOK_MB - tap, 0)
        taps_out[j, tap : tap + 1, cols] = jnp.sum(masked * pltpu.roll(x, tap, 0), axis=0, keepdims=True)
    return grad_x


def backward_kernel(heads_here, qkv_ref, logit_ref, taps_ref, gain_ref, masks_ref, seg_col_ref, seg_row_ref,
                    system_ref, attend_ref, inverse_ref, fresh_ref, out_ref, grad_ref,
                    grad_qkv_ref, grad_logit_ref, grad_taps_ref, grad_gain_ref):
    step = pl.program_id(0)

    @pl.when(step == 0)
    def _():
        grad_logit_ref[...] = jnp.zeros(grad_logit_ref.shape, F32)
        grad_gain_ref[...] = jnp.zeros(grad_gain_ref.shape, F32)

    masks = [masks_ref[i] for i in range(CONV - 1)]
    logits = logit_ref[...]
    lane = lax.broadcasted_iota(jnp.int32, logits.shape, 1)
    wide = lax.broadcasted_iota(jnp.int32, (TOK_MB, HEAD_DIM), 1)
    row = lax.broadcasted_iota(jnp.int32, (BLOCK, BLOCK), 0)
    col = lax.broadcasted_iota(jnp.int32, (BLOCK, BLOCK), 1)
    strict = col < row
    lower = col <= row
    same = {}
    for b in range(BLOCKS):
        for c in range(b + 1):
            same[b, c] = seg_col_ref[rows_of(b), :] == seg_row_ref[:, rows_of(c)]
    for h in range(heads_here):
        cols = slice(h * HEAD_DIM, (h + 1) * HEAD_DIM)
        taps = [taps_ref[j, :, cols] for j in range(3)]
        inputs = [qkv_ref[j, :, cols] for j in range(3)]
        pre_q, gate_q, conv_q = stream(inputs[0], taps[0], masks)
        pre_k, gate_k, conv_k = stream(inputs[1], taps[1], masks)
        pre_v, gate_v, value = stream(inputs[2], taps[2], masks)
        scale_q = lax.rsqrt(jnp.sum(conv_q * conv_q, axis=-1, keepdims=True) + EPS)
        scale_k = lax.rsqrt(jnp.sum(conv_k * conv_k, axis=-1, keepdims=True) + EPS)
        unit_q = conv_q * scale_q
        key = conv_k * scale_k
        query = (unit_q * HEAD_DIM**-0.5).astype(BF16)
        key_b = key.astype(BF16)
        logit = jnp.sum(jnp.where(lane == step * heads_here + h, logits, 0.0), axis=1, keepdims=True)
        beta = jax.nn.sigmoid(logit)

        out = out_ref[:, cols]
        grad_mixed = grad_ref[:, cols]
        mean = jnp.mean(out * out, axis=-1, keepdims=True)
        scale = lax.rsqrt(jnp.maximum(mean, OUT_FLOOR))
        unit = out * scale
        grad_gain_ref[...] += jnp.sum((grad_mixed * unit).reshape(TOK_MB // 8, 8, HEAD_DIM), axis=0)
        grad_unit = grad_mixed * gain_ref[...]
        through = jnp.where(mean > OUT_FLOOR, 1.0, jnp.where(mean == OUT_FLOOR, 0.5, 0.0))
        grad_out = scale * (
            grad_unit - unit * (through * jnp.mean(grad_unit * unit, axis=-1, keepdims=True))
        )
        grad_out = grad_out.astype(BF16)
        fresh = [fresh_ref[rows_of(b), cols] for b in range(BLOCKS)]
        d_out = [grad_out[rows_of(b)] for b in range(BLOCKS)]
        d_fresh = [None] * BLOCKS
        for c in range(BLOCKS):
            total = t_mm(attend_ref[h, rows_of(c), rows_of(c)], d_out[c])
            for b in range(c + 1, BLOCKS):
                total = total + t_mm(attend_ref[h, rows_of(b), rows_of(c)], d_out[b])
            d_fresh[c] = total
        d_target = [None] * BLOCKS
        for b in reversed(range(BLOCKS)):
            d_target[b] = t_mm(inverse_ref[h, b], d_fresh[b])
            for c in range(b):
                d_fresh[c] = d_fresh[c] - t_mm(system_ref[h, rows_of(b), rows_of(c)], d_target[b])
        d_target_b = [d.astype(BF16) for d in d_target]
        grad_query = []
        inner = []
        grad_key = [None] * BLOCKS
        key_blocks = [key_b[rows_of(b)] for b in range(BLOCKS)]
        for b in range(BLOCKS):
            dq = None
            da = None
            beta_row = beta[rows_of(b)]
            for c in range(b + 1):
                d_attend = mm_t(d_out[b], fresh[c])
                keep = same[b, c] & lower if b == c else same[b, c]
                d_attend = jnp.where(keep, d_attend, 0.0).astype(BF16)
                d_system = mm_t(d_target_b[b], fresh[c])
                keep = same[b, c] & strict if b == c else same[b, c]
                d_system = jnp.where(keep, -d_system, 0.0)
                part = mm(d_attend, key_blocks[c])
                dq = part if dq is None else dq + part
                part = mm(d_system, key_blocks[c])
                da = part if da is None else da + part
                part = t_mm(d_attend, query[rows_of(b)]) + t_mm(d_system * beta_row, key_blocks[b])
                grad_key[c] = part if grad_key[c] is None else grad_key[c] + part
            grad_query.append(dq)
            inner.append(da)
        inner = jnp.concatenate(inner, axis=0)
        grad_query = jnp.concatenate(grad_query, axis=0)
        grad_key = jnp.concatenate(grad_key, axis=0) + beta * inner
        d_target = jnp.concatenate(d_target, axis=0)
        grad_beta = jnp.sum(inner * key + d_target * value, axis=-1, keepdims=True)
        grad_logit = grad_beta * beta * (1.0 - beta)
        grad_logit_ref[...] += jnp.where(wide == step * heads_here + h, grad_logit, 0.0)
        grad_value = beta * d_target
        grad_conv_q = (HEAD_DIM**-0.5 * scale_q) * (
            grad_query - unit_q * jnp.sum(grad_query * unit_q, axis=-1, keepdims=True)
        )
        grad_conv_k = scale_k * (grad_key - key * jnp.sum(grad_key * key, axis=-1, keepdims=True))
        for j, (grad, pre, gate) in enumerate(
            ((grad_conv_q, pre_q, gate_q), (grad_conv_k, pre_k, gate_k), (grad_value, pre_v, gate_v))
        ):
            grad_x = stream_back(grad, inputs[j], pre, gate, taps[j], masks, grad_taps_ref, j, cols)
            grad_qkv_ref[j, :, cols] = grad_x.astype(BF16)


def mix_backward(qkv, logit, taps, gain, masks, seg_col, seg_row, saved, grad_mixed, per=1):
    heads = logit.shape[1]
    width = per * HEAD_DIM
    full = lambda shape: pl.BlockSpec(shape, lambda h: (0,) * len(shape))
    rows = pl.BlockSpec((TOK_MB, width), lambda h: (0, h))
    return pl.pallas_call(
        functools.partial(backward_kernel, per),
        grid=(heads // per,),
        in_specs=[
            pl.BlockSpec((3, TOK_MB, width), lambda h: (0, 0, h)),
            full(logit.shape),
            pl.BlockSpec((3, CONV, width), lambda h: (0, 0, h)),
            full(gain.shape),
            full(masks.shape),
            full(seg_col.shape),
            full(seg_row.shape),
            pl.BlockSpec((per, TOK_MB, TOK_MB), lambda h: (h, 0, 0)),
            pl.BlockSpec((per, TOK_MB, TOK_MB), lambda h: (h, 0, 0)),
            pl.BlockSpec((per, BLOCKS, BLOCK, BLOCK), lambda h: (h, 0, 0, 0)),
            rows,
            rows,
            rows,
        ],
        out_specs=[
            pl.BlockSpec((3, TOK_MB, width), lambda h: (0, 0, h)),
            full((TOK_MB, HEAD_DIM)),
            pl.BlockSpec((3, CONV, width), lambda h: (0, 0, h)),
            full((8, HEAD_DIM)),
        ],
        out_shape=[
            jax.ShapeDtypeStruct((3, TOK_MB, heads * HEAD_DIM), BF16),
            jax.ShapeDtypeStruct((TOK_MB, HEAD_DIM), F32),
            jax.ShapeDtypeStruct((3, CONV, heads * HEAD_DIM), F32),
            jax.ShapeDtypeStruct((8, HEAD_DIM), F32),
        ],
        compiler_params=pltpu.CompilerParams(vmem_limit_bytes=48 * 1024 * 1024),
        cost_estimate=pl.CostEstimate(flops=heads * 10**9, bytes_accessed=heads * 2 * 10**6, transcendentals=0),
    )(qkv, logit, taps, gain, masks, seg_col, seg_row, *saved, grad_mixed)


def tap_masks(segment):
    masks = []
    for tap in range(1, CONV):
        earlier = jnp.concatenate([jnp.full((tap,), -1, jnp.int32), segment[: TOK_MB - tap]], axis=0)
        masks.append(jnp.broadcast_to((earlier == segment).astype(F32)[:, None], (TOK_MB, HEAD_DIM)))
    return jnp.stack(masks)


def narrow(values):
    return values.astype(BF16)


def product(left, right):
    return jnp.dot(left, right, preferred_element_type=F32)


def product_left(left, right):
    return lax.dot_general(left, right, (((0,), (0,)), ((), ())), preferred_element_type=F32)


def product_right(left, right):
    return lax.dot_general(left, right, (((1,), (1,)), ((), ())), preferred_element_type=F32)


def rms_parts(values):
    scale = lax.rsqrt(jnp.mean(values * values, axis=-1, keepdims=True) + EPS)
    return (values * scale, scale)


def norm_back(grad_normed, normed, scale, gain):
    grad_scaled = grad_normed * gain
    return scale * (grad_scaled - normed * jnp.mean(grad_scaled * normed, axis=-1, keepdims=True))


def segment_ids(lengths, count):
    ends = jnp.cumsum(lengths)
    places = jnp.arange(count, dtype=jnp.int32)
    return jnp.sum((places[:, None] >= ends[None, :]).astype(jnp.int32), axis=1, dtype=jnp.int32)


def flipped(values, axis, bit):
    return lax.ppermute(values, axis, [(i, i ^ bit) for i in range(lax.axis_size(axis))])


def shifted(values, axis, distance):
    devices = range(lax.axis_size(axis))
    return lax.ppermute(values, axis, [(i, i + distance) for i in devices if i + distance in devices])


def bits_of(axis):
    size = lax.axis_size(axis)
    bits = [1 << k for k in range(size.bit_length() - 1)]
    assert 1 << len(bits) == size
    return bits


def summed(values, axes):
    for axis in axes:
        for bit in bits_of(axis):
            values = values + flipped(values, axis, bit)
    return values


def gather(shard):
    me = lax.axis_index("head")
    parts = shard
    for place, bit in enumerate(reversed(bits_of("head"))):
        other = flipped(parts, "head", bit)
        low = (me & bit) == 0
        parts = jnp.stack([jnp.where(low, parts, other), jnp.where(low, other, parts)], axis=place)
    return parts.reshape(-1, shard.shape[-1])


def scatter(partial):
    me = lax.axis_index("head")
    bits = bits_of("head")
    parts = narrow(partial).reshape([2] * len(bits) + [-1, partial.shape[-1]])
    for place, bit in enumerate(bits):
        axis = len(bits) - 1 - place
        side = (me // bit) % 2
        mine = lax.dynamic_index_in_dim(parts, side, axis, keepdims=False)
        other = lax.dynamic_index_in_dim(parts, 1 - side, axis, keepdims=False)
        total = mine.astype(F32) + flipped(other, "head", bit).astype(F32)
        parts = narrow(total)
    return total


def per_device(
    tokens,
    lengths,
    cotangent,
    attn_in,
    beta_weight,
    conv_weight,
    o_gain,
    attn_out,
    mlp_in,
    mlp_out,
    norm_gains,
):
    section = lax.axis_index("section")
    sections = lax.axis_size("section")
    member = lax.axis_index("head")
    micro = tokens.shape[0]
    width = tokens.shape[2]
    heads = beta_weight.shape[2]
    share = TOK_MB // lax.axis_size("head")
    projections = attn_in[0]
    gate_proj = beta_weight[0]
    taps = conv_weight[0]
    head_gain = o_gain
    merge_weight = attn_out[0]
    expand = mlp_in[0]
    contract_weight = mlp_out[0]
    gains = norm_gains[0]
    every = range(micro)
    segments = [segment_ids(lengths[m], TOK_MB) for m in every]
    masks = [(tap_masks(s), s[:, None], s[None, :]) for s in segments]
    own_rows = lambda values: lax.dynamic_slice_in_dim(values, member * share, share, 0).astype(F32)
    tokens_own = [own_rows(tokens[m]) for m in every]
    cotangent_own = [own_rows(cotangent[m]) for m in every]

    def forward(x, m, save):
        unit, scale = rms_parts(x)
        normed = gather(narrow(unit * gains[0]))
        qkv = jnp.stack([product(normed, projections[j]) for j in range(3)])
        logit = product(normed, gate_proj)
        mixed, *saved = mix_forward(qkv, logit, taps, head_gain, *masks[m], save, heads)
        middle = x + scatter(product(mixed, merge_weight))
        unit_mid, scale_mid = rms_parts(middle)
        normed_mid = gather(narrow(unit_mid * gains[1]))
        gate_in = product(normed_mid, expand[0])
        up_in = product(normed_mid, expand[1])
        hidden = narrow(jax.nn.silu(gate_in) * up_in)
        result = middle + scatter(product(hidden, contract_weight))
        kept = (unit, scale, normed, qkv, logit, mixed, saved, unit_mid, scale_mid, normed_mid, gate_in, up_in, hidden)
        return result, kept

    def backward(incoming, m, kept):
        unit, scale, normed, qkv, logit, mixed, saved, unit_mid, scale_mid, normed_mid, gate_in, up_in, hidden = kept
        grad_out = gather(narrow(incoming))
        sigmoid_gate = jax.nn.sigmoid(gate_in)
        silu_gate = gate_in * sigmoid_gate
        grad_hidden = product_right(grad_out, contract_weight)
        grad_gate = narrow(grad_hidden * up_in * sigmoid_gate * (1.0 + gate_in * (1.0 - sigmoid_gate)))
        grad_up = narrow(grad_hidden * silu_gate)
        grad_mid = scatter(product_right(grad_gate, expand[0]) + product_right(grad_up, expand[1]))
        grad_middle = incoming + norm_back(grad_mid, unit_mid, scale_mid, gains[1])
        gain_two = jnp.sum(grad_mid * unit_mid, axis=0)
        grad_branch = gather(narrow(grad_middle))
        grad_mixed = product_right(grad_branch, merge_weight)
        grad_qkv, grad_logit, grad_taps, grad_head_gain = mix_backward(
            qkv, logit, taps, head_gain, *masks[m], saved, grad_mixed, 2 if heads % 2 == 0 else 1
        )
        grad_logit = narrow(grad_logit[:, :heads])
        grad_norm = product_right(grad_logit, gate_proj)
        for j in range(3):
            grad_norm = grad_norm + product_right(grad_qkv[j], projections[j])
        grad_norm = scatter(grad_norm)
        grad_inputs = grad_middle + norm_back(grad_norm, unit, scale, gains[0])
        gain_one = jnp.sum(grad_norm * unit, axis=0)
        big = (normed, grad_qkv, grad_logit, mixed, grad_branch, normed_mid, grad_gate, grad_up, hidden, grad_out)
        small = (grad_taps, jnp.sum(grad_head_gain, axis=0), jnp.stack([gain_one, gain_two]))
        return grad_inputs, big, small

    inputs = tokens_own
    for turn in range(sections):
        results = [forward(inputs[m], m, turn == sections - 1) for m in every]
        if turn < sections - 1:
            arrived = [shifted(narrow(result), "section", 1).astype(F32) for result, _ in results]
            inputs = [jnp.where(section == 0, tokens_own[m], arrived[m]) for m in every]
    kept = [k for _, k in results]
    incoming = cotangent_own
    for turn in range(sections):
        results = [backward(incoming[m], m, kept[m]) for m in every]
        if turn < sections - 1:
            arrived = [shifted(narrow(result[0]), "section", -1).astype(F32) for result in results]
            incoming = [jnp.where(section == sections - 1, cotangent_own[m], arrived[m]) for m in every]
    rows_out = jnp.stack([result[0] for result in results])
    half = width // sections
    moved = shifted(narrow(rows_out[:, :, half:]), "section", 1).astype(F32)
    grad_tokens = jnp.where(section == 0, rows_out[:, :, :half], moved)

    def joined(place, axis=0):
        return jnp.concatenate([result[1][place] for result in results], axis=axis)

    normed, grad_qkv, grad_logit = joined(0), joined(1, 1), joined(2)
    mixed, grad_branch, normed_mid = joined(3), joined(4), joined(5)
    grad_gate, grad_up, hidden, grad_out = joined(6), joined(7), joined(8), joined(9)

    def spread(value, axis):
        return lax.psum_scatter(narrow(value), "dp", scatter_dimension=axis, tiled=True).astype(F32)

    grad_expand = spread(jnp.stack([product_left(normed_mid, grad_gate), product_left(normed_mid, grad_up)]), 1)
    grad_contract = spread(product_left(hidden, grad_out), 1)
    grad_merge = spread(product_left(mixed, grad_branch), 1)
    grad_project = spread(jnp.stack([product_left(normed, grad_qkv[j]) for j in range(3)]), 1)
    grad_beta = spread(product_left(normed, grad_logit), 0)
    grad_taps, grad_head_gain, grad_gains = (
        sum(result[2][place] for result in results) for place in range(3)
    )
    grad_gains = summed(jnp.concatenate([grad_gains.reshape(-1), grad_head_gain]), ("dp", "head"))
    grad_gains, grad_head_gain = grad_gains[: 2 * width].reshape(2, width), grad_gains[2 * width :]
    grad_taps = summed(grad_taps, ("dp",))
    return (
        grad_tokens,
        grad_project[None],
        grad_beta[None],
        grad_taps[None],
        grad_head_gain[None],
        grad_merge[None],
        grad_expand[None],
        grad_contract[None],
        grad_gains[None],
    )


def solution(mesh):
    return jax.shard_map(
        per_device,
        mesh=mesh,
        in_specs=(
            P("dp", None, None),
            P("dp", None),
            P("dp", None, None),
            P("section", None, None, "head"),
            P("section", None, "head"),
            P("section", None, None, "head"),
            P("section", None),
            P("section", "head", None),
            P("section", None, None, "head"),
            P("section", "head", None),
            P("section", None, None),
        ),
        out_specs=(
            P("dp", "head", "section"),
            P("section", None, "dp", "head"),
            P("section", "dp", "head"),
            P("section", None, None, "head"),
            P("section", None),
            P("section", "head", "dp"),
            P("section", None, "dp", "head"),
            P("section", "head", "dp"),
            P("section", None, None),
        ),
        check_vma=False,
    )
```

time: 3640 us -> 1160 us (0.32)
  other arithmetic: 1540 us -> 88.6 us
  matrix products: 781 us -> 194 us
  local copies, waits for them, and re-layouts: 451 us -> 62.3 us
  blocking collectives: 81.8 us -> 0 us
  Pallas kernels: 0 us -> 75.5 us
  waiting for transfers between devices: 716 us -> 641 us
  starting transfers between devices: 23.2 us -> 65.6 us
    another operation x145 -> x76, other arithmetic: 1100 us -> 31.2 us  [the longest x64 16.5 us: gather(): jnp.stack([jnp.where(low, parts, other), jnp.where(low, other, parts)], a...]
    dot_general x541 -> x28, matrix products: 572 us -> 67.3 us  [product(): return jnp.dot(left, right, preferred_element_type=F32)]
    psum x11 -> x0, waiting for transfers between devices: 400 us -> none  [the longest x5 256 us: settle(): return lax.psum(values, 'head')]
    ppermute x5 -> x71, waiting for transfers between devices: 70.7 us -> 272 us  [the longest x66 242 us: flipped(): lax.ppermute(values, axis, [(i, i ^ bit) for i in range(lax.axis_size(axi...]
    reduce_scatter x4, waiting for transfers between devices: 244 us -> 369 us  [spread(): lax.psum_scatter(narrow(value), 'dp', scatter_dimension=axis, tiled=True)]
    convert_element_type x112 -> x30, other arithmetic: 148 us -> 25.4 us  [the longest x28 25.2 us: narrow(): return values.astype(BF16)]
    psum x2 -> x0, blocking collectives: 81.8 us -> none  [the longest x1 60 us: per_device(): lax.psum((grad_gains, grad_head_gain), ('dp', 'head'))]
    pallas_call x0 -> x8, Pallas kernels: none -> 75.5 us  [the longest x4 50.9 us: mix_backward(): pl.pallas_call(functools.partial(backward_kernel, per), grid=(heads // pe...]
  transfers between devices with their start and end apart: 21 -> 76, of which waited for: 14 -> 51; matrix products, arithmetic and copies ran while one was open for 27% -> 18% of each run, Pallas kernels for 0% -> 3%
where the time goes in v1:
time: 1160 us; the launch traced here: 1140 us
  waiting for transfers between devices  641 us (55%)
  matrix products  194 us (17%)
  other arithmetic  88.6 us (8%)
  Pallas kernels  75.5 us (7%)
  starting transfers between devices  65.6 us (6%)
  local copies, waits for them, and re-layouts  62.3 us (5%)
  between operations  17.7 us (2%)
    reduce_scatter x4, waiting for transfers between devices, spread(): lax.psum_scatter(narrow(value), 'dp', scatter_dimension=axis, tiled=True)  369 us
    ppermute x66, waiting for transfers between devices, flipped(): lax.ppermute(values, axis, [(i, i ^ bit) for i in range(lax.axis_size(axi...  242 us
    dot_general x32, matrix products, product_right(): lax.dot_general(left, right, (((1,), (1,)), ((), ())), preferred_element_...  89.5 us
    dot_general x28, matrix products, product(): return jnp.dot(left, right, preferred_element_type=F32)  67.3 us
    ppermute x66, starting transfers between devices, flipped(): lax.ppermute(values, axis, [(i, i ^ bit) for i in range(lax.axis_size(axi...  52.9 us
    pallas_call x4, Pallas kernels, mix_backward(): pl.pallas_call(functools.partial(backward_kernel, per), grid=(heads // pe...  50.9 us
    unnamed x352, local copies, waits for them, and re-layouts  38.9 us
    dot_general x8, matrix products, product_left(): lax.dot_general(left, right, (((0,), (0,)), ((), ())), preferred_element_...  36.7 us
  transfers between devices with their start and end apart: 76, of which 51 were waited for; matrix products, arithmetic and copies ran while one was open for 18% of the time, Pallas kernels for 3%

profile of v1, /device:TPU:0, one launch (start us, length us, event | category | flops | bytes accessed | tf_op | source)
XLA Modules:
  0.0 1144.4 jit_solution(10800638111231505623)
XLA Ops:
  16.9 9.1 collective-permute-done
  54.9 9.6 collective-permute-done.3
  69.1 8.6 collective-permute-done.4
  81.7 7.0 fusion.44
  88.7 11.6 %fusion.76 = bf16[384,2048]{1,0:T(8,128)(2,1)} fusion(bf16[1,1408,2048]{2,1,0:T(8,128)(2,1)} %param.20, bf16[384,2048]{1,0:T(8,128)(2,1)} %bitcast.880, f32[384,1408]{1,0:T(8,128)} %fusion.44, bf16[1,2,2048,1408]{3,2,1,0:T(8,128)(2,1)} %param.19), kind=kOutput, calls=%fused_computation.77 | convolution fusion | flops 4433215488 | bytes 16842752 | tf_op jit(solution)/shard_map/dot_general | solution.py:355
  106.1 9.4 collective-permute-done.7
  136.6 7.7 collective-permute-done.9
  144.5 8.2 collective-permute-done.13
  152.9 5.6 collective-permute-done.32
  171.4 7.2 shard_map.179
  192.7 8.8 collective-permute-done.12
  202.9 6.1 collective-permute-done.35
  212.2 9.5 collective-permute-done.15
  241.8 7.0 add_convert_fusion.7
  257.1 5.7 collective-permute-done.18
  266.8 12.1 %fusion.79 = bf16[384,2048]{1,0:T(8,128)(2,1)} fusion(bf16[1,1408,2048]{2,1,0:T(8,128)(2,1)} %param.20, bf16[384,2048]{1,0:T(8,128)(2,1)} %bitcast.859, f32[384,1408]{1,0:T(8,128)} %fusion.36, bf16[1,2,2048,1408]{3,2,1,0:T(8,128)(2,1)} %param.19), kind=kOutput, calls=%fused_computation.78 | convolution fusion | flops 4433215488 | bytes 16842752 | tf_op jit(solution)/shard_map/dot_general | solution.py:355
  286.4 12.8 %shard_map.180 = (bf16[3,384,512]{2,1,0:T(8,128)(2,1)S(1)}, f32[384,128]{1,0:T(8,128)S(1)}, f32[3,4,512]{2,1,0:T(4,128)}, f32[8,128]{1,0:T(8,128)}) custom-call(f32[3,384,512]{2,1,0:T(8,128)} %pad_maximum_fusion.5.qkv_ref, f32[384,4]{1,0:T(8,128)S(1)} %copy-done.18, f32[3,4,512]{2,1,0:T(4,128)S(1)} %bitcast.796, f32[1,128]{1,0:T(1,128)S(1)} %copy-done.16, ...), custom_call_target="tpu_custom_call" | custom-call | flops 4000000000 | bytes 8000000 | tf_op jit(solution)/shard_map/pallas_call | solution.py:307
  311.3 6.7 collective-permute-done.40
  324.4 8.7 collective-permute-done.41
  342.1 7.0 shard_map.183
  357.0 10.4 collective-permute-done.44
  373.6 7.9 collective-permute-done.47
  403.2 7.0 fusion.16
  410.2 8.1 add_convert_fusion.3
  420.9 7.1 multiply_convert_fusion.1
  428.0 5.5 fusion.22
  443.1 8.7 collective-permute-done.50
  451.8 7.5 collective-permute-done.27
  465.0 10.0 collective-permute-done.28
  475.3 6.3 collective-permute-done.51
  486.2 12.7 %shard_map.181 = (bf16[3,384,512]{2,1,0:T(8,128)(2,1)S(1)}, f32[384,128]{1,0:T(8,128)S(1)}, f32[3,4,512]{2,1,0:T(4,128)S(1)}, f32[8,128]{1,0:T(8,128)S(1)}) custom-call(f32[3,384,512]{2,1,0:T(8,128)} %pad_maximum_fusion.5.qkv_ref, f32[384,4]{1,0:T(8,128)S(1)} %copy-done.19, f32[3,4,512]{2,1,0:T(4,128)S(1)} %bitcast.798, f32[1,128]{1,0:T(1,128)S(1)} %copy-done.16, ...), custom_call_target="tpu_custom_call" | custom-call | flops 4000000000 | bytes 8000000 | tf_op jit(solution)/shard_map/pallas_call | solution.py:307
  507.9 13.1 %shard_map.184 = (bf16[3,384,512]{2,1,0:T(8,128)(2,1)S(1)}, f32[384,128]{1,0:T(8,128)S(1)}, f32[3,4,512]{2,1,0:T(4,128)}, f32[8,128]{1,0:T(8,128)}) custom-call(f32[3,384,512]{2,1,0:T(8,128)} %pad_maximum_fusion.7.qkv_ref, f32[384,4]{1,0:T(8,128)S(1)} %copy-done.21, f32[3,4,512]{2,1,0:T(4,128)S(1)} %bitcast.799, f32[1,128]{1,0:T(1,128)S(1)} %copy-done.16, ...), custom_call_target="tpu_custom_call" | custom-call | flops 4000000000 | bytes 8000000 | tf_op jit(solution)/shard_map/pallas_call | solution.py:307
  533.0 8.3 collective-permute-done.31
  541.3 8.0 collective-permute-done.54
  553.7 11.3 collective-permute-done.55
  566.5 8.4 collective-permute-done.56
  580.2 7.2 multiply_convert_fusion
  597.0 9.8 collective-permute-done.59
  610.3 8.9 collective-permute-done.60
  628.5 12.3 %shard_map.185 = (bf16[3,384,512]{2,1,0:T(8,128)(2,1)S(1)}, f32[384,128]{1,0:T(8,128)S(1)}, f32[3,4,512]{2,1,0:T(4,128)S(1)}, f32[8,128]{1,0:T(8,128)S(1)}) custom-call(f32[3,384,512]{2,1,0:T(8,128)} %pad_maximum_fusion.7.qkv_ref, f32[384,4]{1,0:T(8,128)S(1)} %copy-done.22, f32[3,4,512]{2,1,0:T(4,128)S(1)} %bitcast.800, f32[1,128]{1,0:T(1,128)S(1)} %copy-done.16, ...), custom_call_target="tpu_custom_call" | custom-call | flops 4000000000 | bytes 8000000 | tf_op jit(solution)/shard_map/pallas_call | solution.py:307
  653.7 9.9 convolution_convert_fusion
  675.9 7.5 fusion
  717.7 5.8 collective-permute-done.63
  726.7 6.5 collective-permute-done.67
  735.4 6.1 collective-permute-done.68
  756.5 65.2 %reduce-scatter.14.cloned.1.call-done = bf16[1408,512]{1,0:T(8,128)(2,1)} async-done(((bf16[1408,2048]{1,0:T(8,128)(2,1)}), bf16[1408,512]{1,0:T(8,128)(2,1)}) %reduce-scatter.14.cloned.1.call-update) | async-done | bytes 1441808 | tf_op jit(solution)/shard_map/reduce_scatter | solution.py:533
  825.0 109.9 %reduce-scatter.8.cloned.1.call-done = bf16[3,512,512]{2,1,0:T(8,128)(2,1)} async-done(((bf16[3,2048,512]{2,1,0:T(8,128)(2,1)}), bf16[3,512,512]{2,1,0:T(8,128)(2,1)}) %reduce-scatter.8.cloned.1.call-update) | async-done | bytes 1572880 | tf_op jit(solution)/shard_map/reduce_scatter | solution.py:533
  938.5 194.3 %reduce-scatter.12.cloned.1.call-done = bf16[2,512,1408]{2,1,0:T(8,128)(2,1)} async-done(((bf16[2,2048,1408]{2,1,0:T(8,128)(2,1)}), bf16[2,512,1408]{2,1,0:T(8,128)(2,1)}) %reduce-scatter.12.cloned.1.call-update) | async-done | bytes 2883600 | tf_op jit(solution)/shard_map/reduce_scatter | solution.py:533
  (766 shorter events, 374.7 us)
Async XLA Ops:
  7.2 708.9 %reduce-scatter.16.cloned.1.call-start = ((), (), s32[]{:S(2)}) async-start(), calls=%async_computation.9 | async-start | bytes 655360
  13.9 12.1 %collective-permute-start = (bf16[96,2048]{1,0:T(8,128)(2,1)S(1)}, bf16[96,2048]{1,0:T(8,128)(2,1)S(1)}, u32[]{:S(2)}, u32[]{:S(2)}) collective-permute-start(bf16[96,2048]{1,0:T(8,128)(2,1)S(1)} %fusion.226), channel_id=1, source_target_pairs={{0,2},{1,3},{2,0},{3,1},{4,6},{5,7},{6,4},{7,5},{8,10},{9,11},{10,... | collective-permute-start | bytes 1179656 | tf_op jit(solution)/shard_map/ppermute | solution.py:383
  53.2 11.4 collective-permute-start.3
  67.3 10.4 collective-permute-start.4
  104.3 11.2 collective-permute-start.7
  117.6 11.8 %collective-permute-start.8 = (bf16[96,2048]{1,0:T(8,128)(2,1)}, bf16[96,2048]{1,0:T(8,128)(2,1)S(1)}, u32[]{:S(2)}, u32[]{:S(2)}) collective-permute-start(bf16[96,2048]{1,0:T(8,128)(2,1)} %fusion.245), channel_id=1, source_target_pairs={{0,16},{1,17},{2,18},{3,19},{4,20},{5,21},{6,22},{7,23},{8,24},{9,... | collective-permute-start | bytes 1179656 | tf_op jit(solution)/shard_map/ppermute | solution.py:388
  132.2 12.1 %collective-permute-start.9 = (bf16[96,2048]{1,0:T(8,128)(2,1)S(1)}, bf16[96,2048]{1,0:T(8,128)(2,1)S(1)}, u32[]{:S(2)}, u32[]{:S(2)}) collective-permute-start(bf16[96,2048]{1,0:T(8,128)(2,1)S(1)} %get-tuple-element.161), channel_id=1, source_target_pairs={{0,2},{1,3},{2,0},{3,1},{4,6},{5,7},{6,4},{7,5},{8,10},{9,11},{10,... | collective-permute-start | bytes 1179656 | tf_op jit(solution)/shard_map/ppermute | solution.py:383
  133.8 19.0 %collective-permute-start.13 = (bf16[96,2048]{1,0:T(8,128)(2,1)S(1)}, bf16[96,2048]{1,0:T(8,128)(2,1)S(1)}, u32[]{:S(2)}, u32[]{:S(2)}) collective-permute-start(bf16[96,2048]{1,0:T(8,128)(2,1)S(1)} %dynamic-slice_bitcast_fusion.29), channel_id=1, source_target_pairs={{0,2},{1,3},{2,0},{3,1},{4,6},{5,7},{6,4},{7,5},{8,10},{9,11},{10,... | collective-permute-start | bytes 1179656 | tf_op jit(solution)/shard_map/ppermute | solution.py:383
  135.0 23.5 %collective-permute-start.32 = (bf16[96,2048]{1,0:T(8,128)(2,1)S(1)}, bf16[96,2048]{1,0:T(8,128)(2,1)S(1)}, u32[]{:S(2)}, u32[]{:S(2)}) collective-permute-start(bf16[96,2048]{1,0:T(8,128)(2,1)S(1)} %get-tuple-element.160), channel_id=1, source_target_pairs={{0,2},{1,3},{2,0},{3,1},{4,6},{5,7},{6,4},{7,5},{8,10},{9,11},{10,... | collective-permute-start | bytes 1179656 | tf_op jit(solution)/shard_map/ppermute | solution.py:383
  144.5 14.3 %collective-permute-start.10 = (bf16[2,96,2048]{2,1,0:T(8,128)(2,1)S(1)}, bf16[2,96,2048]{2,1,0:T(8,128)(2,1)S(1)}, u32[]{:S(2)}, u32[]{:S(2)}) collective-permute-start(bf16[2,96,2048]{2,1,0:T(8,128)(2,1)S(1)} %pad_maximum_fusion.29), channel_id=1, source_target_pairs={{0,1},{1,0},{2,3},{3,2},{4,5},{5,4},{6,7},{7,6},{8,9},{9,8},{10,11... | collective-permute-start | bytes 2359304 | tf_op jit(solution)/shard_map/ppermute | solution.py:383
  188.6 22.6 %collective-permute-start.14 = (bf16[2,96,2048]{2,1,0:T(8,128)(2,1)S(1)}, bf16[2,96,2048]{2,1,0:T(8,128)(2,1)S(1)}, u32[]{:S(2)}, u32[]{:S(2)}) collective-permute-start(bf16[2,96,2048]{2,1,0:T(8,128)(2,1)S(1)} %pad_maximum_fusion.30), channel_id=1, source_target_pairs={{0,1},{1,0},{2,3},{3,2},{4,5},{5,4},{6,7},{7,6},{8,9},{9,8},{10,11... | collective-permute-start | bytes 2359304 | tf_op jit(solution)/shard_map/ppermute | solution.py:383
  189.5 12.0 %collective-permute-start.12 = (bf16[96,2048]{1,0:T(8,128)(2,1)S(1)}, bf16[96,2048]{1,0:T(8,128)(2,1)S(1)}, u32[]{:S(2)}, u32[]{:S(2)}) collective-permute-start(bf16[96,2048]{1,0:T(8,128)(2,1)S(1)} %dynamic-slice_bitcast_fusion.26), channel_id=1, source_target_pairs={{0,2},{1,3},{2,0},{3,1},{4,6},{5,7},{6,4},{7,5},{8,10},{9,11},{10,... | collective-permute-start | bytes 1179656 | tf_op jit(solution)/shard_map/ppermute | solution.py:383
  191.4 17.6 %collective-permute-start.35 = (bf16[96,2048]{1,0:T(8,128)(2,1)S(1)}, bf16[96,2048]{1,0:T(8,128)(2,1)S(1)}, u32[]{:S(2)}, u32[]{:S(2)}) collective-permute-start(bf16[96,2048]{1,0:T(8,128)(2,1)S(1)} %dynamic-slice_bitcast_fusion.20), channel_id=1, source_target_pairs={{0,2},{1,3},{2,0},{3,1},{4,6},{5,7},{6,4},{7,5},{8,10},{9,11},{10,... | collective-permute-start | bytes 1179656 | tf_op jit(solution)/shard_map/ppermute | solution.py:383
  209.6 12.1 %collective-permute-start.15 = (bf16[96,2048]{1,0:T(8,128)(2,1)S(1)}, bf16[96,2048]{1,0:T(8,128)(2,1)S(1)}, u32[]{:S(2)}, u32[]{:S(2)}) collective-permute-start(bf16[96,2048]{1,0:T(8,128)(2,1)S(1)} %get-tuple-element.159), channel_id=1, source_target_pairs={{0,2},{1,3},{2,0},{3,1},{4,6},{5,7},{6,4},{7,5},{8,10},{9,11},{10,... | collective-permute-start | bytes 1179656 | tf_op jit(solution)/shard_map/ppermute | solution.py:383
  211.6 16.7 %collective-permute-start.36 = (bf16[96,2048]{1,0:T(8,128)(2,1)S(1)}, bf16[96,2048]{1,0:T(8,128)(2,1)S(1)}, u32[]{:S(2)}, u32[]{:S(2)}) collective-permute-start(bf16[96,2048]{1,0:T(8,128)(2,1)S(1)} %get-tuple-element.158), channel_id=1, source_target_pairs={{0,2},{1,3},{2,0},{3,1},{4,6},{5,7},{6,4},{7,5},{8,10},{9,11},{10,... | collective-permute-start | bytes 1179656 | tf_op jit(solution)/shard_map/ppermute | solution.py:383
  228.4 20.6 %collective-permute-start.37 = (bf16[2,96,2048]{2,1,0:T(8,128)(2,1)S(1)}, bf16[2,96,2048]{2,1,0:T(8,128)(2,1)S(1)}, u32[]{:S(2)}, u32[]{:S(2)}) collective-permute-start(bf16[2,96,2048]{2,1,0:T(8,128)(2,1)S(1)} %pad_maximum_fusion.36), channel_id=1, source_target_pairs={{0,1},{1,0},{2,3},{3,2},{4,5},{5,4},{6,7},{7,6},{8,9},{9,8},{10,11... | collective-permute-start | bytes 2359304 | tf_op jit(solution)/shard_map/ppermute | solution.py:383
  251.6 11.2 collective-permute-start.18
  265.3 15.0 %collective-permute-start.19 = (bf16[96,2048]{1,0:T(8,128)(2,1)}, bf16[96,2048]{1,0:T(8,128)(2,1)}, u32[]{:S(2)}, u32[]{:S(2)}) collective-permute-start(bf16[96,2048]{1,0:T(8,128)(2,1)} %fusion.340), channel_id=1, source_target_pairs={{0,2},{1,3},{2,0},{3,1},{4,6},{5,7},{6,4},{7,5},{8,10},{9,11},{10,... | collective-permute-start | bytes 1179656 | tf_op jit(solution)/shard_map/ppermute | solution.py:383
  283.6 19.7 %collective-permute-start.39 = (bf16[96,2048]{1,0:T(8,128)(2,1)}, bf16[96,2048]{1,0:T(8,128)(2,1)}, u32[]{:S(2)}, u32[]{:S(2)}) collective-permute-start(bf16[96,2048]{1,0:T(8,128)(2,1)} %dynamic-slice_bitcast_fusion.19), channel_id=1, source_target_pairs={{0,2},{1,3},{2,0},{3,1},{4,6},{5,7},{6,4},{7,5},{8,10},{9,11},{10,... | collective-permute-start | bytes 1179656 | tf_op jit(solution)/shard_map/ppermute | solution.py:383
  304.8 13.2 %collective-permute-start.40 = (bf16[96,2048]{1,0:T(8,128)(2,1)S(1)}, bf16[96,2048]{1,0:T(8,128)(2,1)S(1)}, u32[]{:S(2)}, u32[]{:S(2)}) collective-permute-start(bf16[96,2048]{1,0:T(8,128)(2,1)S(1)} %fusion.240), channel_id=1, source_target_pairs={{0,16},{1,17},{2,18},{3,19},{4,20},{5,21},{6,22},{7,23},{8,24},{9,... | collective-permute-start | bytes 1179656 | tf_op jit(solution)/shard_map/ppermute | solution.py:388
  309.8 11.0 collective-permute-start.22
  323.0 10.1 collective-permute-start.41
  335.2 18.3 %collective-permute-start.45 = (bf16[96,2048]{1,0:T(8,128)(2,1)}, bf16[96,2048]{1,0:T(8,128)(2,1)}, u32[]{:S(2)}, u32[]{:S(2)}) collective-permute-start(bf16[96,2048]{1,0:T(8,128)(2,1)} %dynamic-slice_bitcast_fusion.21), channel_id=1, source_target_pairs={{0,2},{1,3},{2,0},{3,1},{4,6},{5,7},{6,4},{7,5},{8,10},{9,11},{10,... | collective-permute-start | bytes 1179656 | tf_op jit(solution)/shard_map/ppermute | solution.py:383
  356.1 11.3 collective-permute-start.44
  356.9 14.8 %collective-permute-start.46 = (bf16[2,96,2048]{2,1,0:T(8,128)(2,1)S(1)}, bf16[2,96,2048]{2,1,0:T(8,128)(2,1)S(1)}, u32[]{:S(2)}, u32[]{:S(2)}) collective-permute-start(bf16[2,96,2048]{2,1,0:T(8,128)(2,1)S(1)} %pad_maximum_fusion.38), channel_id=1, source_target_pairs={{0,1},{1,0},{2,3},{3,2},{4,5},{5,4},{6,7},{7,6},{8,9},{9,8},{10,11... | collective-permute-start | bytes 2359304 | tf_op jit(solution)/shard_map/ppermute | solution.py:383
  371.0 10.5 collective-permute-start.47
  372.2 12.1 %collective-permute-start.23 = (bf16[96,2048]{1,0:T(8,128)(2,1)S(1)}, bf16[96,2048]{1,0:T(8,128)(2,1)S(1)}, u32[]{:S(2)}, u32[]{:S(2)}) collective-permute-start(bf16[96,2048]{1,0:T(8,128)(2,1)S(1)} %get-tuple-element.155), channel_id=1, source_target_pairs={{16,0},{17,1},{18,2},{19,3},{20,4},{21,5},{22,6},{23,7},{24,8},{25... | collective-permute-start | bytes 1179656 | tf_op jit(solution)/shard_map/ppermute | solution.py:388
  381.6 12.3 %collective-permute-start.48 = (bf16[2,96,2048]{2,1,0:T(8,128)(2,1)S(1)}, bf16[2,96,2048]{2,1,0:T(8,128)(2,1)S(1)}, u32[]{:S(2)}, u32[]{:S(2)}) collective-permute-start(bf16[2,96,2048]{2,1,0:T(8,128)(2,1)S(1)} %pad_maximum_fusion.39), channel_id=1, source_target_pairs={{0,1},{1,0},{2,3},{3,2},{4,5},{5,4},{6,7},{7,6},{8,9},{9,8},{10,11... | collective-permute-start | bytes 2359304 | tf_op jit(solution)/shard_map/ppermute | solution.py:383
  393.9 24.5 %collective-permute-start.25 = (bf16[2,96,2048]{2,1,0:T(8,128)(2,1)S(1)}, bf16[2,96,2048]{2,1,0:T(8,128)(2,1)S(1)}, u32[]{:S(2)}, u32[]{:S(2)}) collective-permute-start(bf16[2,96,2048]{2,1,0:T(8,128)(2,1)S(1)} %pad_maximum_fusion.33), channel_id=1, source_target_pairs={{0,1},{1,0},{2,3},{3,2},{4,5},{5,4},{6,7},{7,6},{8,9},{9,8},{10,11... | collective-permute-start | bytes 2359304 | tf_op jit(solution)/shard_map/ppermute | solution.py:383
  418.3 21.1 %collective-permute-start.49 = (bf16[2,96,2048]{2,1,0:T(8,128)(2,1)S(1)}, bf16[2,96,2048]{2,1,0:T(8,128)(2,1)S(1)}, u32[]{:S(2)}, u32[]{:S(2)}) collective-permute-start(bf16[2,96,2048]{2,1,0:T(8,128)(2,1)S(1)} %dynamic-slice_bitcast_fusion.3), channel_id=1, source_target_pairs={{0,1},{1,0},{2,3},{3,2},{4,5},{5,4},{6,7},{7,6},{8,9},{9,8},{10,11... | collective-permute-start | bytes 2359304 | tf_op jit(solution)/shard_map/ppermute | solution.py:383
  439.8 12.0 %collective-permute-start.50 = (bf16[96,2048]{1,0:T(8,128)(2,1)S(1)}, bf16[96,2048]{1,0:T(8,128)(2,1)S(1)}, u32[]{:S(2)}, u32[]{:S(2)}) collective-permute-start(bf16[96,2048]{1,0:T(8,128)(2,1)S(1)} %dynamic-slice_bitcast_fusion.17), channel_id=1, source_target_pairs={{0,2},{1,3},{2,0},{3,1},{4,6},{5,7},{6,4},{7,5},{8,10},{9,11},{10,... | collective-permute-start | bytes 1179656 | tf_op jit(solution)/shard_map/ppermute | solution.py:383
  441.7 17.6 %collective-permute-start.27 = (bf16[96,2048]{1,0:T(8,128)(2,1)S(1)}, bf16[96,2048]{1,0:T(8,128)(2,1)S(1)}, u32[]{:S(2)}, u32[]{:S(2)}) collective-permute-start(bf16[96,2048]{1,0:T(8,128)(2,1)S(1)} %dynamic-slice_bitcast_fusion.23), channel_id=1, source_target_pairs={{0,2},{1,3},{2,0},{3,1},{4,6},{5,7},{6,4},{7,5},{8,10},{9,11},{10,... | collective-permute-start | bytes 1179656 | tf_op jit(solution)/shard_map/ppermute | solution.py:383
  463.0 12.1 %collective-permute-start.28 = (bf16[96,2048]{1,0:T(8,128)(2,1)S(1)}, bf16[96,2048]{1,0:T(8,128)(2,1)S(1)}, u32[]{:S(2)}, u32[]{:S(2)}) collective-permute-start(bf16[96,2048]{1,0:T(8,128)(2,1)S(1)} %get-tuple-element.69), channel_id=1, source_target_pairs={{0,2},{1,3},{2,0},{3,1},{4,6},{5,7},{6,4},{7,5},{8,10},{9,11},{10,... | collective-permute-start | bytes 1179656 | tf_op jit(solution)/shard_map/ppermute | solution.py:383
  464.4 17.2 %collective-permute-start.51 = (bf16[96,2048]{1,0:T(8,128)(2,1)S(1)}, bf16[96,2048]{1,0:T(8,128)(2,1)S(1)}, u32[]{:S(2)}, u32[]{:S(2)}) collective-permute-start(bf16[96,2048]{1,0:T(8,128)(2,1)S(1)} %get-tuple-element.153), channel_id=1, source_target_pairs={{0,2},{1,3},{2,0},{3,1},{4,6},{5,7},{6,4},{7,5},{8,10},{9,11},{10,... | collective-permute-start | bytes 1179656 | tf_op jit(solution)/shard_map/ppermute | solution.py:383
  482.7 21.6 %collective-permute-start.52 = (bf16[2,96,2048]{2,1,0:T(8,128)(2,1)}, bf16[2,96,2048]{2,1,0:T(8,128)(2,1)}, u32[]{:S(2)}, u32[]{:S(2)}) collective-permute-start(bf16[2,96,2048]{2,1,0:T(8,128)(2,1)} %pad_maximum_fusion.40), channel_id=1, source_target_pairs={{0,1},{1,0},{2,3},{3,2},{4,5},{5,4},{6,7},{7,6},{8,9},{9,8},{10,11... | collective-permute-start | bytes 2359304 | tf_op jit(solution)/shard_map/ppermute | solution.py:383
  529.3 12.0 %collective-permute-start.31 = (bf16[96,2048]{1,0:T(8,128)(2,1)S(1)}, bf16[96,2048]{1,0:T(8,128)(2,1)S(1)}, u32[]{:S(2)}, u32[]{:S(2)}) collective-permute-start(bf16[96,2048]{1,0:T(8,128)(2,1)S(1)} %dynamic-slice_bitcast_fusion.22), channel_id=1, source_target_pairs={{0,2},{1,3},{2,0},{3,1},{4,6},{5,7},{6,4},{7,5},{8,10},{9,11},{10,... | collective-permute-start | bytes 1179656 | tf_op jit(solution)/shard_map/ppermute | solution.py:383
  531.5 17.7 %collective-permute-start.54 = (bf16[96,2048]{1,0:T(8,128)(2,1)S(1)}, bf16[96,2048]{1,0:T(8,128)(2,1)S(1)}, u32[]{:S(2)}, u32[]{:S(2)}) collective-permute-start(bf16[96,2048]{1,0:T(8,128)(2,1)S(1)} %dynamic-slice_bitcast_fusion.16), channel_id=1, source_target_pairs={{0,2},{1,3},{2,0},{3,1},{4,6},{5,7},{6,4},{7,5},{8,10},{9,11},{10,... | collective-permute-start | bytes 1179656 | tf_op jit(solution)/shard_map/ppermute | solution.py:383
  552.4 12.6 %collective-permute-start.55 = (bf16[96,2048]{1,0:T(8,128)(2,1)S(1)}, bf16[96,2048]{1,0:T(8,128)(2,1)S(1)}, u32[]{:S(2)}, u32[]{:S(2)}) collective-permute-start(bf16[96,2048]{1,0:T(8,128)(2,1)S(1)} %add_convert_fusion.8), channel_id=1, source_target_pairs={{16,0},{17,1},{18,2},{19,3},{20,4},{21,5},{22,6},{23,7},{24,8},{25... | collective-permute-start | bytes 1179656 | tf_op jit(solution)/shard_map/ppermute | solution.py:388
  565.0 9.9 collective-permute-start.56
  595.6 11.2 collective-permute-start.59
  608.9 10.3 collective-permute-start.60
  648.3 106.1 %reduce-scatter.10.cloned.1.call-start = ((), (), s32[]{:S(2)}) async-start(), calls=%async_computation.6 | async-start | bytes 2621440 | tf_op jit(solution)/shard_map/reduce_scatter | solution.py:533
  653.7 168.0 %reduce-scatter.14.cloned.1.call-start = ((), (), s32[]{:S(2)}) async-start(), calls=%async_computation.8 | async-start | bytes 7208960 | tf_op jit(solution)/shard_map/reduce_scatter | solution.py:533
  663.6 271.4 %reduce-scatter.8.cloned.1.call-start = ((), (), s32[]{:S(2)}) async-start(), calls=%async_computation.5 | async-start | bytes 7864320 | tf_op jit(solution)/shard_map/reduce_scatter | solution.py:533
  674.7 458.1 %reduce-scatter.12.cloned.1.call-start = ((), (), s32[]{:S(2)}) async-start(), calls=%async_computation.7 | async-start | bytes 14417920 | tf_op jit(solution)/shard_map/reduce_scatter | solution.py:533
  712.2 11.3 collective-permute-start.63
  713.4 31.2 %collective-permute-start.66 = (f32[3,4,512]{2,1,0:T(4,128)S(1)}, f32[3,4,512]{2,1,0:T(4,128)S(1)}, u32[]{:S(2)}, u32[]{:S(2)}) collective-permute-start(f32[3,4,512]{2,1,0:T(4,128)S(1)} %add.501), channel_id=1, source_target_pairs={{0,8},{4,12},{8,0},{12,4},{1,9},{5,13},{9,1},{13,5},{2,10},{6,14},... | collective-permute-start | bytes 73736 | tf_op jit(solution)/shard_map/ppermute | solution.py:383
  741.7 10.6 collective-permute-start.64
  (202 other events, 2233.8 us)
Sparse Core Ops, SparseCore 0:
  648.5 21.8 reduce-scatter.15
  673.2 42.6 reduce-scatter.9
  718.9 102.7 reduce-scatter.13
  824.0 110.9 reduce-scatter.7
  937.3 195.4 reduce-scatter.11

commit v2 on v1

--- a/solution.py
+++ b/solution.py
@@ -426,6 +426,27 @@
     return total
 
 
+def line_scatter(parts, axes):
+    count = lax.axis_size("dp")
+    me = lax.axis_index("dp")
+
+    def block(part, axis, index):
+        size = part.shape[axis] // count
+        index = jnp.clip(index, 0, count - 1)
+        return lax.dynamic_slice_in_dim(part, index * size, size, axis).astype(F32)
+
+    up = [0.0] * len(parts)
+    down = [0.0] * len(parts)
+    for step in range(1, count):
+        up = [narrow(block(p, a, count - step + me) + u) for p, a, u in zip(parts, axes, up)]
+        down = [narrow(block(p, a, step - count + me) + d) for p, a, d in zip(parts, axes, down)]
+        rising = [(i, i + 1) for i in range(count - 1) if i < step]
+        up = [lax.ppermute(u, "dp", rising).astype(F32) for u in up]
+        falling = [(count - 1 - i, count - 2 - i) for i in range(count - 1) if i < step]
+        down = [lax.ppermute(d, "dp", falling).astype(F32) for d in down]
+    return [block(p, a, me) + u + d for p, a, u, d in zip(parts, axes, up, down)]
+
+
 def per_device(
     tokens,
     lengths,
@@ -461,12 +482,12 @@
     tokens_own = [own_rows(tokens[m]) for m in every]
     cotangent_own = [own_rows(cotangent[m]) for m in every]
 
-    def forward(x, m, save):
+    def forward(x, mine):
         unit, scale = rms_parts(x)
         normed = gather(narrow(unit * gains[0]))
         qkv = jnp.stack([product(normed, projections[j]) for j in range(3)])
         logit = product(normed, gate_proj)
-        mixed, *saved = mix_forward(qkv, logit, taps, head_gain, *masks[m], save, heads)
+        mixed, *saved = mix_forward(qkv, logit, taps, head_gain, *mine, True, heads)
         middle = x + scatter(product(mixed, merge_weight))
         unit_mid, scale_mid = rms_parts(middle)
         normed_mid = gather(narrow(unit_mid * gains[1]))
@@ -477,7 +498,7 @@
         kept = (unit, scale, normed, qkv, logit, mixed, saved, unit_mid, scale_mid, normed_mid, gate_in, up_in, hidden)
         return result, kept
 
-    def backward(incoming, m, kept):
+    def backward(incoming, mine, kept, early=None):
         unit, scale, normed, qkv, logit, mixed, saved, unit_mid, scale_mid, normed_mid, gate_in, up_in, hidden = kept
         grad_out = gather(narrow(incoming))
         sigmoid_gate = jax.nn.sigmoid(gate_in)
@@ -487,11 +508,15 @@
         grad_up = narrow(grad_hidden * silu_gate)
         grad_mid = scatter(product_right(grad_gate, expand[0]) + product_right(grad_up, expand[1]))
         grad_middle = incoming + norm_back(grad_mid, unit_mid, scale_mid, gains[1])
+        spread_early = None
+        if early is not None:
+            spread_early = early(normed_mid, grad_gate, grad_up, hidden, grad_out)
+            grad_middle, spread_early = lax.optimization_barrier((grad_middle, spread_early))
         gain_two = jnp.sum(grad_mid * unit_mid, axis=0)
         grad_branch = gather(narrow(grad_middle))
         grad_mixed = product_right(grad_branch, merge_weight)
         grad_qkv, grad_logit, grad_taps, grad_head_gain = mix_backward(
-            qkv, logit, taps, head_gain, *masks[m], saved, grad_mixed, 2 if heads % 2 == 0 else 1
+            qkv, logit, taps, head_gain, *mine, saved, grad_mixed, 2 if heads % 2 == 0 else 1
         )
         grad_logit = narrow(grad_logit[:, :heads])
         grad_norm = product_right(grad_logit, gate_proj)
@@ -501,44 +526,66 @@
         grad_inputs = grad_middle + norm_back(grad_norm, unit, scale, gains[0])
         gain_one = jnp.sum(grad_norm * unit, axis=0)
         big = (normed, grad_qkv, grad_logit, mixed, grad_branch, normed_mid, grad_gate, grad_up, hidden, grad_out)
+        if early is not None:
+            big = big[:5] + spread_early
         small = (grad_taps, jnp.sum(grad_head_gain, axis=0), jnp.stack([gain_one, gain_two]))
         return grad_inputs, big, small
 
-    inputs = tokens_own
-    for turn in range(sections):
-        results = [forward(inputs[m], m, turn == sections - 1) for m in every]
-        if turn < sections - 1:
-            arrived = [shifted(narrow(result), "section", 1).astype(F32) for result, _ in results]
-            inputs = [jnp.where(section == 0, tokens_own[m], arrived[m]) for m in every]
-    kept = [k for _, k in results]
-    incoming = cotangent_own
-    for turn in range(sections):
-        results = [backward(incoming[m], m, kept[m]) for m in every]
-        if turn < sections - 1:
-            arrived = [shifted(narrow(result[0]), "section", -1).astype(F32) for result in results]
-            incoming = [jnp.where(section == sections - 1, cotangent_own[m], arrived[m]) for m in every]
-    rows_out = jnp.stack([result[0] for result in results])
+    last = sections - 1
+    zero = jnp.zeros((share, width), F32)
+    steps = micro + last
+    kept = []
+    arrived = zero
+    for step in range(steps):
+        first = tokens_own[min(step, micro - 1)]
+        inputs = jnp.where(section == 0, first, arrived)
+        mine = [jnp.where(section == 0, a, b) for a, b in zip(masks[min(step, micro - 1)], masks[max(step - last, 0)])]
+        result, saved = forward(inputs, mine)
+        kept.append((saved, mine))
+        if step < steps - 1:
+            arrived = shifted(narrow(result), "section", 1).astype(F32)
+    def joined(own, place, axis=0):
+        picked = [terms[i][0][place] for i in range(last, micro)]
+        picked.append(jnp.where(section < last, own, terms[micro][0][place]))
+        return jnp.concatenate(picked, axis=axis)
+
+    def mlp_terms(*own):
+        normed_mid, grad_gate, grad_up, hidden, grad_out = (
+            joined(own[place], 5 + place) for place in range(5)
+        )
+        grad_expand = jnp.stack([product_left(normed_mid, grad_gate), product_left(normed_mid, grad_up)])
+        return narrow(grad_expand), narrow(product_left(hidden, grad_out))
+
+    arrived = zero
+    terms = [None] * steps
+    finals = [None] * micro
+    for step in reversed(range(steps)):
+        place = step - last
+        top = cotangent_own[place] if place >= 0 else zero
+        incoming = jnp.where(section == last, top, arrived if step < micro else zero)
+        saved, mine = kept[step]
+        result, big, small = backward(incoming, mine, saved, mlp_terms if step == 0 else None)
+        terms[step] = (big, small)
+        if step < micro:
+            finals[step] = result
+        if step > 0:
+            arrived = shifted(narrow(result), "section", -1).astype(F32)
+    rows_out = jnp.stack(finals)
     half = width // sections
     moved = shifted(narrow(rows_out[:, :, half:]), "section", 1).astype(F32)
     grad_tokens = jnp.where(section == 0, rows_out[:, :, :half], moved)
 
-    def joined(place, axis=0):
-        return jnp.concatenate([result[1][place] for result in results], axis=axis)
-
-    normed, grad_qkv, grad_logit = joined(0), joined(1, 1), joined(2)
-    mixed, grad_branch, normed_mid = joined(3), joined(4), joined(5)
-    grad_gate, grad_up, hidden, grad_out = joined(6), joined(7), joined(8), joined(9)
-
-    def spread(value, axis):
-        return lax.psum_scatter(narrow(value), "dp", scatter_dimension=axis, tiled=True).astype(F32)
-
-    grad_expand = spread(jnp.stack([product_left(normed_mid, grad_gate), product_left(normed_mid, grad_up)]), 1)
-    grad_contract = spread(product_left(hidden, grad_out), 1)
-    grad_merge = spread(product_left(mixed, grad_branch), 1)
-    grad_project = spread(jnp.stack([product_left(normed, grad_qkv[j]) for j in range(3)]), 1)
-    grad_beta = spread(product_left(normed, grad_logit), 0)
+    own = terms[0][0]
+    normed, grad_qkv, grad_logit = joined(own[0], 0), joined(own[1], 1, 1), joined(own[2], 2)
+    mixed, grad_branch = joined(own[3], 3), joined(own[4], 4)
+    early = line_scatter([own[5], own[6]], [1, 1])
+    grad_project = narrow(jnp.stack([product_left(normed, grad_qkv[j]) for j in range(3)]))
+    late = [grad_project, narrow(product_left(mixed, grad_branch)), narrow(product_left(normed, grad_logit))]
+    late, early = lax.optimization_barrier((late, early))
+    grad_expand, grad_contract = early
+    grad_project, grad_merge, grad_beta = line_scatter(late, [1, 1, 0])
     grad_taps, grad_head_gain, grad_gains = (
-        sum(result[2][place] for result in results) for place in range(3)
+        sum(term[1][place] for term in terms) for place in range(3)
     )
     grad_gains = summed(jnp.concatenate([grad_gains.reshape(-1), grad_head_gain]), ("dp", "head"))
     grad_gains, grad_head_gain = grad_gains[: 2 * width].reshape(2, width), grad_gains[2 * width :]

time: 1160 us -> 1130 us (0.974)
  starting transfers between devices: 65.6 us -> 188 us
  waiting for transfers between devices: 641 us -> 536 us
  matrix products: 194 us -> 157 us
  other arithmetic: 88.6 us -> 115 us
  Pallas kernels: 75.5 us -> 57.2 us
  between operations: 17.7 us -> 4.54 us
    reduce_scatter x4 -> x0, waiting for transfers between devices: 369 us -> none  [spread(): lax.psum_scatter(narrow(value), 'dp', scatter_dimension=axis, tiled=True)]
    ppermute x0 -> x30, waiting for transfers between devices: none -> 247 us  [the longest x15 209 us: line_scatter(): up = [lax.ppermute(u, 'dp', rising).astype(F32) for u in up]]
    ppermute x0 -> x30, starting transfers between devices: none -> 128 us  [the longest x15 111 us: line_scatter(): up = [lax.ppermute(u, 'dp', rising).astype(F32) for u in up]]
    convert_element_type x28 -> x42, other arithmetic: 25.2 us -> 47.6 us  [narrow(): return values.astype(BF16)]
    dot_general x32 -> x24, matrix products: 89.5 us -> 68.3 us  [product_right(): lax.dot_general(left, right, (((1,), (1,)), ((), ())), preferred_element_...]
    pallas_call x4 -> x3, Pallas kernels: 50.9 us -> 36.1 us  [mix_backward(): pl.pallas_call(functools.partial(backward_kernel, per), grid=(heads // pe...]
    unnamed x352 -> x369, local copies, waits for them, and re-layouts: 38.9 us -> 26.4 us
    ppermute x66 -> x52, waiting for transfers between devices: 242 us -> 251 us  [flipped(): lax.ppermute(values, axis, [(i, i ^ bit) for i in range(lax.axis_size(axi...]
  transfers between devices with their start and end apart: 76 -> 87, of which waited for: 51 -> 55; matrix products, arithmetic and copies ran while one was open for 18% -> 11% of each run, Pallas kernels for 3% -> 1%
where the time goes in v2:
time: 1130 us; the launch traced here: 1120 us
  waiting for transfers between devices  536 us (47%)
  starting transfers between devices  188 us (17%)
  matrix products  157 us (14%)
  other arithmetic  115 us (10%)
  local copies, waits for them, and re-layouts  59.1 us (5%)
  Pallas kernels  57.2 us (5%)
    ppermute x52, waiting for transfers between devices, flipped(): lax.ppermute(values, axis, [(i, i ^ bit) for i in range(lax.axis_size(axi...  251 us
    ppermute x15, waiting for transfers between devices, line_scatter(): up = [lax.ppermute(u, 'dp', rising).astype(F32) for u in up]  209 us
    ppermute x15, starting transfers between devices, line_scatter(): up = [lax.ppermute(u, 'dp', rising).astype(F32) for u in up]  111 us
    dot_general x24, matrix products, product_right(): lax.dot_general(left, right, (((1,), (1,)), ((), ())), preferred_element_...  68.3 us
    dot_general x23, matrix products, product(): return jnp.dot(left, right, preferred_element_type=F32)  59.1 us
    convert_element_type x42, other arithmetic, narrow(): return values.astype(BF16)  47.6 us
    ppermute x52, starting transfers between devices, flipped(): lax.ppermute(values, axis, [(i, i ^ bit) for i in range(lax.axis_size(axi...  47.5 us
    ppermute x15, waiting for transfers between devices, line_scatter(): down = [lax.ppermute(d, 'dp', falling).astype(F32) for d in down]  38 us
  transfers between devices with their start and end apart: 87, of which 55 were waited for; matrix products, arithmetic and copies ran while one was open for 11% of the time, Pallas kernels for 1%

profile of v2, /device:TPU:0, one launch (start us, length us, event | category | flops | bytes accessed | tf_op | source)
XLA Modules:
  0.0 1117.3 jit_solution(4792970845855020005)
XLA Ops:
  11.6 9.1 collective-permute-done
  36.0 7.0 shard_map.178
  54.9 9.9 collective-permute-done.3
  68.3 8.8 collective-permute-done.4
  97.9 9.4 collective-permute-done.7
  111.2 7.8 collective-permute-done.8
  121.7 7.9 collective-permute-done.9
  138.9 7.0 shard_map.179
  152.5 9.6 collective-permute-done.12
  164.3 8.8 collective-permute-done.13
  176.2 14.7 %fusion.32 = f32[384,1408]{1,0:T(8,128)S(1)} fusion(bf16[384,2048]{1,0:T(8,128)(2,1)S(1)} %bitcast.654, bf16[1,2,2048,1408]{3,2,1,0:T(8,128)(2,1)S(1)} %bitcast.709), kind=kOutput, calls=%fused_computation.37 | convolution fusion | flops 2214592512 | bytes 9502720 | tf_op jit(solution)/shard_map/dot_general | solution.py:355
  201.8 9.6 collective-permute-done.16
  216.0 7.8 collective-permute-done.17
  226.5 7.9 collective-permute-done.18
  247.8 7.0 shard_map.180
  261.4 9.5 collective-permute-done.22
  271.3 7.3 collective-permute-done.21
  281.8 8.7 collective-permute-done.24
  291.2 6.3 fusion.6
  320.7 9.8 collective-permute-done.27
  334.2 9.0 collective-permute-done.28
  347.6 11.9 %shard_map.181 = (bf16[3,384,512]{2,1,0:T(8,128)(2,1)S(1)}, f32[384,128]{1,0:T(8,128)S(1)}, f32[3,4,512]{2,1,0:T(4,128)S(1)}, f32[8,128]{1,0:T(8,128)S(1)}) custom-call(f32[3,384,512]{2,1,0:T(8,128)} %pad_maximum_fusion.6.qkv_ref, f32[384,4]{1,0:T(8,128)S(1)} %fusion.243.logit_ref, f32[3,4,512]{2,1,0:T(4,128)S(1)} %bitcast.605, f32[1,128]{1,0:T(1,128)S(1)} %copy-done.25, ...), custom_call_target="tpu_custom_call" | custom-call | flops 4000000000 | bytes 8000000 | tf_op jit(solution)/shard_map/pallas_call | solution.py:307
  367.7 9.6 collective-permute-done.31
  381.3 11.1 collective-permute-done.32
  394.1 8.0 collective-permute-done.33
  406.8 8.9 multiply_convert_fusion.4
  430.0 9.6 collective-permute-done.36
  443.3 8.8 collective-permute-done.37
  457.6 12.3 %shard_map.182 = (bf16[3,384,512]{2,1,0:T(8,128)(2,1)S(1)}, f32[384,128]{1,0:T(8,128)S(1)}, f32[3,4,512]{2,1,0:T(4,128)S(1)}, f32[8,128]{1,0:T(8,128)S(1)}) custom-call(f32[3,384,512]{2,1,0:T(8,128)} %pad_maximum_fusion.5.qkv_ref, f32[384,4]{1,0:T(8,128)S(1)} %copy-done.30, f32[3,4,512]{2,1,0:T(4,128)S(1)} %bitcast.606, f32[1,128]{1,0:T(1,128)S(1)} %copy-done.25, ...), custom_call_target="tpu_custom_call" | custom-call | flops 4000000000 | bytes 8000000 | tf_op jit(solution)/shard_map/pallas_call | solution.py:307
  478.2 9.6 collective-permute-done.40
  492.7 10.9 collective-permute-done.41
  506.8 8.2 collective-permute-done.42
  541.7 6.5 convolution_convert_fusion
  590.9 53.2 %collective-permute-done.51 = bf16[2,512,1408]{2,1,0:T(8,128)(2,1)} collective-permute-done((bf16[2,512,1408]{2,1,0:T(8,128)(2,1)}, bf16[2,512,1408]{2,1,0:T(8,128)(2,1)}, u32[]{:S(2)}, u32[]{:S(2)}) %collective-permute-start.51) | collective-permute-done | bytes 2883616 | tf_op jit(solution)/shard_map/ppermute | solution.py:444
  674.6 12.0 %shard_map.183 = (bf16[3,384,512]{2,1,0:T(8,128)(2,1)S(1)}, f32[384,128]{1,0:T(8,128)S(1)}, f32[3,4,512]{2,1,0:T(4,128)S(1)}, f32[8,128]{1,0:T(8,128)S(1)}) custom-call(f32[3,384,512]{2,1,0:T(8,128)} %pad_maximum_fusion.4.qkv_ref, f32[384,4]{1,0:T(8,128)S(1)} %copy-done.28, f32[3,4,512]{2,1,0:T(4,128)S(1)} %bitcast.607, f32[1,128]{1,0:T(1,128)S(1)} %copy-done.26, ...), custom_call_target="tpu_custom_call" | custom-call | flops 4000000000 | bytes 8000000 | tf_op jit(solution)/shard_map/pallas_call | solution.py:307
  691.2 25.7 %collective-permute-done.52 = bf16[2,512,1408]{2,1,0:T(8,128)(2,1)} collective-permute-done((bf16[2,512,1408]{2,1,0:T(8,128)(2,1)}, bf16[2,512,1408]{2,1,0:T(8,128)(2,1)}, u32[]{:S(2)}, u32[]{:S(2)}) %collective-permute-start.52) | collective-permute-done | bytes 2883616 | tf_op jit(solution)/shard_map/ppermute | solution.py:444
  717.0 8.2 add_convert_fusion.2
  726.2 19.4 %collective-permute-done.57 = bf16[1408,512]{1,0:T(8,128)(2,1)} collective-permute-done((bf16[1408,512]{1,0:T(8,128)(2,1)}, bf16[1408,512]{1,0:T(8,128)(2,1)}, u32[]{:S(2)}, u32[]{:S(2)}) %collective-permute-start.57) | collective-permute-done | bytes 1441824 | tf_op jit(solution)/shard_map/ppermute | solution.py:444
  763.2 17.8 %collective-permute-done.58 = bf16[1408,512]{1,0:T(8,128)(2,1)S(1)} collective-permute-done((bf16[1408,512]{1,0:T(8,128)(2,1)S(1)}, bf16[1408,512]{1,0:T(8,128)(2,1)S(1)}, u32[]{:S(2)}, u32[]{:S(2)}) %collective-permute-start.58) | collective-permute-done | bytes 1441824 | tf_op jit(solution)/shard_map/ppermute | solution.py:444
  785.8 6.5 collective-permute-start.53
  813.2 67.6 %collective-permute-done.59 = bf16[1408,512]{1,0:T(8,128)(2,1)S(1)} collective-permute-done((bf16[1408,512]{1,0:T(8,128)(2,1)}, bf16[1408,512]{1,0:T(8,128)(2,1)S(1)}, u32[]{:S(2)}, u32[]{:S(2)}) %collective-permute-start.59) | collective-permute-done | bytes 1441824 | tf_op jit(solution)/shard_map/ppermute | solution.py:444
  880.7 7.9 collective-permute-done.62
  890.9 7.0 convert_add_fusion
  899.9 28.5 %collective-permute-start.63 = (bf16[3,512,512]{2,1,0:T(8,128)(2,1)}, bf16[3,512,512]{2,1,0:T(8,128)(2,1)}, u32[]{:S(2)}, u32[]{:S(2)}) collective-permute-start(bf16[3,512,512]{2,1,0:T(8,128)(2,1)} %get-tuple-element.119), channel_id=1, source_target_pairs={{0,4},{1,5},{2,6},{3,7},{16,20},{17,21},{18,22},{19,23}} | collective-permute-start | bytes 4718600 | tf_op jit(solution)/shard_map/ppermute | solution.py:444
  936.7 22.2 %collective-permute-done.63 = bf16[3,512,512]{2,1,0:T(8,128)(2,1)} collective-permute-done((bf16[3,512,512]{2,1,0:T(8,128)(2,1)}, bf16[3,512,512]{2,1,0:T(8,128)(2,1)}, u32[]{:S(2)}, u32[]{:S(2)}) %collective-permute-start.63) | collective-permute-done | bytes 1572896 | tf_op jit(solution)/shard_map/ppermute | solution.py:444
  967.6 29.7 %collective-permute-done.75 = f32[3,4,512]{2,1,0:T(4,128)S(1)} collective-permute-done((f32[3,4,512]{2,1,0:T(4,128)S(1)}, f32[3,4,512]{2,1,0:T(4,128)S(1)}, u32[]{:S(2)}, u32[]{:S(2)}) %collective-permute-start.75) | collective-permute-done | bytes 24608 | tf_op jit(solution)/shard_map/ppermute | solution.py:383
  1045.1 23.6 %collective-permute-start.71 = (bf16[512,4]{0,1:T(4,128)(2,1)S(1)}, bf16[512,4]{0,1:T(4,128)(2,1)S(1)}, u32[]{:S(2)}, u32[]{:S(2)}) collective-permute-start(bf16[512,4]{0,1:T(4,128)(2,1)S(1)} %get-tuple-element.190), channel_id=1, source_target_pairs={{0,4},{4,8},{8,12},{1,5},{5,9},{9,13},{2,6},{6,10},{10,14},{3,7},{... | collective-permute-start | bytes 12296 | tf_op jit(solution)/shard_map/ppermute | solution.py:444
  1079.5 30.1 %collective-permute-done.74 = bf16[512,4]{0,1:T(4,128)(2,1)S(1)} collective-permute-done((bf16[512,4]{0,1:T(4,128)(2,1)S(1)}, bf16[512,4]{0,1:T(4,128)(2,1)S(1)}, u32[]{:S(2)}, u32[]{:S(2)}) %collective-permute-start.74) | collective-permute-done | bytes 4128 | tf_op jit(solution)/shard_map/ppermute | solution.py:446
  (786 shorter events, 455.0 us)
Async XLA Ops:
  8.6 12.1 %collective-permute-start = (bf16[96,2048]{1,0:T(8,128)(2,1)S(1)}, bf16[96,2048]{1,0:T(8,128)(2,1)S(1)}, u32[]{:S(2)}, u32[]{:S(2)}) collective-permute-start(bf16[96,2048]{1,0:T(8,128)(2,1)S(1)} %multiply_convert_fusion.14), channel_id=1, source_target_pairs={{0,2},{1,3},{2,0},{3,1},{4,6},{5,7},{6,4},{7,5},{8,10},{9,11},{10,... | collective-permute-start | bytes 1179656 | tf_op jit(solution)/shard_map/ppermute | solution.py:383
  53.1 11.7 %collective-permute-start.3 = (bf16[96,2048]{1,0:T(8,128)(2,1)}, bf16[96,2048]{1,0:T(8,128)(2,1)}, u32[]{:S(2)}, u32[]{:S(2)}) collective-permute-start(bf16[96,2048]{1,0:T(8,128)(2,1)} %dynamic-slice_bitcast_fusion.21), channel_id=1, source_target_pairs={{0,2},{1,3},{2,0},{3,1},{4,6},{5,7},{6,4},{7,5},{8,10},{9,11},{10,... | collective-permute-start | bytes 1179656 | tf_op jit(solution)/shard_map/ppermute | solution.py:383
  107.5 11.5 %collective-permute-start.8 = (bf16[96,2048]{1,0:T(8,128)(2,1)S(1)}, bf16[96,2048]{1,0:T(8,128)(2,1)S(1)}, u32[]{:S(2)}, u32[]{:S(2)}) collective-permute-start(bf16[96,2048]{1,0:T(8,128)(2,1)S(1)} %fusion.204), channel_id=1, source_target_pairs={{0,16},{1,17},{2,18},{3,19},{4,20},{5,21},{6,22},{7,23},{8,24},{9,... | collective-permute-start | bytes 1179656 | tf_op jit(solution)/shard_map/ppermute | solution.py:388
  150.9 11.2 %collective-permute-start.12 = (bf16[96,2048]{1,0:T(8,128)(2,1)S(1)}, bf16[96,2048]{1,0:T(8,128)(2,1)S(1)}, u32[]{:S(2)}, u32[]{:S(2)}) collective-permute-start(bf16[96,2048]{1,0:T(8,128)(2,1)S(1)} %dynamic-slice_bitcast_fusion.19), channel_id=1, source_target_pairs={{0,2},{1,3},{2,0},{3,1},{4,6},{5,7},{6,4},{7,5},{8,10},{9,11},{10,... | collective-permute-start | bytes 1179656 | tf_op jit(solution)/shard_map/ppermute | solution.py:383
  211.6 12.2 %collective-permute-start.17 = (bf16[96,2048]{1,0:T(8,128)(2,1)S(1)}, bf16[96,2048]{1,0:T(8,128)(2,1)S(1)}, u32[]{:S(2)}, u32[]{:S(2)}) collective-permute-start(bf16[96,2048]{1,0:T(8,128)(2,1)S(1)} %fusion.201), channel_id=1, source_target_pairs={{0,16},{1,17},{2,18},{3,19},{4,20},{5,21},{6,22},{7,23},{8,24},{9,... | collective-permute-start | bytes 1179656 | tf_op jit(solution)/shard_map/ppermute | solution.py:388
  258.9 12.0 %collective-permute-start.22 = (bf16[96,2048]{1,0:T(8,128)(2,1)S(1)}, bf16[96,2048]{1,0:T(8,128)(2,1)S(1)}, u32[]{:S(2)}, u32[]{:S(2)}) collective-permute-start(bf16[96,2048]{1,0:T(8,128)(2,1)S(1)} %bitcast_convert_fusion), channel_id=1, source_target_pairs={{0,2},{1,3},{2,0},{3,1},{4,6},{5,7},{6,4},{7,5},{8,10},{9,11},{10,... | collective-permute-start | bytes 1179656 | tf_op jit(solution)/shard_map/ppermute | solution.py:383
  260.9 17.7 %collective-permute-start.21 = (bf16[96,2048]{1,0:T(8,128)(2,1)S(1)}, bf16[96,2048]{1,0:T(8,128)(2,1)S(1)}, u32[]{:S(2)}, u32[]{:S(2)}) collective-permute-start(bf16[96,2048]{1,0:T(8,128)(2,1)S(1)} %dynamic-slice_bitcast_fusion.17), channel_id=1, source_target_pairs={{0,2},{1,3},{2,0},{3,1},{4,6},{5,7},{6,4},{7,5},{8,10},{9,11},{10,... | collective-permute-start | bytes 1179656 | tf_op jit(solution)/shard_map/ppermute | solution.py:383
  319.1 11.5 %collective-permute-start.27 = (bf16[96,2048]{1,0:T(8,128)(2,1)S(1)}, bf16[96,2048]{1,0:T(8,128)(2,1)S(1)}, u32[]{:S(2)}, u32[]{:S(2)}) collective-permute-start(bf16[96,2048]{1,0:T(8,128)(2,1)S(1)} %dynamic-slice_bitcast_fusion.16), channel_id=1, source_target_pairs={{0,2},{1,3},{2,0},{3,1},{4,6},{5,7},{6,4},{7,5},{8,10},{9,11},{10,... | collective-permute-start | bytes 1179656 | tf_op jit(solution)/shard_map/ppermute | solution.py:383
  366.1 11.2 %collective-permute-start.31 = (bf16[96,2048]{1,0:T(8,128)(2,1)S(1)}, bf16[96,2048]{1,0:T(8,128)(2,1)S(1)}, u32[]{:S(2)}, u32[]{:S(2)}) collective-permute-start(bf16[96,2048]{1,0:T(8,128)(2,1)S(1)} %dynamic-slice_bitcast_fusion.15), channel_id=1, source_target_pairs={{0,2},{1,3},{2,0},{3,1},{4,6},{5,7},{6,4},{7,5},{8,10},{9,11},{10,... | collective-permute-start | bytes 1179656 | tf_op jit(solution)/shard_map/ppermute | solution.py:383
  380.0 12.4 %collective-permute-start.32 = (bf16[96,2048]{1,0:T(8,128)(2,1)S(1)}, bf16[96,2048]{1,0:T(8,128)(2,1)S(1)}, u32[]{:S(2)}, u32[]{:S(2)}) collective-permute-start(bf16[96,2048]{1,0:T(8,128)(2,1)S(1)} %add_convert_fusion.22), channel_id=1, source_target_pairs={{16,0},{17,1},{18,2},{19,3},{20,4},{21,5},{22,6},{23,7},{24,8},{25... | collective-permute-start | bytes 1179656 | tf_op jit(solution)/shard_map/ppermute | solution.py:388
  428.4 11.2 %collective-permute-start.36 = (bf16[96,2048]{1,0:T(8,128)(2,1)S(1)}, bf16[96,2048]{1,0:T(8,128)(2,1)S(1)}, u32[]{:S(2)}, u32[]{:S(2)}) collective-permute-start(bf16[96,2048]{1,0:T(8,128)(2,1)S(1)} %dynamic-slice_bitcast_fusion.14), channel_id=1, source_target_pairs={{0,2},{1,3},{2,0},{3,1},{4,6},{5,7},{6,4},{7,5},{8,10},{9,11},{10,... | collective-permute-start | bytes 1179656 | tf_op jit(solution)/shard_map/ppermute | solution.py:383
  476.6 11.2 %collective-permute-start.40 = (bf16[96,2048]{1,0:T(8,128)(2,1)S(1)}, bf16[96,2048]{1,0:T(8,128)(2,1)S(1)}, u32[]{:S(2)}, u32[]{:S(2)}) collective-permute-start(bf16[96,2048]{1,0:T(8,128)(2,1)S(1)} %dynamic-slice_bitcast_fusion.13), channel_id=1, source_target_pairs={{0,2},{1,3},{2,0},{3,1},{4,6},{5,7},{6,4},{7,5},{8,10},{9,11},{10,... | collective-permute-start | bytes 1179656 | tf_op jit(solution)/shard_map/ppermute | solution.py:383
  491.5 12.2 %collective-permute-start.41 = (bf16[96,2048]{1,0:T(8,128)(2,1)S(1)}, bf16[96,2048]{1,0:T(8,128)(2,1)S(1)}, u32[]{:S(2)}, u32[]{:S(2)}) collective-permute-start(bf16[96,2048]{1,0:T(8,128)(2,1)S(1)} %get-tuple-element.101), channel_id=1, source_target_pairs={{16,0},{17,1},{18,2},{19,3},{20,4},{21,5},{22,6},{23,7},{24,8},{25... | collective-permute-start | bytes 1179656 | tf_op jit(solution)/shard_map/ppermute | solution.py:388
  541.6 17.5 %collective-permute-start.44 = (bf16[2,96,2048]{2,1,0:T(8,128)(2,1)S(1)}, bf16[2,96,2048]{2,1,0:T(8,128)(2,1)S(1)}, u32[]{:S(2)}, u32[]{:S(2)}) collective-permute-start(bf16[2,96,2048]{2,1,0:T(8,128)(2,1)S(1)} %dynamic-slice_bitcast_fusion.1), channel_id=1, source_target_pairs={{0,1},{1,0},{2,3},{3,2},{4,5},{5,4},{6,7},{7,6},{8,9},{9,8},{10,11... | collective-permute-start | bytes 2359304 | tf_op jit(solution)/shard_map/ppermute | solution.py:383
  559.4 11.6 %collective-permute-start.45 = (bf16[96,2048]{1,0:T(8,128)(2,1)S(1)}, bf16[96,2048]{1,0:T(8,128)(2,1)S(1)}, u32[]{:S(2)}, u32[]{:S(2)}) collective-permute-start(bf16[96,2048]{1,0:T(8,128)(2,1)S(1)} %dynamic-slice_bitcast_fusion.12), channel_id=1, source_target_pairs={{0,2},{1,3},{2,0},{3,1},{4,6},{5,7},{6,4},{7,5},{8,10},{9,11},{10,... | collective-permute-start | bytes 1179656 | tf_op jit(solution)/shard_map/ppermute | solution.py:383
  578.7 65.4 %collective-permute-start.51 = (bf16[2,512,1408]{2,1,0:T(8,128)(2,1)}, bf16[2,512,1408]{2,1,0:T(8,128)(2,1)}, u32[]{:S(2)}, u32[]{:S(2)}) collective-permute-start(bf16[2,512,1408]{2,1,0:T(8,128)(2,1)} %get-tuple-element.115), channel_id=1, source_target_pairs={{0,4},{1,5},{2,6},{3,7},{16,20},{17,21},{18,22},{19,23}} | collective-permute-start | bytes 8650760 | tf_op jit(solution)/shard_map/ppermute | solution.py:444
  586.8 68.5 %collective-permute-start.46 = (bf16[96,2048]{1,0:T(8,128)(2,1)S(1)}, bf16[96,2048]{1,0:T(8,128)(2,1)S(1)}, u32[]{:S(2)}, u32[]{:S(2)}) collective-permute-start(bf16[96,2048]{1,0:T(8,128)(2,1)S(1)} %convert_element_type.781), channel_id=1, source_target_pairs={{0,2},{1,3},{2,0},{3,1},{4,6},{5,7},{6,4},{7,5},{8,10},{9,11},{10,... | collective-permute-start | bytes 1179656 | tf_op jit(solution)/shard_map/ppermute | solution.py:383
  588.3 102.9 %collective-permute-start.54 = (bf16[2,512,1408]{2,1,0:T(8,128)(2,1)}, bf16[2,512,1408]{2,1,0:T(8,128)(2,1)}, u32[]{:S(2)}, u32[]{:S(2)}) collective-permute-start(bf16[2,512,1408]{2,1,0:T(8,128)(2,1)} %get-tuple-element.116), channel_id=1, source_target_pairs={{12,8},{13,9},{14,10},{15,11},{28,24},{29,25},{30,26},{31,27}} | collective-permute-start | bytes 8650760 | tf_op jit(solution)/shard_map/ppermute | solution.py:446
  649.1 67.9 %collective-permute-start.52 = (bf16[2,512,1408]{2,1,0:T(8,128)(2,1)}, bf16[2,512,1408]{2,1,0:T(8,128)(2,1)}, u32[]{:S(2)}, u32[]{:S(2)}) collective-permute-start(bf16[2,512,1408]{2,1,0:T(8,128)(2,1)} %add_convert_fusion.3), channel_id=1, source_target_pairs={{0,4},{4,8},{1,5},{5,9},{2,6},{6,10},{3,7},{7,11},{16,20},{20,24},... | collective-permute-start | bytes 8650760 | tf_op jit(solution)/shard_map/ppermute | solution.py:444
  657.1 13.2 %collective-permute-start.47 = (bf16[2,96,2048]{2,1,0:T(8,128)(2,1)}, bf16[2,96,2048]{2,1,0:T(8,128)(2,1)}, u32[]{:S(2)}, u32[]{:S(2)}) collective-permute-start(bf16[2,96,2048]{2,1,0:T(8,128)(2,1)} %pad_maximum_fusion.34), channel_id=1, source_target_pairs={{0,1},{1,0},{2,3},{3,2},{4,5},{5,4},{6,7},{7,6},{8,9},{9,8},{10,11... | collective-permute-start | bytes 2359304 | tf_op jit(solution)/shard_map/ppermute | solution.py:383
  666.2 79.4 %collective-permute-start.57 = (bf16[1408,512]{1,0:T(8,128)(2,1)}, bf16[1408,512]{1,0:T(8,128)(2,1)}, u32[]{:S(2)}, u32[]{:S(2)}) collective-permute-start(bf16[1408,512]{1,0:T(8,128)(2,1)} %get-tuple-element.123), channel_id=1, source_target_pairs={{0,4},{1,5},{2,6},{3,7},{16,20},{17,21},{18,22},{19,23}} | collective-permute-start | bytes 4325384 | tf_op jit(solution)/shard_map/ppermute | solution.py:444
  668.5 94.7 %collective-permute-start.60 = (bf16[1408,512]{1,0:T(8,128)(2,1)}, bf16[1408,512]{1,0:T(8,128)(2,1)}, u32[]{:S(2)}, u32[]{:S(2)}) collective-permute-start(bf16[1408,512]{1,0:T(8,128)(2,1)} %get-tuple-element.124), channel_id=1, source_target_pairs={{12,8},{13,9},{14,10},{15,11},{28,24},{29,25},{30,26},{31,27}} | collective-permute-start | bytes 4325384 | tf_op jit(solution)/shard_map/ppermute | solution.py:446
  725.2 67.0 %collective-permute-start.55 = (bf16[2,512,1408]{2,1,0:T(8,128)(2,1)}, bf16[2,512,1408]{2,1,0:T(8,128)(2,1)S(1)}, u32[]{:S(2)}, u32[]{:S(2)}) collective-permute-start(bf16[2,512,1408]{2,1,0:T(8,128)(2,1)} %get-tuple-element.114), channel_id=1, source_target_pairs={{12,8},{8,4},{13,9},{9,5},{14,10},{10,6},{15,11},{11,7},{28,24},{2... | collective-permute-start | bytes 8650760 | tf_op jit(solution)/shard_map/ppermute | solution.py:446
  747.5 33.4 %collective-permute-start.58 = (bf16[1408,512]{1,0:T(8,128)(2,1)S(1)}, bf16[1408,512]{1,0:T(8,128)(2,1)S(1)}, u32[]{:S(2)}, u32[]{:S(2)}) collective-permute-start(bf16[1408,512]{1,0:T(8,128)(2,1)S(1)} %add_convert_fusion.17), channel_id=1, source_target_pairs={{0,4},{4,8},{1,5},{5,9},{2,6},{6,10},{3,7},{7,11},{16,20},{20,24},... | collective-permute-start | bytes 4325384 | tf_op jit(solution)/shard_map/ppermute | solution.py:444
  784.6 16.8 %collective-permute-start.61 = (bf16[1408,512]{1,0:T(8,128)(2,1)S(1)}, bf16[1408,512]{1,0:T(8,128)(2,1)S(1)}, u32[]{:S(2)}, u32[]{:S(2)}) collective-permute-start(bf16[1408,512]{1,0:T(8,128)(2,1)S(1)} %get-tuple-element.122), channel_id=1, source_target_pairs={{12,8},{8,4},{13,9},{9,5},{14,10},{10,6},{15,11},{11,7},{28,24},{2... | collective-permute-start | bytes 4325384 | tf_op jit(solution)/shard_map/ppermute | solution.py:446
  785.8 105.1 %collective-permute-start.53 = (bf16[2,512,1408]{2,1,0:T(8,128)(2,1)}, bf16[2,512,1408]{2,1,0:T(8,128)(2,1)}, u32[]{:S(2)}, u32[]{:S(2)}) collective-permute-start(bf16[2,512,1408]{2,1,0:T(8,128)(2,1)} %get-tuple-element.113), channel_id=1, source_target_pairs={{0,4},{4,8},{8,12},{1,5},{5,9},{9,13},{2,6},{6,10},{10,14},{3,7},{... | collective-permute-start | bytes 8650760 | tf_op jit(solution)/shard_map/ppermute | solution.py:444
  794.7 96.1 %collective-permute-start.56 = (bf16[2,512,1408]{2,1,0:T(8,128)(2,1)S(1)}, bf16[2,512,1408]{2,1,0:T(8,128)(2,1)}, u32[]{:S(2)}, u32[]{:S(2)}) collective-permute-start(bf16[2,512,1408]{2,1,0:T(8,128)(2,1)S(1)} %add_convert_fusion), channel_id=1, source_target_pairs={{12,8},{8,4},{4,0},{13,9},{9,5},{5,1},{14,10},{10,6},{6,2},{15,11}... | collective-permute-start | bytes 8650760 | tf_op jit(solution)/shard_map/ppermute | solution.py:446
  796.6 84.1 %collective-permute-start.59 = (bf16[1408,512]{1,0:T(8,128)(2,1)}, bf16[1408,512]{1,0:T(8,128)(2,1)S(1)}, u32[]{:S(2)}, u32[]{:S(2)}) collective-permute-start(bf16[1408,512]{1,0:T(8,128)(2,1)} %get-tuple-element.121), channel_id=1, source_target_pairs={{0,4},{4,8},{8,12},{1,5},{5,9},{9,13},{2,6},{6,10},{10,14},{3,7},{... | collective-permute-start | bytes 4325384 | tf_op jit(solution)/shard_map/ppermute | solution.py:444
  802.0 86.6 %collective-permute-start.62 = (bf16[1408,512]{1,0:T(8,128)(2,1)S(1)}, bf16[1408,512]{1,0:T(8,128)(2,1)S(1)}, u32[]{:S(2)}, u32[]{:S(2)}) collective-permute-start(bf16[1408,512]{1,0:T(8,128)(2,1)S(1)} %add_convert_fusion.14), channel_id=1, source_target_pairs={{12,8},{8,4},{4,0},{13,9},{9,5},{5,1},{14,10},{10,6},{6,2},{15,11}... | collective-permute-start | bytes 4325384 | tf_op jit(solution)/shard_map/ppermute | solution.py:446
  899.9 59.0 %collective-permute-start.63 = (bf16[3,512,512]{2,1,0:T(8,128)(2,1)}, bf16[3,512,512]{2,1,0:T(8,128)(2,1)}, u32[]{:S(2)}, u32[]{:S(2)}) collective-permute-start(bf16[3,512,512]{2,1,0:T(8,128)(2,1)} %get-tuple-element.119), channel_id=1, source_target_pairs={{0,4},{1,5},{2,6},{3,7},{16,20},{17,21},{18,22},{19,23}} | collective-permute-start | bytes 4718600 | tf_op jit(solution)/shard_map/ppermute | solution.py:444
  935.8 75.4 %collective-permute-start.66 = (bf16[3,512,512]{2,1,0:T(8,128)(2,1)}, bf16[3,512,512]{2,1,0:T(8,128)(2,1)S(1)}, u32[]{:S(2)}, u32[]{:S(2)}) collective-permute-start(bf16[3,512,512]{2,1,0:T(8,128)(2,1)} %get-tuple-element.120), channel_id=1, source_target_pairs={{12,8},{13,9},{14,10},{15,11},{28,24},{29,25},{30,26},{31,27}} | collective-permute-start | bytes 4718600 | tf_op jit(solution)/shard_map/ppermute | solution.py:446
  961.3 50.0 %collective-permute-start.64 = (bf16[3,512,512]{2,1,0:T(8,128)(2,1)S(1)}, bf16[3,512,512]{2,1,0:T(8,128)(2,1)S(1)}, u32[]{:S(2)}, u32[]{:S(2)}) collective-permute-start(bf16[3,512,512]{2,1,0:T(8,128)(2,1)S(1)} %add_convert_fusion.7), channel_id=1, source_target_pairs={{0,4},{4,8},{1,5},{5,9},{2,6},{6,10},{3,7},{7,11},{16,20},{20,24},... | collective-permute-start | bytes 4718600 | tf_op jit(solution)/shard_map/ppermute | solution.py:444
  966.0 31.4 %collective-permute-start.49 = (bf16[96,2048]{1,0:T(8,128)(2,1)S(1)}, bf16[96,2048]{1,0:T(8,128)(2,1)S(1)}, u32[]{:S(2)}, u32[]{:S(2)}) collective-permute-start(bf16[96,2048]{1,0:T(8,128)(2,1)S(1)} %dynamic-slice_bitcast_fusion.11), channel_id=1, source_target_pairs={{0,2},{1,3},{2,0},{3,1},{4,6},{5,7},{6,4},{7,5},{8,10},{9,11},{10,... | collective-permute-start | bytes 1179656 | tf_op jit(solution)/shard_map/ppermute | solution.py:383
  967.5 29.8 %collective-permute-start.75 = (f32[3,4,512]{2,1,0:T(4,128)S(1)}, f32[3,4,512]{2,1,0:T(4,128)S(1)}, u32[]{:S(2)}, u32[]{:S(2)}) collective-permute-start(f32[3,4,512]{2,1,0:T(4,128)S(1)} %add_add_fusion), channel_id=1, source_target_pairs={{0,4},{4,0},{8,12},{12,8},{1,5},{5,1},{9,13},{13,9},{2,6},{6,2},{1... | collective-permute-start | bytes 73736 | tf_op jit(solution)/shard_map/ppermute | solution.py:383
  1003.0 11.4 %collective-permute-start.78 = (f32[4224]{0:T(1024)S(1)}, f32[4224]{0:T(1024)S(1)}, u32[]{:S(2)}, u32[]{:S(2)}) collective-permute-start(f32[4224]{0:T(1024)S(1)} %fusion.268), channel_id=1, source_target_pairs={{0,8},{4,12},{8,0},{12,4},{1,9},{5,13},{9,1},{13,5},{2,10},{6,14},... | collective-permute-start | bytes 50696 | tf_op jit(solution)/shard_map/ppermute | solution.py:383
  1013.5 26.0 %collective-permute-start.67 = (bf16[3,512,512]{2,1,0:T(8,128)(2,1)S(1)}, bf16[3,512,512]{2,1,0:T(8,128)(2,1)S(1)}, u32[]{:S(2)}, u32[]{:S(2)}) collective-permute-start(bf16[3,512,512]{2,1,0:T(8,128)(2,1)S(1)} %get-tuple-element.118), channel_id=1, source_target_pairs={{12,8},{8,4},{13,9},{9,5},{14,10},{10,6},{15,11},{11,7},{28,24},{2... | collective-permute-start | bytes 4718600 | tf_op jit(solution)/shard_map/ppermute | solution.py:446
  1014.5 19.1 %collective-permute-start.84 = (bf16[512,512]{1,0:T(8,128)(2,1)S(1)}, bf16[512,512]{1,0:T(8,128)(2,1)S(1)}, u32[]{:S(2)}, u32[]{:S(2)}) collective-permute-start(bf16[512,512]{1,0:T(8,128)(2,1)S(1)} %get-tuple-element.138), channel_id=1, source_target_pairs={{12,8},{13,9},{14,10},{15,11},{28,24},{29,25},{30,26},{31,27}} | collective-permute-start | bytes 1572872 | tf_op jit(solution)/shard_map/ppermute | solution.py:446
  1018.1 15.6 %collective-permute-start.82 = (bf16[512,512]{1,0:T(8,128)(2,1)S(1)}, bf16[512,512]{1,0:T(8,128)(2,1)S(1)}, u32[]{:S(2)}, u32[]{:S(2)}) collective-permute-start(bf16[512,512]{1,0:T(8,128)(2,1)S(1)} %add_convert_fusion.21), channel_id=1, source_target_pairs={{0,4},{4,8},{1,5},{5,9},{2,6},{6,10},{3,7},{7,11},{16,20},{20,24},... | collective-permute-start | bytes 1572872 | tf_op jit(solution)/shard_map/ppermute | solution.py:444
  1027.8 15.8 %collective-permute-start.72 = (bf16[512,4]{0,1:T(4,128)(2,1)S(1)}, bf16[512,4]{0,1:T(4,128)(2,1)S(1)}, u32[]{:S(2)}, u32[]{:S(2)}) collective-permute-start(bf16[512,4]{0,1:T(4,128)(2,1)S(1)} %get-tuple-element.193), channel_id=1, source_target_pairs={{12,8},{13,9},{14,10},{15,11},{28,24},{29,25},{30,26},{31,27}} | collective-permute-start | bytes 12296 | tf_op jit(solution)/shard_map/ppermute | solution.py:446
  1029.3 15.8 %collective-permute-start.70 = (bf16[512,4]{0,1:T(4,128)(2,1)S(1)}, bf16[512,4]{0,1:T(4,128)(2,1)S(1)}, u32[]{:S(2)}, u32[]{:S(2)}) collective-permute-start(bf16[512,4]{0,1:T(4,128)(2,1)S(1)} %add_convert_fusion.26), channel_id=1, source_target_pairs={{0,4},{4,8},{1,5},{5,9},{2,6},{6,10},{3,7},{7,11},{16,20},{20,24},... | collective-permute-start | bytes 12296 | tf_op jit(solution)/shard_map/ppermute | solution.py:444
  1035.1 33.6 %collective-permute-start.85 = (bf16[512,512]{1,0:T(8,128)(2,1)}, bf16[512,512]{1,0:T(8,128)(2,1)S(1)}, u32[]{:S(2)}, u32[]{:S(2)}) collective-permute-start(bf16[512,512]{1,0:T(8,128)(2,1)} %get-tuple-element.136), channel_id=1, source_target_pairs={{12,8},{8,4},{13,9},{9,5},{14,10},{10,6},{15,11},{11,7},{28,24},{2... | collective-permute-start | bytes 1572872 | tf_op jit(solution)/shard_map/ppermute | solution.py:446
  1035.8 76.7 %collective-permute-start.65 = (bf16[3,512,512]{2,1,0:T(8,128)(2,1)}, bf16[3,512,512]{2,1,0:T(8,128)(2,1)}, u32[]{:S(2)}, u32[]{:S(2)}) collective-permute-start(bf16[3,512,512]{2,1,0:T(8,128)(2,1)} %get-tuple-element.117), channel_id=1, source_target_pairs={{0,4},{4,8},{8,12},{1,5},{5,9},{9,13},{2,6},{6,10},{10,14},{3,7},{... | collective-permute-start | bytes 4718600 | tf_op jit(solution)/shard_map/ppermute | solution.py:444
  1041.2 71.3 %collective-permute-start.68 = (bf16[3,512,512]{2,1,0:T(8,128)(2,1)}, bf16[3,512,512]{2,1,0:T(8,128)(2,1)}, u32[]{:S(2)}, u32[]{:S(2)}) collective-permute-start(bf16[3,512,512]{2,1,0:T(8,128)(2,1)} %add_convert_fusion.4), channel_id=1, source_target_pairs={{12,8},{8,4},{4,0},{13,9},{9,5},{5,1},{14,10},{10,6},{6,2},{15,11}... | collective-permute-start | bytes 4718600 | tf_op jit(solution)/shard_map/ppermute | solution.py:446
  1043.6 26.9 %collective-permute-start.50 = (bf16[2,96,1024]{2,1,0:T(8,128)(2,1)}, bf16[2,96,1024]{2,1,0:T(8,128)(2,1)S(1)}, u32[]{:S(2)}, u32[]{:S(2)}) collective-permute-start(bf16[2,96,1024]{2,1,0:T(8,128)(2,1)} %fusion.195), channel_id=1, source_target_pairs={{0,16},{1,17},{2,18},{3,19},{4,20},{5,21},{6,22},{7,23},{8,24},{9,... | collective-permute-start | bytes 1179656 | tf_op jit(solution)/shard_map/ppermute | solution.py:388
  1045.1 32.2 %collective-permute-start.71 = (bf16[512,4]{0,1:T(4,128)(2,1)S(1)}, bf16[512,4]{0,1:T(4,128)(2,1)S(1)}, u32[]{:S(2)}, u32[]{:S(2)}) collective-permute-start(bf16[512,4]{0,1:T(4,128)(2,1)S(1)} %get-tuple-element.190), channel_id=1, source_target_pairs={{0,4},{4,8},{8,12},{1,5},{5,9},{9,13},{2,6},{6,10},{10,14},{3,7},{... | collective-permute-start | bytes 12296 | tf_op jit(solution)/shard_map/ppermute | solution.py:444
  1070.5 39.7 %collective-permute-start.83 = (bf16[512,512]{1,0:T(8,128)(2,1)}, bf16[512,512]{1,0:T(8,128)(2,1)S(1)}, u32[]{:S(2)}, u32[]{:S(2)}) collective-permute-start(bf16[512,512]{1,0:T(8,128)(2,1)} %get-tuple-element.135), channel_id=1, source_target_pairs={{0,4},{4,8},{8,12},{1,5},{5,9},{9,13},{2,6},{6,10},{10,14},{3,7},{... | collective-permute-start | bytes 1572872 | tf_op jit(solution)/shard_map/ppermute | solution.py:444
  1075.9 34.3 %collective-permute-start.86 = (bf16[512,512]{1,0:T(8,128)(2,1)S(1)}, bf16[512,512]{1,0:T(8,128)(2,1)S(1)}, u32[]{:S(2)}, u32[]{:S(2)}) collective-permute-start(bf16[512,512]{1,0:T(8,128)(2,1)S(1)} %add_convert_fusion.18), channel_id=1, source_target_pairs={{12,8},{8,4},{4,0},{13,9},{9,5},{5,1},{14,10},{10,6},{6,2},{15,11}... | collective-permute-start | bytes 1572872 | tf_op jit(solution)/shard_map/ppermute | solution.py:446
  1077.3 32.4 %collective-permute-start.74 = (bf16[512,4]{0,1:T(4,128)(2,1)S(1)}, bf16[512,4]{0,1:T(4,128)(2,1)S(1)}, u32[]{:S(2)}, u32[]{:S(2)}) collective-permute-start(bf16[512,4]{0,1:T(4,128)(2,1)S(1)} %add_convert_fusion.23), channel_id=1, source_target_pairs={{12,8},{8,4},{4,0},{13,9},{9,5},{5,1},{14,10},{10,6},{6,2},{15,11}... | collective-permute-start | bytes 12296 | tf_op jit(solution)/shard_map/ppermute | solution.py:446
  (223 other events, 2690.7 us)

commit v3 on v2

--- a/solution.py
+++ b/solution.py
@@ -426,25 +426,20 @@
     return total
 
 
-def line_scatter(parts, axes):
+def swapped(shard):
     count = lax.axis_size("dp")
     me = lax.axis_index("dp")
-
-    def block(part, axis, index):
-        size = part.shape[axis] // count
-        index = jnp.clip(index, 0, count - 1)
-        return lax.dynamic_slice_in_dim(part, index * size, size, axis).astype(F32)
-
-    up = [0.0] * len(parts)
-    down = [0.0] * len(parts)
-    for step in range(1, count):
-        up = [narrow(block(p, a, count - step + me) + u) for p, a, u in zip(parts, axes, up)]
-        down = [narrow(block(p, a, step - count + me) + d) for p, a, d in zip(parts, axes, down)]
-        rising = [(i, i + 1) for i in range(count - 1) if i < step]
-        up = [lax.ppermute(u, "dp", rising).astype(F32) for u in up]
-        falling = [(count - 1 - i, count - 2 - i) for i in range(count - 1) if i < step]
-        down = [lax.ppermute(d, "dp", falling).astype(F32) for d in down]
-    return [block(p, a, me) + u + d for p, a, u, d in zip(parts, axes, up, down)]
+    rows, width = shard.shape
+    blocks = shard.reshape(rows, count, width // count)
+    arrived = []
+    for distance in range(count):
+        block = lax.dynamic_index_in_dim(blocks, (me + distance) % count, 1, keepdims=False)
+        if distance:
+            block = lax.ppermute(block, "dp", [(i, (i + distance) % count) for i in range(count)])
+        arrived.append(block)
+    arrived = jnp.stack(arrived)
+    ordered = [lax.dynamic_index_in_dim(arrived, (me - q) % count, 0, keepdims=False) for q in range(count)]
+    return jnp.concatenate(ordered, axis=1)
 
 
 def per_device(
@@ -510,7 +505,7 @@
         grad_middle = incoming + norm_back(grad_mid, unit_mid, scale_mid, gains[1])
         spread_early = None
         if early is not None:
-            spread_early = early(normed_mid, grad_gate, grad_up, hidden, grad_out)
+            spread_early = early(normed_mid, grad_gate, grad_up)
             grad_middle, spread_early = lax.optimization_barrier((grad_middle, spread_early))
         gain_two = jnp.sum(grad_mid * unit_mid, axis=0)
         grad_branch = gather(narrow(grad_middle))
@@ -525,9 +520,8 @@
         grad_norm = scatter(grad_norm)
         grad_inputs = grad_middle + norm_back(grad_norm, unit, scale, gains[0])
         gain_one = jnp.sum(grad_norm * unit, axis=0)
-        big = (normed, grad_qkv, grad_logit, mixed, grad_branch, normed_mid, grad_gate, grad_up, hidden, grad_out)
-        if early is not None:
-            big = big[:5] + spread_early
+        big = (normed, grad_qkv, grad_logit, narrow(incoming), narrow(grad_middle))
+        big += (normed_mid, grad_gate, grad_up) if early is None else (spread_early,)
         small = (grad_taps, jnp.sum(grad_head_gain, axis=0), jnp.stack([gain_one, gain_two]))
         return grad_inputs, big, small
 
@@ -544,17 +538,25 @@
         kept.append((saved, mine))
         if step < steps - 1:
             arrived = shifted(narrow(result), "section", 1).astype(F32)
+    def picked(values, own=None):
+        chosen = [values[i] for i in range(last, micro)]
+        for i in range(last):
+            first = values[i] if own is None else own
+            chosen.append(jnp.where(section <= i, first, values[i + micro]))
+        return chosen
+
     def joined(own, place, axis=0):
-        picked = [terms[i][0][place] for i in range(last, micro)]
-        picked.append(jnp.where(section < last, own, terms[micro][0][place]))
-        return jnp.concatenate(picked, axis=axis)
+        return jnp.concatenate(picked([term and term[0][place] for term in terms], own), axis=axis)
 
     def mlp_terms(*own):
-        normed_mid, grad_gate, grad_up, hidden, grad_out = (
-            joined(own[place], 5 + place) for place in range(5)
-        )
-        grad_expand = jnp.stack([product_left(normed_mid, grad_gate), product_left(normed_mid, grad_up)])
-        return narrow(grad_expand), narrow(product_left(hidden, grad_out))
+        normed_mid, grad_gate, grad_up = (joined(own[place], 5 + place) for place in range(3))
+        return narrow(jnp.stack([product_left(normed_mid, grad_gate), product_left(normed_mid, grad_up)]))
+
+    def every_row(values):
+        return [lax.all_gather(value, "dp", axis=0) for value in picked(values)]
+
+    hidden_rows = every_row([saved[-1] for saved, _ in kept])
+    mixed_rows = every_row([saved[5] for saved, _ in kept])
 
     arrived = zero
     terms = [None] * steps
@@ -564,6 +566,11 @@
         top = cotangent_own[place] if place >= 0 else zero
         incoming = jnp.where(section == last, top, arrived if step < micro else zero)
         saved, mine = kept[step]
+        if step < len(hidden_rows):
+            turn = len(hidden_rows) - 1 - step
+            incoming, hidden_rows[turn], mixed_rows[turn] = lax.optimization_barrier(
+                (incoming, hidden_rows[turn], mixed_rows[turn])
+            )
         result, big, small = backward(incoming, mine, saved, mlp_terms if step == 0 else None)
         terms[step] = (big, small)
         if step < micro:
@@ -575,21 +582,38 @@
     moved = shifted(narrow(rows_out[:, :, half:]), "section", 1).astype(F32)
     grad_tokens = jnp.where(section == 0, rows_out[:, :, :half], moved)
 
+    def spread(value, axis):
+        return lax.psum_scatter(value, "dp", scatter_dimension=axis, tiled=True)
+
     own = terms[0][0]
+    early = spread(own[5], 1)
     normed, grad_qkv, grad_logit = joined(own[0], 0), joined(own[1], 1, 1), joined(own[2], 2)
-    mixed, grad_branch = joined(own[3], 3), joined(own[4], 4)
-    early = line_scatter([own[5], own[6]], [1, 1])
     grad_project = narrow(jnp.stack([product_left(normed, grad_qkv[j]) for j in range(3)]))
-    late = [grad_project, narrow(product_left(mixed, grad_branch)), narrow(product_left(normed, grad_logit))]
-    late, early = lax.optimization_barrier((late, early))
-    grad_expand, grad_contract = early
-    grad_project, grad_merge, grad_beta = line_scatter(late, [1, 1, 0])
+    grad_beta = product_left(normed, grad_logit)
+    grad_project, early = lax.optimization_barrier((grad_project, early))
+    grad_expand = early.astype(F32)
+    grad_project = spread(grad_project, 1).astype(F32)
+
+    def from_rows(rows, place):
+        total = 0.0
+        for left, right in zip(rows, picked([term[0][place] for term in terms])):
+            right = gather(swapped(right)).reshape(TOK_MB, left.shape[0], -1)
+            total = total + lax.dot_general(
+                left, right, (((0, 1), (1, 0)), ((), ())), preferred_element_type=F32
+            )
+        return total
+
+    grad_contract = from_rows(hidden_rows, 3)
+    grad_merge = from_rows(mixed_rows, 4)
     grad_taps, grad_head_gain, grad_gains = (
         sum(term[1][place] for term in terms) for place in range(3)
     )
     grad_gains = summed(jnp.concatenate([grad_gains.reshape(-1), grad_head_gain]), ("dp", "head"))
     grad_gains, grad_head_gain = grad_gains[: 2 * width].reshape(2, width), grad_gains[2 * width :]
-    grad_taps = summed(grad_taps, ("dp",))
+    flat = summed(jnp.concatenate([grad_taps.reshape(-1), grad_beta.reshape(-1)]), ("dp",))
+    grad_taps, grad_beta = flat[: grad_taps.size].reshape(grad_taps.shape), flat[grad_taps.size :]
+    rows = width // lax.axis_size("dp")
+    grad_beta = lax.dynamic_slice_in_dim(grad_beta.reshape(width, heads), lax.axis_index("dp") * rows, rows, 0)
     return (
         grad_tokens,
         grad_project[None],

time: 1130 us -> 1040 us (0.920)
  starting transfers between devices: 188 us -> 87.9 us
  local copies, waits for them, and re-layouts: 59.1 us -> 105 us
  waiting for transfers between devices: 536 us -> 494 us
  between operations: 4.54 us -> 18.2 us
    ppermute x30 -> x12, waiting for transfers between devices: 247 us -> 58 us  [swapped(): lax.ppermute(block, 'dp', [(i, (i + distance) % count) for i in range(cou...]
    ppermute x30 -> x12, starting transfers between devices: 128 us -> 21.6 us  [swapped(): lax.ppermute(block, 'dp', [(i, (i + distance) % count) for i in range(cou...]
    all_gather x0 -> x4, waiting for transfers between devices: none -> 83 us  [every_row(): return [lax.all_gather(value, 'dp', axis=0) for value in picked(values)]]
    reduce_scatter x0 -> x2, waiting for transfers between devices: none -> 54.8 us  [spread(): return lax.psum_scatter(value, 'dp', scatter_dimension=axis, tiled=True)]
    convert_element_type x42 -> x25, other arithmetic: 47.6 us -> 18.4 us  [narrow(): return values.astype(BF16)]
    another operation x48 -> x64, other arithmetic: 15.2 us -> 34.2 us  [gather(): jnp.stack([jnp.where(low, parts, other), jnp.where(low, other, parts)], a...]
    dot_general x24, matrix products: 68.3 us -> 50.3 us  [product_right(): lax.dot_general(left, right, (((1,), (1,)), ((), ())), preferred_element_...]
    another operation x1 -> x6, local copies, waits for them, and re-layouts: 0.01 us -> 17.2 us  [the longest x4 15.8 us: from_rows(): right = gather(swapped(right)).reshape(TOK_MB, left.shape[0], -1)]
  transfers between devices with their start and end apart: 87 -> 83, of which waited for: 55 -> 58; matrix products, arithmetic and copies ran while one was open for 11% -> 19% of each run, Pallas kernels for 1% -> 4%
where the time goes in v3:
time: 1040 us
  waiting for transfers between devices  494 us (48%)
  matrix products  152 us (15%)
  other arithmetic  121 us (12%)
  local copies, waits for them, and re-layouts  105 us (10%)
  starting transfers between devices  87.9 us (8%)
  Pallas kernels  58.8 us (6%)
  between operations  18.2 us (2%)
    ppermute x60, waiting for transfers between devices, flipped(): lax.ppermute(values, axis, [(i, i ^ bit) for i in range(lax.axis_size(axi...  261 us
    all_gather x4, waiting for transfers between devices, every_row(): return [lax.all_gather(value, 'dp', axis=0) for value in picked(values)]  83 us
    dot_general x23, matrix products, product(): return jnp.dot(left, right, preferred_element_type=F32)  66.6 us
    ppermute x12, waiting for transfers between devices, swapped(): lax.ppermute(block, 'dp', [(i, (i + distance) % count) for i in range(cou...  58 us
    reduce_scatter x2, waiting for transfers between devices, spread(): return lax.psum_scatter(value, 'dp', scatter_dimension=axis, tiled=True)  54.8 us
    ppermute x60, starting transfers between devices, flipped(): lax.ppermute(values, axis, [(i, i ^ bit) for i in range(lax.axis_size(axi...  51 us
    dot_general x24, matrix products, product_right(): lax.dot_general(left, right, (((1,), (1,)), ((), ())), preferred_element_...  50.3 us
    unnamed x455, local copies, waits for them, and re-layouts  38.8 us
  transfers between devices with their start and end apart: 83, of which 58 were waited for; matrix products, arithmetic and copies ran while one was open for 19% of the time, Pallas kernels for 4%

profile of v3, /device:TPU:0, one launch (start us, length us, event | category | flops | bytes accessed | tf_op | source)
XLA Modules:
  0.0 1036.9 jit_solution(13396347122879220790)
XLA Ops:
  18.2 9.1 collective-permute-done
  42.6 7.0 shard_map.178
  61.5 9.9 collective-permute-done.3
  75.0 8.8 collective-permute-done.4
  87.2 6.1 fusion.34
  104.5 9.4 collective-permute-done.7
  117.8 7.8 collective-permute-done.8
  128.2 7.9 collective-permute-done.9
  144.4 7.8 shard_map.179
  163.2 9.7 collective-permute-done.12
  175.9 8.8 collective-permute-done.13
  187.9 14.6 %fusion.32 = f32[384,1408]{1,0:T(8,128)S(1)} fusion(bf16[384,2048]{1,0:T(8,128)(2,1)S(1)} %bitcast.802, bf16[1,2,2048,1408]{3,2,1,0:T(8,128)(2,1)S(1)} %bitcast.871), kind=kOutput, calls=%fused_computation.36 | convolution fusion | flops 2214592512 | bytes 9502720 | tf_op jit(solution)/shard_map/dot_general | solution.py:355
  206.8 5.6 fusion.47
  216.7 9.7 collective-permute-done.16
  230.9 7.8 collective-permute-done.17
  241.4 7.9 collective-permute-done.18
  265.9 7.1 shard_map.180
  280.6 9.5 collective-permute-done.22
  290.5 7.3 collective-permute-done.21
  300.9 8.7 collective-permute-done.24
  335.4 9.8 collective-permute-done.27
  351.2 8.8 collective-permute-done.28
  367.2 12.2 %shard_map.181 = (bf16[3,384,512]{2,1,0:T(8,128)(2,1)S(1)}, f32[384,128]{1,0:T(8,128)S(1)}, f32[3,4,512]{2,1,0:T(4,128)S(1)}, f32[8,128]{1,0:T(8,128)S(1)}) custom-call(f32[3,384,512]{2,1,0:T(8,128)} %pad_maximum_fusion.6.qkv_ref, f32[384,4]{1,0:T(8,128)S(1)} %copy-done.33, f32[3,4,512]{2,1,0:T(4,128)S(1)} %bitcast.761, f32[1,128]{1,0:T(1,128)S(1)} %copy-done.27, ...), custom_call_target="tpu_custom_call" | custom-call | flops 4000000000 | bytes 8000000 | tf_op jit(solution)/shard_map/pallas_call | solution.py:307
  387.7 9.7 collective-permute-done.31
  401.7 10.9 %collective-permute-done.32 = bf16[96,2048]{1,0:T(8,128)(2,1)S(1)} collective-permute-done((bf16[96,2048]{1,0:T(8,128)(2,1)S(1)}, bf16[96,2048]{1,0:T(8,128)(2,1)S(1)}, u32[]{:S(2)}, u32[]{:S(2)}) %collective-permute-start.32) | collective-permute-done | bytes 393248 | tf_op jit(solution)/shard_map/ppermute | solution.py:388
  414.5 42.7 %all-gather.9.cloned.1.call-done = bf16[1536,1408]{1,0:T(8,128)(2,1)} async-done(((bf16[384,1408]{1,0:T(8,128)(2,1)}), bf16[1536,1408]{1,0:T(8,128)(2,1)}) %all-gather.9.cloned.1.call-update) | async-done | bytes 4325392 | tf_op jit(solution)/shard_map/all_gather | solution.py:556
  460.0 9.4 collective-permute-done.33
  475.3 6.1 multiply_convert_fusion.4
  494.5 8.1 collective-permute-done.36
  508.8 8.9 collective-permute-done.37
  525.9 12.2 %shard_map.182 = (bf16[3,384,512]{2,1,0:T(8,128)(2,1)S(1)}, f32[384,128]{1,0:T(8,128)S(1)}, f32[3,4,512]{2,1,0:T(4,128)S(1)}, f32[8,128]{1,0:T(8,128)S(1)}) custom-call(f32[3,384,512]{2,1,0:T(8,128)} %pad_maximum_fusion.5.qkv_ref, f32[384,4]{1,0:T(8,128)S(1)} %copy-done.31, f32[3,4,512]{2,1,0:T(4,128)S(1)} %bitcast.762, f32[1,128]{1,0:T(1,128)S(1)} %copy-done.27, ...), custom_call_target="tpu_custom_call" | custom-call | flops 4000000000 | bytes 8000000 | tf_op jit(solution)/shard_map/pallas_call | solution.py:307
  546.3 9.7 collective-permute-done.40
  560.9 11.0 %collective-permute-done.41 = bf16[96,2048]{1,0:T(8,128)(2,1)S(1)} collective-permute-done((bf16[96,2048]{1,0:T(8,128)(2,1)S(1)}, bf16[96,2048]{1,0:T(8,128)(2,1)S(1)}, u32[]{:S(2)}, u32[]{:S(2)}) %collective-permute-start.41) | collective-permute-done | bytes 393248 | tf_op jit(solution)/shard_map/ppermute | solution.py:388
  572.9 40.3 %all-gather.13.cloned.1.call-done = bf16[1536,1408]{1,0:T(8,128)(2,1)} async-done(((bf16[384,1408]{1,0:T(8,128)(2,1)}), bf16[1536,1408]{1,0:T(8,128)(2,1)}) %all-gather.13.cloned.1.call-update) | async-done | bytes 4325392 | tf_op jit(solution)/shard_map/all_gather | solution.py:556
  617.0 9.4 collective-permute-done.42
  631.1 9.6 broadcast_select_fusion.4
  647.8 5.4 fusion.1
  688.1 5.8 collective-permute-done.69
  693.9 11.4 %collective-permute-done.68 = bf16[96,512]{1,0:T(8,128)(2,1)} collective-permute-done((bf16[96,512]{1,0:T(8,128)(2,1)}, bf16[96,512]{1,0:T(8,128)(2,1)}, u32[]{:S(2)}, u32[]{:S(2)}) %collective-permute-start.68) | collective-permute-done | bytes 98336 | tf_op jit(solution)/shard_map/ppermute | solution.py:438
  707.9 9.1 collective-permute-done.70
  744.4 13.6 %collective-permute-done.58 = bf16[96,512]{1,0:T(8,128)(2,1)} collective-permute-done((bf16[96,512]{1,0:T(8,128)(2,1)}, bf16[96,512]{1,0:T(8,128)(2,1)}, u32[]{:S(2)}, u32[]{:S(2)}) %collective-permute-start.58) | collective-permute-done | bytes 98336 | tf_op jit(solution)/shard_map/ppermute | solution.py:438
  762.2 9.0 collective-permute-done.60
  793.7 10.4 %collective-permute-done.73 = bf16[96,512]{1,0:T(8,128)(2,1)} collective-permute-done((bf16[96,512]{1,0:T(8,128)(2,1)}, bf16[96,512]{1,0:T(8,128)(2,1)}, u32[]{:S(2)}, u32[]{:S(2)}) %collective-permute-start.73) | collective-permute-done | bytes 98336 | tf_op jit(solution)/shard_map/ppermute | solution.py:438
  811.2 12.5 %shard_map.183 = (bf16[3,384,512]{2,1,0:T(8,128)(2,1)S(1)}, f32[384,128]{1,0:T(8,128)S(1)}, f32[3,4,512]{2,1,0:T(4,128)S(1)}, f32[8,128]{1,0:T(8,128)S(1)}) custom-call(f32[3,384,512]{2,1,0:T(8,128)} %pad_maximum_fusion.4.qkv_ref, f32[384,4]{1,0:T(8,128)S(1)} %copy-done.29, f32[3,4,512]{2,1,0:T(4,128)S(1)} %bitcast.763, f32[1,128]{1,0:T(1,128)S(1)} %copy-done.27, ...), custom_call_target="tpu_custom_call" | custom-call | flops 4000000000 | bytes 8000000 | tf_op jit(solution)/shard_map/pallas_call | solution.py:307
  834.6 54.8 %reduce-scatter.3.cloned.1.call-done = bf16[2,512,1408]{2,1,0:T(8,128)(2,1)} async-done(((bf16[2,2048,1408]{2,1,0:T(8,128)(2,1)}), bf16[2,512,1408]{2,1,0:T(8,128)(2,1)}) %reduce-scatter.3.cloned.1.call-update) | async-done | bytes 2883600 | tf_op jit(solution)/shard_map/reduce_scatter | solution.py:586
  914.4 6.3 collective-permute-start.63
  926.1 16.8 %collective-permute-done.63 = bf16[96,512]{1,0:T(8,128)(2,1)S(1)} collective-permute-done((bf16[96,512]{1,0:T(8,128)(2,1)S(1)}, bf16[96,512]{1,0:T(8,128)(2,1)S(1)}, u32[]{:S(2)}, u32[]{:S(2)}) %collective-permute-start.63) | collective-permute-done | bytes 98336 | tf_op jit(solution)/shard_map/ppermute | solution.py:438
  965.1 5.9 collective-permute-done.51
  (902 shorter events, 468.5 us)
Async XLA Ops:
  7.2 407.3 %all-gather.11.cloned.1.call-start = ((), (), s32[]{:S(2)}) async-start(), calls=%async_computation.5 | async-start | bytes 1966080 | tf_op jit(solution)/shard_map/all_gather | solution.py:556
  15.2 12.1 %collective-permute-start = (bf16[96,2048]{1,0:T(8,128)(2,1)S(1)}, bf16[96,2048]{1,0:T(8,128)(2,1)S(1)}, u32[]{:S(2)}, u32[]{:S(2)}) collective-permute-start(bf16[96,2048]{1,0:T(8,128)(2,1)S(1)} %multiply_convert_fusion.14), channel_id=1, source_target_pairs={{0,2},{1,3},{2,0},{3,1},{4,6},{5,7},{6,4},{7,5},{8,10},{9,11},{10,... | collective-permute-start | bytes 1179656 | tf_op jit(solution)/shard_map/ppermute | solution.py:383
  59.8 11.7 %collective-permute-start.3 = (bf16[96,2048]{1,0:T(8,128)(2,1)}, bf16[96,2048]{1,0:T(8,128)(2,1)}, u32[]{:S(2)}, u32[]{:S(2)}) collective-permute-start(bf16[96,2048]{1,0:T(8,128)(2,1)} %dynamic-slice_bitcast_fusion.21), channel_id=1, source_target_pairs={{0,2},{1,3},{2,0},{3,1},{4,6},{5,7},{6,4},{7,5},{8,10},{9,11},{10,... | collective-permute-start | bytes 1179656 | tf_op jit(solution)/shard_map/ppermute | solution.py:383
  73.2 10.6 %collective-permute-start.4 = (bf16[96,2048]{1,0:T(8,128)(2,1)S(1)}, bf16[96,2048]{1,0:T(8,128)(2,1)S(1)}, u32[]{:S(2)}, u32[]{:S(2)}) collective-permute-start(bf16[96,2048]{1,0:T(8,128)(2,1)S(1)} %multiply_convert_fusion.13), channel_id=1, source_target_pairs={{0,2},{1,3},{2,0},{3,1},{4,6},{5,7},{6,4},{7,5},{8,10},{9,11},{10,... | collective-permute-start | bytes 1179656 | tf_op jit(solution)/shard_map/ppermute | solution.py:383
  102.7 11.2 %collective-permute-start.7 = (bf16[96,2048]{1,0:T(8,128)(2,1)S(1)}, bf16[96,2048]{1,0:T(8,128)(2,1)S(1)}, u32[]{:S(2)}, u32[]{:S(2)}) collective-permute-start(bf16[96,2048]{1,0:T(8,128)(2,1)S(1)} %dynamic-slice_bitcast_fusion.20), channel_id=1, source_target_pairs={{0,2},{1,3},{2,0},{3,1},{4,6},{5,7},{6,4},{7,5},{8,10},{9,11},{10,... | collective-permute-start | bytes 1179656 | tf_op jit(solution)/shard_map/ppermute | solution.py:383
  114.1 11.5 %collective-permute-start.8 = (bf16[96,2048]{1,0:T(8,128)(2,1)S(1)}, bf16[96,2048]{1,0:T(8,128)(2,1)S(1)}, u32[]{:S(2)}, u32[]{:S(2)}) collective-permute-start(bf16[96,2048]{1,0:T(8,128)(2,1)S(1)} %fusion.208), channel_id=1, source_target_pairs={{0,16},{1,17},{2,18},{3,19},{4,20},{5,21},{6,22},{7,23},{8,24},{9,... | collective-permute-start | bytes 1179656 | tf_op jit(solution)/shard_map/ppermute | solution.py:388
  161.6 11.2 %collective-permute-start.12 = (bf16[96,2048]{1,0:T(8,128)(2,1)S(1)}, bf16[96,2048]{1,0:T(8,128)(2,1)S(1)}, u32[]{:S(2)}, u32[]{:S(2)}) collective-permute-start(bf16[96,2048]{1,0:T(8,128)(2,1)S(1)} %dynamic-slice_bitcast_fusion.19), channel_id=1, source_target_pairs={{0,2},{1,3},{2,0},{3,1},{4,6},{5,7},{6,4},{7,5},{8,10},{9,11},{10,... | collective-permute-start | bytes 1179656 | tf_op jit(solution)/shard_map/ppermute | solution.py:383
  215.2 11.2 %collective-permute-start.16 = (bf16[96,2048]{1,0:T(8,128)(2,1)S(1)}, bf16[96,2048]{1,0:T(8,128)(2,1)S(1)}, u32[]{:S(2)}, u32[]{:S(2)}) collective-permute-start(bf16[96,2048]{1,0:T(8,128)(2,1)S(1)} %dynamic-slice_bitcast_fusion.18), channel_id=1, source_target_pairs={{0,2},{1,3},{2,0},{3,1},{4,6},{5,7},{6,4},{7,5},{8,10},{9,11},{10,... | collective-permute-start | bytes 1179656 | tf_op jit(solution)/shard_map/ppermute | solution.py:383
  226.5 12.2 %collective-permute-start.17 = (bf16[96,2048]{1,0:T(8,128)(2,1)S(1)}, bf16[96,2048]{1,0:T(8,128)(2,1)S(1)}, u32[]{:S(2)}, u32[]{:S(2)}) collective-permute-start(bf16[96,2048]{1,0:T(8,128)(2,1)S(1)} %fusion.205), channel_id=1, source_target_pairs={{0,16},{1,17},{2,18},{3,19},{4,20},{5,21},{6,22},{7,23},{8,24},{9,... | collective-permute-start | bytes 1179656 | tf_op jit(solution)/shard_map/ppermute | solution.py:388
  278.1 12.0 %collective-permute-start.22 = (bf16[96,2048]{1,0:T(8,128)(2,1)S(1)}, bf16[96,2048]{1,0:T(8,128)(2,1)S(1)}, u32[]{:S(2)}, u32[]{:S(2)}) collective-permute-start(bf16[96,2048]{1,0:T(8,128)(2,1)S(1)} %bitcast_convert_fusion.2), channel_id=1, source_target_pairs={{0,2},{1,3},{2,0},{3,1},{4,6},{5,7},{6,4},{7,5},{8,10},{9,11},{10,... | collective-permute-start | bytes 1179656 | tf_op jit(solution)/shard_map/ppermute | solution.py:383
  280.0 17.8 %collective-permute-start.21 = (bf16[96,2048]{1,0:T(8,128)(2,1)S(1)}, bf16[96,2048]{1,0:T(8,128)(2,1)S(1)}, u32[]{:S(2)}, u32[]{:S(2)}) collective-permute-start(bf16[96,2048]{1,0:T(8,128)(2,1)S(1)} %dynamic-slice_bitcast_fusion.17), channel_id=1, source_target_pairs={{0,2},{1,3},{2,0},{3,1},{4,6},{5,7},{6,4},{7,5},{8,10},{9,11},{10,... | collective-permute-start | bytes 1179656 | tf_op jit(solution)/shard_map/ppermute | solution.py:383
  333.8 11.4 %collective-permute-start.27 = (bf16[96,2048]{1,0:T(8,128)(2,1)}, bf16[96,2048]{1,0:T(8,128)(2,1)S(1)}, u32[]{:S(2)}, u32[]{:S(2)}) collective-permute-start(bf16[96,2048]{1,0:T(8,128)(2,1)} %dynamic-slice_bitcast_fusion.16), channel_id=1, source_target_pairs={{0,2},{1,3},{2,0},{3,1},{4,6},{5,7},{6,4},{7,5},{8,10},{9,11},{10,... | collective-permute-start | bytes 1179656 | tf_op jit(solution)/shard_map/ppermute | solution.py:383
  335.3 121.9 %all-gather.9.cloned.1.call-start = ((), (), s32[]{:S(2)}) async-start(), calls=%async_computation.4 | async-start | bytes 5406720 | tf_op jit(solution)/shard_map/all_gather | solution.py:556
  361.1 211.9 %all-gather.15.cloned.1.call-start = ((), (), s32[]{:S(2)}) async-start(), calls=%async_computation.7 | async-start | bytes 1966080 | tf_op jit(solution)/shard_map/all_gather | solution.py:556
  386.2 11.2 %collective-permute-start.31 = (bf16[96,2048]{1,0:T(8,128)(2,1)S(1)}, bf16[96,2048]{1,0:T(8,128)(2,1)S(1)}, u32[]{:S(2)}, u32[]{:S(2)}) collective-permute-start(bf16[96,2048]{1,0:T(8,128)(2,1)S(1)} %dynamic-slice_bitcast_fusion.15), channel_id=1, source_target_pairs={{0,2},{1,3},{2,0},{3,1},{4,6},{5,7},{6,4},{7,5},{8,10},{9,11},{10,... | collective-permute-start | bytes 1179656 | tf_op jit(solution)/shard_map/ppermute | solution.py:383
  400.2 12.4 %collective-permute-start.32 = (bf16[96,2048]{1,0:T(8,128)(2,1)S(1)}, bf16[96,2048]{1,0:T(8,128)(2,1)S(1)}, u32[]{:S(2)}, u32[]{:S(2)}) collective-permute-start(bf16[96,2048]{1,0:T(8,128)(2,1)S(1)} %add_convert_fusion.6), channel_id=1, source_target_pairs={{16,0},{17,1},{18,2},{19,3},{20,4},{21,5},{22,6},{23,7},{24,8},{25... | collective-permute-start | bytes 1179656 | tf_op jit(solution)/shard_map/ppermute | solution.py:388
  458.4 10.9 %collective-permute-start.33 = (bf16[96,2048]{1,0:T(8,128)(2,1)S(1)}, bf16[96,2048]{1,0:T(8,128)(2,1)S(1)}, u32[]{:S(2)}, u32[]{:S(2)}) collective-permute-start(bf16[96,2048]{1,0:T(8,128)(2,1)S(1)} %convert_element_type.500), channel_id=1, source_target_pairs={{0,2},{1,3},{2,0},{3,1},{4,6},{5,7},{6,4},{7,5},{8,10},{9,11},{10,... | collective-permute-start | bytes 1179656 | tf_op jit(solution)/shard_map/ppermute | solution.py:383
  491.2 11.5 %collective-permute-start.36 = (bf16[96,2048]{1,0:T(8,128)(2,1)}, bf16[96,2048]{1,0:T(8,128)(2,1)}, u32[]{:S(2)}, u32[]{:S(2)}) collective-permute-start(bf16[96,2048]{1,0:T(8,128)(2,1)} %dynamic-slice_bitcast_fusion.14), channel_id=1, source_target_pairs={{0,2},{1,3},{2,0},{3,1},{4,6},{5,7},{6,4},{7,5},{8,10},{9,11},{10,... | collective-permute-start | bytes 1179656 | tf_op jit(solution)/shard_map/ppermute | solution.py:383
  494.5 118.8 %all-gather.13.cloned.1.call-start = ((), (), s32[]{:S(2)}) async-start(), calls=%async_computation.6 | async-start | bytes 5406720 | tf_op jit(solution)/shard_map/all_gather | solution.py:556
  521.3 368.1 %reduce-scatter.3.cloned.1.call-start = ((), (), s32[]{:S(2)}) async-start(), calls=%async_computation.2 | async-start | bytes 14417920 | tf_op jit(solution)/shard_map/reduce_scatter | solution.py:586
  544.8 11.2 %collective-permute-start.40 = (bf16[96,2048]{1,0:T(8,128)(2,1)S(1)}, bf16[96,2048]{1,0:T(8,128)(2,1)S(1)}, u32[]{:S(2)}, u32[]{:S(2)}) collective-permute-start(bf16[96,2048]{1,0:T(8,128)(2,1)S(1)} %dynamic-slice_bitcast_fusion.13), channel_id=1, source_target_pairs={{0,2},{1,3},{2,0},{3,1},{4,6},{5,7},{6,4},{7,5},{8,10},{9,11},{10,... | collective-permute-start | bytes 1179656 | tf_op jit(solution)/shard_map/ppermute | solution.py:383
  559.7 12.3 %collective-permute-start.41 = (bf16[96,2048]{1,0:T(8,128)(2,1)S(1)}, bf16[96,2048]{1,0:T(8,128)(2,1)S(1)}, u32[]{:S(2)}, u32[]{:S(2)}) collective-permute-start(bf16[96,2048]{1,0:T(8,128)(2,1)S(1)} %get-tuple-element.109), channel_id=1, source_target_pairs={{16,0},{17,1},{18,2},{19,3},{20,4},{21,5},{22,6},{23,7},{24,8},{25... | collective-permute-start | bytes 1179656 | tf_op jit(solution)/shard_map/ppermute | solution.py:388
  615.5 10.9 %collective-permute-start.42 = (bf16[96,2048]{1,0:T(8,128)(2,1)S(1)}, bf16[96,2048]{1,0:T(8,128)(2,1)S(1)}, u32[]{:S(2)}, u32[]{:S(2)}) collective-permute-start(bf16[96,2048]{1,0:T(8,128)(2,1)S(1)} %get-tuple-element.102), channel_id=1, source_target_pairs={{0,2},{1,3},{2,0},{3,1},{4,6},{5,7},{6,4},{7,5},{8,10},{9,11},{10,... | collective-permute-start | bytes 1179656 | tf_op jit(solution)/shard_map/ppermute | solution.py:383
  647.6 11.1 %collective-permute-start.44 = (bf16[2,96,2048]{2,1,0:T(8,128)(2,1)S(1)}, bf16[2,96,2048]{2,1,0:T(8,128)(2,1)S(1)}, u32[]{:S(2)}, u32[]{:S(2)}) collective-permute-start(bf16[2,96,2048]{2,1,0:T(8,128)(2,1)S(1)} %dynamic-slice_bitcast_fusion.1), channel_id=1, source_target_pairs={{0,1},{1,0},{2,3},{3,2},{4,5},{5,4},{6,7},{7,6},{8,9},{9,8},{10,11... | collective-permute-start | bytes 2359304 | tf_op jit(solution)/shard_map/ppermute | solution.py:383
  660.6 11.7 %collective-permute-start.45 = (bf16[96,2048]{1,0:T(8,128)(2,1)}, bf16[96,2048]{1,0:T(8,128)(2,1)}, u32[]{:S(2)}, u32[]{:S(2)}) collective-permute-start(bf16[96,2048]{1,0:T(8,128)(2,1)} %dynamic-slice_bitcast_fusion.12), channel_id=1, source_target_pairs={{0,2},{1,3},{2,0},{3,1},{4,6},{5,7},{6,4},{7,5},{8,10},{9,11},{10,... | collective-permute-start | bytes 1179656 | tf_op jit(solution)/shard_map/ppermute | solution.py:383
  676.8 349.5 %reduce-scatter.5.cloned.1.call-start = ((), (), s32[]{:S(2)}) async-start(), calls=%async_computation.3 | async-start | bytes 7864320 | tf_op jit(solution)/shard_map/reduce_scatter | solution.py:586
  683.0 10.9 %collective-permute-start.69 = (bf16[96,512]{1,0:T(8,128)(2,1)}, bf16[96,512]{1,0:T(8,128)(2,1)}, u32[]{:S(2)}, u32[]{:S(2)}) collective-permute-start(bf16[96,512]{1,0:T(8,128)(2,1)} %bitcast.740), channel_id=1, source_target_pairs={{0,12},{4,0},{8,4},{12,8},{1,13},{5,1},{9,5},{13,9},{2,14},{6,2},{... | collective-permute-start | bytes 294920 | tf_op jit(solution)/shard_map/ppermute | solution.py:438
  684.3 21.0 %collective-permute-start.68 = (bf16[96,512]{1,0:T(8,128)(2,1)}, bf16[96,512]{1,0:T(8,128)(2,1)}, u32[]{:S(2)}, u32[]{:S(2)}) collective-permute-start(bf16[96,512]{1,0:T(8,128)(2,1)} %bitcast.741), channel_id=1, source_target_pairs={{0,8},{4,12},{8,0},{12,4},{1,9},{5,13},{9,1},{13,5},{2,10},{6,14},... | collective-permute-start | bytes 294920 | tf_op jit(solution)/shard_map/ppermute | solution.py:438
  685.1 20.2 %collective-permute-start.67 = (bf16[96,512]{1,0:T(8,128)(2,1)}, bf16[96,512]{1,0:T(8,128)(2,1)}, u32[]{:S(2)}, u32[]{:S(2)}) collective-permute-start(bf16[96,512]{1,0:T(8,128)(2,1)} %bitcast.742), channel_id=1, source_target_pairs={{0,4},{4,8},{8,12},{12,0},{1,5},{5,9},{9,13},{13,1},{2,6},{6,10},{... | collective-permute-start | bytes 294920 | tf_op jit(solution)/shard_map/ppermute | solution.py:438
  706.4 10.6 %collective-permute-start.70 = (bf16[96,2048]{1,0:T(8,128)(2,1)S(1)}, bf16[96,2048]{1,0:T(8,128)(2,1)S(1)}, u32[]{:S(2)}, u32[]{:S(2)}) collective-permute-start(bf16[96,2048]{1,0:T(8,128)(2,1)S(1)} %pad_maximum_fusion.50), channel_id=1, source_target_pairs={{0,2},{1,3},{2,0},{3,1},{4,6},{5,7},{6,4},{7,5},{8,10},{9,11},{10,... | collective-permute-start | bytes 1179656 | tf_op jit(solution)/shard_map/ppermute | solution.py:383
  732.6 11.7 %collective-permute-start.59 = (bf16[96,512]{1,0:T(8,128)(2,1)}, bf16[96,512]{1,0:T(8,128)(2,1)}, u32[]{:S(2)}, u32[]{:S(2)}) collective-permute-start(bf16[96,512]{1,0:T(8,128)(2,1)} %bitcast.748), channel_id=1, source_target_pairs={{0,12},{4,0},{8,4},{12,8},{1,13},{5,1},{9,5},{13,9},{2,14},{6,2},{... | collective-permute-start | bytes 294920 | tf_op jit(solution)/shard_map/ppermute | solution.py:438
  733.3 24.7 %collective-permute-start.58 = (bf16[96,512]{1,0:T(8,128)(2,1)}, bf16[96,512]{1,0:T(8,128)(2,1)}, u32[]{:S(2)}, u32[]{:S(2)}) collective-permute-start(bf16[96,512]{1,0:T(8,128)(2,1)} %bitcast.749), channel_id=1, source_target_pairs={{0,8},{4,12},{8,0},{12,4},{1,9},{5,13},{9,1},{13,5},{2,10},{6,14},... | collective-permute-start | bytes 294920 | tf_op jit(solution)/shard_map/ppermute | solution.py:438
  737.1 20.9 %collective-permute-start.57 = (bf16[96,512]{1,0:T(8,128)(2,1)}, bf16[96,512]{1,0:T(8,128)(2,1)}, u32[]{:S(2)}, u32[]{:S(2)}) collective-permute-start(bf16[96,512]{1,0:T(8,128)(2,1)} %bitcast.750), channel_id=1, source_target_pairs={{0,4},{4,8},{8,12},{12,0},{1,5},{5,9},{9,13},{13,1},{2,6},{6,10},{... | collective-permute-start | bytes 294920 | tf_op jit(solution)/shard_map/ppermute | solution.py:438
  759.1 12.0 %collective-permute-start.60 = (bf16[96,2048]{1,0:T(8,128)(2,1)S(1)}, bf16[96,2048]{1,0:T(8,128)(2,1)S(1)}, u32[]{:S(2)}, u32[]{:S(2)}) collective-permute-start(bf16[96,2048]{1,0:T(8,128)(2,1)S(1)} %pad_maximum_fusion.46), channel_id=1, source_target_pairs={{0,2},{1,3},{2,0},{3,1},{4,6},{5,7},{6,4},{7,5},{8,10},{9,11},{10,... | collective-permute-start | bytes 1179656 | tf_op jit(solution)/shard_map/ppermute | solution.py:383
  761.7 17.2 %collective-permute-start.46 = (bf16[96,2048]{1,0:T(8,128)(2,1)}, bf16[96,2048]{1,0:T(8,128)(2,1)}, u32[]{:S(2)}, u32[]{:S(2)}) collective-permute-start(bf16[96,2048]{1,0:T(8,128)(2,1)} %get-tuple-element.104), channel_id=1, source_target_pairs={{0,2},{1,3},{2,0},{3,1},{4,6},{5,7},{6,4},{7,5},{8,10},{9,11},{10,... | collective-permute-start | bytes 1179656 | tf_op jit(solution)/shard_map/ppermute | solution.py:383
  781.7 25.8 %collective-permute-start.47 = (bf16[2,96,2048]{2,1,0:T(8,128)(2,1)}, bf16[2,96,2048]{2,1,0:T(8,128)(2,1)}, u32[]{:S(2)}, u32[]{:S(2)}) collective-permute-start(bf16[2,96,2048]{2,1,0:T(8,128)(2,1)} %pad_maximum_fusion.38), channel_id=1, source_target_pairs={{0,1},{1,0},{2,3},{3,2},{4,5},{5,4},{6,7},{7,6},{8,9},{9,8},{10,11... | collective-permute-start | bytes 2359304 | tf_op jit(solution)/shard_map/ppermute | solution.py:383
  784.5 19.5 %collective-permute-start.73 = (bf16[96,512]{1,0:T(8,128)(2,1)}, bf16[96,512]{1,0:T(8,128)(2,1)}, u32[]{:S(2)}, u32[]{:S(2)}) collective-permute-start(bf16[96,512]{1,0:T(8,128)(2,1)} %bitcast.737), channel_id=1, source_target_pairs={{0,8},{4,12},{8,0},{12,4},{1,9},{5,13},{9,1},{13,5},{2,10},{6,14},... | collective-permute-start | bytes 294920 | tf_op jit(solution)/shard_map/ppermute | solution.py:438
  786.9 17.2 %collective-permute-start.72 = (bf16[96,512]{1,0:T(8,128)(2,1)}, bf16[96,512]{1,0:T(8,128)(2,1)}, u32[]{:S(2)}, u32[]{:S(2)}) collective-permute-start(bf16[96,512]{1,0:T(8,128)(2,1)} %bitcast.738), channel_id=1, source_target_pairs={{0,4},{4,8},{8,12},{12,0},{1,5},{5,9},{9,13},{13,1},{2,6},{6,10},{... | collective-permute-start | bytes 294920 | tf_op jit(solution)/shard_map/ppermute | solution.py:438
  789.8 102.7 %collective-permute-start.61 = (bf16[2,96,2048]{2,1,0:T(8,128)(2,1)}, bf16[2,96,2048]{2,1,0:T(8,128)(2,1)}, u32[]{:S(2)}, u32[]{:S(2)}) collective-permute-start(bf16[2,96,2048]{2,1,0:T(8,128)(2,1)} %pad_maximum_fusion.39), channel_id=1, source_target_pairs={{0,1},{1,0},{2,3},{3,2},{4,5},{5,4},{6,7},{7,6},{8,9},{9,8},{10,11... | collective-permute-start | bytes 2359304 | tf_op jit(solution)/shard_map/ppermute | solution.py:383
  806.0 83.5 %collective-permute-start.75 = (bf16[96,2048]{1,0:T(8,128)(2,1)}, bf16[96,2048]{1,0:T(8,128)(2,1)}, u32[]{:S(2)}, u32[]{:S(2)}) collective-permute-start(bf16[96,2048]{1,0:T(8,128)(2,1)} %pad_maximum_fusion.52), channel_id=1, source_target_pairs={{0,2},{1,3},{2,0},{3,1},{4,6},{5,7},{6,4},{7,5},{8,10},{9,11},{10,... | collective-permute-start | bytes 1179656 | tf_op jit(solution)/shard_map/ppermute | solution.py:383
  892.5 10.7 %collective-permute-start.76 = (bf16[2,96,2048]{2,1,0:T(8,128)(2,1)}, bf16[2,96,2048]{2,1,0:T(8,128)(2,1)}, u32[]{:S(2)}, u32[]{:S(2)}) collective-permute-start(bf16[2,96,2048]{2,1,0:T(8,128)(2,1)} %pad_maximum_fusion.42), channel_id=1, source_target_pairs={{0,1},{1,0},{2,3},{3,2},{4,5},{5,4},{6,7},{7,6},{8,9},{9,8},{10,11... | collective-permute-start | bytes 2359304 | tf_op jit(solution)/shard_map/ppermute | solution.py:383
  911.2 14.9 %collective-permute-start.64 = (bf16[96,512]{1,0:T(8,128)(2,1)S(1)}, bf16[96,512]{1,0:T(8,128)(2,1)S(1)}, u32[]{:S(2)}, u32[]{:S(2)}) collective-permute-start(bf16[96,512]{1,0:T(8,128)(2,1)S(1)} %bitcast.856), channel_id=1, source_target_pairs={{0,12},{4,0},{8,4},{12,8},{1,13},{5,1},{9,5},{13,9},{2,14},{6,2},{... | collective-permute-start | bytes 294920 | tf_op jit(solution)/shard_map/ppermute | solution.py:438
  914.4 28.5 %collective-permute-start.63 = (bf16[96,512]{1,0:T(8,128)(2,1)S(1)}, bf16[96,512]{1,0:T(8,128)(2,1)S(1)}, u32[]{:S(2)}, u32[]{:S(2)}) collective-permute-start(bf16[96,512]{1,0:T(8,128)(2,1)S(1)} %bitcast.857), channel_id=1, source_target_pairs={{0,8},{4,12},{8,0},{12,4},{1,9},{5,13},{9,1},{13,5},{2,10},{6,14},... | collective-permute-start | bytes 294920 | tf_op jit(solution)/shard_map/ppermute | solution.py:438
  920.7 22.2 %collective-permute-start.62 = (bf16[96,512]{1,0:T(8,128)(2,1)S(1)}, bf16[96,512]{1,0:T(8,128)(2,1)S(1)}, u32[]{:S(2)}, u32[]{:S(2)}) collective-permute-start(bf16[96,512]{1,0:T(8,128)(2,1)S(1)} %bitcast.858), channel_id=1, source_target_pairs={{0,4},{4,8},{8,12},{12,0},{1,5},{5,9},{9,13},{13,1},{2,6},{6,10},{... | collective-permute-start | bytes 294920 | tf_op jit(solution)/shard_map/ppermute | solution.py:438
  953.0 25.2 %collective-permute-start.66 = (bf16[2,96,2048]{2,1,0:T(8,128)(2,1)}, bf16[2,96,2048]{2,1,0:T(8,128)(2,1)}, u32[]{:S(2)}, u32[]{:S(2)}) collective-permute-start(bf16[2,96,2048]{2,1,0:T(8,128)(2,1)} %pad_maximum_fusion.40), channel_id=1, source_target_pairs={{0,1},{1,0},{2,3},{3,2},{4,5},{5,4},{6,7},{7,6},{8,9},{9,8},{10,11... | collective-permute-start | bytes 2359304 | tf_op jit(solution)/shard_map/ppermute | solution.py:383
  958.5 15.3 %collective-permute-start.48 = (bf16[2,96,2048]{2,1,0:T(8,128)(2,1)}, bf16[2,96,2048]{2,1,0:T(8,128)(2,1)}, u32[]{:S(2)}, u32[]{:S(2)}) collective-permute-start(bf16[2,96,2048]{2,1,0:T(8,128)(2,1)} %dynamic-slice_bitcast_fusion), channel_id=1, source_target_pairs={{0,1},{1,0},{2,3},{3,2},{4,5},{5,4},{6,7},{7,6},{8,9},{9,8},{10,11... | collective-permute-start | bytes 2359304 | tf_op jit(solution)/shard_map/ppermute | solution.py:383
  971.6 36.8 %collective-permute-start.52 = (f32[14336]{0:T(1024)}, f32[14336]{0:T(1024)}, u32[]{:S(2)}, u32[]{:S(2)}) collective-permute-start(f32[14336]{0:T(1024)} %add.540), channel_id=1, source_target_pairs={{0,8},{4,12},{8,0},{12,4},{1,9},{5,13},{9,1},{13,5},{2,10},{6,14},... | collective-permute-start | bytes 172040 | tf_op jit(solution)/shard_map/ppermute | solution.py:383
  998.0 21.7 %collective-permute-start.50 = (bf16[2,96,1024]{2,1,0:T(8,128)(2,1)}, bf16[2,96,1024]{2,1,0:T(8,128)(2,1)S(1)}, u32[]{:S(2)}, u32[]{:S(2)}) collective-permute-start(bf16[2,96,1024]{2,1,0:T(8,128)(2,1)} %fusion.202), channel_id=1, source_target_pairs={{0,16},{1,17},{2,18},{3,19},{4,20},{5,21},{6,22},{7,23},{8,24},{9,... | collective-permute-start | bytes 1179656 | tf_op jit(solution)/shard_map/ppermute | solution.py:388
  (253 other events, 2057.1 us)
Sparse Core Ops, SparseCore 0:
  335.5 38.3 all-gather.10
  375.4 81.7 all-gather.8
  494.6 34.7 all-gather.14
  531.4 81.8 all-gather.12
  676.9 212.4 reduce-scatter.2
  891.6 125.7 reduce-scatter.4

commit v4 on v3

v4 whole, which is shorter than its diff:
```python
import functools

import jax
import jax.numpy as jnp
from jax import lax
from jax.experimental import pallas as pl
from jax.experimental.pallas import tpu as pltpu
from jax.sharding import PartitionSpec as P

HEAD_DIM = 128
CONV = 4
TOK_MB = 384
BLOCK = 128
BLOCKS = TOK_MB // BLOCK
EPS = 1e-06
OUT_FLOOR = 0.0001
F32 = jnp.float32
BF16 = jnp.bfloat16
BASE = 4
LANES = 128
TILE = 256
QUARTERS = 4
VMEM_LIMIT = 44 * 1024 * 1024


def mm(left, right):
    return lax.dot_general(
        left.astype(BF16), right.astype(BF16), (((1,), (0,)), ((), ())), preferred_element_type=F32
    )


def mm_t(left, right):
    return lax.dot_general(
        left.astype(BF16), right.astype(BF16), (((1,), (1,)), ((), ())), preferred_element_type=F32
    )


def t_mm(left, right):
    return lax.dot_general(
        left.astype(BF16), right.astype(BF16), (((0,), (0,)), ((), ())), preferred_element_type=F32
    )


def rows_of(b):
    return slice(b * BLOCK, (b + 1) * BLOCK)


def tiles_of(size, tile=TILE):
    return [slice(start, min(start + tile, size)) for start in range(0, size, tile)]


def quarters(size):
    return tiles_of(size, size // QUARTERS)


def relative_order(count):
    order, bit = [0], count // 2
    while bit:
        order = order + [k ^ bit for k in order]
        bit //= 2
    return order


def place_of(me_ref, difference, share):
    return pl.ds(pl.multiple_of((me_ref[0] ^ difference) * share, 16), share)


def stream(x, taps, masks):
    pre = taps[0:1] * x
    for tap in range(1, CONV):
        pre = pre + taps[tap : tap + 1] * (pltpu.roll(x, tap, 0) * masks[tap - 1])
    gate = jax.nn.sigmoid(pre)
    return pre, gate, pre * gate


def unit_inverses(systems):
    size = systems[0].shape[0]
    row = lax.broadcasted_iota(jnp.int32, (size, size), 0)
    col = lax.broadcasted_iota(jnp.int32, (size, size), 1)
    eye = (row == col).astype(F32)
    near = (row // BASE == col // BASE).astype(F32)
    first = [-a * near for a in systems]
    total = [eye + n for n in first]
    second = [mm(n, n) for n in first]
    third = [mm(n, s) for n, s in zip(first, second)]
    total = [t + s + r for t, s, r in zip(total, second, third)]
    step = BASE
    while step < size:
        span = 2 * step
        off = ((row // span == col // span) & (row // step != col // step)).astype(F32)
        inner = [mm(a * off, t) for a, t in zip(systems, total)]
        outer = [mm(t, i) for t, i in zip(total, inner)]
        total = [t - o for t, o in zip(total, outer)]
        step = span
    return total


def block_masks(seg_col_ref, seg_row_ref):
    row = lax.broadcasted_iota(jnp.int32, (BLOCK, BLOCK), 0)
    col = lax.broadcasted_iota(jnp.int32, (BLOCK, BLOCK), 1)
    strict, lower = {}, {}
    for b in range(BLOCKS):
        for c in range(b + 1):
            same = seg_col_ref[rows_of(b), :] == seg_row_ref[:, rows_of(c)]
            strict[b, c] = same & (col < row) if b == c else same
            lower[b, c] = same & (col <= row) if b == c else same
    return strict, lower


class Fetch:

    def __init__(self, pairs, sems, ahead):
        self.copies = [pltpu.make_async_copy(src, dst, sems.at[i]) for i, (src, dst) in enumerate(pairs)]
        self.ahead = ahead
        self.started = 0
        self.start_to(ahead)

    def start_to(self, place):
        while self.started < min(place, len(self.copies)):
            self.copies[self.started].start()
            self.started += 1

    def wait(self, place):
        self.copies[place].wait()
        self.start_to(place + 1 + self.ahead)

    def wait_group(self, group):
        for place in range(QUARTERS):
            self.wait(QUARTERS * group + place)


def attend_kernel(heads, count, me_ref, seg_col_ref, seg_row_ref, masks_ref, taps_ref, gain_ref, *refs):
    shards, refs = refs[:count], refs[count:]
    project_hbm, beta_hbm, merge_hbm = refs[:3]
    qkv_ref, logit_ref, mixed_ref, system_ref, attend_ref, inverse_ref, fresh_ref, out_ref = refs[3:11]
    partials = refs[11 : 11 + count]
    rows_ref, mixed_abs, project_ref, beta_ref, merge_ref, sems = refs[11 + count :]
    order = relative_order(count)
    share = TOK_MB // count
    fetch = Fetch(
        [(project_hbm.at[0, j], project_ref.at[j]) for j in range(3)]
        + [(beta_hbm, beta_ref), (merge_hbm.at[0], merge_ref)],
        sems,
        5,
    )
    for k in range(count):
        rows_ref[k * share : (k + 1) * share, :] = shards[k][...]
    rows = rows_ref[...]

    def spread(ref, value, *lead):
        for k, difference in enumerate(order):
            ref[(*lead, place_of(me_ref, difference, share), slice(None))] = value[k * share : (k + 1) * share]

    for j in range(3):
        fetch.wait(j)
        for cols in tiles_of(heads * HEAD_DIM):
            value = mm(rows, project_ref[j, :, cols])
            for k, difference in enumerate(order):
                qkv_ref[j, place_of(me_ref, difference, share), cols] = value[k * share : (k + 1) * share]
    fetch.wait(3)
    spread(logit_ref, mm(rows, beta_ref[...]))

    masks = [masks_ref[i] for i in range(CONV - 1)]
    strict, lower = block_masks(seg_col_ref, seg_row_ref)
    queries, keys, values, betas = [], [], [], []
    for h in range(heads):
        cols = slice(h * HEAD_DIM, (h + 1) * HEAD_DIM)
        taps = [taps_ref[0, j, :, cols] for j in range(3)]
        _, _, query = stream(qkv_ref[0, :, cols], taps[0], masks)
        _, _, key = stream(qkv_ref[1, :, cols], taps[1], masks)
        _, _, value = stream(qkv_ref[2, :, cols], taps[2], masks)
        query = query * lax.rsqrt(jnp.sum(query * query, axis=-1, keepdims=True) + EPS) * HEAD_DIM**-0.5
        key = key * lax.rsqrt(jnp.sum(key * key, axis=-1, keepdims=True) + EPS)
        beta = jax.nn.sigmoid(logit_ref[:, h : h + 1])
        queries.append(query.astype(BF16))
        keys.append(key.astype(BF16))
        values.append(value * beta)
        betas.append(beta)
    attend, system = {}, {}
    for h in range(heads):
        for b in range(BLOCKS):
            for c in range(b + 1):
                inner = mm_t(keys[h][rows_of(b)], keys[h][rows_of(c)])
                system[h, b, c] = jnp.where(strict[b, c], inner * betas[h][rows_of(b)], 0.0)
                scores = mm_t(queries[h][rows_of(b)], keys[h][rows_of(c)])
                attend[h, b, c] = jnp.where(lower[b, c], scores, 0.0).astype(BF16)
                attend_ref[h, rows_of(b), rows_of(c)] = attend[h, b, c]
                if c < b:
                    system[h, b, c] = system[h, b, c].astype(BF16)
                    system_ref[h, rows_of(b), rows_of(c)] = system[h, b, c]
    index = [(h, b) for h in range(heads) for b in range(BLOCKS)]
    inverse = dict(zip(index, unit_inverses([system[h, b, b] for h, b in index])))
    for h, b in index:
        inverse[h, b] = inverse[h, b].astype(BF16)
        inverse_ref[h, b] = inverse[h, b]
    fresh = {}
    for b in range(BLOCKS):
        for h in range(heads):
            target = values[h][rows_of(b)]
            for c in range(b):
                target = target - mm(system[h, b, c], fresh[h, c])
            fresh[h, b] = mm(inverse[h, b], target).astype(BF16)
            fresh_ref[rows_of(b), h * HEAD_DIM : (h + 1) * HEAD_DIM] = fresh[h, b]
    for h in range(heads):
        cols = slice(h * HEAD_DIM, (h + 1) * HEAD_DIM)
        for b in range(BLOCKS):
            out = mm(attend[h, b, 0], fresh[h, 0])
            for c in range(1, b + 1):
                out = out + mm(attend[h, b, c], fresh[h, c])
            mean = jnp.mean(out * out, axis=-1, keepdims=True)
            out_ref[rows_of(b), cols] = out
            mixed_abs[rows_of(b), cols] = (
                out * lax.rsqrt(jnp.maximum(mean, OUT_FLOOR)) * gain_ref[...]
            ).astype(BF16)
    for k, difference in enumerate(order):
        mixed_ref[k * share : (k + 1) * share, :] = mixed_abs[place_of(me_ref, difference, share), :]
    fetch.wait(4)
    write_partials(partials, merge_ref.shape[1], share, lambda cols: mm(mixed_ref[...], merge_ref[:, cols]))


def write_partials(partials, width, share, product):
    for cols in tiles_of(width):
        value = product(cols)
        for k, ref in enumerate(partials):
            ref[:, cols] = value[k * share : (k + 1) * share].astype(ref.dtype)


def partial_shapes(count, width):
    share = TOK_MB // count
    return [jax.ShapeDtypeStruct((share, width), F32 if k < count // 2 else BF16) for k in range(count)]


def call(kernel, operands, hbm, out_shape, scratch_shapes):
    vmem = pl.BlockSpec(memory_space=pltpu.VMEM)
    return pl.pallas_call(
        kernel,
        in_specs=[pl.BlockSpec(memory_space=pltpu.SMEM)]
        + [vmem] * (len(operands) - 1)
        + [pl.BlockSpec(memory_space=pl.ANY)] * len(hbm),
        out_specs=[vmem] * len(out_shape),
        out_shape=out_shape,
        scratch_shapes=scratch_shapes,
        compiler_params=pltpu.CompilerParams(vmem_limit_bytes=VMEM_LIMIT),
        cost_estimate=pl.CostEstimate(flops=10**6, bytes_accessed=10**5, transcendentals=0),
    )(*operands, *hbm)


def attend_forward(me, mine, shards, taps, gain, project, beta_weight, merge):
    masks, seg_col, seg_row = mine
    heads = merge.shape[1] // HEAD_DIM
    width = heads * HEAD_DIM
    model = merge.shape[2]
    count = len(shards)
    out = [
        jax.ShapeDtypeStruct((3, TOK_MB, width), F32),
        jax.ShapeDtypeStruct((TOK_MB, LANES), F32),
        jax.ShapeDtypeStruct((TOK_MB, width), BF16),
        jax.ShapeDtypeStruct((heads, TOK_MB, TOK_MB), BF16),
        jax.ShapeDtypeStruct((heads, TOK_MB, TOK_MB), BF16),
        jax.ShapeDtypeStruct((heads, BLOCKS, BLOCK, BLOCK), BF16),
        jax.ShapeDtypeStruct((TOK_MB, width), BF16),
        jax.ShapeDtypeStruct((TOK_MB, width), F32),
    ] + partial_shapes(count, model)
    results = call(
        functools.partial(attend_kernel, heads, count),
        (me, seg_col, seg_row, masks, taps, gain, *shards),
        (project, beta_weight, merge),
        out,
        [
            pltpu.VMEM((TOK_MB, model), BF16),
            pltpu.VMEM((TOK_MB, width), BF16),
            pltpu.VMEM(project.shape[1:], BF16),
            pltpu.VMEM(beta_weight.shape, BF16),
            pltpu.VMEM(merge.shape[1:], BF16),
            pltpu.SemaphoreType.DMA((5,)),
        ],
    )
    return results[:8], results[8:]


def expand_kernel(count, me_ref, *refs):
    shards, refs = refs[:count], refs[count:]
    expand_hbm, contract_hbm, hidden_ref, silu_ref, slope_ref = refs[:5]
    partials = refs[5 : 5 + count]
    rows_ref, gate_ref, expand_ref, contract_ref, sems = refs[5 + count :]
    share = TOK_MB // count
    tiles = tiles_of(hidden_ref.shape[1])
    fetch = Fetch(
        [(expand_hbm.at[0, j, s, :], expand_ref.at[j, s, :]) for j in range(2) for s in quarters(expand_ref.shape[1])]
        + [(contract_hbm.at[0, s, :], contract_ref.at[s, :]) for s in quarters(contract_ref.shape[0])],
        sems,
        QUARTERS,
    )
    for k in range(count):
        rows_ref[k * share : (k + 1) * share, :] = shards[k][...]
    fetch.wait_group(0)
    for t in tiles:
        gate_ref[:, t] = mm(rows_ref[...], expand_ref[0, :, t])
    fetch.wait_group(1)
    for t in tiles:
        up_in = mm(rows_ref[...], expand_ref[1, :, t])
        gate_in = gate_ref[:, t]
        gate = jax.nn.sigmoid(gate_in)
        silu = gate_in * gate
        hidden_ref[:, t] = (silu * up_in).astype(BF16)
        silu_ref[:, t] = silu.astype(BF16)
        slope_ref[:, t] = (up_in * gate * (1.0 + gate_in * (1.0 - gate))).astype(BF16)
    fetch.wait_group(2)
    write_partials(partials, rows_ref.shape[1], share, lambda cols: mm(hidden_ref[...], contract_ref[:, cols]))


def expand_forward(me, shards, expand, contract):
    count = len(shards)
    model, units = expand.shape[2:]
    kept = jax.ShapeDtypeStruct((TOK_MB, units), BF16)
    results = call(
        functools.partial(expand_kernel, count),
        (me, *shards),
        (expand, contract),
        [kept, kept, kept] + partial_shapes(count, model),
        [
            pltpu.VMEM((TOK_MB, model), BF16),
            pltpu.VMEM((TOK_MB, units), F32),
            pltpu.VMEM(expand.shape[1:], BF16),
            pltpu.VMEM(contract.shape[1:], BF16),
            pltpu.SemaphoreType.DMA((3 * QUARTERS,)),
        ],
    )
    return results[:3], results[3:]


def expand_back_kernel(count, me_ref, silu_ref, slope_ref, *refs):
    shards, refs = refs[:count], refs[count:]
    expand_hbm, contract_hbm, gate_ref, up_ref = refs[:4]
    partials = refs[4 : 4 + count]
    rows_ref, expand_ref, contract_ref, sems = refs[4 + count :]
    share = TOK_MB // count
    tiles = tiles_of(gate_ref.shape[1])
    spans = tiles_of(rows_ref.shape[1], 2 * TILE)
    fetch = Fetch(
        [(contract_hbm.at[0, s, :], contract_ref.at[s, :]) for s in quarters(contract_ref.shape[0])]
        + [(expand_hbm.at[0, j, s, :], expand_ref.at[j, s, :]) for s in spans for j in range(2)],
        sems,
        4,
    )
    for k in range(count):
        rows_ref[k * share : (k + 1) * share, :] = shards[k][...]
    fetch.wait_group(0)
    for t in tiles:
        grad_hidden = mm_t(rows_ref[...], contract_ref[t, :])
        gate_ref[:, t] = (grad_hidden * slope_ref[:, t].astype(F32)).astype(BF16)
        up_ref[:, t] = (grad_hidden * silu_ref[:, t].astype(F32)).astype(BF16)
    for i, span in enumerate(spans):
        for j in range(2):
            fetch.wait(QUARTERS + 2 * i + j)
        for s in tiles_of(span.stop - span.start):
            s = slice(span.start + s.start, span.start + s.stop)
            value = mm_t(gate_ref[...], expand_ref[0, s, :]) + mm_t(up_ref[...], expand_ref[1, s, :])
            for k, ref in enumerate(partials):
                ref[:, s] = value[k * share : (k + 1) * share].astype(ref.dtype)


def expand_backward(me, shards, silu, slope, expand, contract):
    count = len(shards)
    model, units = expand.shape[2:]
    kept = jax.ShapeDtypeStruct((TOK_MB, units), BF16)
    results = call(
        functools.partial(expand_back_kernel, count),
        (me, silu, slope, *shards),
        (expand, contract),
        [kept, kept] + partial_shapes(count, model),
        [
            pltpu.VMEM((TOK_MB, model), BF16),
            pltpu.VMEM(expand.shape[1:], BF16),
            pltpu.VMEM(contract.shape[1:], BF16),
            pltpu.SemaphoreType.DMA((QUARTERS + 2 * len(tiles_of(model, 2 * TILE)),)),
        ],
    )
    return results[:2], results[2:]


def stream_back(grad, x, pre, gate, taps, masks, taps_out, j, cols):
    grad_pre = grad * gate * (1.0 + pre * (1.0 - gate))
    grad_x = taps[0:1] * grad_pre
    taps_out[j, 0:1, cols] = jnp.sum(grad_pre * x, axis=0, keepdims=True)
    for tap in range(1, CONV):
        masked = grad_pre * masks[tap - 1]
        grad_x = grad_x + taps[tap : tap + 1] * pltpu.roll(masked, TOK_MB - tap, 0)
        taps_out[j, tap : tap + 1, cols] = jnp.sum(masked * pltpu.roll(x, tap, 0), axis=0, keepdims=True)
    return grad_x


def attend_back_kernel(heads, count, me_ref, seg_col_ref, seg_row_ref, masks_ref, taps_ref, gain_ref,
                       qkv_ref, logit_ref, system_ref, attend_ref, inverse_ref, fresh_ref, out_ref, *refs):
    shards, refs = refs[:count], refs[count:]
    project_hbm, beta_hbm, merge_hbm = refs[:3]
    grad_qkv_ref, grad_logit_ref, grad_taps_ref, grad_gain_ref = refs[3:7]
    partials = refs[7 : 7 + count]
    rows_ref, grad_mixed_ref, grad_abs_ref, logit_abs_ref, project_ref, beta_ref, merge_ref, sems = refs[7 + count :]
    order = relative_order(count)
    share = TOK_MB // count
    model = rows_ref.shape[1]
    width = heads * HEAD_DIM
    fetch = Fetch(
        [(merge_hbm.at[0], merge_ref), (beta_hbm, beta_ref)]
        + [(project_hbm.at[0, j], project_ref.at[j]) for j in range(3)],
        sems,
        0,
    )
    fetch.start_to(5)
    for k in range(count):
        rows_ref[k * share : (k + 1) * share, :] = shards[k][...]
    fetch.wait(0)
    for cols in tiles_of(heads * HEAD_DIM):
        value = mm_t(rows_ref[...], merge_ref[cols, :])
        for k, difference in enumerate(order):
            grad_mixed_ref[place_of(me_ref, difference, share), cols] = value[k * share : (k + 1) * share]

    masks = [masks_ref[i] for i in range(CONV - 1)]
    strict, lower = block_masks(seg_col_ref, seg_row_ref)
    lane = lax.broadcasted_iota(jnp.int32, (TOK_MB, LANES), 1)
    everyone = range(heads)
    columns = [slice(h * HEAD_DIM, (h + 1) * HEAD_DIM) for h in everyone]
    grad_gain = jnp.zeros((8, HEAD_DIM), F32)
    grad_outs, queries, keys, values, betas, convs = [], [], [], [], [], []
    for h in everyone:
        cols = columns[h]
        taps = [taps_ref[0, j, :, cols] for j in range(3)]
        _, _, conv_q = stream(qkv_ref[0, :, cols], taps[0], masks)
        _, _, conv_k = stream(qkv_ref[1, :, cols], taps[1], masks)
        scale_q = lax.rsqrt(jnp.sum(conv_q * conv_q, axis=-1, keepdims=True) + EPS)
        scale_k = lax.rsqrt(jnp.sum(conv_k * conv_k, axis=-1, keepdims=True) + EPS)
        queries.append((conv_q * (scale_q * HEAD_DIM**-0.5)).astype(BF16))
        keys.append((conv_k * scale_k).astype(BF16))
        betas.append(jax.nn.sigmoid(logit_ref[:, h : h + 1]))
        out = out_ref[:, cols]
        grad_mixed = grad_mixed_ref[:, cols]
        mean = jnp.mean(out * out, axis=-1, keepdims=True)
        scale = lax.rsqrt(jnp.maximum(mean, OUT_FLOOR))
        unit = out * scale
        grad_gain = grad_gain + jnp.sum((grad_mixed * unit).reshape(TOK_MB // 8, 8, HEAD_DIM), axis=0)
        grad_unit = grad_mixed * gain_ref[...]
        through = jnp.where(mean > OUT_FLOOR, 1.0, jnp.where(mean == OUT_FLOOR, 0.5, 0.0))
        grad_out = scale * (
            grad_unit - unit * (through * jnp.mean(grad_unit * unit, axis=-1, keepdims=True))
        )
        grad_outs.append(grad_out.astype(BF16))
    grad_gain_ref[...] = grad_gain
    fresh = {(h, b): fresh_ref[rows_of(b), columns[h]] for h in everyone for b in range(BLOCKS)}
    d_out = {(h, b): grad_outs[h][rows_of(b)] for h in everyone for b in range(BLOCKS)}
    key_blocks = {(h, b): keys[h][rows_of(b)] for h in everyone for b in range(BLOCKS)}
    d_fresh, d_target, d_target_b = {}, {}, {}
    for c in range(BLOCKS):
        for h in everyone:
            total = t_mm(attend_ref[h, rows_of(c), rows_of(c)], d_out[h, c])
            for b in range(c + 1, BLOCKS):
                total = total + t_mm(attend_ref[h, rows_of(b), rows_of(c)], d_out[h, b])
            d_fresh[h, c] = total
    for b in reversed(range(BLOCKS)):
        for h in everyone:
            d_target[h, b] = t_mm(inverse_ref[h, b], d_fresh[h, b])
            d_target_b[h, b] = d_target[h, b].astype(BF16)
        for h in everyone:
            for c in range(b):
                d_fresh[h, c] = d_fresh[h, c] - t_mm(system_ref[h, rows_of(b), rows_of(c)], d_target_b[h, b])
    grad_query, inner, grad_key = {}, {}, {}
    for b in range(BLOCKS):
        for c in range(b + 1):
            for h in everyone:
                d_attend = jnp.where(lower[b, c], mm_t(d_out[h, b], fresh[h, c]), 0.0).astype(BF16)
                d_system = jnp.where(strict[b, c], -mm_t(d_target_b[h, b], fresh[h, c]), 0.0)
                for store, place, part in (
                    (grad_query, b, mm(d_attend, key_blocks[h, c])),
                    (inner, b, mm(d_system, key_blocks[h, c])),
                    (grad_key, c, t_mm(d_attend, queries[h][rows_of(b)])
                     + t_mm(d_system * betas[h][rows_of(b)], key_blocks[h, b])),
                ):
                    store[h, place] = store[h, place] + part if (h, place) in store else part

    def whole(store, h):
        return jnp.concatenate([store[h, b] for b in range(BLOCKS)], axis=0)

    grad_logits = jnp.zeros((TOK_MB, LANES), F32)
    for h in everyone:
        cols = columns[h]
        beta = betas[h]
        taps = [taps_ref[0, j, :, cols] for j in range(3)]
        inputs = [qkv_ref[j, :, cols] for j in range(3)]
        pre_q, gate_q, conv_q = stream(inputs[0], taps[0], masks)
        pre_k, gate_k, conv_k = stream(inputs[1], taps[1], masks)
        pre_v, gate_v, value = stream(inputs[2], taps[2], masks)
        scale_q = lax.rsqrt(jnp.sum(conv_q * conv_q, axis=-1, keepdims=True) + EPS)
        scale_k = lax.rsqrt(jnp.sum(conv_k * conv_k, axis=-1, keepdims=True) + EPS)
        unit_q, key = conv_q * scale_q, conv_k * scale_k
        within = whole(inner, h)
        target = whole(d_target, h)
        grad_q = whole(grad_query, h)
        grad_k = whole(grad_key, h) + beta * within
        grad_beta = jnp.sum(within * key + target * value, axis=-1, keepdims=True)
        grad_logits = jnp.where(lane == h, grad_beta * beta * (1.0 - beta), grad_logits)
        grad_conv_q = (HEAD_DIM**-0.5 * scale_q) * (
            grad_q - unit_q * jnp.sum(grad_q * unit_q, axis=-1, keepdims=True)
        )
        grad_conv_k = scale_k * (grad_k - key * jnp.sum(grad_k * key, axis=-1, keepdims=True))
        for j, (grad, pre, gate) in enumerate(
            ((grad_conv_q, pre_q, gate_q), (grad_conv_k, pre_k, gate_k), (beta * target, pre_v, gate_v))
        ):
            grad_x = stream_back(grad, inputs[j], pre, gate, taps[j], masks, grad_taps_ref, j, cols)
            grad_abs_ref[j, :, cols] = grad_x.astype(BF16)
    logit_abs_ref[...] = grad_logits.astype(BF16)
    for k, difference in enumerate(order):
        here = slice(k * share, (k + 1) * share)
        there = place_of(me_ref, difference, share)
        grad_logit_ref[here, :] = logit_abs_ref[there, :]
        for j in range(3):
            grad_qkv_ref[here, j * width : (j + 1) * width] = grad_abs_ref[j, there, :]
    for place in range(1, 5):
        fetch.wait(place)
    for span in tiles_of(model):
        value = mm_t(grad_logit_ref[...], beta_ref[span, :])
        for j in range(3):
            value = value + mm_t(grad_qkv_ref[:, j * width : (j + 1) * width], project_ref[j, span, :])
        for k, ref in enumerate(partials):
            ref[:, span] = value[k * share : (k + 1) * share].astype(ref.dtype)


def attend_backward(me, mine, shards, kept, taps, gain, project, beta_weight, merge):
    masks, seg_col, seg_row = mine
    heads = merge.shape[1] // HEAD_DIM
    width = heads * HEAD_DIM
    model = merge.shape[2]
    count = len(shards)
    qkv, logit, _, system, attend, inverse, fresh, out = kept
    results = call(
        functools.partial(attend_back_kernel, heads, count),
        (me, seg_col, seg_row, masks, taps, gain, qkv, logit, system, attend, inverse, fresh, out, *shards),
        (project, beta_weight, merge),
        [
            jax.ShapeDtypeStruct((TOK_MB, 3 * width), BF16),
            jax.ShapeDtypeStruct((TOK_MB, LANES), BF16),
            jax.ShapeDtypeStruct((3, CONV, width), F32),
            jax.ShapeDtypeStruct((8, HEAD_DIM), F32),
        ]
        + partial_shapes(count, model),
        [
            pltpu.VMEM((TOK_MB, model), BF16),
            pltpu.VMEM((TOK_MB, width), F32),
            pltpu.VMEM((3, TOK_MB, width), BF16),
            pltpu.VMEM((TOK_MB, LANES), BF16),
            pltpu.VMEM(project.shape[1:], BF16),
            pltpu.VMEM(beta_weight.shape, BF16),
            pltpu.VMEM(merge.shape[1:], BF16),
            pltpu.SemaphoreType.DMA((5,)),
        ],
    )
    return results[:4], results[4:]


def tap_masks(segment):
    masks = []
    for tap in range(1, CONV):
        earlier = jnp.concatenate([jnp.full((tap,), -1, jnp.int32), segment[: TOK_MB - tap]], axis=0)
        masks.append(jnp.broadcast_to((earlier == segment).astype(F32)[:, None], (TOK_MB, HEAD_DIM)))
    return jnp.stack(masks)


def narrow(values):
    return values.astype(BF16)


def product(left, right):
    return jnp.dot(left, right, preferred_element_type=F32)


def product_left(left, right):
    return lax.dot_general(left, right, (((0,), (0,)), ((), ())), preferred_element_type=F32)


def product_right(left, right):
    return lax.dot_general(left, right, (((1,), (1,)), ((), ())), preferred_element_type=F32)


def rms_parts(values):
    scale = lax.rsqrt(jnp.mean(values * values, axis=-1, keepdims=True) + EPS)
    return (values * scale, scale)


def norm_back(grad_normed, normed, scale, gain):
    grad_scaled = grad_normed * gain
    return scale * (grad_scaled - normed * jnp.mean(grad_scaled * normed, axis=-1, keepdims=True))


def segment_ids(lengths, count):
    ends = jnp.cumsum(lengths)
    places = jnp.arange(count, dtype=jnp.int32)
    return jnp.sum((places[:, None] >= ends[None, :]).astype(jnp.int32), axis=1, dtype=jnp.int32)


def flipped(values, axis, bit):
    return lax.ppermute(values, axis, [(i, i ^ bit) for i in range(lax.axis_size(axis))])


def shifted(values, axis, distance):
    devices = range(lax.axis_size(axis))
    return lax.ppermute(values, axis, [(i, i + distance) for i in devices if i + distance in devices])


def bits_of(axis):
    size = lax.axis_size(axis)
    bits = [1 << k for k in range(size.bit_length() - 1)]
    assert 1 << len(bits) == size
    return bits


def summed(values, axes):
    for axis in axes:
        for bit in bits_of(axis):
            values = values + flipped(values, axis, bit)
    return values


def gather(shard):
    parts = [shard]
    for bit in reversed(bits_of("head")):
        parts = parts + [flipped(part, "head", bit) for part in parts]
    return parts


def scatter(parts):
    for bit in bits_of("head"):
        half = len(parts) // 2
        arrived = [flipped(narrow(part), "head", bit) for part in parts[half:]]
        parts = [part.astype(F32) + other.astype(F32) for part, other in zip(parts[:half], arrived)]
    return parts[0]


def swapped(shard):
    count = lax.axis_size("dp")
    me = lax.axis_index("dp")
    rows, width = shard.shape
    blocks = shard.reshape(rows, count, width // count)
    arrived = []
    for distance in range(count):
        block = lax.dynamic_index_in_dim(blocks, (me + distance) % count, 1, keepdims=False)
        if distance:
            block = lax.ppermute(block, "dp", [(i, (i + distance) % count) for i in range(count)])
        arrived.append(block)
    arrived = jnp.stack(arrived)
    ordered = [lax.dynamic_index_in_dim(arrived, (me - q) % count, 0, keepdims=False) for q in range(count)]
    return jnp.concatenate(ordered, axis=1)


def per_device(
    tokens,
    lengths,
    cotangent,
    attn_in,
    beta_weight,
    conv_weight,
    o_gain,
    attn_out,
    mlp_in,
    mlp_out,
    norm_gains,
):
    section = lax.axis_index("section")
    sections = lax.axis_size("section")
    member = lax.axis_index("head")
    micro = tokens.shape[0]
    width = tokens.shape[2]
    heads = beta_weight.shape[2]
    share = TOK_MB // lax.axis_size("head")
    me = member[None]
    beta_wide = jnp.pad(beta_weight[0], ((0, 0), (0, LANES - heads)))
    gains = norm_gains[0]
    every = range(micro)
    segments = [segment_ids(lengths[m], TOK_MB) for m in every]
    masks = [(tap_masks(s), s[:, None], s[None, :]) for s in segments]
    own_rows = lambda values: lax.dynamic_slice_in_dim(values, member * share, share, 0).astype(F32)
    tokens_own = [own_rows(tokens[m]) for m in every]
    cotangent_own = [own_rows(cotangent[m]) for m in every]

    def forward(x, mine):
        unit, scale = rms_parts(x)
        normed = gather(narrow(unit * gains[0]))
        kept, partials = attend_forward(me, mine, normed, conv_weight, o_gain, attn_in, beta_wide, attn_out)
        middle = x + scatter(partials)
        unit_mid, scale_mid = rms_parts(middle)
        normed_mid = gather(narrow(unit_mid * gains[1]))
        (hidden, silu, slope), partials = expand_forward(me, normed_mid, mlp_in, mlp_out)
        result = middle + scatter(partials)
        return result, (unit, scale, normed, kept, unit_mid, scale_mid, normed_mid, hidden, silu, slope)

    def backward(incoming, mine, saved, early=None):
        unit, scale, normed, kept, unit_mid, scale_mid, normed_mid, _, silu, slope = saved
        (grad_gate, grad_up), partials = expand_backward(
            me, gather(narrow(incoming)), silu, slope, mlp_in, mlp_out
        )
        grad_mid = scatter(partials)
        grad_middle = incoming + norm_back(grad_mid, unit_mid, scale_mid, gains[1])
        big = (normed_mid, grad_gate, grad_up)
        if early is not None:
            big = early(*big)
            grad_middle, big = lax.optimization_barrier((grad_middle, big))
        gain_two = jnp.sum(grad_mid * unit_mid, axis=0)
        (grad_qkv, grad_logit, grad_taps, grad_head_gain), partials = attend_backward(
            me, mine, gather(narrow(grad_middle)), kept, conv_weight, o_gain, attn_in, beta_wide, attn_out
        )
        grad_norm = scatter(partials)
        grad_inputs = grad_middle + norm_back(grad_norm, unit, scale, gains[0])
        gain_one = jnp.sum(grad_norm * unit, axis=0)
        big = (normed, grad_qkv, grad_logit, narrow(incoming), narrow(grad_middle)) + big
        small = (grad_taps, jnp.sum(grad_head_gain, axis=0), jnp.stack([gain_one, gain_two]))
        return grad_inputs, big, small

    last = sections - 1
    zero = jnp.zeros((share, width), F32)
    steps = micro + last
    kept = []
    arrived = zero
    for step in range(steps):
        first = tokens_own[min(step, micro - 1)]
        inputs = jnp.where(section == 0, first, arrived)
        mine = [jnp.where(section == 0, a, b) for a, b in zip(masks[min(step, micro - 1)], masks[max(step - last, 0)])]
        result, saved = forward(inputs, mine)
        kept.append((saved, mine))
        if step < steps - 1:
            arrived = shifted(narrow(result), "section", 1).astype(F32)
    def picked(values, own=None):
        chosen = [values[i] for i in range(last, micro)]
        for i in range(last):
            first = values[i] if own is None else own
            chosen.append(jax.tree.map(lambda a, b: jnp.where(section <= i, a, b), first, values[i + micro]))
        return chosen

    def joined(own, place):
        chosen = picked([term and term[0][place] for term in terms], own)
        if isinstance(own, list):
            chosen = [part for parts in chosen for part in parts]
        return jnp.concatenate(chosen, axis=0)

    def mlp_terms(*own):
        normed_mid, grad_gate, grad_up = (joined(own[place], 5 + place) for place in range(3))
        return narrow(product_left(normed_mid, grad_gate)), narrow(product_left(normed_mid, grad_up))

    def every_row(values):
        return [lax.all_gather(value, "dp", axis=0) for value in picked(values)]

    hidden_rows = every_row([saved[7] for saved, _ in kept])
    mixed_rows = every_row([saved[3][2] for saved, _ in kept])

    arrived = zero
    terms = [None] * steps
    finals = [None] * micro
    for step in reversed(range(steps)):
        place = step - last
        top = cotangent_own[place] if place >= 0 else zero
        incoming = jnp.where(section == last, top, arrived if step < micro else zero)
        saved, mine = kept[step]
        if step < len(hidden_rows):
            turn = len(hidden_rows) - 1 - step
            incoming, hidden_rows[turn], mixed_rows[turn] = lax.optimization_barrier(
                (incoming, hidden_rows[turn], mixed_rows[turn])
            )
        result, big, small = backward(incoming, mine, saved, mlp_terms if step == 0 else None)
        terms[step] = (big, small)
        if step < micro:
            finals[step] = result
        if step > 0:
            arrived = shifted(narrow(result), "section", -1).astype(F32)
    rows_out = jnp.stack(finals)
    half = width // sections
    moved = shifted(narrow(rows_out[:, :, half:]), "section", 1).astype(F32)
    grad_tokens = jnp.where(section == 0, rows_out[:, :, :half], moved)

    def spread(value, axis):
        return lax.psum_scatter(value, "dp", scatter_dimension=axis, tiled=True)

    own = terms[0][0]
    early = [spread(part, 0) for part in own[5:]]
    normed, grad_qkv, grad_logit = (joined(own[place], place) for place in range(3))
    grad_project = narrow(product_left(normed, grad_qkv))
    grad_beta = product_left(normed, grad_logit)[:, :heads]
    grad_project, early = lax.optimization_barrier((grad_project, early))
    grad_expand = jnp.stack(early).astype(F32)
    grad_project = jnp.stack(jnp.split(spread(grad_project, 0), 3, axis=1)).astype(F32)

    def from_rows(rows, place):
        total = 0.0
        for left, right in zip(rows, picked([term[0][place] for term in terms])):
            right = jnp.concatenate(gather(swapped(right)), axis=0).reshape(TOK_MB, left.shape[0], -1)
            total = total + lax.dot_general(
                left, right, (((0, 1), (1, 0)), ((), ())), preferred_element_type=F32
            )
        return total

    grad_contract = from_rows(hidden_rows, 3)
    grad_merge = from_rows(mixed_rows, 4)
    grad_taps, grad_head_gain, grad_gains = (
        sum(term[1][place] for term in terms) for place in range(3)
    )
    grad_gains = summed(jnp.concatenate([grad_gains.reshape(-1), grad_head_gain]), ("dp", "head"))
    grad_gains, grad_head_gain = grad_gains[: 2 * width].reshape(2, width), grad_gains[2 * width :]
    flat = summed(jnp.concatenate([grad_taps.reshape(-1), grad_beta.reshape(-1)]), ("dp",))
    grad_taps, grad_beta = flat[: grad_taps.size].reshape(grad_taps.shape), flat[grad_taps.size :]
    rows = width // lax.axis_size("dp")
    grad_beta = lax.dynamic_slice_in_dim(grad_beta.reshape(width, heads), lax.axis_index("dp") * rows, rows, 0)
    return (
        grad_tokens,
        grad_project[None],
        grad_beta[None],
        grad_taps[None],
        grad_head_gain[None],
        grad_merge[None],
        grad_expand[None],
        grad_contract[None],
        grad_gains[None],
    )


def solution(mesh):
    return jax.shard_map(
        per_device,
        mesh=mesh,
        in_specs=(
            P("dp", None, None),
            P("dp", None),
            P("dp", None, None),
            P("section", None, None, "head"),
            P("section", None, "head"),
            P("section", None, None, "head"),
            P("section", None),
            P("section", "head", None),
            P("section", None, None, "head"),
            P("section", "head", None),
            P("section", None, None),
        ),
        out_specs=(
            P("dp", "head", "section"),
            P("section", None, "dp", "head"),
            P("section", "dp", "head"),
            P("section", None, None, "head"),
            P("section", None),
            P("section", "head", "dp"),
            P("section", None, "dp", "head"),
            P("section", "head", "dp"),
            P("section", None, None),
        ),
        check_vma=False,
    )
```

time: 1040 us -> 957 us (0.920)
  matrix products: 152 us -> 37.9 us
  Pallas kernels: 58.8 us -> 164 us
  local copies, waits for them, and re-layouts: 105 us -> 54.3 us
  waiting for transfers between devices: 494 us -> 459 us
  starting transfers between devices: 87.9 us -> 119 us
  other arithmetic: 121 us -> 94.7 us
    dot_general x47 -> x0, matrix products: 117 us -> none  [the longest x23 66.6 us: product(): return jnp.dot(left, right, preferred_element_type=F32)]
    reduce_scatter x2 -> x3, waiting for transfers between devices: 54.8 us -> 163 us  [spread(): return lax.psum_scatter(value, 'dp', scatter_dimension=axis, tiled=True)]
    pallas_call x6 -> x12, Pallas kernels: 58.8 us -> 164 us  [call(): pl.pallas_call(kernel, in_specs=[pl.BlockSpec(memory_space=pltpu.SMEM)] +...]
    all_gather x4, waiting for transfers between devices: 83 us -> 0.01 us  [every_row(): return [lax.all_gather(value, 'dp', axis=0) for value in picked(values)]]
    another operation x73 -> x3, other arithmetic: 48.6 us -> 1.15 us  [the longest x64 34.2 us: gather(): jnp.stack([jnp.where(low, parts, other), jnp.where(low, other, parts)], a...]
    ppermute x60 -> x87, waiting for transfers between devices: 261 us -> 229 us  [flipped(): lax.ppermute(values, axis, [(i, i ^ bit) for i in range(lax.axis_size(axi...]
    ppermute x12, waiting for transfers between devices: 58 us -> 30.7 us  [swapped(): lax.ppermute(block, 'dp', [(i, (i + distance) % count) for i in range(cou...]
    another operation x20 -> x2, local copies, waits for them, and re-layouts: 22 us -> 1.47 us  [the longest x1 1.47 us: per_device(): jnp.stack(jnp.split(spread(grad_project, 0), 3, axis=1)).astype(F32)]
  transfers between devices with their start and end apart: 83 -> 111, of which waited for: 58 -> 61; matrix products, arithmetic and copies ran while one was open for 19% -> 15% of each run, Pallas kernels for 4% -> 11%
where the time goes in v4:
time: 957 us; the launch traced here: 945 us
  waiting for transfers between devices  459 us (48%)
  Pallas kernels  164 us (17%)
  starting transfers between devices  119 us (12%)
  other arithmetic  94.7 us (10%)
  local copies, waits for them, and re-layouts  54.3 us (6%)
  matrix products  37.9 us (4%)
  between operations  17 us (2%)
    ppermute x87, waiting for transfers between devices, flipped(): lax.ppermute(values, axis, [(i, i ^ bit) for i in range(lax.axis_size(axi...  229 us
    pallas_call x12, Pallas kernels, call(): pl.pallas_call(kernel, in_specs=[pl.BlockSpec(memory_space=pltpu.SMEM)] +...  164 us
    reduce_scatter x3, waiting for transfers between devices, spread(): return lax.psum_scatter(value, 'dp', scatter_dimension=axis, tiled=True)  163 us
    ppermute x87, starting transfers between devices, flipped(): lax.ppermute(values, axis, [(i, i ^ bit) for i in range(lax.axis_size(axi...  63.3 us
    ppermute x12, starting transfers between devices, swapped(): lax.ppermute(block, 'dp', [(i, (i + distance) % count) for i in range(cou...  39.6 us
    ppermute x5, waiting for transfers between devices, shifted(): lax.ppermute(values, axis, [(i, i + distance) for i in devices if i + dis...  35.4 us
    ppermute x12, waiting for transfers between devices, swapped(): lax.ppermute(block, 'dp', [(i, (i + distance) % count) for i in range(cou...  30.7 us
    unnamed x342, local copies, waits for them, and re-layouts  27 us
  transfers between devices with their start and end apart: 111, of which 61 were waited for; matrix products, arithmetic and copies ran while one was open for 15% of the time, Pallas kernels for 11%

profile of v4, /device:TPU:0, one launch (start us, length us, event | category | flops | bytes accessed | tf_op | source)
XLA Modules:
  0.0 945.2 jit_solution(4985077139947857196)
XLA Ops:
  16.7 9.0 collective-permute-done.refs_1_
  27.6 13.0 %shard_map.178 = (f32[3,384,512]{2,1,0:T(8,128)}, f32[384,128]{1,0:T(8,128)S(1)}, bf16[384,512]{1,0:T(8,128)(2,1)S(1)}, bf16[4,384,384]{2,1,0:T(8,128)(2,1)S(1)}...) custom-call(s32[1]{0:T(128)} %bitcast.5.me_ref, ...), custom_call_target="tpu_custom_call" | custom-call | flops 1000000 | bytes 100000 | tf_op jit(solution)/shard_map/pallas_call | solution.py:235
  44.4 9.6 %collective-permute-done.5 = bf16[96,2048]{1,0:T(8,128)(2,1)S(1)} collective-permute-done((bf16[96,2048]{1,0:T(8,128)(2,1)S(1)}, bf16[96,2048]{1,0:T(8,128)(2,1)S(1)}, u32[]{:S(2)}, u32[]{:S(2)}) %collective-permute-start.5) | collective-permute-done | bytes 393248 | tf_op jit(solution)/shard_map/ppermute | solution.py:600
  58.8 8.8 collective-permute-done.6.refs_1_
  69.3 11.4 %shard_map.179 = (bf16[384,1408]{1,0:T(8,128)(2,1)S(1)}, bf16[384,1408]{1,0:T(8,128)(2,1)S(1)}, bf16[384,1408]{1,0:T(8,128)(2,1)S(1)}, f32[96,2048]{1,0:T(8,128)...) custom-call(s32[1]{0:T(128)} %bitcast.5.me_ref, ...), custom_call_target="tpu_custom_call" | custom-call | flops 1000000 | bytes 100000 | tf_op jit(solution)/shard_map/pallas_call | solution.py:235
  84.5 9.4 collective-permute-done.11
  97.8 7.8 collective-permute-done.12
  109.0 7.9 collective-permute-done.13.refs_1_
  118.6 12.0 %shard_map.180 = (f32[3,384,512]{2,1,0:T(8,128)}, f32[384,128]{1,0:T(8,128)S(1)}, bf16[384,512]{1,0:T(8,128)(2,1)}, bf16[4,384,384]{2,1,0:T(8,128)(2,1)S(1)}, bf...) custom-call(s32[1]{0:T(128)} %bitcast.5.me_ref, ...), custom_call_target="tpu_custom_call" | custom-call | flops 1000000 | bytes 100000 | tf_op jit(solution)/shard_map/pallas_call | solution.py:235
  134.2 9.7 %collective-permute-done.18 = bf16[96,2048]{1,0:T(8,128)(2,1)S(1)} collective-permute-done((bf16[96,2048]{1,0:T(8,128)(2,1)S(1)}, bf16[96,2048]{1,0:T(8,128)(2,1)S(1)}, u32[]{:S(2)}, u32[]{:S(2)}) %collective-permute-start.18) | collective-permute-done | bytes 393248 | tf_op jit(solution)/shard_map/ppermute | solution.py:600
  147.5 8.8 collective-permute-done.19.refs_1_
  158.0 12.0 %shard_map.181 = (bf16[384,1408]{1,0:T(8,128)(2,1)S(1)}, bf16[384,1408]{1,0:T(8,128)(2,1)S(1)}, bf16[384,1408]{1,0:T(8,128)(2,1)S(1)}, f32[96,2048]{1,0:T(8,128)...) custom-call(s32[1]{0:T(128)} %bitcast.5.me_ref, ...), custom_call_target="tpu_custom_call" | custom-call | flops 1000000 | bytes 100000 | tf_op jit(solution)/shard_map/pallas_call | solution.py:235
  177.9 9.2 collective-permute-done.24
  195.6 6.5 collective-permute-done.25
  207.3 7.9 collective-permute-done.26.refs_1_
  216.9 12.3 %shard_map.182 = (f32[3,384,512]{2,1,0:T(8,128)}, f32[384,128]{1,0:T(8,128)S(1)}, bf16[384,512]{1,0:T(8,128)(2,1)S(1)}, bf16[4,384,384]{2,1,0:T(8,128)(2,1)S(1)}...) custom-call(s32[1]{0:T(128)} %bitcast.5.me_ref, ...), custom_call_target="tpu_custom_call" | custom-call | flops 1000000 | bytes 100000 | tf_op jit(solution)/shard_map/pallas_call | solution.py:235
  246.6 8.0 collective-permute-done.31
  260.6 9.9 %collective-permute-done.32.refs_1_ = bf16[96,2048]{1,0:T(8,128)(2,1)S(1)} collective-permute-done((bf16[96,2048]{1,0:T(8,128)(2,1)S(1)}, bf16[96,2048]{1,0:T(8,128)(2,1)S(1)}, u32[]{:S(2)}, u32[]{:S(2)}) %collective-permute-start.32) | collective-permute-done | bytes 393248 | tf_op jit(solution)/shard_map/ppermute | solution.py:600
  271.0 6.4 collective-permute-done.35.refs_1_
  277.4 12.6 %shard_map.183 = (bf16[384,1408]{1,0:T(8,128)(2,1)S(1)}, bf16[384,1408]{1,0:T(8,128)(2,1)S(1)}, bf16[384,1408]{1,0:T(8,128)(2,1)S(1)}, f32[96,2048]{1,0:T(8,128)...) custom-call(s32[1]{0:T(128)} %bitcast.5.me_ref, ...), custom_call_target="tpu_custom_call" | custom-call | flops 1000000 | bytes 100000 | tf_op jit(solution)/shard_map/pallas_call | solution.py:235
  291.0 11.2 %shard_map.184 = (bf16[384,1408]{1,0:T(8,128)(2,1)S(1)}, bf16[384,1408]{1,0:T(8,128)(2,1)S(1)}, f32[96,2048]{1,0:T(8,128)S(1)}, f32[96,2048]{1,0:T(8,128)S(1)}, ...) custom-call(s32[1]{0:T(128)} %bitcast.5.me_ref, bf16[384,1408]{1,0:T(8,128)(2,1)S(1)} %get-tuple-element.136.silu_ref, ...), custom_call_target="tpu_custom_call" | custom-call | flops 1000000 | bytes 100000 | tf_op jit(solution)/shard_map/pallas_call | solution.py:235
  306.0 9.9 %collective-permute-done.40 = bf16[96,2048]{1,0:T(8,128)(2,1)S(1)} collective-permute-done((bf16[96,2048]{1,0:T(8,128)(2,1)S(1)}, bf16[96,2048]{1,0:T(8,128)(2,1)S(1)}, u32[]{:S(2)}, u32[]{:S(2)}) %collective-permute-start.40) | collective-permute-done | bytes 393248 | tf_op jit(solution)/shard_map/ppermute | solution.py:600
  321.2 9.2 collective-permute-done.41.refs_1_
  332.1 18.9 %shard_map.185 = (bf16[384,1536]{1,0:T(8,128)(2,1)S(1)}, bf16[384,128]{1,0:T(8,128)(2,1)S(1)}, f32[3,4,512]{2,1,0:T(4,128)S(1)}, f32[8,128]{1,0:T(8,128)S(1)}, f...) custom-call(s32[1]{0:T(128)} %bitcast.5.me_ref, ...), custom_call_target="tpu_custom_call" | custom-call | flops 1000000 | bytes 100000 | tf_op jit(solution)/shard_map/pallas_call | solution.py:235
  357.1 9.0 collective-permute-done.46
  371.3 10.9 %collective-permute-done.47 = bf16[96,2048]{1,0:T(8,128)(2,1)S(1)} collective-permute-done((bf16[96,2048]{1,0:T(8,128)(2,1)S(1)}, bf16[96,2048]{1,0:T(8,128)(2,1)S(1)}, u32[]{:S(2)}, u32[]{:S(2)}) %collective-permute-start.47) | collective-permute-done | bytes 393248 | tf_op jit(solution)/shard_map/ppermute | solution.py:605
  387.0 8.0 collective-permute-done.48.refs_1_
  399.9 12.3 %shard_map.186 = (bf16[384,1408]{1,0:T(8,128)(2,1)S(1)}, bf16[384,1408]{1,0:T(8,128)(2,1)S(1)}, f32[96,2048]{1,0:T(8,128)S(1)}, f32[96,2048]{1,0:T(8,128)S(1)}, ...) custom-call(s32[1]{0:T(128)} %bitcast.5.me_ref, bf16[384,1408]{1,0:T(8,128)(2,1)S(1)} %copy-done.50, ...), custom_call_target="tpu_custom_call" | custom-call | flops 1000000 | bytes 100000 | tf_op jit(solution)/shard_map/pallas_call | solution.py:235
  416.7 9.9 %collective-permute-done.53 = bf16[96,2048]{1,0:T(8,128)(2,1)S(1)} collective-permute-done((bf16[96,2048]{1,0:T(8,128)(2,1)S(1)}, bf16[96,2048]{1,0:T(8,128)(2,1)S(1)}, u32[]{:S(2)}, u32[]{:S(2)}) %collective-permute-start.53) | collective-permute-done | bytes 393248 | tf_op jit(solution)/shard_map/ppermute | solution.py:600
  431.0 9.2 collective-permute-done.54.refs_1_
  442.0 18.3 %shard_map.187 = (bf16[384,1536]{1,0:T(8,128)(2,1)S(1)}, bf16[384,128]{1,0:T(8,128)(2,1)S(1)}, f32[3,4,512]{2,1,0:T(4,128)S(1)}, f32[8,128]{1,0:T(8,128)S(1)}, f...) custom-call(s32[1]{0:T(128)} %bitcast.5.me_ref, ...), custom_call_target="tpu_custom_call" | custom-call | flops 1000000 | bytes 100000 | tf_op jit(solution)/shard_map/pallas_call | solution.py:235
  463.7 9.7 %collective-permute-done.59 = bf16[96,2048]{1,0:T(8,128)(2,1)S(1)} collective-permute-done((bf16[96,2048]{1,0:T(8,128)(2,1)S(1)}, bf16[96,2048]{1,0:T(8,128)(2,1)S(1)}, u32[]{:S(2)}, u32[]{:S(2)}) %collective-permute-start.59) | collective-permute-done | bytes 393248 | tf_op jit(solution)/shard_map/ppermute | solution.py:600
  479.5 10.1 %collective-permute-done.60 = bf16[96,2048]{1,0:T(8,128)(2,1)S(1)} collective-permute-done((bf16[96,2048]{1,0:T(8,128)(2,1)S(1)}, bf16[96,2048]{1,0:T(8,128)(2,1)S(1)}, u32[]{:S(2)}, u32[]{:S(2)}) %collective-permute-start.60) | collective-permute-done | bytes 393248 | tf_op jit(solution)/shard_map/ppermute | solution.py:605
  495.2 7.2 collective-permute-done.61.refs_1_
  504.1 11.3 %shard_map.188 = (bf16[384,1408]{1,0:T(8,128)(2,1)S(1)}, bf16[384,1408]{1,0:T(8,128)(2,1)S(1)}, f32[96,2048]{1,0:T(8,128)S(1)}, f32[96,2048]{1,0:T(8,128)S(1)}, ...) custom-call(s32[1]{0:T(128)} %bitcast.5.me_ref, bf16[384,1408]{1,0:T(8,128)(2,1)S(1)} %copy-done.46, ...), custom_call_target="tpu_custom_call" | custom-call | flops 1000000 | bytes 100000 | tf_op jit(solution)/shard_map/pallas_call | solution.py:235
  518.3 7.0 convolution_convert_fusion.1
  530.1 9.1 convolution_convert_fusion.2
  552.3 8.0 collective-permute-done.67.refs_1_
  562.1 18.6 %shard_map.189 = (bf16[384,1536]{1,0:T(8,128)(2,1)S(1)}, bf16[384,128]{1,0:T(8,128)(2,1)S(1)}, f32[3,4,512]{2,1,0:T(4,128)S(1)}, f32[8,128]{1,0:T(8,128)S(1)}, f...) custom-call(s32[1]{0:T(128)} %bitcast.5.me_ref, ...), custom_call_target="tpu_custom_call" | custom-call | flops 1000000 | bytes 100000 | tf_op jit(solution)/shard_map/pallas_call | solution.py:235
  583.1 7.3 convolution_convert_fusion
  590.4 57.5 %reduce-scatter.4.cloned.1.call-done = bf16[512,1408]{1,0:T(8,128)(2,1)} async-done(((bf16[2048,1408]{1,0:T(8,128)(2,1)}), bf16[512,1408]{1,0:T(8,128)(2,1)}) %reduce-scatter.4.cloned.1.call-update) | async-done | bytes 1441808 | tf_op jit(solution)/shard_map/reduce_scatter | solution.py:777
  647.9 105.5 %reduce-scatter.6.cloned.1.call-done = bf16[512,1408]{1,0:T(8,128)(2,1)} async-done(((bf16[2048,1408]{1,0:T(8,128)(2,1)}), bf16[512,1408]{1,0:T(8,128)(2,1)}) %reduce-scatter.6.cloned.1.call-update) | async-done | bytes 1441808 | tf_op jit(solution)/shard_map/reduce_scatter | solution.py:777
  766.7 10.0 %collective-permute-start.80 = (bf16[96,512]{1,0:T(8,128)(2,1)S(1)}, bf16[96,512]{1,0:T(8,128)(2,1)S(1)}, u32[]{:S(2)}, u32[]{:S(2)}) collective-permute-start(bf16[96,512]{1,0:T(8,128)(2,1)S(1)} %bitcast.256), channel_id=1, source_target_pairs={{0,4},{4,8},{8,12},{12,0},{1,5},{5,9},{9,13},{13,1},{2,6},{6,10},{... | collective-permute-start | bytes 294920 | tf_op jit(solution)/shard_map/ppermute | solution.py:646
  791.3 8.1 collective-permute-start.98
  809.4 5.9 collective-permute-done.99
  819.3 8.1 collective-permute-done.101
  877.2 6.0 collective-permute-done.89
  885.4 6.6 collective-permute-start.74
  (692 shorter events, 313.2 us)
Async XLA Ops:
  7.2 377.0 %all-gather.11.cloned.1.call-start = ((), (), s32[]{:S(2)}) async-start(), calls=%async_computation.7 | async-start | bytes 1966080 | tf_op jit(solution)/shard_map/all_gather | solution.py:747
  13.3 12.4 %collective-permute-start = (bf16[96,2048]{1,0:T(8,128)(2,1)}, bf16[96,2048]{1,0:T(8,128)(2,1)}, u32[]{:S(2)}, u32[]{:S(2)}) collective-permute-start(bf16[96,2048]{1,0:T(8,128)(2,1)} %multiply_convert_fusion.5.refs_0_), channel_id=1, source_target_pairs={{0,2},{1,3},{2,0},{3,1},{4,6},{5,7},{6,4},{7,5},{8,10},{9,11},{10,... | collective-permute-start | bytes 1179656 | tf_op jit(solution)/shard_map/ppermute | solution.py:600
  42.6 11.5 %collective-permute-start.5 = (bf16[96,2048]{1,0:T(8,128)(2,1)S(1)}, bf16[96,2048]{1,0:T(8,128)(2,1)S(1)}, u32[]{:S(2)}, u32[]{:S(2)}) collective-permute-start(bf16[96,2048]{1,0:T(8,128)(2,1)S(1)} %add_convert_fusion.13), channel_id=1, source_target_pairs={{0,2},{1,3},{2,0},{3,1},{4,6},{5,7},{6,4},{7,5},{8,10},{9,11},{10,... | collective-permute-start | bytes 1179656 | tf_op jit(solution)/shard_map/ppermute | solution.py:600
  82.7 11.2 %collective-permute-start.11 = (bf16[96,2048]{1,0:T(8,128)(2,1)S(1)}, bf16[96,2048]{1,0:T(8,128)(2,1)S(1)}, u32[]{:S(2)}, u32[]{:S(2)}) collective-permute-start(bf16[96,2048]{1,0:T(8,128)(2,1)S(1)} %add_convert_fusion.12), channel_id=1, source_target_pairs={{0,2},{1,3},{2,0},{3,1},{4,6},{5,7},{6,4},{7,5},{8,10},{9,11},{10,... | collective-permute-start | bytes 1179656 | tf_op jit(solution)/shard_map/ppermute | solution.py:600
  94.1 11.5 %collective-permute-start.12 = (bf16[96,2048]{1,0:T(8,128)(2,1)S(1)}, bf16[96,2048]{1,0:T(8,128)(2,1)S(1)}, u32[]{:S(2)}, u32[]{:S(2)}) collective-permute-start(bf16[96,2048]{1,0:T(8,128)(2,1)S(1)} %add_convert_fusion.11), channel_id=1, source_target_pairs={{0,16},{1,17},{2,18},{3,19},{4,20},{5,21},{6,22},{7,23},{8,24},{9,... | collective-permute-start | bytes 1179656 | tf_op jit(solution)/shard_map/ppermute | solution.py:605
  132.6 11.2 %collective-permute-start.18 = (bf16[96,2048]{1,0:T(8,128)(2,1)S(1)}, bf16[96,2048]{1,0:T(8,128)(2,1)S(1)}, u32[]{:S(2)}, u32[]{:S(2)}) collective-permute-start(bf16[96,2048]{1,0:T(8,128)(2,1)S(1)} %add_convert_fusion.10), channel_id=1, source_target_pairs={{0,2},{1,3},{2,0},{3,1},{4,6},{5,7},{6,4},{7,5},{8,10},{9,11},{10,... | collective-permute-start | bytes 1179656 | tf_op jit(solution)/shard_map/ppermute | solution.py:600
  175.6 11.5 %collective-permute-start.24 = (bf16[96,2048]{1,0:T(8,128)(2,1)}, bf16[96,2048]{1,0:T(8,128)(2,1)}, u32[]{:S(2)}, u32[]{:S(2)}) collective-permute-start(bf16[96,2048]{1,0:T(8,128)(2,1)} %add_convert_fusion.9), channel_id=1, source_target_pairs={{0,2},{1,3},{2,0},{3,1},{4,6},{5,7},{6,4},{7,5},{8,10},{9,11},{10,... | collective-permute-start | bytes 1179656 | tf_op jit(solution)/shard_map/ppermute | solution.py:600
  189.6 12.5 %collective-permute-start.25 = (bf16[96,2048]{1,0:T(8,128)(2,1)}, bf16[96,2048]{1,0:T(8,128)(2,1)S(1)}, u32[]{:S(2)}, u32[]{:S(2)}) collective-permute-start(bf16[96,2048]{1,0:T(8,128)(2,1)} %add_convert_fusion.8), channel_id=1, source_target_pairs={{0,16},{1,17},{2,18},{3,19},{4,20},{5,21},{6,22},{7,23},{8,24},{9,... | collective-permute-start | bytes 1179656 | tf_op jit(solution)/shard_map/ppermute | solution.py:605
  194.8 189.4 %all-gather.9.cloned.1.call-start = ((), (), s32[]{:S(2)}) async-start(), calls=%async_computation.6 | async-start | bytes 5406720 | tf_op jit(solution)/shard_map/all_gather | solution.py:747
  243.0 11.5 %collective-permute-start.31 = (bf16[96,2048]{1,0:T(8,128)(2,1)}, bf16[96,2048]{1,0:T(8,128)(2,1)}, u32[]{:S(2)}, u32[]{:S(2)}) collective-permute-start(bf16[96,2048]{1,0:T(8,128)(2,1)} %add_convert_fusion.7), channel_id=1, source_target_pairs={{0,2},{1,3},{2,0},{3,1},{4,6},{5,7},{6,4},{7,5},{8,10},{9,11},{10,... | collective-permute-start | bytes 1179656 | tf_op jit(solution)/shard_map/ppermute | solution.py:600
  245.3 245.3 %all-gather.15.cloned.1.call-start = ((), (), s32[]{:S(2)}) async-start(), calls=%async_computation.9 | async-start | bytes 1966080 | tf_op jit(solution)/shard_map/all_gather | solution.py:747
  258.4 12.1 %collective-permute-start.32 = (bf16[96,2048]{1,0:T(8,128)(2,1)S(1)}, bf16[96,2048]{1,0:T(8,128)(2,1)S(1)}, u32[]{:S(2)}, u32[]{:S(2)}) collective-permute-start(bf16[96,2048]{1,0:T(8,128)(2,1)S(1)} %get-tuple-element.244.refs_0_), channel_id=1, source_target_pairs={{0,2},{1,3},{2,0},{3,1},{4,6},{5,7},{6,4},{7,5},{8,10},{9,11},{10,... | collective-permute-start | bytes 1179656 | tf_op jit(solution)/shard_map/ppermute | solution.py:600
  260.1 17.3 %collective-permute-start.35 = (bf16[96,2048]{1,0:T(8,128)(2,1)S(1)}, bf16[96,2048]{1,0:T(8,128)(2,1)S(1)}, u32[]{:S(2)}, u32[]{:S(2)}) collective-permute-start(bf16[96,2048]{1,0:T(8,128)(2,1)S(1)} %bitcast_convert_fusion.refs_0_), channel_id=1, source_target_pairs={{0,2},{1,3},{2,0},{3,1},{4,6},{5,7},{6,4},{7,5},{8,10},{9,11},{10,... | collective-permute-start | bytes 1179656 | tf_op jit(solution)/shard_map/ppermute | solution.py:600
  260.6 16.8 %collective-permute-start.33 = (bf16[96,2048]{1,0:T(8,128)(2,1)S(1)}, bf16[96,2048]{1,0:T(8,128)(2,1)S(1)}, u32[]{:S(2)}, u32[]{:S(2)}) collective-permute-start(bf16[96,2048]{1,0:T(8,128)(2,1)S(1)} %get-tuple-element.244.refs_0_), channel_id=1, source_target_pairs={{0,1},{1,0},{2,3},{3,2},{4,5},{5,4},{6,7},{7,6},{8,9},{9,8},{10,11... | collective-permute-start | bytes 1179656 | tf_op jit(solution)/shard_map/ppermute | solution.py:600
  270.5 20.5 %collective-permute-start.36 = (bf16[96,2048]{1,0:T(8,128)(2,1)S(1)}, bf16[96,2048]{1,0:T(8,128)(2,1)S(1)}, u32[]{:S(2)}, u32[]{:S(2)}) collective-permute-start(bf16[96,2048]{1,0:T(8,128)(2,1)S(1)} %bitcast_convert_fusion.refs_0_), channel_id=1, source_target_pairs={{0,1},{1,0},{2,3},{3,2},{4,5},{5,4},{6,7},{7,6},{8,9},{9,8},{10,11... | collective-permute-start | bytes 1179656 | tf_op jit(solution)/shard_map/ppermute | solution.py:600
  277.4 13.6 %collective-permute-start.37 = (bf16[96,2048]{1,0:T(8,128)(2,1)S(1)}, bf16[96,2048]{1,0:T(8,128)(2,1)S(1)}, u32[]{:S(2)}, u32[]{:S(2)}) collective-permute-start(bf16[96,2048]{1,0:T(8,128)(2,1)S(1)} %collective-permute-done.35.refs_1_), channel_id=1, source_target_pairs={{0,1},{1,0},{2,3},{3,2},{4,5},{5,4},{6,7},{7,6},{8,9},{9,8},{10,11... | collective-permute-start | bytes 1179656 | tf_op jit(solution)/shard_map/ppermute | solution.py:600
  304.2 11.6 %collective-permute-start.40 = (bf16[96,2048]{1,0:T(8,128)(2,1)S(1)}, bf16[96,2048]{1,0:T(8,128)(2,1)S(1)}, u32[]{:S(2)}, u32[]{:S(2)}) collective-permute-start(bf16[96,2048]{1,0:T(8,128)(2,1)S(1)} %add_convert_fusion.6), channel_id=1, source_target_pairs={{0,2},{1,3},{2,0},{3,1},{4,6},{5,7},{6,4},{7,5},{8,10},{9,11},{10,... | collective-permute-start | bytes 1179656 | tf_op jit(solution)/shard_map/ppermute | solution.py:600
  354.6 11.5 %collective-permute-start.46 = (bf16[96,2048]{1,0:T(8,128)(2,1)}, bf16[96,2048]{1,0:T(8,128)(2,1)}, u32[]{:S(2)}, u32[]{:S(2)}) collective-permute-start(bf16[96,2048]{1,0:T(8,128)(2,1)} %add_convert_fusion.5), channel_id=1, source_target_pairs={{0,2},{1,3},{2,0},{3,1},{4,6},{5,7},{6,4},{7,5},{8,10},{9,11},{10,... | collective-permute-start | bytes 1179656 | tf_op jit(solution)/shard_map/ppermute | solution.py:600
  357.0 133.6 %all-gather.13.cloned.1.call-start = ((), (), s32[]{:S(2)}) async-start(), calls=%async_computation.8 | async-start | bytes 5406720 | tf_op jit(solution)/shard_map/all_gather | solution.py:747
  370.0 12.2 %collective-permute-start.47 = (bf16[96,2048]{1,0:T(8,128)(2,1)S(1)}, bf16[96,2048]{1,0:T(8,128)(2,1)S(1)}, u32[]{:S(2)}, u32[]{:S(2)}) collective-permute-start(bf16[96,2048]{1,0:T(8,128)(2,1)S(1)} %add_convert_fusion.4), channel_id=1, source_target_pairs={{16,0},{17,1},{18,2},{19,3},{20,4},{21,5},{22,6},{23,7},{24,8},{25... | collective-permute-start | bytes 1179656 | tf_op jit(solution)/shard_map/ppermute | solution.py:605
  397.4 250.5 %reduce-scatter.4.cloned.1.call-start = ((), (), s32[]{:S(2)}) async-start(), calls=%async_computation.3 | async-start | bytes 7208960 | tf_op jit(solution)/shard_map/reduce_scatter | solution.py:777
  415.1 11.5 %collective-permute-start.53 = (bf16[96,2048]{1,0:T(8,128)(2,1)S(1)}, bf16[96,2048]{1,0:T(8,128)(2,1)S(1)}, u32[]{:S(2)}, u32[]{:S(2)}) collective-permute-start(bf16[96,2048]{1,0:T(8,128)(2,1)S(1)} %add_convert_fusion.3), channel_id=1, source_target_pairs={{0,2},{1,3},{2,0},{3,1},{4,6},{5,7},{6,4},{7,5},{8,10},{9,11},{10,... | collective-permute-start | bytes 1179656 | tf_op jit(solution)/shard_map/ppermute | solution.py:600
  477.2 12.5 %collective-permute-start.60 = (bf16[96,2048]{1,0:T(8,128)(2,1)S(1)}, bf16[96,2048]{1,0:T(8,128)(2,1)S(1)}, u32[]{:S(2)}, u32[]{:S(2)}) collective-permute-start(bf16[96,2048]{1,0:T(8,128)(2,1)S(1)} %get-tuple-element.247), channel_id=1, source_target_pairs={{16,0},{17,1},{18,2},{19,3},{20,4},{21,5},{22,6},{23,7},{24,8},{25... | collective-permute-start | bytes 1179656 | tf_op jit(solution)/shard_map/ppermute | solution.py:605
  516.5 22.7 %collective-permute-start.64 = (bf16[96,2048]{1,0:T(8,128)(2,1)S(1)}, bf16[96,2048]{1,0:T(8,128)(2,1)}, u32[]{:S(2)}, u32[]{:S(2)}) collective-permute-start(bf16[96,2048]{1,0:T(8,128)(2,1)S(1)} %get-tuple-element.181), channel_id=1, source_target_pairs={{0,1},{1,0},{2,3},{3,2},{4,5},{5,4},{6,7},{7,6},{8,9},{9,8},{10,11... | collective-permute-start | bytes 1179656 | tf_op jit(solution)/shard_map/ppermute | solution.py:600
  528.6 11.4 %collective-permute-start.66 = (bf16[96,2048]{1,0:T(8,128)(2,1)}, bf16[96,2048]{1,0:T(8,128)(2,1)S(1)}, u32[]{:S(2)}, u32[]{:S(2)}) collective-permute-start(bf16[96,2048]{1,0:T(8,128)(2,1)} %add_convert_fusion.1), channel_id=1, source_target_pairs={{0,2},{1,3},{2,0},{3,1},{4,6},{5,7},{6,4},{7,5},{8,10},{9,11},{10,... | collective-permute-start | bytes 1179656 | tf_op jit(solution)/shard_map/ppermute | solution.py:600
  545.3 208.2 %reduce-scatter.6.cloned.1.call-start = ((), (), s32[]{:S(2)}) async-start(), calls=%async_computation.4 | async-start | bytes 7208960 | tf_op jit(solution)/shard_map/reduce_scatter | solution.py:777
  545.9 388.6 %reduce-scatter.8.cloned.1.call-start = ((), (), s32[]{:S(2)}) async-start(), calls=%async_computation.5 | async-start | bytes 7864320 | tf_op jit(solution)/shard_map/reduce_scatter | solution.py:777
  766.7 17.1 %collective-permute-start.80 = (bf16[96,512]{1,0:T(8,128)(2,1)S(1)}, bf16[96,512]{1,0:T(8,128)(2,1)S(1)}, u32[]{:S(2)}, u32[]{:S(2)}) collective-permute-start(bf16[96,512]{1,0:T(8,128)(2,1)S(1)} %bitcast.256), channel_id=1, source_target_pairs={{0,4},{4,8},{8,12},{12,0},{1,5},{5,9},{9,13},{13,1},{2,6},{6,10},{... | collective-permute-start | bytes 294920 | tf_op jit(solution)/shard_map/ppermute | solution.py:646
  778.7 11.3 %collective-permute-start.82 = (bf16[96,512]{1,0:T(8,128)(2,1)S(1)}, bf16[96,512]{1,0:T(8,128)(2,1)S(1)}, u32[]{:S(2)}, u32[]{:S(2)}) collective-permute-start(bf16[96,512]{1,0:T(8,128)(2,1)S(1)} %bitcast.258), channel_id=1, source_target_pairs={{0,12},{4,0},{8,4},{12,8},{1,13},{5,1},{9,5},{13,9},{2,14},{6,2},{... | collective-permute-start | bytes 294920 | tf_op jit(solution)/shard_map/ppermute | solution.py:646
  780.0 38.1 %collective-permute-start.95 = (bf16[96,2048]{1,0:T(8,128)(2,1)}, bf16[96,2048]{1,0:T(8,128)(2,1)S(1)}, u32[]{:S(2)}, u32[]{:S(2)}) collective-permute-start(bf16[96,2048]{1,0:T(8,128)(2,1)} %pad_maximum_fusion.12), channel_id=1, source_target_pairs={{0,2},{1,3},{2,0},{3,1},{4,6},{5,7},{6,4},{7,5},{8,10},{9,11},{10,... | collective-permute-start | bytes 1179656 | tf_op jit(solution)/shard_map/ppermute | solution.py:600
  781.5 37.2 %collective-permute-start.96 = (bf16[96,2048]{1,0:T(8,128)(2,1)}, bf16[96,2048]{1,0:T(8,128)(2,1)}, u32[]{:S(2)}, u32[]{:S(2)}) collective-permute-start(bf16[96,2048]{1,0:T(8,128)(2,1)} %pad_maximum_fusion.12), channel_id=1, source_target_pairs={{0,1},{1,0},{2,3},{3,2},{4,5},{5,4},{6,7},{7,6},{8,9},{9,8},{10,11... | collective-permute-start | bytes 1179656 | tf_op jit(solution)/shard_map/ppermute | solution.py:600
  791.3 16.6 %collective-permute-start.98 = (bf16[96,512]{1,0:T(8,128)(2,1)S(1)}, bf16[96,512]{1,0:T(8,128)(2,1)S(1)}, u32[]{:S(2)}, u32[]{:S(2)}) collective-permute-start(bf16[96,512]{1,0:T(8,128)(2,1)S(1)} %bitcast.261), channel_id=1, source_target_pairs={{0,4},{4,8},{8,12},{12,0},{1,5},{5,9},{9,13},{13,1},{2,6},{6,10},{... | collective-permute-start | bytes 294920 | tf_op jit(solution)/shard_map/ppermute | solution.py:646
  799.4 15.9 %collective-permute-start.99 = (bf16[96,512]{1,0:T(8,128)(2,1)S(1)}, bf16[96,512]{1,0:T(8,128)(2,1)S(1)}, u32[]{:S(2)}, u32[]{:S(2)}) collective-permute-start(bf16[96,512]{1,0:T(8,128)(2,1)S(1)} %bitcast.259), channel_id=1, source_target_pairs={{0,8},{4,12},{8,0},{12,4},{1,9},{5,13},{9,1},{13,5},{2,10},{6,14},... | collective-permute-start | bytes 294920 | tf_op jit(solution)/shard_map/ppermute | solution.py:646
  802.9 13.0 %collective-permute-start.100 = (bf16[96,512]{1,0:T(8,128)(2,1)S(1)}, bf16[96,512]{1,0:T(8,128)(2,1)S(1)}, u32[]{:S(2)}, u32[]{:S(2)}) collective-permute-start(bf16[96,512]{1,0:T(8,128)(2,1)S(1)} %bitcast.262), channel_id=1, source_target_pairs={{0,12},{4,0},{8,4},{12,8},{1,13},{5,1},{9,5},{13,9},{2,14},{6,2},{... | collective-permute-start | bytes 294920 | tf_op jit(solution)/shard_map/ppermute | solution.py:646
  818.1 16.4 %collective-permute-start.84 = (bf16[96,2048]{1,0:T(8,128)(2,1)}, bf16[96,2048]{1,0:T(8,128)(2,1)}, u32[]{:S(2)}, u32[]{:S(2)}) collective-permute-start(bf16[96,2048]{1,0:T(8,128)(2,1)} %pad_maximum_fusion.8), channel_id=1, source_target_pairs={{0,1},{1,0},{2,3},{3,2},{4,5},{5,4},{6,7},{7,6},{8,9},{9,8},{10,11... | collective-permute-start | bytes 1179656 | tf_op jit(solution)/shard_map/ppermute | solution.py:600
  818.7 15.9 %collective-permute-start.85 = (bf16[96,2048]{1,0:T(8,128)(2,1)S(1)}, bf16[96,2048]{1,0:T(8,128)(2,1)}, u32[]{:S(2)}, u32[]{:S(2)}) collective-permute-start(bf16[96,2048]{1,0:T(8,128)(2,1)S(1)} %collective-permute-done.83), channel_id=1, source_target_pairs={{0,1},{1,0},{2,3},{3,2},{4,5},{5,4},{6,7},{7,6},{8,9},{9,8},{10,11... | collective-permute-start | bytes 1179656 | tf_op jit(solution)/shard_map/ppermute | solution.py:600
  818.7 22.8 %collective-permute-start.102 = (bf16[96,2048]{1,0:T(8,128)(2,1)}, bf16[96,2048]{1,0:T(8,128)(2,1)}, u32[]{:S(2)}, u32[]{:S(2)}) collective-permute-start(bf16[96,2048]{1,0:T(8,128)(2,1)} %pad_maximum_fusion.14), channel_id=1, source_target_pairs={{0,1},{1,0},{2,3},{3,2},{4,5},{5,4},{6,7},{7,6},{8,9},{9,8},{10,11... | collective-permute-start | bytes 1179656 | tf_op jit(solution)/shard_map/ppermute | solution.py:600
  827.3 14.1 %collective-permute-start.103 = (bf16[96,2048]{1,0:T(8,128)(2,1)S(1)}, bf16[96,2048]{1,0:T(8,128)(2,1)}, u32[]{:S(2)}, u32[]{:S(2)}) collective-permute-start(bf16[96,2048]{1,0:T(8,128)(2,1)S(1)} %collective-permute-done.101), channel_id=1, source_target_pairs={{0,1},{1,0},{2,3},{3,2},{4,5},{5,4},{6,7},{7,6},{8,9},{9,8},{10,11... | collective-permute-start | bytes 1179656 | tf_op jit(solution)/shard_map/ppermute | solution.py:600
  849.6 14.5 %collective-permute-start.86 = (bf16[96,512]{1,0:T(8,128)(2,1)S(1)}, bf16[96,512]{1,0:T(8,128)(2,1)S(1)}, u32[]{:S(2)}, u32[]{:S(2)}) collective-permute-start(bf16[96,512]{1,0:T(8,128)(2,1)S(1)} %bitcast.260), channel_id=1, source_target_pairs={{0,4},{4,8},{8,12},{12,0},{1,5},{5,9},{9,13},{13,1},{2,6},{6,10},{... | collective-permute-start | bytes 294920 | tf_op jit(solution)/shard_map/ppermute | solution.py:646
  855.4 14.5 %collective-permute-start.87 = (bf16[96,512]{1,0:T(8,128)(2,1)S(1)}, bf16[96,512]{1,0:T(8,128)(2,1)S(1)}, u32[]{:S(2)}, u32[]{:S(2)}) collective-permute-start(bf16[96,512]{1,0:T(8,128)(2,1)S(1)} %bitcast.263), channel_id=1, source_target_pairs={{0,8},{4,12},{8,0},{12,4},{1,9},{5,13},{9,1},{13,5},{2,10},{6,14},... | collective-permute-start | bytes 294920 | tf_op jit(solution)/shard_map/ppermute | solution.py:646
  858.8 12.1 %collective-permute-start.88 = (bf16[96,512]{1,0:T(8,128)(2,1)S(1)}, bf16[96,512]{1,0:T(8,128)(2,1)S(1)}, u32[]{:S(2)}, u32[]{:S(2)}) collective-permute-start(bf16[96,512]{1,0:T(8,128)(2,1)S(1)} %bitcast.264), channel_id=1, source_target_pairs={{0,12},{4,0},{8,4},{12,8},{1,13},{5,1},{9,5},{13,9},{2,14},{6,2},{... | collective-permute-start | bytes 294920 | tf_op jit(solution)/shard_map/ppermute | solution.py:646
  871.8 11.4 %collective-permute-start.89 = (bf16[96,2048]{1,0:T(8,128)(2,1)}, bf16[96,2048]{1,0:T(8,128)(2,1)}, u32[]{:S(2)}, u32[]{:S(2)}) collective-permute-start(bf16[96,2048]{1,0:T(8,128)(2,1)} %pad_maximum_fusion.10), channel_id=1, source_target_pairs={{0,2},{1,3},{2,0},{3,1},{4,6},{5,7},{6,4},{7,5},{8,10},{9,11},{10,... | collective-permute-start | bytes 1179656 | tf_op jit(solution)/shard_map/ppermute | solution.py:600
  877.2 23.5 %collective-permute-start.90 = (bf16[96,2048]{1,0:T(8,128)(2,1)}, bf16[96,2048]{1,0:T(8,128)(2,1)}, u32[]{:S(2)}, u32[]{:S(2)}) collective-permute-start(bf16[96,2048]{1,0:T(8,128)(2,1)} %pad_maximum_fusion.10), channel_id=1, source_target_pairs={{0,1},{1,0},{2,3},{3,2},{4,5},{5,4},{6,7},{7,6},{8,9},{9,8},{10,11... | collective-permute-start | bytes 1179656 | tf_op jit(solution)/shard_map/ppermute | solution.py:600
  883.2 17.5 %collective-permute-start.91 = (bf16[96,2048]{1,0:T(8,128)(2,1)}, bf16[96,2048]{1,0:T(8,128)(2,1)}, u32[]{:S(2)}, u32[]{:S(2)}) collective-permute-start(bf16[96,2048]{1,0:T(8,128)(2,1)} %collective-permute-done.89), channel_id=1, source_target_pairs={{0,1},{1,0},{2,3},{3,2},{4,5},{5,4},{6,7},{7,6},{8,9},{9,8},{10,11... | collective-permute-start | bytes 1179656 | tf_op jit(solution)/shard_map/ppermute | solution.py:600
  883.2 14.9 %collective-permute-start.71 = (bf16[96,2048]{1,0:T(8,128)(2,1)S(1)}, bf16[96,2048]{1,0:T(8,128)(2,1)}, u32[]{:S(2)}, u32[]{:S(2)}) collective-permute-start(bf16[96,2048]{1,0:T(8,128)(2,1)S(1)} %get-tuple-element.201), channel_id=1, source_target_pairs={{0,1},{1,0},{2,3},{3,2},{4,5},{5,4},{6,7},{7,6},{8,9},{9,8},{10,11... | collective-permute-start | bytes 1179656 | tf_op jit(solution)/shard_map/ppermute | solution.py:600
  883.7 23.0 %collective-permute-start.70 = (bf16[96,2048]{1,0:T(8,128)(2,1)S(1)}, bf16[96,2048]{1,0:T(8,128)(2,1)S(1)}, u32[]{:S(2)}, u32[]{:S(2)}) collective-permute-start(bf16[96,2048]{1,0:T(8,128)(2,1)S(1)} %get-tuple-element.199), channel_id=1, source_target_pairs={{0,1},{1,0},{2,3},{3,2},{4,5},{5,4},{6,7},{7,6},{8,9},{9,8},{10,11... | collective-permute-start | bytes 1179656 | tf_op jit(solution)/shard_map/ppermute | solution.py:600
  894.6 28.0 %collective-permute-start.75 = (f32[14336]{0:T(1024)S(1)}, f32[14336]{0:T(1024)}, u32[]{:S(2)}, u32[]{:S(2)}) collective-permute-start(f32[14336]{0:T(1024)S(1)} %add.422), channel_id=1, source_target_pairs={{0,8},{4,12},{8,0},{12,4},{1,9},{5,13},{9,1},{13,5},{2,10},{6,14},... | collective-permute-start | bytes 172040 | tf_op jit(solution)/shard_map/ppermute | solution.py:600
  916.2 13.4 %collective-permute-start.73 = (bf16[2,96,1024]{2,1,0:T(8,128)(2,1)}, bf16[2,96,1024]{2,1,0:T(8,128)(2,1)}, u32[]{:S(2)}, u32[]{:S(2)}) collective-permute-start(bf16[2,96,1024]{2,1,0:T(8,128)(2,1)} %fusion.15), channel_id=1, source_target_pairs={{0,16},{1,17},{2,18},{3,19},{4,20},{5,21},{6,22},{7,23},{8,24},{9,... | collective-permute-start | bytes 1179656 | tf_op jit(solution)/shard_map/ppermute | solution.py:605
  (221 other events, 2394.2 us)
Sparse Core Ops, SparseCore 0:
  194.9 37.3 all-gather.10
  245.4 84.1 all-gather.8
  357.1 38.0 all-gather.14
  397.5 83.3 all-gather.12
  545.4 102.4 reduce-scatter.3
  650.6 102.7 reduce-scatter.5
  755.7 131.2 reduce-scatter.7

commit v5 on v4

--- a/solution.py
+++ b/solution.py
@@ -691,83 +691,60 @@
         result = middle + scatter(partials)
         return result, (unit, scale, normed, kept, unit_mid, scale_mid, normed_mid, hidden, silu, slope)
 
-    def backward(incoming, mine, saved, early=None):
-        unit, scale, normed, kept, unit_mid, scale_mid, normed_mid, _, silu, slope = saved
-        (grad_gate, grad_up), partials = expand_backward(
-            me, gather(narrow(incoming)), silu, slope, mlp_in, mlp_out
-        )
+    def backward_mlp(incoming, saved):
+        unit_mid, scale_mid, silu, slope = saved[4], saved[5], saved[8], saved[9]
+        grads, partials = expand_backward(me, gather(narrow(incoming)), silu, slope, mlp_in, mlp_out)
         grad_mid = scatter(partials)
         grad_middle = incoming + norm_back(grad_mid, unit_mid, scale_mid, gains[1])
-        big = (normed_mid, grad_gate, grad_up)
-        if early is not None:
-            big = early(*big)
-            grad_middle, big = lax.optimization_barrier((grad_middle, big))
-        gain_two = jnp.sum(grad_mid * unit_mid, axis=0)
+        return grad_middle, grads, jnp.sum(grad_mid * unit_mid, axis=0)
+
+    def backward_mix(grad_middle, gain_two, mine, saved):
+        unit, scale, _, kept = saved[:4]
         (grad_qkv, grad_logit, grad_taps, grad_head_gain), partials = attend_backward(
             me, mine, gather(narrow(grad_middle)), kept, conv_weight, o_gain, attn_in, beta_wide, attn_out
         )
         grad_norm = scatter(partials)
         grad_inputs = grad_middle + norm_back(grad_norm, unit, scale, gains[0])
         gain_one = jnp.sum(grad_norm * unit, axis=0)
-        big = (normed, grad_qkv, grad_logit, narrow(incoming), narrow(grad_middle)) + big
         small = (grad_taps, jnp.sum(grad_head_gain, axis=0), jnp.stack([gain_one, gain_two]))
-        return grad_inputs, big, small
+        return grad_inputs, grad_qkv, grad_logit, small
+
+    def forward_turn(inputs):
+        results = [forward(inputs[m], masks[m]) for m in every]
+        return [result for result, _ in results], [saved for _, saved in results]
 
     last = sections - 1
-    zero = jnp.zeros((share, width), F32)
-    steps = micro + last
-    kept = []
-    arrived = zero
-    for step in range(steps):
-        first = tokens_own[min(step, micro - 1)]
-        inputs = jnp.where(section == 0, first, arrived)
-        mine = [jnp.where(section == 0, a, b) for a, b in zip(masks[min(step, micro - 1)], masks[max(step - last, 0)])]
-        result, saved = forward(inputs, mine)
-        kept.append((saved, mine))
-        if step < steps - 1:
-            arrived = shifted(narrow(result), "section", 1).astype(F32)
-    def picked(values, own=None):
-        chosen = [values[i] for i in range(last, micro)]
-        for i in range(last):
-            first = values[i] if own is None else own
-            chosen.append(jax.tree.map(lambda a, b: jnp.where(section <= i, a, b), first, values[i + micro]))
-        return chosen
-
-    def joined(own, place):
-        chosen = picked([term and term[0][place] for term in terms], own)
-        if isinstance(own, list):
-            chosen = [part for parts in chosen for part in parts]
-        return jnp.concatenate(chosen, axis=0)
-
-    def mlp_terms(*own):
-        normed_mid, grad_gate, grad_up = (joined(own[place], 5 + place) for place in range(3))
-        return narrow(product_left(normed_mid, grad_gate)), narrow(product_left(normed_mid, grad_up))
+    inputs = tokens_own
+    for turn in range(sections):
+        outputs, kept = forward_turn(inputs)
+        if turn < last:
+            arrived = [shifted(narrow(value), "section", 1).astype(F32) for value in outputs]
+            inputs = [jnp.where(section == 0, tokens_own[m], arrived[m]) for m in every]
 
     def every_row(values):
-        return [lax.all_gather(value, "dp", axis=0) for value in picked(values)]
-
-    hidden_rows = every_row([saved[7] for saved, _ in kept])
-    mixed_rows = every_row([saved[3][2] for saved, _ in kept])
-
-    arrived = zero
-    terms = [None] * steps
-    finals = [None] * micro
-    for step in reversed(range(steps)):
-        place = step - last
-        top = cotangent_own[place] if place >= 0 else zero
-        incoming = jnp.where(section == last, top, arrived if step < micro else zero)
-        saved, mine = kept[step]
-        if step < len(hidden_rows):
-            turn = len(hidden_rows) - 1 - step
-            incoming, hidden_rows[turn], mixed_rows[turn] = lax.optimization_barrier(
-                (incoming, hidden_rows[turn], mixed_rows[turn])
-            )
-        result, big, small = backward(incoming, mine, saved, mlp_terms if step == 0 else None)
-        terms[step] = (big, small)
-        if step < micro:
-            finals[step] = result
-        if step > 0:
-            arrived = shifted(narrow(result), "section", -1).astype(F32)
+        return [lax.all_gather(value, "dp", axis=0) for value in values]
+
+    hidden_rows = every_row([saved[7] for saved in kept])
+    mixed_rows = every_row([saved[3][2] for saved in kept])
+
+    incoming = cotangent_own
+    for turn in range(sections):
+        if turn == last:
+            incoming, hidden_rows, mixed_rows = lax.optimization_barrier((incoming, hidden_rows, mixed_rows))
+        halves = [backward_mlp(incoming[m], kept[m]) for m in every]
+        middles = [half[0] for half in halves]
+        if turn == last:
+            normed_mid = jnp.concatenate([part for saved in kept for part in saved[6]], axis=0)
+            expands = [
+                narrow(product_left(normed_mid, jnp.concatenate([half[1][j] for half in halves], axis=0)))
+                for j in range(2)
+            ]
+            middles, expands = lax.optimization_barrier((middles, expands))
+        results = [backward_mix(middles[m], halves[m][2], masks[m], kept[m]) for m in every]
+        finals = [result[0] for result in results]
+        if turn < last:
+            arrived = [shifted(narrow(value), "section", -1).astype(F32) for value in finals]
+            incoming = [jnp.where(section == last, cotangent_own[m], arrived[m]) for m in every]
     rows_out = jnp.stack(finals)
     half = width // sections
     moved = shifted(narrow(rows_out[:, :, half:]), "section", 1).astype(F32)
@@ -776,28 +753,26 @@
     def spread(value, axis):
         return lax.psum_scatter(value, "dp", scatter_dimension=axis, tiled=True)
 
-    own = terms[0][0]
-    early = [spread(part, 0) for part in own[5:]]
-    normed, grad_qkv, grad_logit = (joined(own[place], place) for place in range(3))
+    early = [spread(part, 0) for part in expands]
+    normed = jnp.concatenate([part for saved in kept for part in saved[2]], axis=0)
+    grad_qkv = jnp.concatenate([result[1] for result in results], axis=0)
+    grad_logit = jnp.concatenate([result[2] for result in results], axis=0)
     grad_project = narrow(product_left(normed, grad_qkv))
     grad_beta = product_left(normed, grad_logit)[:, :heads]
-    grad_project, early = lax.optimization_barrier((grad_project, early))
-    grad_expand = jnp.stack(early).astype(F32)
-    grad_project = jnp.stack(jnp.split(spread(grad_project, 0), 3, axis=1)).astype(F32)
-
-    def from_rows(rows, place):
+
+    def from_rows(rows, shards):
         total = 0.0
-        for left, right in zip(rows, picked([term[0][place] for term in terms])):
+        for left, right in zip(rows, shards):
             right = jnp.concatenate(gather(swapped(right)), axis=0).reshape(TOK_MB, left.shape[0], -1)
             total = total + lax.dot_general(
                 left, right, (((0, 1), (1, 0)), ((), ())), preferred_element_type=F32
             )
         return total
 
-    grad_contract = from_rows(hidden_rows, 3)
-    grad_merge = from_rows(mixed_rows, 4)
+    grad_contract = from_rows(hidden_rows, [narrow(value) for value in incoming])
+    grad_merge = from_rows(mixed_rows, [narrow(value) for value in middles])
     grad_taps, grad_head_gain, grad_gains = (
-        sum(term[1][place] for term in terms) for place in range(3)
+        sum(result[3][place] for result in results) for place in range(3)
     )
     grad_gains = summed(jnp.concatenate([grad_gains.reshape(-1), grad_head_gain]), ("dp", "head"))
     grad_gains, grad_head_gain = grad_gains[: 2 * width].reshape(2, width), grad_gains[2 * width :]
@@ -805,6 +780,11 @@
     grad_taps, grad_beta = flat[: grad_taps.size].reshape(grad_taps.shape), flat[grad_taps.size :]
     rows = width // lax.axis_size("dp")
     grad_beta = lax.dynamic_slice_in_dim(grad_beta.reshape(width, heads), lax.axis_index("dp") * rows, rows, 0)
+    done = (grad_tokens, grad_contract, grad_merge, grad_beta, grad_taps, grad_head_gain, grad_gains, early)
+    grad_project, done = lax.optimization_barrier((grad_project, done))
+    grad_tokens, grad_contract, grad_merge, grad_beta, grad_taps, grad_head_gain, grad_gains, early = done
+    grad_expand = jnp.stack(early).astype(F32)
+    grad_project = jnp.stack(jnp.split(spread(grad_project, 0), 3, axis=1)).astype(F32)
     return (
         grad_tokens,
         grad_project[None],

time: 957 us -> 994 us (1.039)
  Pallas kernels: 164 us -> 228 us
  waiting for transfers between devices: 459 us -> 406 us
  local copies, waits for them, and re-layouts: 54.3 us -> 100 us
  starting transfers between devices: 119 us -> 99.9 us
    pallas_call x12 -> x16, Pallas kernels: 164 us -> 228 us  [call(): pl.pallas_call(kernel, in_specs=[pl.BlockSpec(memory_space=pltpu.SMEM)] +...]
    reduce_scatter x3, waiting for transfers between devices: 163 us -> 105 us  [spread(): return lax.psum_scatter(value, 'dp', scatter_dimension=axis, tiled=True)]
    unnamed x342 -> x369, local copies, waits for them, and re-layouts: 27 us -> 55.3 us
    ppermute x5, waiting for transfers between devices: 35.4 us -> 16.5 us  [shifted(): lax.ppermute(values, axis, [(i, i + distance) for i in devices if i + dis...]
    ppermute x12, starting transfers between devices: 39.6 us -> 21.6 us  [swapped(): lax.ppermute(block, 'dp', [(i, (i + distance) % count) for i in range(cou...]
    ppermute x87 -> x108, waiting for transfers between devices: 229 us -> 242 us  [flipped(): lax.ppermute(values, axis, [(i, i ^ bit) for i in range(lax.axis_size(axi...]
    ppermute x12, waiting for transfers between devices: 30.7 us -> 42.4 us  [swapped(): lax.ppermute(block, 'dp', [(i, (i + distance) % count) for i in range(cou...]
    ppermute x87 -> x108, starting transfers between devices: 63.3 us -> 66.8 us  [flipped(): lax.ppermute(values, axis, [(i, i ^ bit) for i in range(lax.axis_size(axi...]
  transfers between devices with their start and end apart: 111 -> 132, of which waited for: 61 -> 40; matrix products, arithmetic and copies ran while one was open for 15% -> 18% of each run, Pallas kernels for 11% -> 22%
where the time goes in v5:
time: 994 us; the launch traced here: 984 us
  waiting for transfers between devices  406 us (41%)
  Pallas kernels  228 us (23%)
  local copies, waits for them, and re-layouts  100 us (10%)
  starting transfers between devices  99.9 us (10%)
  other arithmetic  89 us (9%)
  matrix products  43.6 us (4%)
  between operations  17.1 us (2%)
    ppermute x108, waiting for transfers between devices, flipped(): lax.ppermute(values, axis, [(i, i ^ bit) for i in range(lax.axis_size(axi...  242 us
    pallas_call x16, Pallas kernels, call(): pl.pallas_call(kernel, in_specs=[pl.BlockSpec(memory_space=pltpu.SMEM)] +...  228 us
    reduce_scatter x3, waiting for transfers between devices, spread(): return lax.psum_scatter(value, 'dp', scatter_dimension=axis, tiled=True)  105 us
    ppermute x108, starting transfers between devices, flipped(): lax.ppermute(values, axis, [(i, i ^ bit) for i in range(lax.axis_size(axi...  66.8 us
    unnamed x369, local copies, waits for them, and re-layouts  55.3 us
    ppermute x12, waiting for transfers between devices, swapped(): lax.ppermute(block, 'dp', [(i, (i + distance) % count) for i in range(cou...  42.4 us
    dot_general x4, matrix products, product_left(): lax.dot_general(left, right, (((0,), (0,)), ((), ())), preferred_element_...  25.2 us
    convert_element_type x24, other arithmetic, narrow(): return values.astype(BF16)  22.5 us
  transfers between devices with their start and end apart: 132, of which 40 were waited for; matrix products, arithmetic and copies ran while one was open for 18% of the time, Pallas kernels for 22%

profile of v5, /device:TPU:0, one launch (start us, length us, event | category | flops | bytes accessed | tf_op | source)
XLA Modules:
  0.0 984.3 jit_solution(4620243807009194952)
XLA Ops:
  18.5 8.9 collective-permute-done.16.refs_1_
  37.8 14.2 %shard_map.180 = (f32[3,384,512]{2,1,0:T(8,128)}, f32[384,128]{1,0:T(8,128)}, bf16[384,512]{1,0:T(8,128)(2,1)}, bf16[4,384,384]{2,1,0:T(8,128)(2,1)}, bf16[4,384...) custom-call(s32[1]{0:T(128)} %bitcast.2.me_ref, ...), custom_call_target="tpu_custom_call" | custom-call | flops 1000000 | bytes 100000 | tf_op jit(solution)/shard_map/pallas_call | solution.py:235
  54.1 14.2 %shard_map.178 = (f32[3,384,512]{2,1,0:T(8,128)}, f32[384,128]{1,0:T(8,128)}, bf16[384,512]{1,0:T(8,128)(2,1)}, bf16[4,384,384]{2,1,0:T(8,128)(2,1)}, bf16[4,384...) custom-call(s32[1]{0:T(128)} %bitcast.2.me_ref, ...), custom_call_target="tpu_custom_call" | custom-call | flops 1000000 | bytes 100000 | tf_op jit(solution)/shard_map/pallas_call | solution.py:235
  72.0 9.1 collective-permute-done.21
  92.4 8.9 collective-permute-done.6.refs_1_
  103.0 11.3 %shard_map.179 = (bf16[384,1408]{1,0:T(8,128)(2,1)}, bf16[384,1408]{1,0:T(8,128)(2,1)}, bf16[384,1408]{1,0:T(8,128)(2,1)}, f32[96,2048]{1,0:T(8,128)S(1)}, f32[9...) custom-call(s32[1]{0:T(128)} %bitcast.2.me_ref, ...), custom_call_target="tpu_custom_call" | custom-call | flops 1000000 | bytes 100000 | tf_op jit(solution)/shard_map/pallas_call | solution.py:235
  118.0 8.6 collective-permute-done.22.refs_1_
  126.5 7.8 collective-permute-done.11
  143.1 12.0 %shard_map.181 = (bf16[384,1408]{1,0:T(8,128)(2,1)}, bf16[384,1408]{1,0:T(8,128)(2,1)}, bf16[384,1408]{1,0:T(8,128)(2,1)}, f32[96,2048]{1,0:T(8,128)S(1)}, f32[9...) custom-call(s32[1]{0:T(128)} %bitcast.2.me_ref, ...), custom_call_target="tpu_custom_call" | custom-call | flops 1000000 | bytes 100000 | tf_op jit(solution)/shard_map/pallas_call | solution.py:235
  161.1 9.8 collective-permute-done.13.refs_1_
  170.9 7.5 collective-permute-done.27
  181.5 12.5 %shard_map.182 = (f32[3,384,512]{2,1,0:T(8,128)}, f32[384,128]{1,0:T(8,128)S(1)}, bf16[384,512]{1,0:T(8,128)(2,1)S(1)}, bf16[4,384,384]{2,1,0:T(8,128)(2,1)S(1)}...) custom-call(s32[1]{0:T(128)} %bitcast.2.me_ref, ...), custom_call_target="tpu_custom_call" | custom-call | flops 1000000 | bytes 100000 | tf_op jit(solution)/shard_map/pallas_call | solution.py:235
  209.3 8.8 collective-permute-done.29.refs_1_
  220.3 11.9 %shard_map.186 = (f32[3,384,512]{2,1,0:T(8,128)}, f32[384,128]{1,0:T(8,128)S(1)}, bf16[384,512]{1,0:T(8,128)(2,1)S(1)}, bf16[4,384,384]{2,1,0:T(8,128)(2,1)S(1)}...) custom-call(s32[1]{0:T(128)} %bitcast.2.me_ref, ...), custom_call_target="tpu_custom_call" | custom-call | flops 1000000 | bytes 100000 | tf_op jit(solution)/shard_map/pallas_call | solution.py:235
  244.4 9.7 collective-permute-done.34
  258.4 9.0 collective-permute-done.35.refs_1_
  269.1 12.4 %shard_map.183 = (bf16[384,1408]{1,0:T(8,128)(2,1)S(1)}, bf16[384,1408]{1,0:T(8,128)(2,1)S(1)}, bf16[384,1408]{1,0:T(8,128)(2,1)S(1)}, f32[96,2048]{1,0:T(8,128)...) custom-call(s32[1]{0:T(128)} %bitcast.2.me_ref, ...), custom_call_target="tpu_custom_call" | custom-call | flops 1000000 | bytes 100000 | tf_op jit(solution)/shard_map/pallas_call | solution.py:235
  291.6 15.9 %collective-permute-done.53 = bf16[96,2048]{1,0:T(8,128)(2,1)S(1)} collective-permute-done((bf16[96,2048]{1,0:T(8,128)(2,1)S(1)}, bf16[96,2048]{1,0:T(8,128)(2,1)S(1)}, u32[]{:S(2)}, u32[]{:S(2)}) %collective-permute-start.53) | collective-permute-done | bytes 393248 | tf_op jit(solution)/shard_map/ppermute | solution.py:600
  313.4 9.4 collective-permute-done.54.refs_1_
  322.9 7.0 collective-permute-done.57.refs_1_
  330.3 12.2 %shard_map.184 = (bf16[384,1408]{1,0:T(8,128)(2,1)}, bf16[384,1408]{1,0:T(8,128)(2,1)}, f32[96,2048]{1,0:T(8,128)S(1)}, f32[96,2048]{1,0:T(8,128)S(1)}, bf16[96,...) custom-call(s32[1]{0:T(128)} %bitcast.2.me_ref, bf16[384,1408]{1,0:T(8,128)(2,1)S(1)} %copy-done.6, ...), custom_call_target="tpu_custom_call" | custom-call | flops 1000000 | bytes 100000 | tf_op jit(solution)/shard_map/pallas_call | solution.py:235
  344.0 12.5 %shard_map.187 = (bf16[384,1408]{1,0:T(8,128)(2,1)S(1)}, bf16[384,1408]{1,0:T(8,128)(2,1)S(1)}, bf16[384,1408]{1,0:T(8,128)(2,1)S(1)}, f32[96,2048]{1,0:T(8,128)...) custom-call(s32[1]{0:T(128)} %bitcast.2.me_ref, ...), custom_call_target="tpu_custom_call" | custom-call | flops 1000000 | bytes 100000 | tf_op jit(solution)/shard_map/pallas_call | solution.py:235
  357.6 13.0 %shard_map.188 = (bf16[384,1408]{1,0:T(8,128)(2,1)}, bf16[384,1408]{1,0:T(8,128)(2,1)}, f32[96,2048]{1,0:T(8,128)S(1)}, f32[96,2048]{1,0:T(8,128)S(1)}, bf16[96,...) custom-call(s32[1]{0:T(128)} %bitcast.2.me_ref, bf16[384,1408]{1,0:T(8,128)(2,1)S(1)} %get-tuple-element.160.silu_ref, ...), custom_call_target="tpu_custom_call" | custom-call | flops 1000000 | bytes 100000 | tf_op jit(solution)/shard_map/pallas_call | solution.py:235
  375.6 9.1 collective-permute-done.43
  384.7 7.9 collective-permute-done.62
  400.5 10.0 %collective-permute-done.63.refs_1_ = bf16[96,2048]{1,0:T(8,128)(2,1)S(1)} collective-permute-done((bf16[96,2048]{1,0:T(8,128)(2,1)S(1)}, bf16[96,2048]{1,0:T(8,128)(2,1)S(1)}, u32[]{:S(2)}, u32[]{:S(2)}) %collective-permute-start.63) | collective-permute-done | bytes 393248 | tf_op jit(solution)/shard_map/ppermute | solution.py:600
  417.6 19.4 %shard_map.189 = (bf16[384,1536]{1,0:T(8,128)(2,1)}, bf16[384,128]{1,0:T(8,128)(2,1)}, f32[3,4,512]{2,1,0:T(4,128)}, f32[8,128]{1,0:T(8,128)}, f32[96,2048]{1,0:...) custom-call(s32[1]{0:T(128)} %bitcast.2.me_ref, ...), custom_call_target="tpu_custom_call" | custom-call | flops 1000000 | bytes 100000 | tf_op jit(solution)/shard_map/pallas_call | solution.py:235
  437.6 18.9 %shard_map.185 = (bf16[384,1536]{1,0:T(8,128)(2,1)}, bf16[384,128]{1,0:T(8,128)(2,1)}, f32[3,4,512]{2,1,0:T(4,128)}, f32[8,128]{1,0:T(8,128)}, f32[96,2048]{1,0:...) custom-call(s32[1]{0:T(128)} %bitcast.2.me_ref, ...), custom_call_target="tpu_custom_call" | custom-call | flops 1000000 | bytes 100000 | tf_op jit(solution)/shard_map/pallas_call | solution.py:235
  460.1 9.2 collective-permute-done.68
  469.2 8.0 collective-permute-done.49
  484.5 11.6 %collective-permute-done.50 = bf16[96,2048]{1,0:T(8,128)(2,1)} collective-permute-done((bf16[96,2048]{1,0:T(8,128)(2,1)}, bf16[96,2048]{1,0:T(8,128)(2,1)}, u32[]{:S(2)}, u32[]{:S(2)}) %collective-permute-start.50) | collective-permute-done | bytes 393248 | tf_op jit(solution)/shard_map/ppermute | solution.py:605
  511.2 7.5 collective-permute-done.70.refs_1_
  526.4 12.2 %shard_map.190 = (bf16[384,1408]{1,0:T(8,128)(2,1)S(1)}, bf16[384,1408]{1,0:T(8,128)(2,1)S(1)}, f32[96,2048]{1,0:T(8,128)S(1)}, f32[96,2048]{1,0:T(8,128)S(1)}, ...) custom-call(s32[1]{0:T(128)} %bitcast.2.me_ref, bf16[384,1408]{1,0:T(8,128)(2,1)S(1)} %copy-done.7, ...), custom_call_target="tpu_custom_call" | custom-call | flops 1000000 | bytes 100000 | tf_op jit(solution)/shard_map/pallas_call | solution.py:235
  541.9 12.6 %shard_map.191 = (bf16[384,1408]{1,0:T(8,128)(2,1)S(1)}, bf16[384,1408]{1,0:T(8,128)(2,1)S(1)}, f32[96,2048]{1,0:T(8,128)S(1)}, f32[96,2048]{1,0:T(8,128)S(1)}, ...) custom-call(s32[1]{0:T(128)} %bitcast.2.me_ref, bf16[384,1408]{1,0:T(8,128)(2,1)S(1)} %copy-done.12, ...), custom_call_target="tpu_custom_call" | custom-call | flops 1000000 | bytes 100000 | tf_op jit(solution)/shard_map/pallas_call | solution.py:235
  557.9 6.9 convolution_convert_fusion.2
  564.8 8.9 convolution_convert_fusion.1
  578.8 8.4 collective-permute-done.81
  622.2 11.4 %collective-permute-done.102 = bf16[96,512]{1,0:T(8,128)(2,1)S(1)} collective-permute-done((bf16[96,512]{1,0:T(8,128)(2,1)S(1)}, bf16[96,512]{1,0:T(8,128)(2,1)S(1)}, u32[]{:S(2)}, u32[]{:S(2)}) %collective-permute-start.102) | collective-permute-done | bytes 98336 | tf_op jit(solution)/shard_map/ppermute | solution.py:646
  637.8 13.5 %collective-permute-done.96 = bf16[96,512]{1,0:T(8,128)(2,1)} collective-permute-done((bf16[96,512]{1,0:T(8,128)(2,1)}, bf16[96,512]{1,0:T(8,128)(2,1)}, u32[]{:S(2)}, u32[]{:S(2)}) %collective-permute-start.96) | collective-permute-done | bytes 98336 | tf_op jit(solution)/shard_map/ppermute | solution.py:646
  657.1 6.8 collective-permute-done.98
  675.9 6.8 convolution_bitcast_fusion
  704.9 9.0 collective-permute-done.114
  721.8 8.5 collective-permute-done.108
  740.7 19.4 %shard_map.193 = (bf16[384,1536]{1,0:T(8,128)(2,1)S(1)}, bf16[384,128]{1,0:T(8,128)(2,1)S(1)}, f32[3,4,512]{2,1,0:T(4,128)S(1)}, f32[8,128]{1,0:T(8,128)S(1)}, f...) custom-call(s32[1]{0:T(128)} %bitcast.2.me_ref, ...), custom_call_target="tpu_custom_call" | custom-call | flops 1000000 | bytes 100000 | tf_op jit(solution)/shard_map/pallas_call | solution.py:235
  762.8 19.5 %shard_map.192 = (bf16[384,1536]{1,0:T(8,128)(2,1)S(1)}, bf16[384,128]{1,0:T(8,128)(2,1)S(1)}, f32[3,4,512]{2,1,0:T(4,128)S(1)}, f32[8,128]{1,0:T(8,128)S(1)}, f...) custom-call(s32[1]{0:T(128)} %bitcast.2.me_ref, ...), custom_call_target="tpu_custom_call" | custom-call | flops 1000000 | bytes 100000 | tf_op jit(solution)/shard_map/pallas_call | solution.py:235
  793.9 8.8 convolution_convert_fusion
  826.2 8.7 collective-permute-done.93
  868.6 105.0 %reduce-scatter.8.cloned.1.call-done = bf16[512,1536]{1,0:T(8,128)(2,1)} async-done(((bf16[2048,1536]{1,0:T(8,128)(2,1)}), bf16[512,1536]{1,0:T(8,128)(2,1)}) %reduce-scatter.8.cloned.1.call-update) | async-done | bytes 1572880 | tf_op jit(solution)/shard_map/reduce_scatter | solution.py:754
  (759 shorter events, 352.8 us)
Async XLA Ops:
  7.2 498.0 %all-gather.13.cloned.1.call-start = ((), (), s32[]{:S(2)}) async-start(), calls=%async_computation.8 | async-start | bytes 1966080 | tf_op jit(solution)/shard_map/all_gather | solution.py:725
  17.5 35.5 %collective-permute-start.1 = (bf16[96,2048]{1,0:T(8,128)(2,1)S(1)}, bf16[96,2048]{1,0:T(8,128)(2,1)}, u32[]{:S(2)}, u32[]{:S(2)}) collective-permute-start(bf16[96,2048]{1,0:T(8,128)(2,1)S(1)} %get-tuple-element.338.refs_0_), channel_id=1, source_target_pairs={{0,1},{1,0},{2,3},{3,2},{4,5},{5,4},{6,7},{7,6},{8,9},{9,8},{10,11... | collective-permute-start | bytes 1179656 | tf_op jit(solution)/shard_map/ppermute | solution.py:600
  118.0 21.7 %collective-permute-start.23 = (bf16[96,2048]{1,0:T(8,128)(2,1)S(1)}, bf16[96,2048]{1,0:T(8,128)(2,1)S(1)}, u32[]{:S(2)}, u32[]{:S(2)}) collective-permute-start(bf16[96,2048]{1,0:T(8,128)(2,1)S(1)} %get-tuple-element.335.refs_0_), channel_id=1, source_target_pairs={{0,1},{1,0},{2,3},{3,2},{4,5},{5,4},{6,7},{7,6},{8,9},{9,8},{10,11... | collective-permute-start | bytes 1179656 | tf_op jit(solution)/shard_map/ppermute | solution.py:600
  135.2 20.5 %collective-permute-start.12 = (bf16[96,2048]{1,0:T(8,128)(2,1)}, bf16[96,2048]{1,0:T(8,128)(2,1)}, u32[]{:S(2)}, u32[]{:S(2)}) collective-permute-start(bf16[96,2048]{1,0:T(8,128)(2,1)} %add_convert_fusion.15), channel_id=1, source_target_pairs={{0,16},{1,17},{2,18},{3,19},{4,20},{5,21},{6,22},{7,23},{8,24},{9,... | collective-permute-start | bytes 1179656 | tf_op jit(solution)/shard_map/ppermute | solution.py:605
  161.1 20.4 %collective-permute-start.14 = (bf16[96,2048]{1,0:T(8,128)(2,1)S(1)}, bf16[96,2048]{1,0:T(8,128)(2,1)S(1)}, u32[]{:S(2)}, u32[]{:S(2)}) collective-permute-start(bf16[96,2048]{1,0:T(8,128)(2,1)S(1)} %get-tuple-element.285.refs_0_), channel_id=1, source_target_pairs={{0,1},{1,0},{2,3},{3,2},{4,5},{5,4},{6,7},{7,6},{8,9},{9,8},{10,11... | collective-permute-start | bytes 1179656 | tf_op jit(solution)/shard_map/ppermute | solution.py:600
  179.4 20.6 %collective-permute-start.28 = (bf16[96,2048]{1,0:T(8,128)(2,1)}, bf16[96,2048]{1,0:T(8,128)(2,1)}, u32[]{:S(2)}, u32[]{:S(2)}) collective-permute-start(bf16[96,2048]{1,0:T(8,128)(2,1)} %add_convert_fusion.12), channel_id=1, source_target_pairs={{0,16},{1,17},{2,18},{3,19},{4,20},{5,21},{6,22},{7,23},{8,24},{9,... | collective-permute-start | bytes 1179656 | tf_op jit(solution)/shard_map/ppermute | solution.py:605
  199.9 305.2 %all-gather.15.cloned.1.call-start = ((), (), s32[]{:S(2)}) async-start(), calls=%async_computation.9 | async-start | bytes 1966080 | tf_op jit(solution)/shard_map/all_gather | solution.py:725
  218.1 23.4 %collective-permute-start.33 = (bf16[96,2048]{1,0:T(8,128)(2,1)}, bf16[96,2048]{1,0:T(8,128)(2,1)}, u32[]{:S(2)}, u32[]{:S(2)}) collective-permute-start(bf16[96,2048]{1,0:T(8,128)(2,1)} %get-tuple-element.145), channel_id=1, source_target_pairs={{0,1},{1,0},{2,3},{3,2},{4,5},{5,4},{6,7},{7,6},{8,9},{9,8},{10,11... | collective-permute-start | bytes 1179656 | tf_op jit(solution)/shard_map/ppermute | solution.py:600
  218.6 25.8 %collective-permute-start.32 = (bf16[96,2048]{1,0:T(8,128)(2,1)}, bf16[96,2048]{1,0:T(8,128)(2,1)}, u32[]{:S(2)}, u32[]{:S(2)}) collective-permute-start(bf16[96,2048]{1,0:T(8,128)(2,1)} %get-tuple-element.143), channel_id=1, source_target_pairs={{0,1},{1,0},{2,3},{3,2},{4,5},{5,4},{6,7},{7,6},{8,9},{9,8},{10,11... | collective-permute-start | bytes 1179656 | tf_op jit(solution)/shard_map/ppermute | solution.py:600
  241.4 263.7 %all-gather.9.cloned.1.call-start = ((), (), s32[]{:S(2)}) async-start(), calls=%async_computation.6 | async-start | bytes 5406720 | tf_op jit(solution)/shard_map/all_gather | solution.py:725
  284.6 220.5 %all-gather.11.cloned.1.call-start = ((), (), s32[]{:S(2)}) async-start(), calls=%async_computation.7 | async-start | bytes 5406720 | tf_op jit(solution)/shard_map/all_gather | solution.py:725
  287.8 25.2 %collective-permute-start.38 = (bf16[96,2048]{1,0:T(8,128)(2,1)S(1)}, bf16[96,2048]{1,0:T(8,128)(2,1)S(1)}, u32[]{:S(2)}, u32[]{:S(2)}) collective-permute-start(bf16[96,2048]{1,0:T(8,128)(2,1)S(1)} %dynamic-slice_bitcast_fusion.1.refs_0_), channel_id=1, source_target_pairs={{0,2},{1,3},{2,0},{3,1},{4,6},{5,7},{6,4},{7,5},{8,10},{9,11},{10,... | collective-permute-start | bytes 1179656 | tf_op jit(solution)/shard_map/ppermute | solution.py:600
  313.4 30.0 %collective-permute-start.55 = (bf16[96,2048]{1,0:T(8,128)(2,1)S(1)}, bf16[96,2048]{1,0:T(8,128)(2,1)S(1)}, u32[]{:S(2)}, u32[]{:S(2)}) collective-permute-start(bf16[96,2048]{1,0:T(8,128)(2,1)S(1)} %get-tuple-element.269.refs_0_), channel_id=1, source_target_pairs={{0,1},{1,0},{2,3},{3,2},{4,5},{5,4},{6,7},{7,6},{8,9},{9,8},{10,11... | collective-permute-start | bytes 1179656 | tf_op jit(solution)/shard_map/ppermute | solution.py:600
  322.9 21.1 %collective-permute-start.56 = (bf16[96,2048]{1,0:T(8,128)(2,1)S(1)}, bf16[96,2048]{1,0:T(8,128)(2,1)S(1)}, u32[]{:S(2)}, u32[]{:S(2)}) collective-permute-start(bf16[96,2048]{1,0:T(8,128)(2,1)S(1)} %collective-permute-done.54.refs_1_), channel_id=1, source_target_pairs={{0,1},{1,0},{2,3},{3,2},{4,5},{5,4},{6,7},{7,6},{8,9},{9,8},{10,11... | collective-permute-start | bytes 1179656 | tf_op jit(solution)/shard_map/ppermute | solution.py:600
  329.8 27.8 %collective-permute-start.58 = (bf16[96,2048]{1,0:T(8,128)(2,1)S(1)}, bf16[96,2048]{1,0:T(8,128)(2,1)S(1)}, u32[]{:S(2)}, u32[]{:S(2)}) collective-permute-start(bf16[96,2048]{1,0:T(8,128)(2,1)S(1)} %dynamic-slice_bitcast_fusion.refs_0_), channel_id=1, source_target_pairs={{0,1},{1,0},{2,3},{3,2},{4,5},{5,4},{6,7},{7,6},{8,9},{9,8},{10,11... | collective-permute-start | bytes 1179656 | tf_op jit(solution)/shard_map/ppermute | solution.py:600
  329.8 27.8 %collective-permute-start.59 = (bf16[96,2048]{1,0:T(8,128)(2,1)S(1)}, bf16[96,2048]{1,0:T(8,128)(2,1)S(1)}, u32[]{:S(2)}, u32[]{:S(2)}) collective-permute-start(bf16[96,2048]{1,0:T(8,128)(2,1)S(1)} %collective-permute-done.57.refs_1_), channel_id=1, source_target_pairs={{0,1},{1,0},{2,3},{3,2},{4,5},{5,4},{6,7},{7,6},{8,9},{9,8},{10,11... | collective-permute-start | bytes 1179656 | tf_op jit(solution)/shard_map/ppermute | solution.py:600
  343.4 28.2 %collective-permute-start.42 = (bf16[96,2048]{1,0:T(8,128)(2,1)S(1)}, bf16[96,2048]{1,0:T(8,128)(2,1)S(1)}, u32[]{:S(2)}, u32[]{:S(2)}) collective-permute-start(bf16[96,2048]{1,0:T(8,128)(2,1)S(1)} %get-tuple-element.151), channel_id=1, source_target_pairs={{0,1},{1,0},{2,3},{3,2},{4,5},{5,4},{6,7},{7,6},{8,9},{9,8},{10,11... | collective-permute-start | bytes 1179656 | tf_op jit(solution)/shard_map/ppermute | solution.py:600
  343.5 32.2 %collective-permute-start.41 = (bf16[96,2048]{1,0:T(8,128)(2,1)}, bf16[96,2048]{1,0:T(8,128)(2,1)}, u32[]{:S(2)}, u32[]{:S(2)}) collective-permute-start(bf16[96,2048]{1,0:T(8,128)(2,1)} %get-tuple-element.149), channel_id=1, source_target_pairs={{0,1},{1,0},{2,3},{3,2},{4,5},{5,4},{6,7},{7,6},{8,9},{9,8},{10,11... | collective-permute-start | bytes 1179656 | tf_op jit(solution)/shard_map/ppermute | solution.py:600
  375.6 488.2 %reduce-scatter.4.cloned.1.call-start = ((), (), s32[]{:S(2)}) async-start(), calls=%async_computation.3 | async-start | bytes 7208960 | tf_op jit(solution)/shard_map/reduce_scatter | solution.py:754
  410.5 27.1 %collective-permute-start.45 = (bf16[96,2048]{1,0:T(8,128)(2,1)S(1)}, bf16[96,2048]{1,0:T(8,128)(2,1)S(1)}, u32[]{:S(2)}, u32[]{:S(2)}) collective-permute-start(bf16[96,2048]{1,0:T(8,128)(2,1)S(1)} %get-tuple-element.333.refs_0_), channel_id=1, source_target_pairs={{0,1},{1,0},{2,3},{3,2},{4,5},{5,4},{6,7},{7,6},{8,9},{9,8},{10,11... | collective-permute-start | bytes 1179656 | tf_op jit(solution)/shard_map/ppermute | solution.py:600
  417.5 20.1 %collective-permute-start.46 = (bf16[96,2048]{1,0:T(8,128)(2,1)S(1)}, bf16[96,2048]{1,0:T(8,128)(2,1)S(1)}, u32[]{:S(2)}, u32[]{:S(2)}) collective-permute-start(bf16[96,2048]{1,0:T(8,128)(2,1)S(1)} %collective-permute-done.44.refs_1_), channel_id=1, source_target_pairs={{0,1},{1,0},{2,3},{3,2},{4,5},{5,4},{6,7},{7,6},{8,9},{9,8},{10,11... | collective-permute-start | bytes 1179656 | tf_op jit(solution)/shard_map/ppermute | solution.py:600
  436.9 20.2 %collective-permute-start.67 = (bf16[96,2048]{1,0:T(8,128)(2,1)S(1)}, bf16[96,2048]{1,0:T(8,128)(2,1)S(1)}, u32[]{:S(2)}, u32[]{:S(2)}) collective-permute-start(bf16[96,2048]{1,0:T(8,128)(2,1)S(1)} %get-tuple-element.176), channel_id=1, source_target_pairs={{0,1},{1,0},{2,3},{3,2},{4,5},{5,4},{6,7},{7,6},{8,9},{9,8},{10,11... | collective-permute-start | bytes 1179656 | tf_op jit(solution)/shard_map/ppermute | solution.py:600
  437.5 22.6 %collective-permute-start.66 = (bf16[96,2048]{1,0:T(8,128)(2,1)S(1)}, bf16[96,2048]{1,0:T(8,128)(2,1)S(1)}, u32[]{:S(2)}, u32[]{:S(2)}) collective-permute-start(bf16[96,2048]{1,0:T(8,128)(2,1)S(1)} %get-tuple-element.174), channel_id=1, source_target_pairs={{0,1},{1,0},{2,3},{3,2},{4,5},{5,4},{6,7},{7,6},{8,9},{9,8},{10,11... | collective-permute-start | bytes 1179656 | tf_op jit(solution)/shard_map/ppermute | solution.py:600
  510.7 31.2 %collective-permute-start.77 = (bf16[96,2048]{1,0:T(8,128)(2,1)S(1)}, bf16[96,2048]{1,0:T(8,128)(2,1)S(1)}, u32[]{:S(2)}, u32[]{:S(2)}) collective-permute-start(bf16[96,2048]{1,0:T(8,128)(2,1)S(1)} %convert_element_type.394.refs_0_), channel_id=1, source_target_pairs={{0,1},{1,0},{2,3},{3,2},{4,5},{5,4},{6,7},{7,6},{8,9},{9,8},{10,11... | collective-permute-start | bytes 1179656 | tf_op jit(solution)/shard_map/ppermute | solution.py:600
  541.4 35.4 %collective-permute-start.74 = (bf16[96,2048]{1,0:T(8,128)(2,1)}, bf16[96,2048]{1,0:T(8,128)(2,1)}, u32[]{:S(2)}, u32[]{:S(2)}) collective-permute-start(bf16[96,2048]{1,0:T(8,128)(2,1)} %get-tuple-element.185), channel_id=1, source_target_pairs={{0,1},{1,0},{2,3},{3,2},{4,5},{5,4},{6,7},{7,6},{8,9},{9,8},{10,11... | collective-permute-start | bytes 1179656 | tf_op jit(solution)/shard_map/ppermute | solution.py:600
  541.9 46.8 %collective-permute-start.73 = (bf16[96,2048]{1,0:T(8,128)(2,1)}, bf16[96,2048]{1,0:T(8,128)(2,1)}, u32[]{:S(2)}, u32[]{:S(2)}) collective-permute-start(bf16[96,2048]{1,0:T(8,128)(2,1)} %get-tuple-element.183), channel_id=1, source_target_pairs={{0,1},{1,0},{2,3},{3,2},{4,5},{5,4},{6,7},{7,6},{8,9},{9,8},{10,11... | collective-permute-start | bytes 1179656 | tf_op jit(solution)/shard_map/ppermute | solution.py:600
  557.9 20.9 %collective-permute-start.79 = (bf16[96,2048]{1,0:T(8,128)(2,1)}, bf16[96,2048]{1,0:T(8,128)(2,1)}, u32[]{:S(2)}, u32[]{:S(2)}) collective-permute-start(bf16[96,2048]{1,0:T(8,128)(2,1)} %get-tuple-element.188), channel_id=1, source_target_pairs={{0,1},{1,0},{2,3},{3,2},{4,5},{5,4},{6,7},{7,6},{8,9},{9,8},{10,11... | collective-permute-start | bytes 1179656 | tf_op jit(solution)/shard_map/ppermute | solution.py:600
  600.4 263.4 %reduce-scatter.6.cloned.1.call-start = ((), (), s32[]{:S(2)}) async-start(), calls=%async_computation.4 | async-start | bytes 7208960 | tf_op jit(solution)/shard_map/reduce_scatter | solution.py:754
  610.8 22.8 %collective-permute-start.102 = (bf16[96,512]{1,0:T(8,128)(2,1)S(1)}, bf16[96,512]{1,0:T(8,128)(2,1)S(1)}, u32[]{:S(2)}, u32[]{:S(2)}) collective-permute-start(bf16[96,512]{1,0:T(8,128)(2,1)S(1)} %bitcast.271), channel_id=1, source_target_pairs={{0,8},{4,12},{8,0},{12,4},{1,9},{5,13},{9,1},{13,5},{2,10},{6,14},... | collective-permute-start | bytes 294920 | tf_op jit(solution)/shard_map/ppermute | solution.py:646
  610.9 22.7 %collective-permute-start.101 = (bf16[96,512]{1,0:T(8,128)(2,1)S(1)}, bf16[96,512]{1,0:T(8,128)(2,1)S(1)}, u32[]{:S(2)}, u32[]{:S(2)}) collective-permute-start(bf16[96,512]{1,0:T(8,128)(2,1)S(1)} %bitcast.274), channel_id=1, source_target_pairs={{0,4},{4,8},{8,12},{12,0},{1,5},{5,9},{9,13},{13,1},{2,6},{6,10},{... | collective-permute-start | bytes 294920 | tf_op jit(solution)/shard_map/ppermute | solution.py:646
  613.5 24.4 %collective-permute-start.97 = (bf16[96,512]{1,0:T(8,128)(2,1)}, bf16[96,512]{1,0:T(8,128)(2,1)}, u32[]{:S(2)}, u32[]{:S(2)}) collective-permute-start(bf16[96,512]{1,0:T(8,128)(2,1)} %bitcast.216), channel_id=1, source_target_pairs={{0,12},{4,0},{8,4},{12,8},{1,13},{5,1},{9,5},{13,9},{2,14},{6,2},{... | collective-permute-start | bytes 294920 | tf_op jit(solution)/shard_map/ppermute | solution.py:646
  616.9 34.4 %collective-permute-start.96 = (bf16[96,512]{1,0:T(8,128)(2,1)}, bf16[96,512]{1,0:T(8,128)(2,1)}, u32[]{:S(2)}, u32[]{:S(2)}) collective-permute-start(bf16[96,512]{1,0:T(8,128)(2,1)} %bitcast.217), channel_id=1, source_target_pairs={{0,8},{4,12},{8,0},{12,4},{1,9},{5,13},{9,1},{13,5},{2,10},{6,14},... | collective-permute-start | bytes 294920 | tf_op jit(solution)/shard_map/ppermute | solution.py:646
  619.3 32.0 %collective-permute-start.95 = (bf16[96,512]{1,0:T(8,128)(2,1)}, bf16[96,512]{1,0:T(8,128)(2,1)}, u32[]{:S(2)}, u32[]{:S(2)}) collective-permute-start(bf16[96,512]{1,0:T(8,128)(2,1)} %bitcast.218), channel_id=1, source_target_pairs={{0,4},{4,8},{8,12},{12,0},{1,5},{5,9},{9,13},{13,1},{2,6},{6,10},{... | collective-permute-start | bytes 294920 | tf_op jit(solution)/shard_map/ppermute | solution.py:646
  634.4 339.2 %reduce-scatter.8.cloned.1.call-start = ((), (), s32[]{:S(2)}) async-start(), calls=%async_computation.5 | async-start | bytes 7864320 | tf_op jit(solution)/shard_map/reduce_scatter | solution.py:754
  683.5 49.4 %collective-permute-start.85 = (bf16[96,2048]{1,0:T(8,128)(2,1)}, bf16[96,2048]{1,0:T(8,128)(2,1)}, u32[]{:S(2)}, u32[]{:S(2)}) collective-permute-start(bf16[96,2048]{1,0:T(8,128)(2,1)} %convert_element_type.402.refs_0_), channel_id=1, source_target_pairs={{0,2},{1,3},{2,0},{3,1},{4,6},{5,7},{6,4},{7,5},{8,10},{9,11},{10,... | collective-permute-start | bytes 1179656 | tf_op jit(solution)/shard_map/ppermute | solution.py:600
  685.3 48.2 %collective-permute-start.86 = (bf16[96,2048]{1,0:T(8,128)(2,1)}, bf16[96,2048]{1,0:T(8,128)(2,1)}, u32[]{:S(2)}, u32[]{:S(2)}) collective-permute-start(bf16[96,2048]{1,0:T(8,128)(2,1)} %convert_element_type.402.refs_0_), channel_id=1, source_target_pairs={{0,1},{1,0},{2,3},{3,2},{4,5},{5,4},{6,7},{7,6},{8,9},{9,8},{10,11... | collective-permute-start | bytes 1179656 | tf_op jit(solution)/shard_map/ppermute | solution.py:600
  693.1 20.8 %collective-permute-start.114 = (bf16[96,512]{1,0:T(8,128)(2,1)}, bf16[96,512]{1,0:T(8,128)(2,1)}, u32[]{:S(2)}, u32[]{:S(2)}) collective-permute-start(bf16[96,512]{1,0:T(8,128)(2,1)} %bitcast.205), channel_id=1, source_target_pairs={{0,8},{4,12},{8,0},{12,4},{1,9},{5,13},{9,1},{13,5},{2,10},{6,14},... | collective-permute-start | bytes 294920 | tf_op jit(solution)/shard_map/ppermute | solution.py:646
  730.3 31.5 %collective-permute-start.83 = (bf16[96,2048]{1,0:T(8,128)(2,1)S(1)}, bf16[96,2048]{1,0:T(8,128)(2,1)S(1)}, u32[]{:S(2)}, u32[]{:S(2)}) collective-permute-start(bf16[96,2048]{1,0:T(8,128)(2,1)S(1)} %copy-done.17), channel_id=1, source_target_pairs={{0,1},{1,0},{2,3},{3,2},{4,5},{5,4},{6,7},{7,6},{8,9},{9,8},{10,11... | collective-permute-start | bytes 1179656 | tf_op jit(solution)/shard_map/ppermute | solution.py:600
  730.4 31.9 %collective-permute-start.116 = (bf16[96,2048]{1,0:T(8,128)(2,1)}, bf16[96,2048]{1,0:T(8,128)(2,1)}, u32[]{:S(2)}, u32[]{:S(2)}) collective-permute-start(bf16[96,2048]{1,0:T(8,128)(2,1)} %pad_maximum_fusion.14), channel_id=1, source_target_pairs={{0,2},{1,3},{2,0},{3,1},{4,6},{5,7},{6,4},{7,5},{8,10},{9,11},{10,... | collective-permute-start | bytes 1179656 | tf_op jit(solution)/shard_map/ppermute | solution.py:600
  732.9 29.5 %collective-permute-start.110 = (bf16[96,2048]{1,0:T(8,128)(2,1)}, bf16[96,2048]{1,0:T(8,128)(2,1)}, u32[]{:S(2)}, u32[]{:S(2)}) collective-permute-start(bf16[96,2048]{1,0:T(8,128)(2,1)} %pad_maximum_fusion.12), channel_id=1, source_target_pairs={{0,2},{1,3},{2,0},{3,1},{4,6},{5,7},{6,4},{7,5},{8,10},{9,11},{10,... | collective-permute-start | bytes 1179656 | tf_op jit(solution)/shard_map/ppermute | solution.py:600
  733.4 29.4 %collective-permute-start.84 = (bf16[96,2048]{1,0:T(8,128)(2,1)S(1)}, bf16[96,2048]{1,0:T(8,128)(2,1)S(1)}, u32[]{:S(2)}, u32[]{:S(2)}) collective-permute-start(bf16[96,2048]{1,0:T(8,128)(2,1)S(1)} %collective-permute-done.82.refs_1_), channel_id=1, source_target_pairs={{0,1},{1,0},{2,3},{3,2},{4,5},{5,4},{6,7},{7,6},{8,9},{9,8},{10,11... | collective-permute-start | bytes 1179656 | tf_op jit(solution)/shard_map/ppermute | solution.py:600
  740.5 63.0 %collective-permute-start.117 = (bf16[96,2048]{1,0:T(8,128)(2,1)}, bf16[96,2048]{1,0:T(8,128)(2,1)}, u32[]{:S(2)}, u32[]{:S(2)}) collective-permute-start(bf16[96,2048]{1,0:T(8,128)(2,1)} %pad_maximum_fusion.14), channel_id=1, source_target_pairs={{0,1},{1,0},{2,3},{3,2},{4,5},{5,4},{6,7},{7,6},{8,9},{9,8},{10,11... | collective-permute-start | bytes 1179656 | tf_op jit(solution)/shard_map/ppermute | solution.py:600
  761.8 46.5 %collective-permute-start.111 = (bf16[96,2048]{1,0:T(8,128)(2,1)}, bf16[96,2048]{1,0:T(8,128)(2,1)}, u32[]{:S(2)}, u32[]{:S(2)}) collective-permute-start(bf16[96,2048]{1,0:T(8,128)(2,1)} %pad_maximum_fusion.12), channel_id=1, source_target_pairs={{0,1},{1,0},{2,3},{3,2},{4,5},{5,4},{6,7},{7,6},{8,9},{9,8},{10,11... | collective-permute-start | bytes 1179656 | tf_op jit(solution)/shard_map/ppermute | solution.py:600
  762.3 41.7 %collective-permute-start.118 = (bf16[96,2048]{1,0:T(8,128)(2,1)}, bf16[96,2048]{1,0:T(8,128)(2,1)}, u32[]{:S(2)}, u32[]{:S(2)}) collective-permute-start(bf16[96,2048]{1,0:T(8,128)(2,1)} %collective-permute-done.116), channel_id=1, source_target_pairs={{0,1},{1,0},{2,3},{3,2},{4,5},{5,4},{6,7},{7,6},{8,9},{9,8},{10,11... | collective-permute-start | bytes 1179656 | tf_op jit(solution)/shard_map/ppermute | solution.py:600
  762.4 46.4 %collective-permute-start.112 = (bf16[96,2048]{1,0:T(8,128)(2,1)}, bf16[96,2048]{1,0:T(8,128)(2,1)}, u32[]{:S(2)}, u32[]{:S(2)}) collective-permute-start(bf16[96,2048]{1,0:T(8,128)(2,1)} %collective-permute-done.110), channel_id=1, source_target_pairs={{0,1},{1,0},{2,3},{3,2},{4,5},{5,4},{6,7},{7,6},{8,9},{9,8},{10,11... | collective-permute-start | bytes 1179656 | tf_op jit(solution)/shard_map/ppermute | solution.py:600
  802.8 21.6 %collective-permute-start.89 = (bf16[96,2048]{1,0:T(8,128)(2,1)}, bf16[96,2048]{1,0:T(8,128)(2,1)}, u32[]{:S(2)}, u32[]{:S(2)}) collective-permute-start(bf16[96,2048]{1,0:T(8,128)(2,1)} %get-tuple-element.202), channel_id=1, source_target_pairs={{0,1},{1,0},{2,3},{3,2},{4,5},{5,4},{6,7},{7,6},{8,9},{9,8},{10,11... | collective-permute-start | bytes 1179656 | tf_op jit(solution)/shard_map/ppermute | solution.py:600
  803.5 32.9 %collective-permute-start.88 = (bf16[96,2048]{1,0:T(8,128)(2,1)}, bf16[96,2048]{1,0:T(8,128)(2,1)S(1)}, u32[]{:S(2)}, u32[]{:S(2)}) collective-permute-start(bf16[96,2048]{1,0:T(8,128)(2,1)} %get-tuple-element.200), channel_id=1, source_target_pairs={{0,1},{1,0},{2,3},{3,2},{4,5},{5,4},{6,7},{7,6},{8,9},{9,8},{10,11... | collective-permute-start | bytes 1179656 | tf_op jit(solution)/shard_map/ppermute | solution.py:600
  808.9 47.0 %collective-permute-start.120 = (f32[14336]{0:T(1024)}, f32[14336]{0:T(1024)S(1)}, u32[]{:S(2)}, u32[]{:S(2)}) collective-permute-start(f32[14336]{0:T(1024)} %add.495), channel_id=1, source_target_pairs={{0,8},{4,12},{8,0},{12,4},{1,9},{5,13},{9,1},{13,5},{2,10},{6,14},... | collective-permute-start | bytes 172040 | tf_op jit(solution)/shard_map/ppermute | solution.py:600
  (253 other events, 3010.1 us)
Sparse Core Ops, SparseCore 0:
  200.1 37.3 all-gather.12
  241.6 37.3 all-gather.14
  284.7 83.1 all-gather.8
  375.7 83.0 all-gather.10
  600.5 126.3 reduce-scatter.3
  729.7 113.6 reduce-scatter.5
  863.9 109.6 reduce-scatter.7

commit v6 on v5

--- a/solution.py
+++ b/solution.py
@@ -129,12 +129,14 @@
             self.wait(QUARTERS * group + place)
 
 
-def attend_kernel(heads, count, me_ref, seg_col_ref, seg_row_ref, masks_ref, taps_ref, gain_ref, *refs):
+def attend_kernel(heads, count, save, me_ref, seg_col_ref, seg_row_ref, masks_ref, taps_ref, gain_ref, *refs):
     shards, refs = refs[:count], refs[count:]
     project_hbm, beta_hbm, merge_hbm = refs[:3]
-    qkv_ref, logit_ref, mixed_ref, system_ref, attend_ref, inverse_ref, fresh_ref, out_ref = refs[3:11]
-    partials = refs[11 : 11 + count]
-    rows_ref, mixed_abs, project_ref, beta_ref, merge_ref, sems = refs[11 + count :]
+    partials, refs = refs[3 : 3 + count], refs[3 + count :]
+    rows_ref, qkv_ref, logit_ref, mixed_ref, refs = *refs[:4], refs[4:]
+    if save:
+        system_ref, attend_ref, inverse_ref, fresh_ref, out_ref, refs = *refs[:5], refs[5:]
+    mixed_abs, project_ref, beta_ref, merge_ref, sems = refs
     order = relative_order(count)
     share = TOK_MB // count
     fetch = Fetch(
@@ -184,15 +186,18 @@
                 system[h, b, c] = jnp.where(strict[b, c], inner * betas[h][rows_of(b)], 0.0)
                 scores = mm_t(queries[h][rows_of(b)], keys[h][rows_of(c)])
                 attend[h, b, c] = jnp.where(lower[b, c], scores, 0.0).astype(BF16)
-                attend_ref[h, rows_of(b), rows_of(c)] = attend[h, b, c]
                 if c < b:
                     system[h, b, c] = system[h, b, c].astype(BF16)
-                    system_ref[h, rows_of(b), rows_of(c)] = system[h, b, c]
+                if save:
+                    attend_ref[h, rows_of(b), rows_of(c)] = attend[h, b, c]
+                    if c < b:
+                        system_ref[h, rows_of(b), rows_of(c)] = system[h, b, c]
     index = [(h, b) for h in range(heads) for b in range(BLOCKS)]
     inverse = dict(zip(index, unit_inverses([system[h, b, b] for h, b in index])))
     for h, b in index:
         inverse[h, b] = inverse[h, b].astype(BF16)
-        inverse_ref[h, b] = inverse[h, b]
+        if save:
+            inverse_ref[h, b] = inverse[h, b]
     fresh = {}
     for b in range(BLOCKS):
         for h in range(heads):
@@ -200,7 +205,8 @@
             for c in range(b):
                 target = target - mm(system[h, b, c], fresh[h, c])
             fresh[h, b] = mm(inverse[h, b], target).astype(BF16)
-            fresh_ref[rows_of(b), h * HEAD_DIM : (h + 1) * HEAD_DIM] = fresh[h, b]
+            if save:
+                fresh_ref[rows_of(b), h * HEAD_DIM : (h + 1) * HEAD_DIM] = fresh[h, b]
     for h in range(heads):
         cols = slice(h * HEAD_DIM, (h + 1) * HEAD_DIM)
         for b in range(BLOCKS):
@@ -208,7 +214,8 @@
             for c in range(1, b + 1):
                 out = out + mm(attend[h, b, c], fresh[h, c])
             mean = jnp.mean(out * out, axis=-1, keepdims=True)
-            out_ref[rows_of(b), cols] = out
+            if save:
+                out_ref[rows_of(b), cols] = out
             mixed_abs[rows_of(b), cols] = (
                 out * lax.rsqrt(jnp.maximum(mean, OUT_FLOOR)) * gain_ref[...]
             ).astype(BF16)
@@ -245,29 +252,36 @@
     )(*operands, *hbm)
 
 
-def attend_forward(me, mine, shards, taps, gain, project, beta_weight, merge):
+def as_scratch(shapes):
+    return [pltpu.VMEM(shape.shape, shape.dtype) for shape in shapes]
+
+
+def attend_forward(me, mine, shards, taps, gain, project, beta_weight, merge, save):
     masks, seg_col, seg_row = mine
     heads = merge.shape[1] // HEAD_DIM
     width = heads * HEAD_DIM
     model = merge.shape[2]
     count = len(shards)
-    out = [
+    kept = [
+        jax.ShapeDtypeStruct((TOK_MB, model), BF16),
         jax.ShapeDtypeStruct((3, TOK_MB, width), F32),
         jax.ShapeDtypeStruct((TOK_MB, LANES), F32),
         jax.ShapeDtypeStruct((TOK_MB, width), BF16),
+    ]
+    more = [
         jax.ShapeDtypeStruct((heads, TOK_MB, TOK_MB), BF16),
         jax.ShapeDtypeStruct((heads, TOK_MB, TOK_MB), BF16),
         jax.ShapeDtypeStruct((heads, BLOCKS, BLOCK, BLOCK), BF16),
         jax.ShapeDtypeStruct((TOK_MB, width), BF16),
         jax.ShapeDtypeStruct((TOK_MB, width), F32),
-    ] + partial_shapes(count, model)
+    ]
     results = call(
-        functools.partial(attend_kernel, heads, count),
+        functools.partial(attend_kernel, heads, count, save),
         (me, seg_col, seg_row, masks, taps, gain, *shards),
         (project, beta_weight, merge),
-        out,
-        [
-            pltpu.VMEM((TOK_MB, model), BF16),
+        partial_shapes(count, model) + (kept + more if save else []),
+        ([] if save else as_scratch(kept))
+        + [
             pltpu.VMEM((TOK_MB, width), BF16),
             pltpu.VMEM(project.shape[1:], BF16),
             pltpu.VMEM(beta_weight.shape, BF16),
@@ -275,14 +289,17 @@
             pltpu.SemaphoreType.DMA((5,)),
         ],
     )
-    return results[:8], results[8:]
-
-
-def expand_kernel(count, me_ref, *refs):
+    return results[count:], results[:count]
+
+
+def expand_kernel(count, save, me_ref, *refs):
     shards, refs = refs[:count], refs[count:]
-    expand_hbm, contract_hbm, hidden_ref, silu_ref, slope_ref = refs[:5]
-    partials = refs[5 : 5 + count]
-    rows_ref, gate_ref, expand_ref, contract_ref, sems = refs[5 + count :]
+    expand_hbm, contract_hbm = refs[:2]
+    partials, refs = refs[2 : 2 + count], refs[2 + count :]
+    rows_ref, hidden_ref, refs = *refs[:2], refs[2:]
+    if save:
+        silu_ref, slope_ref, refs = *refs[:2], refs[2:]
+    gate_ref, expand_ref, contract_ref, sems = refs
     share = TOK_MB // count
     tiles = tiles_of(hidden_ref.shape[1])
     fetch = Fetch(
@@ -303,30 +320,31 @@
         gate = jax.nn.sigmoid(gate_in)
         silu = gate_in * gate
         hidden_ref[:, t] = (silu * up_in).astype(BF16)
-        silu_ref[:, t] = silu.astype(BF16)
-        slope_ref[:, t] = (up_in * gate * (1.0 + gate_in * (1.0 - gate))).astype(BF16)
+        if save:
+            silu_ref[:, t] = silu.astype(BF16)
+            slope_ref[:, t] = (up_in * gate * (1.0 + gate_in * (1.0 - gate))).astype(BF16)
     fetch.wait_group(2)
     write_partials(partials, rows_ref.shape[1], share, lambda cols: mm(hidden_ref[...], contract_ref[:, cols]))
 
 
-def expand_forward(me, shards, expand, contract):
+def expand_forward(me, shards, expand, contract, save):
     count = len(shards)
     model, units = expand.shape[2:]
-    kept = jax.ShapeDtypeStruct((TOK_MB, units), BF16)
+    kept = [jax.ShapeDtypeStruct((TOK_MB, model), BF16)] + [jax.ShapeDtypeStruct((TOK_MB, units), BF16)] * 3
     results = call(
-        functools.partial(expand_kernel, count),
+        functools.partial(expand_kernel, count, save),
         (me, *shards),
         (expand, contract),
-        [kept, kept, kept] + partial_shapes(count, model),
-        [
-            pltpu.VMEM((TOK_MB, model), BF16),
+        partial_shapes(count, model) + (kept if save else []),
+        ([] if save else as_scratch(kept[:2]))
+        + [
             pltpu.VMEM((TOK_MB, units), F32),
             pltpu.VMEM(expand.shape[1:], BF16),
             pltpu.VMEM(contract.shape[1:], BF16),
             pltpu.SemaphoreType.DMA((3 * QUARTERS,)),
         ],
     )
-    return results[:3], results[3:]
+    return results[count:], results[:count]
 
 
 def expand_back_kernel(count, me_ref, silu_ref, slope_ref, *refs):
@@ -530,7 +548,7 @@
     width = heads * HEAD_DIM
     model = merge.shape[2]
     count = len(shards)
-    qkv, logit, _, system, attend, inverse, fresh, out = kept
+    _, qkv, logit, _, system, attend, inverse, fresh, out = kept
     results = call(
         functools.partial(attend_back_kernel, heads, count),
         (me, seg_col, seg_row, masks, taps, gain, qkv, logit, system, attend, inverse, fresh, out, *shards),
@@ -626,28 +644,57 @@
     return parts
 
 
-def scatter(parts):
-    for bit in bits_of("head"):
+def added(parts, arrived):
+    return [part.astype(F32) + other.astype(F32) for part, other in zip(parts, arrived)]
+
+
+def scatter_near(parts):
+    half = len(parts) // 2
+    return added(parts[:half], [flipped(part, "head", 1) for part in parts[half:]])
+
+
+def scatter_far(parts):
+    for bit in bits_of("head")[1:]:
         half = len(parts) // 2
-        arrived = [flipped(narrow(part), "head", bit) for part in parts[half:]]
-        parts = [part.astype(F32) + other.astype(F32) for part, other in zip(parts[:half], arrived)]
+        parts = added(parts[:half], [flipped(narrow(part), "head", bit) for part in parts[half:]])
     return parts[0]
 
 
-def swapped(shard):
+def in_turn(kernel, shards):
+    results, near = [], None
+    for parts in shards:
+        if near is not None:
+            (parts, near) = lax.optimization_barrier((parts, near))
+            results[-1] = (results[-1][0], near)
+        kept, partials = kernel(len(results), parts)
+        near = scatter_near(partials)
+        results.append((kept, near))
+    return [kept for kept, _ in results], [scatter_far(near) for _, near in results]
+
+
+def gather_in_turn(shards):
+    gathered = []
+    for shard in shards:
+        if gathered:
+            shard, gathered[-1][1] = lax.optimization_barrier((shard, gathered[-1][1]))
+        gathered.append(gather(shard))
+    return gathered
+
+
+def swapped(shards):
     count = lax.axis_size("dp")
     me = lax.axis_index("dp")
-    rows, width = shard.shape
-    blocks = shard.reshape(rows, count, width // count)
+    values = jnp.stack(shards)
+    wide = values.shape[-1] // count
     arrived = []
     for distance in range(count):
-        block = lax.dynamic_index_in_dim(blocks, (me + distance) % count, 1, keepdims=False)
+        block = lax.dynamic_slice_in_dim(values, ((me + distance) % count) * wide, wide, 2)
         if distance:
             block = lax.ppermute(block, "dp", [(i, (i + distance) % count) for i in range(count)])
         arrived.append(block)
     arrived = jnp.stack(arrived)
     ordered = [lax.dynamic_index_in_dim(arrived, (me - q) % count, 0, keepdims=False) for q in range(count)]
-    return jnp.concatenate(ordered, axis=1)
+    return jnp.stack(ordered, axis=1)
 
 
 def per_device(
@@ -680,68 +727,67 @@
     tokens_own = [own_rows(tokens[m]) for m in every]
     cotangent_own = [own_rows(cotangent[m]) for m in every]
 
-    def forward(x, mine):
-        unit, scale = rms_parts(x)
-        normed = gather(narrow(unit * gains[0]))
-        kept, partials = attend_forward(me, mine, normed, conv_weight, o_gain, attn_in, beta_wide, attn_out)
-        middle = x + scatter(partials)
-        unit_mid, scale_mid = rms_parts(middle)
-        normed_mid = gather(narrow(unit_mid * gains[1]))
-        (hidden, silu, slope), partials = expand_forward(me, normed_mid, mlp_in, mlp_out)
-        result = middle + scatter(partials)
-        return result, (unit, scale, normed, kept, unit_mid, scale_mid, normed_mid, hidden, silu, slope)
-
-    def backward_mlp(incoming, saved):
-        unit_mid, scale_mid, silu, slope = saved[4], saved[5], saved[8], saved[9]
-        grads, partials = expand_backward(me, gather(narrow(incoming)), silu, slope, mlp_in, mlp_out)
-        grad_mid = scatter(partials)
-        grad_middle = incoming + norm_back(grad_mid, unit_mid, scale_mid, gains[1])
-        return grad_middle, grads, jnp.sum(grad_mid * unit_mid, axis=0)
-
-    def backward_mix(grad_middle, gain_two, mine, saved):
-        unit, scale, _, kept = saved[:4]
-        (grad_qkv, grad_logit, grad_taps, grad_head_gain), partials = attend_backward(
-            me, mine, gather(narrow(grad_middle)), kept, conv_weight, o_gain, attn_in, beta_wide, attn_out
+    def forward_turn(inputs, save):
+        parts = [rms_parts(x) for x in inputs]
+        normed = gather_in_turn([narrow(unit * gains[0]) for unit, _ in parts])
+        kept, sums = in_turn(
+            lambda m, rows: attend_forward(
+                me, masks[m], rows, conv_weight, o_gain, attn_in, beta_wide, attn_out, save
+            ),
+            normed,
         )
-        grad_norm = scatter(partials)
-        grad_inputs = grad_middle + norm_back(grad_norm, unit, scale, gains[0])
-        gain_one = jnp.sum(grad_norm * unit, axis=0)
-        small = (grad_taps, jnp.sum(grad_head_gain, axis=0), jnp.stack([gain_one, gain_two]))
-        return grad_inputs, grad_qkv, grad_logit, small
-
-    def forward_turn(inputs):
-        results = [forward(inputs[m], masks[m]) for m in every]
-        return [result for result, _ in results], [saved for _, saved in results]
+        middles = [x + total for x, total in zip(inputs, sums)]
+        parts_mid = [rms_parts(middle) for middle in middles]
+        normed_mid = [gather(narrow(unit * gains[1])) for unit, _ in parts_mid]
+        kept_mid, sums = in_turn(lambda m, rows: expand_forward(me, rows, mlp_in, mlp_out, save), normed_mid)
+        outputs = [middle + total for middle, total in zip(middles, sums)]
+        return outputs, (parts, kept, parts_mid, kept_mid)
+
+    def backward_expand(incoming, saved):
+        _, _, parts_mid, kept_mid = saved
+        grads, sums = in_turn(
+            lambda m, rows: expand_backward(me, rows, *kept_mid[m][2:], mlp_in, mlp_out),
+            gather_in_turn([narrow(value) for value in incoming]),
+        )
+        middles = [value + norm_back(sums[m], *parts_mid[m], gains[1]) for m, value in enumerate(incoming)]
+        return middles, grads, sum(jnp.sum(sums[m] * parts_mid[m][0], axis=0) for m in every)
+
+    def backward_attend(middles, saved):
+        parts, kept, _, _ = saved
+        grads, sums = in_turn(
+            lambda m, rows: attend_backward(
+                me, masks[m], rows, kept[m], conv_weight, o_gain, attn_in, beta_wide, attn_out
+            ),
+            gather_in_turn([narrow(value) for value in middles]),
+        )
+        finals = [value + norm_back(sums[m], *parts[m], gains[0]) for m, value in enumerate(middles)]
+        return finals, grads, sum(jnp.sum(sums[m] * parts[m][0], axis=0) for m in every)
+
+    def all_rows(values):
+        return jnp.concatenate(values, axis=0)
 
     last = sections - 1
     inputs = tokens_own
     for turn in range(sections):
-        outputs, kept = forward_turn(inputs)
+        outputs, saved = forward_turn(inputs, turn == last)
         if turn < last:
             arrived = [shifted(narrow(value), "section", 1).astype(F32) for value in outputs]
             inputs = [jnp.where(section == 0, tokens_own[m], arrived[m]) for m in every]
 
-    def every_row(values):
-        return [lax.all_gather(value, "dp", axis=0) for value in values]
-
-    hidden_rows = every_row([saved[7] for saved in kept])
-    mixed_rows = every_row([saved[3][2] for saved in kept])
+    hidden_rows = [lax.all_gather(values[1], "dp", axis=0, tiled=True) for values in saved[3]]
+    mixed_rows = [lax.all_gather(values[3], "dp", axis=0, tiled=True) for values in saved[1]]
 
     incoming = cotangent_own
     for turn in range(sections):
         if turn == last:
             incoming, hidden_rows, mixed_rows = lax.optimization_barrier((incoming, hidden_rows, mixed_rows))
-        halves = [backward_mlp(incoming[m], kept[m]) for m in every]
-        middles = [half[0] for half in halves]
+        middles, grads, gain_two = backward_expand(incoming, saved)
         if turn == last:
-            normed_mid = jnp.concatenate([part for saved in kept for part in saved[6]], axis=0)
-            expands = [
-                narrow(product_left(normed_mid, jnp.concatenate([half[1][j] for half in halves], axis=0)))
-                for j in range(2)
-            ]
-            middles, expands = lax.optimization_barrier((middles, expands))
-        results = [backward_mix(middles[m], halves[m][2], masks[m], kept[m]) for m in every]
-        finals = [result[0] for result in results]
+            swapped_out = swapped([narrow(value) for value in incoming])
+            normed_mid = all_rows([values[0] for values in saved[3]])
+            expands = [narrow(product_left(normed_mid, all_rows([grad[j] for grad in grads]))) for j in range(2)]
+            middles, expands, swapped_out = lax.optimization_barrier((middles, expands, swapped_out))
+        finals, grads, gain_one = backward_attend(middles, saved)
         if turn < last:
             arrived = [shifted(narrow(value), "section", -1).astype(F32) for value in finals]
             incoming = [jnp.where(section == last, cotangent_own[m], arrived[m]) for m in every]
@@ -754,28 +800,24 @@
         return lax.psum_scatter(value, "dp", scatter_dimension=axis, tiled=True)
 
     early = [spread(part, 0) for part in expands]
-    normed = jnp.concatenate([part for saved in kept for part in saved[2]], axis=0)
-    grad_qkv = jnp.concatenate([result[1] for result in results], axis=0)
-    grad_logit = jnp.concatenate([result[2] for result in results], axis=0)
-    grad_project = narrow(product_left(normed, grad_qkv))
-    grad_beta = product_left(normed, grad_logit)[:, :heads]
-
-    def from_rows(rows, shards):
+    normed = all_rows([values[0] for values in saved[1]])
+    grad_project = narrow(product_left(normed, all_rows([grad[0] for grad in grads])))
+    grad_beta = product_left(normed, all_rows([grad[1] for grad in grads]))[:, :heads]
+    grad_taps, grad_head_gain = (sum(grad[place] for grad in grads) for place in (2, 3))
+    grad_head_gain = jnp.sum(grad_head_gain, axis=0)
+
+    def from_rows(rows, columns):
         total = 0.0
-        for left, right in zip(rows, shards):
-            right = jnp.concatenate(gather(swapped(right)), axis=0).reshape(TOK_MB, left.shape[0], -1)
-            total = total + lax.dot_general(
-                left, right, (((0, 1), (1, 0)), ((), ())), preferred_element_type=F32
-            )
+        columns = jnp.concatenate(gather(columns), axis=2)
+        for left, right in zip(rows, columns):
+            total = total + product_left(left, right.reshape(left.shape[0], -1))
         return total
 
-    grad_contract = from_rows(hidden_rows, [narrow(value) for value in incoming])
-    grad_merge = from_rows(mixed_rows, [narrow(value) for value in middles])
-    grad_taps, grad_head_gain, grad_gains = (
-        sum(result[3][place] for result in results) for place in range(3)
-    )
-    grad_gains = summed(jnp.concatenate([grad_gains.reshape(-1), grad_head_gain]), ("dp", "head"))
-    grad_gains, grad_head_gain = grad_gains[: 2 * width].reshape(2, width), grad_gains[2 * width :]
+    grad_contract = from_rows(hidden_rows, swapped_out)
+    grad_merge = from_rows(mixed_rows, swapped([narrow(value) for value in middles]))
+    flat = jnp.concatenate([gain_one, gain_two, grad_head_gain])
+    flat = summed(flat, ("dp", "head"))
+    grad_gains, grad_head_gain = flat[: 2 * width].reshape(2, width), flat[2 * width :]
     flat = summed(jnp.concatenate([grad_taps.reshape(-1), grad_beta.reshape(-1)]), ("dp",))
     grad_taps, grad_beta = flat[: grad_taps.size].reshape(grad_taps.shape), flat[grad_taps.size :]
     rows = width // lax.axis_size("dp")

time: 994 us -> 907 us (0.912)
  local copies, waits for them, and re-layouts: 100 us -> 61.5 us
  other arithmetic: 89 us -> 71 us
  starting transfers between devices: 99.9 us -> 87.9 us
    reduce_scatter x3, waiting for transfers between devices: 105 us -> 150 us  [spread(): return lax.psum_scatter(value, 'dp', scatter_dimension=axis, tiled=True)]
    ppermute x108 -> x102, waiting for transfers between devices: 242 us -> 206 us  [flipped(): lax.ppermute(values, axis, [(i, i ^ bit) for i in range(lax.axis_size(axi...]
    ppermute x12 -> x6, waiting for transfers between devices: 42.4 us -> 23.5 us  [swapped(): lax.ppermute(block, 'dp', [(i, (i + distance) % count) for i in range(cou...]
    dot_general x4 -> x0, matrix products: 18.4 us -> none  [from_rows(): lax.dot_general(left, right, (((0, 1), (1, 0)), ((), ())), preferred_elem...]
    concatenate x9 -> x2, other arithmetic: 18.2 us -> 1.94 us  [the longest x1 1.93 us: from_rows(): columns = jnp.concatenate(gather(columns), axis=2)]
    unnamed x369 -> x273, local copies, waits for them, and re-layouts: 55.3 us -> 40.5 us
    dot_general x4 -> x8, matrix products: 25.2 us -> 37.4 us  [product_left(): lax.dot_general(left, right, (((0,), (0,)), ((), ())), preferred_element_...]
    ppermute x108 -> x102, starting transfers between devices: 66.8 us -> 60.3 us  [flipped(): lax.ppermute(values, axis, [(i, i ^ bit) for i in range(lax.axis_size(axi...]
  transfers between devices with their start and end apart: 132 -> 120, of which waited for: 40 -> 55; matrix products, arithmetic and copies ran while one was open for 18% -> 13% of each run, Pallas kernels for 22% -> 21%
where the time goes in v6:
time: 907 us; the launch traced here: 898 us
  waiting for transfers between devices  400 us (44%)
  Pallas kernels  223 us (25%)
  starting transfers between devices  87.9 us (10%)
  other arithmetic  71 us (8%)
  local copies, waits for them, and re-layouts  61.5 us (7%)
  matrix products  37.4 us (4%)
  between operations  16.5 us (2%)
    pallas_call x16, Pallas kernels, call(): pl.pallas_call(kernel, in_specs=[pl.BlockSpec(memory_space=pltpu.SMEM)] +...  223 us
    ppermute x102, waiting for transfers between devices, flipped(): lax.ppermute(values, axis, [(i, i ^ bit) for i in range(lax.axis_size(axi...  206 us
    reduce_scatter x3, waiting for transfers between devices, spread(): return lax.psum_scatter(value, 'dp', scatter_dimension=axis, tiled=True)  150 us
    ppermute x102, starting transfers between devices, flipped(): lax.ppermute(values, axis, [(i, i ^ bit) for i in range(lax.axis_size(axi...  60.3 us
    unnamed x273, local copies, waits for them, and re-layouts  40.5 us
    dot_general x8, matrix products, product_left(): lax.dot_general(left, right, (((0,), (0,)), ((), ())), preferred_element_...  37.4 us
    ppermute x6, waiting for transfers between devices, swapped(): lax.ppermute(block, 'dp', [(i, (i + distance) % count) for i in range(cou...  23.5 us
    ppermute x5, waiting for transfers between devices, shifted(): lax.ppermute(values, axis, [(i, i + distance) for i in devices if i + dis...  20.6 us
  transfers between devices with their start and end apart: 120, of which 55 were waited for; matrix products, arithmetic and copies ran while one was open for 13% of the time, Pallas kernels for 21%

profile of v6, /device:TPU:0, one launch (start us, length us, event | category | flops | bytes accessed | tf_op | source)
XLA Modules:
  0.0 898.1 jit_solution(2084316686723118771)
XLA Ops:
  17.2 8.8 collective-permute-done.refs_1_
  30.7 12.2 %shard_map.178 = (f32[96,2048]{1,0:T(8,128)S(1)}, f32[96,2048]{1,0:T(8,128)S(1)}, bf16[96,2048]{1,0:T(8,128)(2,1)S(1)}, bf16[96,2048]{1,0:T(8,128)(2,1)S(1)}) custom-call(s32[1]{0:T(128)} %bitcast.me_ref, s32[384,1]{1,0:T(8,128)S(1)} %broadcast_in_dim.33.seg_col_ref, s32[1,384]{1,0:T(1,128)S(1)} %broadcast_in_dim.24.seg_row_ref, ...), custom_call_target="tpu_custom_call" | custom-call | flops 1000000 | bytes 100000 | tf_op jit(solution)/shard_map/pallas_call | solution.py:242
  46.7 12.1 %shard_map.179 = (f32[96,2048]{1,0:T(8,128)S(1)}, f32[96,2048]{1,0:T(8,128)S(1)}, bf16[96,2048]{1,0:T(8,128)(2,1)S(1)}, bf16[96,2048]{1,0:T(8,128)(2,1)S(1)}) custom-call(s32[1]{0:T(128)} %bitcast.me_ref, s32[384,1]{1,0:T(8,128)S(1)} %broadcast_in_dim.34.seg_col_ref, s32[1,384]{1,0:T(1,128)S(1)} %broadcast_in_dim.26.seg_row_ref, ...), custom_call_target="tpu_custom_call" | custom-call | flops 1000000 | bytes 100000 | tf_op jit(solution)/shard_map/pallas_call | solution.py:242
  61.3 9.8 %collective-permute-done.8 = bf16[96,2048]{1,0:T(8,128)(2,1)S(1)} collective-permute-done((bf16[96,2048]{1,0:T(8,128)(2,1)S(1)}, bf16[96,2048]{1,0:T(8,128)(2,1)S(1)}, u32[]{:S(2)}, u32[]{:S(2)}) %collective-permute-start.8) | collective-permute-done | bytes 393248 | tf_op jit(solution)/shard_map/ppermute | solution.py:618
  72.4 6.4 collective-permute-done.11
  80.9 10.0 %collective-permute-done.15.refs_1_ = bf16[96,2048]{1,0:T(8,128)(2,1)S(1)} collective-permute-done((bf16[96,2048]{1,0:T(8,128)(2,1)S(1)}, bf16[96,2048]{1,0:T(8,128)(2,1)S(1)}, u32[]{:S(2)}, u32[]{:S(2)}) %collective-permute-start.15) | collective-permute-done | bytes 393248 | tf_op jit(solution)/shard_map/ppermute | solution.py:618
  92.6 12.1 %shard_map.180 = (f32[96,2048]{1,0:T(8,128)S(1)}, f32[96,2048]{1,0:T(8,128)S(1)}, bf16[96,2048]{1,0:T(8,128)(2,1)S(1)}, bf16[96,2048]{1,0:T(8,128)(2,1)S(1)}) custom-call(s32[1]{0:T(128)} %bitcast.me_ref, bf16[96,2048]{1,0:T(8,128)(2,1)S(1)} %get-tuple-element.436.refs_0_, bf16[96,2048]{1,0:T(8,128)(2,1)S(1)} %collective-permute-done.15.refs_1_, ...), custom_call_target="tpu_custom_call" | custom-call | flops 1000000 | bytes 100000 | tf_op jit(solution)/shard_map/pallas_call | solution.py:242
  108.4 11.6 %shard_map.181 = (f32[96,2048]{1,0:T(8,128)S(1)}, f32[96,2048]{1,0:T(8,128)S(1)}, bf16[96,2048]{1,0:T(8,128)(2,1)S(1)}, bf16[96,2048]{1,0:T(8,128)(2,1)S(1)}) custom-call(s32[1]{0:T(128)} %bitcast.me_ref, bf16[96,2048]{1,0:T(8,128)(2,1)S(1)} %get-tuple-element.204.refs_0_, bf16[96,2048]{1,0:T(8,128)(2,1)S(1)} %collective-permute-done.12.refs_1_, ...), custom_call_target="tpu_custom_call" | custom-call | flops 1000000 | bytes 100000 | tf_op jit(solution)/shard_map/pallas_call | solution.py:242
  122.5 9.7 %collective-permute-done.20 = bf16[96,2048]{1,0:T(8,128)(2,1)S(1)} collective-permute-done((bf16[96,2048]{1,0:T(8,128)(2,1)S(1)}, bf16[96,2048]{1,0:T(8,128)(2,1)S(1)}, u32[]{:S(2)}, u32[]{:S(2)}) %collective-permute-start.20) | collective-permute-done | bytes 393248 | tf_op jit(solution)/shard_map/ppermute | solution.py:618
  145.9 7.0 collective-permute-done.25
  156.3 9.1 %collective-permute-done.26.refs_1_ = bf16[96,2048]{1,0:T(8,128)(2,1)S(1)} collective-permute-done((bf16[96,2048]{1,0:T(8,128)(2,1)S(1)}, bf16[96,2048]{1,0:T(8,128)(2,1)S(1)}, u32[]{:S(2)}, u32[]{:S(2)}) %collective-permute-start.26) | collective-permute-done | bytes 393248 | tf_op jit(solution)/shard_map/ppermute | solution.py:618
  167.2 13.2 %shard_map.182 = (f32[96,2048]{1,0:T(8,128)S(1)}, f32[96,2048]{1,0:T(8,128)S(1)}, bf16[96,2048]{1,0:T(8,128)(2,1)S(1)}, bf16[96,2048]{1,0:T(8,128)(2,1)S(1)}, bf...) custom-call(s32[1]{0:T(128)} %bitcast.me_ref, ...), custom_call_target="tpu_custom_call" | custom-call | flops 1000000 | bytes 100000 | tf_op jit(solution)/shard_map/pallas_call | solution.py:242
  189.9 10.0 %collective-permute-done.29.refs_1_ = bf16[96,2048]{1,0:T(8,128)(2,1)S(1)} collective-permute-done((bf16[96,2048]{1,0:T(8,128)(2,1)S(1)}, bf16[96,2048]{1,0:T(8,128)(2,1)S(1)}, u32[]{:S(2)}, u32[]{:S(2)}) %collective-permute-start.29) | collective-permute-done | bytes 393248 | tf_op jit(solution)/shard_map/ppermute | solution.py:618
  202.9 12.8 %shard_map.183 = (f32[96,2048]{1,0:T(8,128)S(1)}, f32[96,2048]{1,0:T(8,128)S(1)}, bf16[96,2048]{1,0:T(8,128)(2,1)}, bf16[96,2048]{1,0:T(8,128)(2,1)}, bf16[384,2...) custom-call(s32[1]{0:T(128)} %bitcast.me_ref, ...), custom_call_target="tpu_custom_call" | custom-call | flops 1000000 | bytes 100000 | tf_op jit(solution)/shard_map/pallas_call | solution.py:242
  226.7 8.4 collective-permute-done.34
  237.1 5.4 collective-permute-done.49
  245.6 9.8 %collective-permute-done.50.refs_1_ = bf16[96,2048]{1,0:T(8,128)(2,1)S(1)} collective-permute-done((bf16[96,2048]{1,0:T(8,128)(2,1)S(1)}, bf16[96,2048]{1,0:T(8,128)(2,1)S(1)}, u32[]{:S(2)}, u32[]{:S(2)}) %collective-permute-start.50) | collective-permute-done | bytes 393248 | tf_op jit(solution)/shard_map/ppermute | solution.py:618
  257.1 12.4 %shard_map.186 = (f32[96,2048]{1,0:T(8,128)}, f32[96,2048]{1,0:T(8,128)}, bf16[96,2048]{1,0:T(8,128)(2,1)}, bf16[96,2048]{1,0:T(8,128)(2,1)}, bf16[384,2048]{1,0...) custom-call(s32[1]{0:T(128)} %bitcast.me_ref, ...), custom_call_target="tpu_custom_call" | custom-call | flops 1000000 | bytes 100000 | tf_op jit(solution)/shard_map/pallas_call | solution.py:242
  278.8 9.8 %collective-permute-done.39.refs_1_ = bf16[96,2048]{1,0:T(8,128)(2,1)S(1)} collective-permute-done((bf16[96,2048]{1,0:T(8,128)(2,1)S(1)}, bf16[96,2048]{1,0:T(8,128)(2,1)S(1)}, u32[]{:S(2)}, u32[]{:S(2)}) %collective-permute-start.39) | collective-permute-done | bytes 393248 | tf_op jit(solution)/shard_map/ppermute | solution.py:618
  289.1 7.1 collective-permute-done.35.refs_1_
  296.9 12.5 %shard_map.184 = (f32[96,2048]{1,0:T(8,128)}, f32[96,2048]{1,0:T(8,128)}, bf16[96,2048]{1,0:T(8,128)(2,1)}, bf16[96,2048]{1,0:T(8,128)(2,1)}, bf16[384,2048]{1,0...) custom-call(s32[1]{0:T(128)} %bitcast.me_ref, ...), custom_call_target="tpu_custom_call" | custom-call | flops 1000000 | bytes 100000 | tf_op jit(solution)/shard_map/pallas_call | solution.py:242
  311.5 13.0 %shard_map.185 = (bf16[384,1408]{1,0:T(8,128)(2,1)}, bf16[384,1408]{1,0:T(8,128)(2,1)}, f32[96,2048]{1,0:T(8,128)S(1)}, f32[96,2048]{1,0:T(8,128)S(1)}, bf16[96,...) custom-call(s32[1]{0:T(128)} %bitcast.me_ref, bf16[384,1408]{1,0:T(8,128)(2,1)S(1)} %get-tuple-element.234.silu_ref, ...), custom_call_target="tpu_custom_call" | custom-call | flops 1000000 | bytes 100000 | tf_op jit(solution)/shard_map/pallas_call | solution.py:242
  329.0 12.3 %shard_map.187 = (bf16[384,1408]{1,0:T(8,128)(2,1)}, bf16[384,1408]{1,0:T(8,128)(2,1)}, f32[96,2048]{1,0:T(8,128)S(1)}, f32[96,2048]{1,0:T(8,128)S(1)}, bf16[96,...) custom-call(s32[1]{0:T(128)} %bitcast.me_ref, bf16[384,1408]{1,0:T(8,128)(2,1)S(1)} %copy-done.11, ...), custom_call_target="tpu_custom_call" | custom-call | flops 1000000 | bytes 100000 | tf_op jit(solution)/shard_map/pallas_call | solution.py:242
  346.3 8.3 collective-permute-done.46
  354.7 7.8 collective-permute-done.55
  370.0 9.0 collective-permute-done.56.refs_1_
  380.8 19.2 %shard_map.188 = (bf16[384,1536]{1,0:T(8,128)(2,1)}, bf16[384,128]{1,0:T(8,128)(2,1)}, f32[3,4,512]{2,1,0:T(4,128)}, f32[8,128]{1,0:T(8,128)}, f32[96,2048]{1,0:...) custom-call(s32[1]{0:T(128)} %bitcast.me_ref, ...), custom_call_target="tpu_custom_call" | custom-call | flops 1000000 | bytes 100000 | tf_op jit(solution)/shard_map/pallas_call | solution.py:242
  403.6 19.2 %shard_map.189 = (bf16[384,1536]{1,0:T(8,128)(2,1)}, bf16[384,128]{1,0:T(8,128)(2,1)}, f32[3,4,512]{2,1,0:T(4,128)}, f32[8,128]{1,0:T(8,128)}, f32[96,2048]{1,0:...) custom-call(s32[1]{0:T(128)} %bitcast.me_ref, ...), custom_call_target="tpu_custom_call" | custom-call | flops 1000000 | bytes 100000 | tf_op jit(solution)/shard_map/pallas_call | solution.py:242
  426.1 8.8 collective-permute-done.64
  434.9 7.9 collective-permute-done.68
  450.6 8.7 collective-permute-done.69
  472.4 8.8 collective-permute-done.70.refs_1_
  489.9 11.2 %shard_map.190 = (bf16[384,1408]{1,0:T(8,128)(2,1)S(1)}, bf16[384,1408]{1,0:T(8,128)(2,1)S(1)}, f32[96,2048]{1,0:T(8,128)S(1)}, f32[96,2048]{1,0:T(8,128)S(1)}, ...) custom-call(s32[1]{0:T(128)} %bitcast.me_ref, bf16[384,1408]{1,0:T(8,128)(2,1)S(1)} %copy-done.17, ...), custom_call_target="tpu_custom_call" | custom-call | flops 1000000 | bytes 100000 | tf_op jit(solution)/shard_map/pallas_call | solution.py:242
  506.5 12.5 %shard_map.191 = (bf16[384,1408]{1,0:T(8,128)(2,1)S(1)}, bf16[384,1408]{1,0:T(8,128)(2,1)S(1)}, f32[96,2048]{1,0:T(8,128)S(1)}, f32[96,2048]{1,0:T(8,128)S(1)}, ...) custom-call(s32[1]{0:T(128)} %bitcast.me_ref, bf16[384,1408]{1,0:T(8,128)(2,1)S(1)} %copy-done.12, ...), custom_call_target="tpu_custom_call" | custom-call | flops 1000000 | bytes 100000 | tf_op jit(solution)/shard_map/pallas_call | solution.py:242
  522.3 6.9 convolution_convert_fusion.2
  532.5 8.9 convolution_convert_fusion.1
  564.3 7.0 collective-permute-done.101
  576.8 8.4 collective-permute-done.102
  585.8 8.1 collective-permute-done.103
  596.3 18.1 %shard_map.192 = (bf16[384,1536]{1,0:T(8,128)(2,1)S(1)}, bf16[384,128]{1,0:T(8,128)(2,1)S(1)}, f32[3,4,512]{2,1,0:T(4,128)S(1)}, f32[8,128]{1,0:T(8,128)S(1)}, f...) custom-call(s32[1]{0:T(128)} %bitcast.me_ref, ...), custom_call_target="tpu_custom_call" | custom-call | flops 1000000 | bytes 100000 | tf_op jit(solution)/shard_map/pallas_call | solution.py:242
  621.4 8.2 collective-permute-done.88.refs_1_
  632.7 19.0 %shard_map.193 = (bf16[384,1536]{1,0:T(8,128)(2,1)S(1)}, bf16[384,128]{1,0:T(8,128)(2,1)S(1)}, f32[3,4,512]{2,1,0:T(4,128)S(1)}, f32[8,128]{1,0:T(8,128)S(1)}, f...) custom-call(s32[1]{0:T(128)} %bitcast.me_ref, ...), custom_call_target="tpu_custom_call" | custom-call | flops 1000000 | bytes 100000 | tf_op jit(solution)/shard_map/pallas_call | solution.py:242
  658.5 9.0 %collective-permute-start.107 = (f32[14336]{0:T(1024)S(1)}, f32[14336]{0:T(1024)S(1)}, u32[]{:S(2)}, u32[]{:S(2)}) collective-permute-start(f32[14336]{0:T(1024)S(1)} %constant_dynamic-update-slice_fusion.9), channel_id=1, source_target_pairs={{0,4},{4,0},{8,12},{12,8},{1,5},{5,1},{9,13},{13,9},{2,6},{6,2},{1... | collective-permute-start | bytes 172040 | tf_op jit(solution)/shard_map/ppermute | solution.py:618
  667.6 9.0 %convolution_convert_fusion = bf16[2048,1536]{1,0:T(8,128)(2,1)} fusion(bf16[768,2048]{1,0:T(8,128)(2,1)} %copy-done.103, bf16[384,1536]{1,0:T(8,128)(2,1)S(1)} %copy-done.73, bf16[384,1536]{1,0:T(8,128)(2,1)S(1)} %copy-done.71), kind=kOutput, calls=%fused_computation | convolution fusion | flops 4839702528 | bytes 11796480 | tf_op jit(solution)/shard_map/dot_general | solution.py:594
  679.6 7.8 collective-permute-done.108
  711.8 5.5 collective-permute-done.109
  733.1 42.1 %reduce-scatter.6.cloned.1.call-done = bf16[512,1408]{1,0:T(8,128)(2,1)} async-done(((bf16[2048,1408]{1,0:T(8,128)(2,1)}), bf16[512,1408]{1,0:T(8,128)(2,1)}) %reduce-scatter.6.cloned.1.call-update) | async-done | bytes 1441808 | tf_op jit(solution)/shard_map/reduce_scatter | solution.py:800
  779.4 108.3 %reduce-scatter.8.cloned.1.call-done = bf16[512,1536]{1,0:T(8,128)(2,1)} async-done(((bf16[2048,1536]{1,0:T(8,128)(2,1)}), bf16[512,1536]{1,0:T(8,128)(2,1)}) %reduce-scatter.8.cloned.1.call-update) | async-done | bytes 1572880 | tf_op jit(solution)/shard_map/reduce_scatter | solution.py:800
  (633 shorter events, 258.3 us)
Async XLA Ops:
  7.2 461.1 %all-gather.9.cloned.1.call-start = ((), (), s32[]{:S(2)}) async-start(), calls=%async_computation.5 | async-start | bytes 1966080 | tf_op jit(solution)/shard_map/all_gather | solution.py:778
  16.7 14.0 %collective-permute-start.4 = (bf16[96,2048]{1,0:T(8,128)(2,1)S(1)}, bf16[96,2048]{1,0:T(8,128)(2,1)}, u32[]{:S(2)}, u32[]{:S(2)}) collective-permute-start(bf16[96,2048]{1,0:T(8,128)(2,1)S(1)} %get-tuple-element.438.refs_0_), channel_id=1, source_target_pairs={{0,1},{1,0},{2,3},{3,2},{4,5},{5,4},{6,7},{7,6},{8,9},{9,8},{10,11... | collective-permute-start | bytes 1179656 | tf_op jit(solution)/shard_map/ppermute | solution.py:618
  28.9 15.4 %collective-permute-start.1 = (bf16[96,2048]{1,0:T(8,128)(2,1)}, bf16[96,2048]{1,0:T(8,128)(2,1)S(1)}, u32[]{:S(2)}, u32[]{:S(2)}) collective-permute-start(bf16[96,2048]{1,0:T(8,128)(2,1)} %get-tuple-element.190.refs_0_), channel_id=1, source_target_pairs={{0,2},{1,3},{2,0},{3,1},{4,6},{5,7},{6,4},{7,5},{8,10},{9,11},{10,... | collective-permute-start | bytes 1179656 | tf_op jit(solution)/shard_map/ppermute | solution.py:618
  60.7 18.2 %collective-permute-start.11 = (bf16[96,2048]{1,0:T(8,128)(2,1)S(1)}, bf16[96,2048]{1,0:T(8,128)(2,1)S(1)}, u32[]{:S(2)}, u32[]{:S(2)}) collective-permute-start(bf16[96,2048]{1,0:T(8,128)(2,1)S(1)} %add_convert_fusion.10), channel_id=1, source_target_pairs={{0,2},{1,3},{2,0},{3,1},{4,6},{5,7},{6,4},{7,5},{8,10},{9,11},{10,... | collective-permute-start | bytes 1179656 | tf_op jit(solution)/shard_map/ppermute | solution.py:618
  90.9 14.5 %collective-permute-start.12 = (bf16[96,2048]{1,0:T(8,128)(2,1)S(1)}, bf16[96,2048]{1,0:T(8,128)(2,1)S(1)}, u32[]{:S(2)}, u32[]{:S(2)}) collective-permute-start(bf16[96,2048]{1,0:T(8,128)(2,1)S(1)} %get-tuple-element.204.refs_0_), channel_id=1, source_target_pairs={{0,2},{1,3},{2,0},{3,1},{4,6},{5,7},{6,4},{7,5},{8,10},{9,11},{10,... | collective-permute-start | bytes 1179656 | tf_op jit(solution)/shard_map/ppermute | solution.py:618
  120.7 15.7 %collective-permute-start.22 = (bf16[96,2048]{1,0:T(8,128)(2,1)S(1)}, bf16[96,2048]{1,0:T(8,128)(2,1)S(1)}, u32[]{:S(2)}, u32[]{:S(2)}) collective-permute-start(bf16[96,2048]{1,0:T(8,128)(2,1)S(1)} %get-tuple-element.209), channel_id=1, source_target_pairs={{0,1},{1,0},{2,3},{3,2},{4,5},{5,4},{6,7},{7,6},{8,9},{9,8},{10,11... | collective-permute-start | bytes 1179656 | tf_op jit(solution)/shard_map/ppermute | solution.py:618
  121.8 18.2 %collective-permute-start.24 = (bf16[96,2048]{1,0:T(8,128)(2,1)S(1)}, bf16[96,2048]{1,0:T(8,128)(2,1)S(1)}, u32[]{:S(2)}, u32[]{:S(2)}) collective-permute-start(bf16[96,2048]{1,0:T(8,128)(2,1)S(1)} %add_convert_fusion.8), channel_id=1, source_target_pairs={{0,2},{1,3},{2,0},{3,1},{4,6},{5,7},{6,4},{7,5},{8,10},{9,11},{10,... | collective-permute-start | bytes 1179656 | tf_op jit(solution)/shard_map/ppermute | solution.py:618
  188.6 279.7 %all-gather.11.cloned.1.call-start = ((), (), s32[]{:S(2)}) async-start(), calls=%async_computation.6 | async-start | bytes 1966080 | tf_op jit(solution)/shard_map/all_gather | solution.py:778
  223.3 13.7 %collective-permute-start.47 = (bf16[96,2048]{1,0:T(8,128)(2,1)}, bf16[96,2048]{1,0:T(8,128)(2,1)}, u32[]{:S(2)}, u32[]{:S(2)}) collective-permute-start(bf16[96,2048]{1,0:T(8,128)(2,1)} %get-tuple-element.244), channel_id=1, source_target_pairs={{0,1},{1,0},{2,3},{3,2},{4,5},{5,4},{6,7},{7,6},{8,9},{9,8},{10,11... | collective-permute-start | bytes 1179656 | tf_op jit(solution)/shard_map/ppermute | solution.py:618
  223.4 244.9 %all-gather.7.cloned.1.call-start = ((), (), s32[]{:S(2)}) async-start(), calls=%async_computation.4 | async-start | bytes 5406720 | tf_op jit(solution)/shard_map/all_gather | solution.py:777
  225.9 16.6 %collective-permute-start.49 = (bf16[96,2048]{1,0:T(8,128)(2,1)S(1)}, bf16[96,2048]{1,0:T(8,128)(2,1)S(1)}, u32[]{:S(2)}, u32[]{:S(2)}) collective-permute-start(bf16[96,2048]{1,0:T(8,128)(2,1)S(1)} %add_convert_fusion.6), channel_id=1, source_target_pairs={{0,2},{1,3},{2,0},{3,1},{4,6},{5,7},{6,4},{7,5},{8,10},{9,11},{10,... | collective-permute-start | bytes 1179656 | tf_op jit(solution)/shard_map/ppermute | solution.py:618
  273.7 194.6 %all-gather.5.cloned.1.call-start = ((), (), s32[]{:S(2)}) async-start(), calls=%async_computation.3 | async-start | bytes 5406720 | tf_op jit(solution)/shard_map/all_gather | solution.py:777
  277.8 18.5 %collective-permute-start.35 = (bf16[96,2048]{1,0:T(8,128)(2,1)S(1)}, bf16[96,2048]{1,0:T(8,128)(2,1)S(1)}, u32[]{:S(2)}, u32[]{:S(2)}) collective-permute-start(bf16[96,2048]{1,0:T(8,128)(2,1)S(1)} %dynamic-slice_bitcast_fusion.1.refs_0_), channel_id=1, source_target_pairs={{0,2},{1,3},{2,0},{3,1},{4,6},{5,7},{6,4},{7,5},{8,10},{9,11},{10,... | collective-permute-start | bytes 1179656 | tf_op jit(solution)/shard_map/ppermute | solution.py:618
  278.8 18.1 %collective-permute-start.40 = (bf16[96,2048]{1,0:T(8,128)(2,1)S(1)}, bf16[96,2048]{1,0:T(8,128)(2,1)S(1)}, u32[]{:S(2)}, u32[]{:S(2)}) collective-permute-start(bf16[96,2048]{1,0:T(8,128)(2,1)S(1)} %copy-done.36), channel_id=1, source_target_pairs={{0,1},{1,0},{2,3},{3,2},{4,5},{5,4},{6,7},{7,6},{8,9},{9,8},{10,11... | collective-permute-start | bytes 1179656 | tf_op jit(solution)/shard_map/ppermute | solution.py:618
  288.6 22.9 %collective-permute-start.42 = (bf16[96,2048]{1,0:T(8,128)(2,1)S(1)}, bf16[96,2048]{1,0:T(8,128)(2,1)S(1)}, u32[]{:S(2)}, u32[]{:S(2)}) collective-permute-start(bf16[96,2048]{1,0:T(8,128)(2,1)S(1)} %dynamic-slice_bitcast_fusion.1.refs_0_), channel_id=1, source_target_pairs={{0,1},{1,0},{2,3},{3,2},{4,5},{5,4},{6,7},{7,6},{8,9},{9,8},{10,11... | collective-permute-start | bytes 1179656 | tf_op jit(solution)/shard_map/ppermute | solution.py:618
  296.2 15.3 %collective-permute-start.43 = (bf16[96,2048]{1,0:T(8,128)(2,1)S(1)}, bf16[96,2048]{1,0:T(8,128)(2,1)S(1)}, u32[]{:S(2)}, u32[]{:S(2)}) collective-permute-start(bf16[96,2048]{1,0:T(8,128)(2,1)S(1)} %collective-permute-done.35.refs_1_), channel_id=1, source_target_pairs={{0,1},{1,0},{2,3},{3,2},{4,5},{5,4},{6,7},{7,6},{8,9},{9,8},{10,11... | collective-permute-start | bytes 1179656 | tf_op jit(solution)/shard_map/ppermute | solution.py:618
  296.3 28.8 %collective-permute-start.36 = (bf16[96,2048]{1,0:T(8,128)(2,1)S(1)}, bf16[96,2048]{1,0:T(8,128)(2,1)S(1)}, u32[]{:S(2)}, u32[]{:S(2)}) collective-permute-start(bf16[96,2048]{1,0:T(8,128)(2,1)S(1)} %dynamic-slice_bitcast_fusion.refs_0_), channel_id=1, source_target_pairs={{0,2},{1,3},{2,0},{3,1},{4,6},{5,7},{6,4},{7,5},{8,10},{9,11},{10,... | collective-permute-start | bytes 1179656 | tf_op jit(solution)/shard_map/ppermute | solution.py:618
  344.8 17.7 %collective-permute-start.55 = (bf16[96,2048]{1,0:T(8,128)(2,1)}, bf16[96,2048]{1,0:T(8,128)(2,1)}, u32[]{:S(2)}, u32[]{:S(2)}) collective-permute-start(bf16[96,2048]{1,0:T(8,128)(2,1)} %add_convert_fusion.5), channel_id=1, source_target_pairs={{0,2},{1,3},{2,0},{3,1},{4,6},{5,7},{6,4},{7,5},{8,10},{9,11},{10,... | collective-permute-start | bytes 1179656 | tf_op jit(solution)/shard_map/ppermute | solution.py:618
  346.3 386.8 %reduce-scatter.4.cloned.1.call-start = ((), (), s32[]{:S(2)}) async-start(), calls=%async_computation.7 | async-start | bytes 7208960 | tf_op jit(solution)/shard_map/reduce_scatter | solution.py:800
  379.0 21.8 %collective-permute-start.57 = (bf16[96,2048]{1,0:T(8,128)(2,1)S(1)}, bf16[96,2048]{1,0:T(8,128)(2,1)S(1)}, u32[]{:S(2)}, u32[]{:S(2)}) collective-permute-start(bf16[96,2048]{1,0:T(8,128)(2,1)S(1)} %get-tuple-element.276.refs_0_), channel_id=1, source_target_pairs={{0,2},{1,3},{2,0},{3,1},{4,6},{5,7},{6,4},{7,5},{8,10},{9,11},{10,... | collective-permute-start | bytes 1179656 | tf_op jit(solution)/shard_map/ppermute | solution.py:618
  424.6 18.1 %collective-permute-start.68 = (bf16[96,2048]{1,0:T(8,128)(2,1)S(1)}, bf16[96,2048]{1,0:T(8,128)(2,1)S(1)}, u32[]{:S(2)}, u32[]{:S(2)}) collective-permute-start(bf16[96,2048]{1,0:T(8,128)(2,1)S(1)} %add_convert_fusion.3), channel_id=1, source_target_pairs={{0,2},{1,3},{2,0},{3,1},{4,6},{5,7},{6,4},{7,5},{8,10},{9,11},{10,... | collective-permute-start | bytes 1179656 | tf_op jit(solution)/shard_map/ppermute | solution.py:618
  445.1 14.2 %collective-permute-start.69 = (bf16[96,2048]{1,0:T(8,128)(2,1)}, bf16[96,2048]{1,0:T(8,128)(2,1)}, u32[]{:S(2)}, u32[]{:S(2)}) collective-permute-start(bf16[96,2048]{1,0:T(8,128)(2,1)} %get-tuple-element.428), channel_id=1, source_target_pairs={{16,0},{17,1},{18,2},{19,3},{20,4},{21,5},{22,6},{23,7},{24,8},{25... | collective-permute-start | bytes 1179656 | tf_op jit(solution)/shard_map/ppermute | solution.py:623
  449.3 17.0 %collective-permute-start.65 = (bf16[96,2048]{1,0:T(8,128)(2,1)S(1)}, bf16[96,2048]{1,0:T(8,128)(2,1)S(1)}, u32[]{:S(2)}, u32[]{:S(2)}) collective-permute-start(bf16[96,2048]{1,0:T(8,128)(2,1)S(1)} %copy-done.125), channel_id=1, source_target_pairs={{16,0},{17,1},{18,2},{19,3},{20,4},{21,5},{22,6},{23,7},{24,8},{25... | collective-permute-start | bytes 1179656 | tf_op jit(solution)/shard_map/ppermute | solution.py:623
  469.6 18.9 %collective-permute-start.74 = (bf16[96,2048]{1,0:T(8,128)(2,1)S(1)}, bf16[96,2048]{1,0:T(8,128)(2,1)S(1)}, u32[]{:S(2)}, u32[]{:S(2)}) collective-permute-start(bf16[96,2048]{1,0:T(8,128)(2,1)S(1)} %convert_element_type.392.refs_0_), channel_id=1, source_target_pairs={{0,1},{1,0},{2,3},{3,2},{4,5},{5,4},{6,7},{7,6},{8,9},{9,8},{10,11... | collective-permute-start | bytes 1179656 | tf_op jit(solution)/shard_map/ppermute | solution.py:618
  481.4 19.8 %collective-permute-start.82 = (bf16[2,96,512]{2,1,0:T(8,128)(2,1)S(1)}, bf16[2,96,512]{2,1,0:T(8,128)(2,1)S(1)}, u32[]{:S(2)}, u32[]{:S(2)}) collective-permute-start(bf16[2,96,512]{2,1,0:T(8,128)(2,1)S(1)} %get-tuple-element.421), channel_id=1, source_target_pairs={{0,4},{4,8},{8,12},{12,0},{1,5},{5,9},{9,13},{13,1},{2,6},{6,10},{... | collective-permute-start | bytes 589832 | tf_op jit(solution)/shard_map/ppermute | solution.py:693
  483.1 18.1 %collective-permute-start.83 = (bf16[2,96,512]{2,1,0:T(8,128)(2,1)S(1)}, bf16[2,96,512]{2,1,0:T(8,128)(2,1)S(1)}, u32[]{:S(2)}, u32[]{:S(2)}) collective-permute-start(bf16[2,96,512]{2,1,0:T(8,128)(2,1)S(1)} %get-tuple-element.422), channel_id=1, source_target_pairs={{0,8},{4,12},{8,0},{12,4},{1,9},{5,13},{9,1},{13,5},{2,10},{6,14},... | collective-permute-start | bytes 589832 | tf_op jit(solution)/shard_map/ppermute | solution.py:693
  485.7 15.5 %collective-permute-start.84 = (bf16[2,96,512]{2,1,0:T(8,128)(2,1)S(1)}, bf16[2,96,512]{2,1,0:T(8,128)(2,1)S(1)}, u32[]{:S(2)}, u32[]{:S(2)}) collective-permute-start(bf16[2,96,512]{2,1,0:T(8,128)(2,1)S(1)} %get-tuple-element.423), channel_id=1, source_target_pairs={{0,12},{4,0},{8,4},{12,8},{1,13},{5,1},{9,5},{13,9},{2,14},{6,2},{... | collective-permute-start | bytes 589832 | tf_op jit(solution)/shard_map/ppermute | solution.py:693
  488.5 14.5 %collective-permute-start.71 = (bf16[96,2048]{1,0:T(8,128)(2,1)S(1)}, bf16[96,2048]{1,0:T(8,128)(2,1)S(1)}, u32[]{:S(2)}, u32[]{:S(2)}) collective-permute-start(bf16[96,2048]{1,0:T(8,128)(2,1)S(1)} %convert_element_type.391.refs_0_), channel_id=1, source_target_pairs={{0,2},{1,3},{2,0},{3,1},{4,6},{5,7},{6,4},{7,5},{8,10},{9,11},{10,... | collective-permute-start | bytes 1179656 | tf_op jit(solution)/shard_map/ppermute | solution.py:618
  505.6 39.3 %collective-permute-start.78 = (bf16[96,2048]{1,0:T(8,128)(2,1)}, bf16[96,2048]{1,0:T(8,128)(2,1)}, u32[]{:S(2)}, u32[]{:S(2)}) collective-permute-start(bf16[96,2048]{1,0:T(8,128)(2,1)} %convert_add_fusion.10), channel_id=1, source_target_pairs={{0,2},{1,3},{2,0},{3,1},{4,6},{5,7},{6,4},{7,5},{8,10},{9,11},{10,... | collective-permute-start | bytes 1179656 | tf_op jit(solution)/shard_map/ppermute | solution.py:618
  521.8 19.7 %collective-permute-start.79 = (bf16[96,2048]{1,0:T(8,128)(2,1)}, bf16[96,2048]{1,0:T(8,128)(2,1)}, u32[]{:S(2)}, u32[]{:S(2)}) collective-permute-start(bf16[96,2048]{1,0:T(8,128)(2,1)} %get-tuple-element.303), channel_id=1, source_target_pairs={{0,1},{1,0},{2,3},{3,2},{4,5},{5,4},{6,7},{7,6},{8,9},{9,8},{10,11... | collective-permute-start | bytes 1179656 | tf_op jit(solution)/shard_map/ppermute | solution.py:618
  550.6 224.6 %reduce-scatter.6.cloned.1.call-start = ((), (), s32[]{:S(2)}) async-start(), calls=%async_computation.8 | async-start | bytes 7208960 | tf_op jit(solution)/shard_map/reduce_scatter | solution.py:800
  554.5 333.2 %reduce-scatter.8.cloned.1.call-start = ((), (), s32[]{:S(2)}) async-start(), calls=%async_computation.9 | async-start | bytes 7864320 | tf_op jit(solution)/shard_map/reduce_scatter | solution.py:800
  557.4 13.9 %collective-permute-start.101 = (bf16[2,96,512]{2,1,0:T(8,128)(2,1)S(1)}, bf16[2,96,512]{2,1,0:T(8,128)(2,1)S(1)}, u32[]{:S(2)}, u32[]{:S(2)}) collective-permute-start(bf16[2,96,512]{2,1,0:T(8,128)(2,1)S(1)} %get-tuple-element.413), channel_id=1, source_target_pairs={{0,4},{4,8},{8,12},{12,0},{1,5},{5,9},{9,13},{13,1},{2,6},{6,10},{... | collective-permute-start | bytes 589832 | tf_op jit(solution)/shard_map/ppermute | solution.py:693
  560.7 24.7 %collective-permute-start.85 = (bf16[96,2048]{1,0:T(8,128)(2,1)S(1)}, bf16[96,2048]{1,0:T(8,128)(2,1)S(1)}, u32[]{:S(2)}, u32[]{:S(2)}) collective-permute-start(bf16[96,2048]{1,0:T(8,128)(2,1)S(1)} %copy-done.35), channel_id=1, source_target_pairs={{0,2},{1,3},{2,0},{3,1},{4,6},{5,7},{6,4},{7,5},{8,10},{9,11},{10,... | collective-permute-start | bytes 1179656 | tf_op jit(solution)/shard_map/ppermute | solution.py:618
  561.5 56.7 %collective-permute-start.99 = (bf16[2,4,96,512]{3,2,0,1:T(8,128)(2,1)S(1)}, bf16[2,4,96,512]{3,2,0,1:T(8,128)(2,1)S(1)}, u32[]{:S(2)}, u32[]{:S(2)}) collective-permute-start(bf16[2,4,96,512]{3,2,0,1:T(8,128)(2,1)S(1)} %copy-done.109), channel_id=1, source_target_pairs={{0,1},{1,0},{2,3},{3,2},{4,5},{5,4},{6,7},{7,6},{8,9},{9,8},{10,11... | collective-permute-start | bytes 2359304 | tf_op jit(solution)/shard_map/ppermute | solution.py:618
  561.6 54.4 %collective-permute-start.98 = (bf16[2,4,96,512]{3,2,0,1:T(8,128)(2,1)S(1)}, bf16[2,4,96,512]{3,2,0,1:T(8,128)(2,1)}, u32[]{:S(2)}, u32[]{:S(2)}) collective-permute-start(bf16[2,4,96,512]{3,2,0,1:T(8,128)(2,1)S(1)} %copy-done.109), channel_id=1, source_target_pairs={{0,2},{1,3},{2,0},{3,1},{4,6},{5,7},{6,4},{7,5},{8,10},{9,11},{10,... | collective-permute-start | bytes 2359304 | tf_op jit(solution)/shard_map/ppermute | solution.py:618
  563.0 22.3 %collective-permute-start.102 = (bf16[2,96,512]{2,1,0:T(8,128)(2,1)S(1)}, bf16[2,96,512]{2,1,0:T(8,128)(2,1)S(1)}, u32[]{:S(2)}, u32[]{:S(2)}) collective-permute-start(bf16[2,96,512]{2,1,0:T(8,128)(2,1)S(1)} %get-tuple-element.414), channel_id=1, source_target_pairs={{0,8},{4,12},{8,0},{12,4},{1,9},{5,13},{9,1},{13,5},{2,10},{6,14},... | collective-permute-start | bytes 589832 | tf_op jit(solution)/shard_map/ppermute | solution.py:693
  571.3 22.5 %collective-permute-start.103 = (bf16[2,96,512]{2,1,0:T(8,128)(2,1)S(1)}, bf16[2,96,512]{2,1,0:T(8,128)(2,1)S(1)}, u32[]{:S(2)}, u32[]{:S(2)}) collective-permute-start(bf16[2,96,512]{2,1,0:T(8,128)(2,1)S(1)} %get-tuple-element.415), channel_id=1, source_target_pairs={{0,12},{4,0},{8,4},{12,8},{1,13},{5,1},{9,5},{13,9},{2,14},{6,2},{... | collective-permute-start | bytes 589832 | tf_op jit(solution)/shard_map/ppermute | solution.py:693
  595.1 34.5 %collective-permute-start.104 = (bf16[2,4,96,512]{3,2,0,1:T(8,128)(2,1)}, bf16[2,4,96,512]{3,2,0,1:T(8,128)(2,1)}, u32[]{:S(2)}, u32[]{:S(2)}) collective-permute-start(bf16[2,4,96,512]{3,2,0,1:T(8,128)(2,1)} %pad_maximum_fusion.5), channel_id=1, source_target_pairs={{0,2},{1,3},{2,0},{3,1},{4,6},{5,7},{6,4},{7,5},{8,10},{9,11},{10,... | collective-permute-start | bytes 2359304 | tf_op jit(solution)/shard_map/ppermute | solution.py:618
  615.6 90.4 %collective-permute-start.105 = (bf16[2,4,96,512]{3,2,0,1:T(8,128)(2,1)}, bf16[2,4,96,512]{3,2,0,1:T(8,128)(2,1)}, u32[]{:S(2)}, u32[]{:S(2)}) collective-permute-start(bf16[2,4,96,512]{3,2,0,1:T(8,128)(2,1)} %pad_maximum_fusion.5), channel_id=1, source_target_pairs={{0,1},{1,0},{2,3},{3,2},{4,5},{5,4},{6,7},{7,6},{8,9},{9,8},{10,11... | collective-permute-start | bytes 2359304 | tf_op jit(solution)/shard_map/ppermute | solution.py:618
  616.0 15.1 %collective-permute-start.89 = (bf16[96,2048]{1,0:T(8,128)(2,1)S(1)}, bf16[96,2048]{1,0:T(8,128)(2,1)S(1)}, u32[]{:S(2)}, u32[]{:S(2)}) collective-permute-start(bf16[96,2048]{1,0:T(8,128)(2,1)S(1)} %convert_element_type.404.refs_0_), channel_id=1, source_target_pairs={{0,1},{1,0},{2,3},{3,2},{4,5},{5,4},{6,7},{7,6},{8,9},{9,8},{10,11... | collective-permute-start | bytes 1179656 | tf_op jit(solution)/shard_map/ppermute | solution.py:618
  629.6 62.0 %collective-permute-start.100 = (bf16[2,4,96,512]{3,2,0,1:T(8,128)(2,1)}, bf16[2,4,96,512]{3,2,0,1:T(8,128)(2,1)}, u32[]{:S(2)}, u32[]{:S(2)}) collective-permute-start(bf16[2,4,96,512]{3,2,0,1:T(8,128)(2,1)} %collective-permute-done.98), channel_id=1, source_target_pairs={{0,1},{1,0},{2,3},{3,2},{4,5},{5,4},{6,7},{7,6},{8,9},{9,8},{10,11... | collective-permute-start | bytes 2359304 | tf_op jit(solution)/shard_map/ppermute | solution.py:618
  630.1 75.9 %collective-permute-start.106 = (bf16[2,4,96,512]{3,2,0,1:T(8,128)(2,1)}, bf16[2,4,96,512]{3,2,0,1:T(8,128)(2,1)}, u32[]{:S(2)}, u32[]{:S(2)}) collective-permute-start(bf16[2,4,96,512]{3,2,0,1:T(8,128)(2,1)} %collective-permute-done.104), channel_id=1, source_target_pairs={{0,1},{1,0},{2,3},{3,2},{4,5},{5,4},{6,7},{7,6},{8,9},{9,8},{10,11... | collective-permute-start | bytes 2359304 | tf_op jit(solution)/shard_map/ppermute | solution.py:618
  654.3 35.0 %collective-permute-start.95 = (bf16[96,2048]{1,0:T(8,128)(2,1)}, bf16[96,2048]{1,0:T(8,128)(2,1)}, u32[]{:S(2)}, u32[]{:S(2)}) collective-permute-start(bf16[96,2048]{1,0:T(8,128)(2,1)} %get-tuple-element.331), channel_id=1, source_target_pairs={{0,1},{1,0},{2,3},{3,2},{4,5},{5,4},{6,7},{7,6},{8,9},{9,8},{10,11... | collective-permute-start | bytes 1179656 | tf_op jit(solution)/shard_map/ppermute | solution.py:618
  658.5 18.0 %collective-permute-start.107 = (f32[14336]{0:T(1024)S(1)}, f32[14336]{0:T(1024)S(1)}, u32[]{:S(2)}, u32[]{:S(2)}) collective-permute-start(f32[14336]{0:T(1024)S(1)} %constant_dynamic-update-slice_fusion.9), channel_id=1, source_target_pairs={{0,4},{4,0},{8,12},{12,8},{1,5},{5,1},{9,13},{13,9},{2,6},{6,2},{1... | collective-permute-start | bytes 172040 | tf_op jit(solution)/shard_map/ppermute | solution.py:618
  687.4 20.8 %collective-permute-start.94 = (bf16[96,2048]{1,0:T(8,128)(2,1)}, bf16[96,2048]{1,0:T(8,128)(2,1)S(1)}, u32[]{:S(2)}, u32[]{:S(2)}) collective-permute-start(bf16[96,2048]{1,0:T(8,128)(2,1)} %copy-done.76), channel_id=1, source_target_pairs={{0,1},{1,0},{2,3},{3,2},{4,5},{5,4},{6,7},{7,6},{8,9},{9,8},{10,11... | collective-permute-start | bytes 1179656 | tf_op jit(solution)/shard_map/ppermute | solution.py:618
  689.3 20.6 %collective-permute-start.93 = (bf16[96,2048]{1,0:T(8,128)(2,1)}, bf16[96,2048]{1,0:T(8,128)(2,1)S(1)}, u32[]{:S(2)}, u32[]{:S(2)}) collective-permute-start(bf16[96,2048]{1,0:T(8,128)(2,1)} %convert_add_fusion.6), channel_id=1, source_target_pairs={{0,2},{1,3},{2,0},{3,1},{4,6},{5,7},{6,4},{7,5},{8,10},{9,11},{10,... | collective-permute-start | bytes 1179656 | tf_op jit(solution)/shard_map/ppermute | solution.py:618
  691.6 17.8 %collective-permute-start.96 = (bf16[96,2048]{1,0:T(8,128)(2,1)S(1)}, bf16[96,2048]{1,0:T(8,128)(2,1)S(1)}, u32[]{:S(2)}, u32[]{:S(2)}) collective-permute-start(bf16[96,2048]{1,0:T(8,128)(2,1)S(1)} %add_convert_fusion), channel_id=1, source_target_pairs={{0,2},{1,3},{2,0},{3,1},{4,6},{5,7},{6,4},{7,5},{8,10},{9,11},{10,... | collective-permute-start | bytes 1179656 | tf_op jit(solution)/shard_map/ppermute | solution.py:618
  (204 other events, 1754.2 us)
Sparse Core Ops, SparseCore 0:
  188.8 38.2 all-gather.8
  228.6 35.9 all-gather.10
  273.8 84.1 all-gather.6
  359.4 81.4 all-gather.4
  550.7 114.8 reduce-scatter.3
  668.4 106.7 reduce-scatter.5
  777.5 110.2 reduce-scatter.7

commit v7 on v6

--- a/solution.py
+++ b/solution.py
@@ -20,7 +20,8 @@
 LANES = 128
 TILE = 256
 QUARTERS = 4
-VMEM_LIMIT = 44 * 1024 * 1024
+ATTEND_KEPT = 9
+VMEM_LIMIT = 50 * 1024 * 1024
 
 
 def mm(left, right):
@@ -129,14 +130,37 @@
             self.wait(QUARTERS * group + place)
 
 
+class Push:
+
+    def __init__(self, sems):
+        self.sems = sems
+        self.copies = []
+
+    def start(self, source, target):
+        copy = pltpu.make_async_copy(source, target, self.sems.at[len(self.copies)])
+        copy.start()
+        self.copies.append(copy)
+
+    def wait(self):
+        for copy in self.copies:
+            copy.wait()
+
+
 def attend_kernel(heads, count, save, me_ref, seg_col_ref, seg_row_ref, masks_ref, taps_ref, gain_ref, *refs):
     shards, refs = refs[:count], refs[count:]
     project_hbm, beta_hbm, merge_hbm = refs[:3]
     partials, refs = refs[3 : 3 + count], refs[3 + count :]
-    rows_ref, qkv_ref, logit_ref, mixed_ref, refs = *refs[:4], refs[4:]
-    if save:
-        system_ref, attend_ref, inverse_ref, fresh_ref, out_ref, refs = *refs[:5], refs[5:]
-    mixed_abs, project_ref, beta_ref, merge_ref, sems = refs
+    targets, refs = (refs[:ATTEND_KEPT], refs[ATTEND_KEPT:]) if save else ([], refs)
+    kept_refs, refs = refs[:ATTEND_KEPT], refs[ATTEND_KEPT:]
+    rows_ref, qkv_ref, logit_ref, mixed_ref, system_ref, attend_ref, inverse_ref, fresh_ref, out_ref = kept_refs
+    mixed_abs, project_ref, beta_ref, merge_ref, sems, push_sems = refs
+    push = Push(push_sems)
+
+    def ready(*places):
+        if save:
+            for place in places:
+                push.start(kept_refs[place], targets[place])
+
     order = relative_order(count)
     share = TOK_MB // count
     fetch = Fetch(
@@ -148,6 +172,7 @@
     for k in range(count):
         rows_ref[k * share : (k + 1) * share, :] = shards[k][...]
     rows = rows_ref[...]
+    ready(0)
 
     def spread(ref, value, *lead):
         for k, difference in enumerate(order):
@@ -161,6 +186,7 @@
                 qkv_ref[j, place_of(me_ref, difference, share), cols] = value[k * share : (k + 1) * share]
     fetch.wait(3)
     spread(logit_ref, mm(rows, beta_ref[...]))
+    ready(1, 2)
 
     masks = [masks_ref[i] for i in range(CONV - 1)]
     strict, lower = block_masks(seg_col_ref, seg_row_ref)
@@ -198,6 +224,7 @@
         inverse[h, b] = inverse[h, b].astype(BF16)
         if save:
             inverse_ref[h, b] = inverse[h, b]
+    ready(4, 5, 6)
     fresh = {}
     for b in range(BLOCKS):
         for h in range(heads):
@@ -221,8 +248,10 @@
             ).astype(BF16)
     for k, difference in enumerate(order):
         mixed_ref[k * share : (k + 1) * share, :] = mixed_abs[place_of(me_ref, difference, share), :]
+    ready(3, 7, 8)
     fetch.wait(4)
     write_partials(partials, merge_ref.shape[1], share, lambda cols: mm(mixed_ref[...], merge_ref[:, cols]))
+    push.wait()
 
 
 def write_partials(partials, width, share, product):
@@ -237,18 +266,17 @@
     return [jax.ShapeDtypeStruct((share, width), F32 if k < count // 2 else BF16) for k in range(count)]
 
 
-def call(kernel, operands, hbm, out_shape, scratch_shapes):
+def call(kernel, operands, hbm, out_shape, hbm_shape, scratch_shapes):
     vmem = pl.BlockSpec(memory_space=pltpu.VMEM)
+    far = pl.BlockSpec(memory_space=pltpu.HBM)
     return pl.pallas_call(
         kernel,
-        in_specs=[pl.BlockSpec(memory_space=pltpu.SMEM)]
-        + [vmem] * (len(operands) - 1)
-        + [pl.BlockSpec(memory_space=pl.ANY)] * len(hbm),
-        out_specs=[vmem] * len(out_shape),
-        out_shape=out_shape,
+        in_specs=[pl.BlockSpec(memory_space=pltpu.SMEM)] + [vmem] * (len(operands) - 1) + [far] * len(hbm),
+        out_specs=[vmem] * len(out_shape) + [far] * len(hbm_shape),
+        out_shape=out_shape + hbm_shape,
         scratch_shapes=scratch_shapes,
         compiler_params=pltpu.CompilerParams(vmem_limit_bytes=VMEM_LIMIT),
-        cost_estimate=pl.CostEstimate(flops=10**6, bytes_accessed=10**5, transcendentals=0),
+        cost_estimate=pl.CostEstimate(flops=2 * 10**9, bytes_accessed=10**5, transcendentals=0),
     )(*operands, *hbm)
 
 
@@ -267,8 +295,6 @@
         jax.ShapeDtypeStruct((3, TOK_MB, width), F32),
         jax.ShapeDtypeStruct((TOK_MB, LANES), F32),
         jax.ShapeDtypeStruct((TOK_MB, width), BF16),
-    ]
-    more = [
         jax.ShapeDtypeStruct((heads, TOK_MB, TOK_MB), BF16),
         jax.ShapeDtypeStruct((heads, TOK_MB, TOK_MB), BF16),
         jax.ShapeDtypeStruct((heads, BLOCKS, BLOCK, BLOCK), BF16),
@@ -279,14 +305,16 @@
         functools.partial(attend_kernel, heads, count, save),
         (me, seg_col, seg_row, masks, taps, gain, *shards),
         (project, beta_weight, merge),
-        partial_shapes(count, model) + (kept + more if save else []),
-        ([] if save else as_scratch(kept))
+        partial_shapes(count, model),
+        kept if save else [],
+        as_scratch(kept)
         + [
             pltpu.VMEM((TOK_MB, width), BF16),
             pltpu.VMEM(project.shape[1:], BF16),
             pltpu.VMEM(beta_weight.shape, BF16),
             pltpu.VMEM(merge.shape[1:], BF16),
             pltpu.SemaphoreType.DMA((5,)),
+            pltpu.SemaphoreType.DMA((ATTEND_KEPT,)),
         ],
     )
     return results[count:], results[:count]
@@ -294,22 +322,27 @@
 
 def expand_kernel(count, save, me_ref, *refs):
     shards, refs = refs[:count], refs[count:]
-    expand_hbm, contract_hbm = refs[:2]
-    partials, refs = refs[2 : 2 + count], refs[2 + count :]
-    rows_ref, hidden_ref, refs = *refs[:2], refs[2:]
+    share = TOK_MB // count
     if save:
-        silu_ref, slope_ref, refs = *refs[:2], refs[2:]
-    gate_ref, expand_ref, contract_ref, sems = refs
-    share = TOK_MB // count
+        expand_hbm, *targets = refs[:5]
+        rows_ref, hidden_ref, silu_ref, slope_ref, gate_ref, expand_ref, sems, push_sems = refs[5:]
+        push = Push(push_sems)
+        contract_copies = []
+    else:
+        expand_hbm, contract_hbm, *partials = refs[: 2 + count]
+        rows_ref, hidden_ref, gate_ref, expand_ref, contract_ref, sems = refs[2 + count :]
+        contract_copies = [(contract_hbm.at[0, s, :], contract_ref.at[s, :]) for s in quarters(contract_ref.shape[0])]
     tiles = tiles_of(hidden_ref.shape[1])
     fetch = Fetch(
         [(expand_hbm.at[0, j, s, :], expand_ref.at[j, s, :]) for j in range(2) for s in quarters(expand_ref.shape[1])]
-        + [(contract_hbm.at[0, s, :], contract_ref.at[s, :]) for s in quarters(contract_ref.shape[0])],
+        + contract_copies,
         sems,
         QUARTERS,
     )
     for k in range(count):
         rows_ref[k * share : (k + 1) * share, :] = shards[k][...]
+    if save:
+        push.start(rows_ref, targets[0])
     fetch.wait_group(0)
     for t in tiles:
         gate_ref[:, t] = mm(rows_ref[...], expand_ref[0, :, t])
@@ -323,8 +356,13 @@
         if save:
             silu_ref[:, t] = silu.astype(BF16)
             slope_ref[:, t] = (up_in * gate * (1.0 + gate_in * (1.0 - gate))).astype(BF16)
-    fetch.wait_group(2)
-    write_partials(partials, rows_ref.shape[1], share, lambda cols: mm(hidden_ref[...], contract_ref[:, cols]))
+    if save:
+        for source, target in zip((hidden_ref, silu_ref, slope_ref), targets[1:]):
+            push.start(source, target)
+        push.wait()
+    else:
+        fetch.wait_group(2)
+        write_partials(partials, rows_ref.shape[1], share, lambda cols: mm(hidden_ref[...], contract_ref[:, cols]))
 
 
 def expand_forward(me, shards, expand, contract, save):
@@ -334,67 +372,85 @@
     results = call(
         functools.partial(expand_kernel, count, save),
         (me, *shards),
-        (expand, contract),
-        partial_shapes(count, model) + (kept if save else []),
-        ([] if save else as_scratch(kept[:2]))
-        + [
-            pltpu.VMEM((TOK_MB, units), F32),
-            pltpu.VMEM(expand.shape[1:], BF16),
-            pltpu.VMEM(contract.shape[1:], BF16),
-            pltpu.SemaphoreType.DMA((3 * QUARTERS,)),
-        ],
-    )
-    return results[count:], results[:count]
-
-
-def expand_back_kernel(count, me_ref, silu_ref, slope_ref, *refs):
+        (expand,) if save else (expand, contract),
+        [] if save else partial_shapes(count, model),
+        kept if save else [],
+        as_scratch(kept if save else kept[:2])
+        + [pltpu.VMEM((TOK_MB, units), F32), pltpu.VMEM(expand.shape[1:], BF16)]
+        + ([] if save else [pltpu.VMEM(contract.shape[1:], BF16)])
+        + [pltpu.SemaphoreType.DMA(((2 if save else 3) * QUARTERS,))]
+        + ([pltpu.SemaphoreType.DMA((4,))] if save else []),
+    )
+    return (results, None) if save else (None, results)
+
+
+def padded(units):
+    return -(-units // LANES) * LANES
+
+
+def expand_back_kernel(count, me_ref, *refs):
     shards, refs = refs[:count], refs[count:]
-    expand_hbm, contract_hbm, gate_ref, up_ref = refs[:4]
-    partials = refs[4 : 4 + count]
-    rows_ref, expand_ref, contract_ref, sems = refs[4 + count :]
+    silu_hbm, slope_hbm, expand_hbm, contract_hbm = refs[:4]
+    partials, refs = refs[4 : 4 + count], refs[4 + count :]
+    both_hbm, rows_ref, silu_ref, slope_ref, both_ref, expand_ref, contract_ref, sems, push_sems = refs
+    push = Push(push_sems)
     share = TOK_MB // count
-    tiles = tiles_of(gate_ref.shape[1])
+    units = silu_ref.shape[1]
+    second = padded(units)
     spans = tiles_of(rows_ref.shape[1], 2 * TILE)
     fetch = Fetch(
         [(contract_hbm.at[0, s, :], contract_ref.at[s, :]) for s in quarters(contract_ref.shape[0])]
+        + [(slope_hbm, slope_ref), (silu_hbm, silu_ref)]
         + [(expand_hbm.at[0, j, s, :], expand_ref.at[j, s, :]) for s in spans for j in range(2)],
         sems,
-        4,
+        QUARTERS + 2,
     )
     for k in range(count):
         rows_ref[k * share : (k + 1) * share, :] = shards[k][...]
+    if second > units:
+        both_ref[...] = jnp.zeros(both_ref.shape, BF16)
     fetch.wait_group(0)
-    for t in tiles:
+    fetch.wait(QUARTERS)
+    fetch.wait(QUARTERS + 1)
+    for t in tiles_of(units):
         grad_hidden = mm_t(rows_ref[...], contract_ref[t, :])
-        gate_ref[:, t] = (grad_hidden * slope_ref[:, t].astype(F32)).astype(BF16)
-        up_ref[:, t] = (grad_hidden * silu_ref[:, t].astype(F32)).astype(BF16)
+        both_ref[:, t] = (grad_hidden * slope_ref[:, t].astype(F32)).astype(BF16)
+        both_ref[:, second + t.start : second + t.stop] = (
+            grad_hidden * silu_ref[:, t].astype(F32)
+        ).astype(BF16)
+    push.start(both_ref, both_hbm)
     for i, span in enumerate(spans):
         for j in range(2):
-            fetch.wait(QUARTERS + 2 * i + j)
+            fetch.wait(QUARTERS + 2 + 2 * i + j)
         for s in tiles_of(span.stop - span.start):
             s = slice(span.start + s.start, span.start + s.stop)
-            value = mm_t(gate_ref[...], expand_ref[0, s, :]) + mm_t(up_ref[...], expand_ref[1, s, :])
+            value = mm_t(both_ref[:, :units], expand_ref[0, s, :])
+            value = value + mm_t(both_ref[:, second : second + units], expand_ref[1, s, :])
             for k, ref in enumerate(partials):
                 ref[:, s] = value[k * share : (k + 1) * share].astype(ref.dtype)
+    push.wait()
 
 
 def expand_backward(me, shards, silu, slope, expand, contract):
     count = len(shards)
     model, units = expand.shape[2:]
-    kept = jax.ShapeDtypeStruct((TOK_MB, units), BF16)
+    both = jax.ShapeDtypeStruct((TOK_MB, 2 * padded(units)), BF16)
     results = call(
         functools.partial(expand_back_kernel, count),
-        (me, silu, slope, *shards),
-        (expand, contract),
-        [kept, kept] + partial_shapes(count, model),
-        [
-            pltpu.VMEM((TOK_MB, model), BF16),
+        (me, *shards),
+        (silu, slope, expand, contract),
+        partial_shapes(count, model),
+        [both],
+        [pltpu.VMEM((TOK_MB, model), BF16)]
+        + as_scratch([silu, slope, both])
+        + [
             pltpu.VMEM(expand.shape[1:], BF16),
             pltpu.VMEM(contract.shape[1:], BF16),
-            pltpu.SemaphoreType.DMA((QUARTERS + 2 * len(tiles_of(model, 2 * TILE)),)),
+            pltpu.SemaphoreType.DMA((QUARTERS + 2 + 2 * len(tiles_of(model, 2 * TILE)),)),
+            pltpu.SemaphoreType.DMA((1,)),
         ],
     )
-    return results[:2], results[2:]
+    return results[count], results[:count]
 
 
 def stream_back(grad, x, pre, gate, taps, masks, taps_out, j, cols):
@@ -408,24 +464,29 @@
     return grad_x
 
 
-def attend_back_kernel(heads, count, me_ref, seg_col_ref, seg_row_ref, masks_ref, taps_ref, gain_ref,
-                       qkv_ref, logit_ref, system_ref, attend_ref, inverse_ref, fresh_ref, out_ref, *refs):
+def attend_back_kernel(heads, count, me_ref, seg_col_ref, seg_row_ref, masks_ref, taps_ref, gain_ref, *refs):
     shards, refs = refs[:count], refs[count:]
+    sources, refs = refs[: ATTEND_KEPT - 2], refs[ATTEND_KEPT - 2 :]
     project_hbm, beta_hbm, merge_hbm = refs[:3]
-    grad_qkv_ref, grad_logit_ref, grad_taps_ref, grad_gain_ref = refs[3:7]
-    partials = refs[7 : 7 + count]
-    rows_ref, grad_mixed_ref, grad_abs_ref, logit_abs_ref, project_ref, beta_ref, merge_ref, sems = refs[7 + count :]
+    partials, refs = refs[3 : 3 + count], refs[3 + count :]
+    grad_taps_ref, grad_gain_ref, grad_qkv_hbm, grad_logit_hbm = refs[:4]
+    kept_refs, refs = refs[4 : 2 + ATTEND_KEPT], refs[2 + ATTEND_KEPT :]
+    qkv_ref, logit_ref, system_ref, attend_ref, inverse_ref, fresh_ref, out_ref = kept_refs
+    rows_ref, grad_mixed_ref, grad_abs_ref, logit_abs_ref, grad_qkv_ref, grad_logit_ref, *refs = refs
+    project_ref, beta_ref, merge_ref, sems, push_sems = refs
+    push = Push(push_sems)
     order = relative_order(count)
     share = TOK_MB // count
     model = rows_ref.shape[1]
     width = heads * HEAD_DIM
     fetch = Fetch(
-        [(merge_hbm.at[0], merge_ref), (beta_hbm, beta_ref)]
+        [(merge_hbm.at[0], merge_ref)]
+        + list(zip(sources, kept_refs))
+        + [(beta_hbm, beta_ref)]
         + [(project_hbm.at[0, j], project_ref.at[j]) for j in range(3)],
         sems,
-        0,
-    )
-    fetch.start_to(5)
+        ATTEND_KEPT,
+    )
     for k in range(count):
         rows_ref[k * share : (k + 1) * share, :] = shards[k][...]
     fetch.wait(0)
@@ -434,6 +495,8 @@
         for k, difference in enumerate(order):
             grad_mixed_ref[place_of(me_ref, difference, share), cols] = value[k * share : (k + 1) * share]
 
+    for place in range(1, ATTEND_KEPT - 1):
+        fetch.wait(place)
     masks = [masks_ref[i] for i in range(CONV - 1)]
     strict, lower = block_masks(seg_col_ref, seg_row_ref)
     lane = lax.broadcasted_iota(jnp.int32, (TOK_MB, LANES), 1)
@@ -532,7 +595,9 @@
         grad_logit_ref[here, :] = logit_abs_ref[there, :]
         for j in range(3):
             grad_qkv_ref[here, j * width : (j + 1) * width] = grad_abs_ref[j, there, :]
-    for place in range(1, 5):
+    push.start(grad_qkv_ref, grad_qkv_hbm)
+    push.start(grad_logit_ref, grad_logit_hbm)
+    for place in range(ATTEND_KEPT - 1, ATTEND_KEPT + 3):
         fetch.wait(place)
     for span in tiles_of(model):
         value = mm_t(grad_logit_ref[...], beta_ref[span, :])
@@ -540,6 +605,7 @@
             value = value + mm_t(grad_qkv_ref[:, j * width : (j + 1) * width], project_ref[j, span, :])
         for k, ref in enumerate(partials):
             ref[:, span] = value[k * share : (k + 1) * share].astype(ref.dtype)
+    push.wait()
 
 
 def attend_backward(me, mine, shards, kept, taps, gain, project, beta_weight, merge):
@@ -548,30 +614,92 @@
     width = heads * HEAD_DIM
     model = merge.shape[2]
     count = len(shards)
-    _, qkv, logit, _, system, attend, inverse, fresh, out = kept
+    kept = kept[1:3] + kept[4:]
+    grads = [jax.ShapeDtypeStruct((TOK_MB, 3 * width), BF16), jax.ShapeDtypeStruct((TOK_MB, LANES), BF16)]
     results = call(
         functools.partial(attend_back_kernel, heads, count),
-        (me, seg_col, seg_row, masks, taps, gain, qkv, logit, system, attend, inverse, fresh, out, *shards),
-        (project, beta_weight, merge),
-        [
-            jax.ShapeDtypeStruct((TOK_MB, 3 * width), BF16),
-            jax.ShapeDtypeStruct((TOK_MB, LANES), BF16),
+        (me, seg_col, seg_row, masks, taps, gain, *shards),
+        (*kept, project, beta_weight, merge),
+        partial_shapes(count, model)
+        + [
             jax.ShapeDtypeStruct((3, CONV, width), F32),
             jax.ShapeDtypeStruct((8, HEAD_DIM), F32),
-        ]
-        + partial_shapes(count, model),
-        [
+        ],
+        grads,
+        as_scratch(kept)
+        + [
             pltpu.VMEM((TOK_MB, model), BF16),
             pltpu.VMEM((TOK_MB, width), F32),
             pltpu.VMEM((3, TOK_MB, width), BF16),
             pltpu.VMEM((TOK_MB, LANES), BF16),
+        ]
+        + as_scratch(grads)
+        + [
             pltpu.VMEM(project.shape[1:], BF16),
             pltpu.VMEM(beta_weight.shape, BF16),
             pltpu.VMEM(merge.shape[1:], BF16),
-            pltpu.SemaphoreType.DMA((5,)),
+            pltpu.SemaphoreType.DMA((ATTEND_KEPT + 3,)),
+            pltpu.SemaphoreType.DMA((2,)),
         ],
     )
-    return results[:4], results[4:]
+    return results[count + 2 :] + results[count : count + 2], results[:count]
+
+
+def small_call(kernel, operands, out_shape):
+    vmem = pl.BlockSpec(memory_space=pltpu.VMEM)
+    return pl.pallas_call(
+        kernel,
+        in_specs=[vmem] * len(operands),
+        out_specs=[vmem] * len(out_shape),
+        out_shape=out_shape,
+        compiler_params=pltpu.CompilerParams(vmem_limit_bytes=16 * 1024 * 1024),
+        cost_estimate=pl.CostEstimate(flops=10**9, bytes_accessed=10**5, transcendentals=0),
+    )(*operands)
+
+
+def norm_kernel(gain_ref, x_ref, *refs):
+    *more, total_ref, normed_ref = refs
+    total = x_ref[...].astype(F32)
+    for ref in more:
+        total = total + ref[...].astype(F32)
+    scale = lax.rsqrt(jnp.mean(total * total, axis=-1, keepdims=True) + EPS)
+    total_ref[...] = total
+    normed_ref[...] = (total * scale * gain_ref[...]).astype(BF16)
+
+
+def norm_of_sum(gain, *terms):
+    shape = terms[0].shape
+    return small_call(
+        norm_kernel, (gain, *terms), [jax.ShapeDtypeStruct(shape, F32), jax.ShapeDtypeStruct(shape, BF16)]
+    )
+
+
+def norm_back_kernel(gain_ref, base_ref, x_ref, near_ref, far_ref, grad_ref, narrow_ref, gain_out):
+    grad_normed = near_ref[...].astype(F32) + far_ref[...].astype(F32)
+    x = x_ref[...].astype(F32)
+    scale = lax.rsqrt(jnp.mean(x * x, axis=-1, keepdims=True) + EPS)
+    unit = x * scale
+    grad_scaled = grad_normed * gain_ref[...]
+    grad = base_ref[...].astype(F32) + scale * (
+        grad_scaled - unit * jnp.mean(grad_scaled * unit, axis=-1, keepdims=True)
+    )
+    grad_ref[...] = grad
+    narrow_ref[...] = grad.astype(BF16)
+    rows, width = x.shape
+    gain_out[...] = jnp.sum((grad_normed * unit).reshape(rows // 8, 8, width), axis=0)
+
+
+def norm_backward(gain, base, x, near, far):
+    shape = x.shape
+    return small_call(
+        norm_back_kernel,
+        (gain, base, x, near, far),
+        [
+            jax.ShapeDtypeStruct(shape, F32),
+            jax.ShapeDtypeStruct(shape, BF16),
+            jax.ShapeDtypeStruct((8, shape[1]), F32),
+        ],
+    )
 
 
 def tap_masks(segment):
@@ -598,16 +726,6 @@
     return lax.dot_general(left, right, (((1,), (1,)), ((), ())), preferred_element_type=F32)
 
 
-def rms_parts(values):
-    scale = lax.rsqrt(jnp.mean(values * values, axis=-1, keepdims=True) + EPS)
-    return (values * scale, scale)
-
-
-def norm_back(grad_normed, normed, scale, gain):
-    grad_scaled = grad_normed * gain
-    return scale * (grad_scaled - normed * jnp.mean(grad_scaled * normed, axis=-1, keepdims=True))
-
-
 def segment_ids(lengths, count):
     ends = jnp.cumsum(lengths)
     places = jnp.arange(count, dtype=jnp.int32)
@@ -637,11 +755,33 @@
     return values
 
 
-def gather(shard):
+class Order:
+
+    def __init__(self):
+        self.last = None
+
+    def flipped(self, values, bit):
+        if bit > 1:
+            if self.last is not None:
+                values, _ = lax.optimization_barrier((values, self.last))
+            self.last = flipped(values, "head", bit)
+            return self.last
+        return flipped(values, "head", bit)
+
+
+def gather_far(shard, order):
     parts = [shard]
-    for bit in reversed(bits_of("head")):
-        parts = parts + [flipped(part, "head", bit) for part in parts]
+    for bit in reversed(bits_of("head")[1:]):
+        parts = parts + [order.flipped(part, bit) for part in parts]
     return parts
+
+
+def gather_near(parts):
+    return parts + [flipped(part, "head", 1) for part in parts]
+
+
+def gather(shard, order):
+    return gather_near(gather_far(shard, order))
 
 
 def added(parts, arrived):
@@ -653,32 +793,64 @@
     return added(parts[:half], [flipped(part, "head", 1) for part in parts[half:]])
 
 
-def scatter_far(parts):
+def scatter_far(parts, order):
     for bit in bits_of("head")[1:]:
         half = len(parts) // 2
-        parts = added(parts[:half], [flipped(narrow(part), "head", bit) for part in parts[half:]])
-    return parts[0]
-
-
-def in_turn(kernel, shards):
-    results, near = [], None
-    for parts in shards:
+        arrived = [order.flipped(narrow(part), bit) for part in parts[half:]]
+        if half == 1:
+            return parts[0], arrived[0]
+        parts = added(parts[:half], arrived)
+
+
+def after(values, earlier):
+    return lax.optimization_barrier((values, earlier))[0]
+
+
+def together(*values):
+    return lax.optimization_barrier(values)
+
+
+def in_turn(kernel, order, shards=None, rows=None, finish=None):
+    if rows is None:
+        fars = [gather_far(shard, order) for shard in shards]
+    kept, sums, near = [], [], None
+    for m in range(len(rows or fars)):
+        parts = gather_near(fars[m]) if rows is None else rows[m]
         if near is not None:
-            (parts, near) = lax.optimization_barrier((parts, near))
-            results[-1] = (results[-1][0], near)
-        kept, partials = kernel(len(results), parts)
-        near = scatter_near(partials)
-        results.append((kept, near))
-    return [kept for kept, _ in results], [scatter_far(near) for _, near in results]
-
-
-def gather_in_turn(shards):
-    gathered = []
-    for shard in shards:
-        if gathered:
-            shard, gathered[-1][1] = lax.optimization_barrier((shard, gathered[-1][1]))
-        gathered.append(gather(shard))
-    return gathered
+            parts, near = together(parts, near)
+            sums.append(scatter_far(near, order))
+        keep, partials = kernel(m, parts)
+        if sums:
+            partials = after(partials, sums[-1][1])
+        if rows is None and m + 1 < len(fars):
+            fars[m + 1], keep, partials = together(fars[m + 1], keep, partials)
+        kept.append(keep)
+        if finish is not None and m + 1 == len(rows or fars):
+            kept = finish(kept)
+            partials = after(partials, kept)
+        if partials is not None:
+            near = scatter_near(partials)
+    if near is not None:
+        sums.append(scatter_far(near, order))
+    return kept, sums
+
+
+def in_order(sums, finish):
+    results = []
+    for m, (near, far) in enumerate(sums):
+        if results:
+            far, results[-1] = together(far, results[-1])
+        results.append(finish(m, near, far))
+    return results
+
+
+def sent(distance, sums, finish):
+    arrived = []
+    for m, (near, far) in enumerate(sums):
+        if arrived:
+            far = after(far, arrived[-1])
+        arrived.append(shifted(finish(m, near, far), "section", distance))
+    return arrived
 
 
 def swapped(shards):
@@ -723,75 +895,88 @@
     every = range(micro)
     segments = [segment_ids(lengths[m], TOK_MB) for m in every]
     masks = [(tap_masks(s), s[:, None], s[None, :]) for s in segments]
-    own_rows = lambda values: lax.dynamic_slice_in_dim(values, member * share, share, 0).astype(F32)
-    tokens_own = [own_rows(tokens[m]) for m in every]
-    cotangent_own = [own_rows(cotangent[m]) for m in every]
-
-    def forward_turn(inputs, save):
-        parts = [rms_parts(x) for x in inputs]
-        normed = gather_in_turn([narrow(unit * gains[0]) for unit, _ in parts])
+    order = Order()
+    relative = relative_order(lax.axis_size("head"))
+
+    def blocks(values):
+        return [lax.dynamic_slice_in_dim(values, (member ^ k) * share, share, 0) for k in relative]
+
+    tokens_own = [blocks(tokens[m])[0] for m in every]
+    cotangent_own = [blocks(cotangent[m])[0] for m in every]
+    gain_in, gain_mid = gains[0:1], gains[1:2]
+
+    def forward_turn(inputs, save, shards=None, rows=None):
         kept, sums = in_turn(
             lambda m, rows: attend_forward(
                 me, masks[m], rows, conv_weight, o_gain, attn_in, beta_wide, attn_out, save
             ),
-            normed,
+            order,
+            shards,
+            rows,
         )
-        middles = [x + total for x, total in zip(inputs, sums)]
-        parts_mid = [rms_parts(middle) for middle in middles]
-        normed_mid = [gather(narrow(unit * gains[1])) for unit, _ in parts_mid]
-        kept_mid, sums = in_turn(lambda m, rows: expand_forward(me, rows, mlp_in, mlp_out, save), normed_mid)
-        outputs = [middle + total for middle, total in zip(middles, sums)]
-        return outputs, (parts, kept, parts_mid, kept_mid)
-
-    def backward_expand(incoming, saved):
-        _, _, parts_mid, kept_mid = saved
+        middles = in_order(sums, lambda m, near, far: norm_of_sum(gain_mid, inputs[m], near, far))
+        kept_mid, sums = in_turn(
+            lambda m, rows: expand_forward(me, rows, mlp_in, mlp_out, save),
+            order,
+            [values[1] for values in middles],
+        )
+        if save:
+            return kept, [values[0] for values in middles], kept_mid
+        return sent(1, sums, lambda m, near, far: narrow(middles[m][0] + near + far.astype(F32)))
+
+    def backward_expand(incoming, slopes, shards=None, rows=None, finish=None):
         grads, sums = in_turn(
-            lambda m, rows: expand_backward(me, rows, *kept_mid[m][2:], mlp_in, mlp_out),
-            gather_in_turn([narrow(value) for value in incoming]),
+            lambda m, rows: expand_backward(me, rows, *slopes[m], mlp_in, mlp_out), order, shards, rows, finish
         )
-        middles = [value + norm_back(sums[m], *parts_mid[m], gains[1]) for m, value in enumerate(incoming)]
-        return middles, grads, sum(jnp.sum(sums[m] * parts_mid[m][0], axis=0) for m in every)
-
-    def backward_attend(middles, saved):
-        parts, kept, _, _ = saved
-        grads, sums = in_turn(
+        return grads, in_order(sums, lambda m, *terms: norm_backward(gain_mid, incoming[m], middles[m], *terms))
+
+    def backward_attend(grad_middles):
+        return in_turn(
             lambda m, rows: attend_backward(
                 me, masks[m], rows, kept[m], conv_weight, o_gain, attn_in, beta_wide, attn_out
             ),
-            gather_in_turn([narrow(value) for value in middles]),
+            order,
+            [values[1] for values in grad_middles],
         )
-        finals = [value + norm_back(sums[m], *parts[m], gains[0]) for m, value in enumerate(middles)]
-        return finals, grads, sum(jnp.sum(sums[m] * parts[m][0], axis=0) for m in every)
 
     def all_rows(values):
         return jnp.concatenate(values, axis=0)
 
     last = sections - 1
     inputs = tokens_own
-    for turn in range(sections):
-        outputs, saved = forward_turn(inputs, turn == last)
-        if turn < last:
-            arrived = [shifted(narrow(value), "section", 1).astype(F32) for value in outputs]
-            inputs = [jnp.where(section == 0, tokens_own[m], arrived[m]) for m in every]
-
-    hidden_rows = [lax.all_gather(values[1], "dp", axis=0, tiled=True) for values in saved[3]]
-    mixed_rows = [lax.all_gather(values[3], "dp", axis=0, tiled=True) for values in saved[1]]
-
+    normed_own, normed = None, [blocks(norm_of_sum(gain_in, tokens[m])[1]) for m in every]
+    for turn in range(last):
+        arrived = forward_turn(inputs, False, normed_own, normed)
+        inputs = [jnp.where(section == 0, tokens_own[m], arrived[m]) for m in every]
+        normed_own = [norm_of_sum(gain_in, value)[1] for value in inputs]
+        normed = None
+    kept, middles, kept_mid = forward_turn(inputs, True, normed_own, normed)
+
+    hidden_rows = [lax.all_gather(values[1], "dp", axis=0, tiled=True) for values in kept_mid]
+    mixed_rows = [lax.all_gather(values[3], "dp", axis=0, tiled=True) for values in kept]
+
+    slopes = [values[2:] for values in kept_mid]
     incoming = cotangent_own
-    for turn in range(sections):
-        if turn == last:
-            incoming, hidden_rows, mixed_rows = lax.optimization_barrier((incoming, hidden_rows, mixed_rows))
-        middles, grads, gain_two = backward_expand(incoming, saved)
-        if turn == last:
-            swapped_out = swapped([narrow(value) for value in incoming])
-            normed_mid = all_rows([values[0] for values in saved[3]])
-            expands = [narrow(product_left(normed_mid, all_rows([grad[j] for grad in grads]))) for j in range(2)]
-            middles, expands, swapped_out = lax.optimization_barrier((middles, expands, swapped_out))
-        finals, grads, gain_one = backward_attend(middles, saved)
-        if turn < last:
-            arrived = [shifted(narrow(value), "section", -1).astype(F32) for value in finals]
-            incoming = [jnp.where(section == last, cotangent_own[m], arrived[m]) for m in every]
-    rows_out = jnp.stack(finals)
+    rows = [blocks(cotangent[m]) for m in every]
+    for turn in range(last):
+        _, grad_middles = backward_expand(incoming, slopes, incoming, rows)
+        _, sums = backward_attend(grad_middles)
+        arrived = sent(
+            -1, sums, lambda m, *terms: norm_backward(gain_in, grad_middles[m][0], inputs[m], *terms)[1]
+        )
+        incoming = [jnp.where(section == last, cotangent_own[m], arrived[m]) for m in every]
+        rows = None
+    normed_mid = all_rows([values[0] for values in kept_mid])
+    slopes[-1], hidden_rows, mixed_rows = together(slopes[-1], hidden_rows, mixed_rows)
+    expands, grad_middles = backward_expand(
+        incoming, slopes, incoming, rows, lambda grads: narrow(product_left(normed_mid, all_rows(grads)))
+    )
+    grads, sums = backward_attend(grad_middles)
+    finals = [norm_backward(gain_in, grad_middles[m][0], inputs[m], *sums[m]) for m in every]
+    gain_one, gain_two = (
+        sum(jnp.sum(values[2], axis=0) for values in group) for group in (finals, grad_middles)
+    )
+    rows_out = jnp.stack([values[0] for values in finals])
     half = width // sections
     moved = shifted(narrow(rows_out[:, :, half:]), "section", 1).astype(F32)
     grad_tokens = jnp.where(section == 0, rows_out[:, :, :half], moved)
@@ -799,22 +984,18 @@
     def spread(value, axis):
         return lax.psum_scatter(value, "dp", scatter_dimension=axis, tiled=True)
 
-    early = [spread(part, 0) for part in expands]
-    normed = all_rows([values[0] for values in saved[1]])
+    early = spread(expands, 0)
+    normed = all_rows([values[0] for values in kept])
     grad_project = narrow(product_left(normed, all_rows([grad[0] for grad in grads])))
     grad_beta = product_left(normed, all_rows([grad[1] for grad in grads]))[:, :heads]
     grad_taps, grad_head_gain = (sum(grad[place] for grad in grads) for place in (2, 3))
     grad_head_gain = jnp.sum(grad_head_gain, axis=0)
 
-    def from_rows(rows, columns):
-        total = 0.0
-        columns = jnp.concatenate(gather(columns), axis=2)
-        for left, right in zip(rows, columns):
-            total = total + product_left(left, right.reshape(left.shape[0], -1))
-        return total
-
-    grad_contract = from_rows(hidden_rows, swapped_out)
-    grad_merge = from_rows(mixed_rows, swapped([narrow(value) for value in middles]))
+    columns = swapped(after(incoming, expands) + [values[1] for values in grad_middles])
+    columns = jnp.concatenate(gather(columns, order), axis=2)
+    columns = [part.reshape(-1, part.shape[-1]) for part in columns]
+    grad_contract = sum(product_left(left, right) for left, right in zip(hidden_rows, columns[:micro]))
+    grad_merge = sum(product_left(left, right) for left, right in zip(mixed_rows, columns[micro:]))
     flat = jnp.concatenate([gain_one, gain_two, grad_head_gain])
     flat = summed(flat, ("dp", "head"))
     grad_gains, grad_head_gain = flat[: 2 * width].reshape(2, width), flat[2 * width :]
@@ -825,7 +1006,8 @@
     done = (grad_tokens, grad_contract, grad_merge, grad_beta, grad_taps, grad_head_gain, grad_gains, early)
     grad_project, done = lax.optimization_barrier((grad_project, done))
     grad_tokens, grad_contract, grad_merge, grad_beta, grad_taps, grad_head_gain, grad_gains, early = done
-    grad_expand = jnp.stack(early).astype(F32)
+    units = mlp_in.shape[3]
+    grad_expand = jnp.stack([part[:, :units] for part in jnp.split(early, 2, axis=1)]).astype(F32)
     grad_project = jnp.stack(jnp.split(spread(grad_project, 0), 3, axis=1)).astype(F32)
     return (
         grad_tokens,

time: 907 us -> 790 us (0.87)
  waiting for transfers between devices: 400 us -> 292 us
  other arithmetic: 71 us -> 35.9 us
  Pallas kernels: 223 us -> 242 us
    ppermute x102 -> x87, waiting for transfers between devices: 206 us -> 114 us  [flipped(): lax.ppermute(values, axis, [(i, i ^ bit) for i in range(lax.axis_size(axi...]
    reduce_scatter x3 -> x2, waiting for transfers between devices: 150 us -> 116 us  [spread(): return lax.psum_scatter(value, 'dp', scatter_dimension=axis, tiled=True)]
    reduce_sum x13 -> x4, other arithmetic: 19.3 us -> 0.08 us  [per_device(): jnp.sum(values[2], axis=0)]
    ppermute x102 -> x87, starting transfers between devices: 60.3 us -> 77.9 us  [flipped(): lax.ppermute(values, axis, [(i, i ^ bit) for i in range(lax.axis_size(axi...]
    pallas_call x0 -> x16, Pallas kernels: none -> 16.8 us  [small_call(): pl.pallas_call(kernel, in_specs=[vmem] * len(operands), out_specs=[vmem]...]
    convert_element_type x19 -> x9, other arithmetic: 19.4 us -> 7.4 us  [narrow(): return values.astype(BF16)]
    ppermute x6 -> x3, starting transfers between devices: 15.6 us -> 3.9 us  [swapped(): lax.ppermute(block, 'dp', [(i, (i + distance) % count) for i in range(cou...]
    all_gather x2, waiting for transfers between devices: 0.01 us -> 11.4 us  [per_device(): lax.all_gather(values[1], 'dp', axis=0, tiled=True)]
  transfers between devices with their start and end apart: 120 -> 101, of which waited for: 55 -> 38; matrix products, arithmetic and copies ran while one was open for 13% -> 9% of each run, Pallas kernels for 21% -> 28%
where the time goes in v7:
time: 790 us; the launch traced here: 781 us
  waiting for transfers between devices  292 us (37%)
  Pallas kernels  242 us (31%)
  starting transfers between devices  96.4 us (12%)
  local copies, waits for them, and re-layouts  62.4 us (8%)
  other arithmetic  35.9 us (5%)
  matrix products  35.3 us (4%)
  between operations  16.3 us (2%)
    pallas_call x16, Pallas kernels, call(): pl.pallas_call(kernel, in_specs=[pl.BlockSpec(memory_space=pltpu.SMEM)] +...  225 us
    reduce_scatter x2, waiting for transfers between devices, spread(): return lax.psum_scatter(value, 'dp', scatter_dimension=axis, tiled=True)  116 us
    ppermute x87, waiting for transfers between devices, flipped(): lax.ppermute(values, axis, [(i, i ^ bit) for i in range(lax.axis_size(axi...  114 us
    ppermute x87, starting transfers between devices, flipped(): lax.ppermute(values, axis, [(i, i ^ bit) for i in range(lax.axis_size(axi...  77.9 us
    unnamed x227, local copies, waits for them, and re-layouts  39.7 us
    dot_general x7, matrix products, product_left(): lax.dot_general(left, right, (((0,), (0,)), ((), ())), preferred_element_...  35.3 us
    ppermute x3, waiting for transfers between devices, swapped(): lax.ppermute(block, 'dp', [(i, (i + distance) % count) for i in range(cou...  27.2 us
    ppermute x5, waiting for transfers between devices, shifted(): lax.ppermute(values, axis, [(i, i + distance) for i in devices if i + dis...  23.7 us
  transfers between devices with their start and end apart: 101, of which 38 were waited for; matrix products, arithmetic and copies ran while one was open for 9% of the time, Pallas kernels for 28%

profile of v7, /device:TPU:0, one launch (start us, length us, event | category | flops | bytes accessed | tf_op | source)
XLA Modules:
  0.0 780.6 jit_solution(9004740962034839363)
XLA Ops:
  9.4 4.4 fusion.28
  18.3 12.0 %shard_map.180 = (f32[96,2048]{1,0:T(8,128)}, f32[96,2048]{1,0:T(8,128)}, bf16[96,2048]{1,0:T(8,128)(2,1)S(1)}, bf16[96,2048]{1,0:T(8,128)(2,1)S(1)}) custom-call(s32[1]{0:T(128)} %bitcast.3.me_ref, s32[384,1]{1,0:T(8,128)S(1)} %broadcast_in_dim.57.seg_col_ref, s32[1,384]{1,0:T(1,128)S(1)} %broadcast_in_dim.49.seg_row_ref, ...), custom_call_target="tpu_custom_call" | custom-call | flops 2000000000 | bytes 100000 | tf_op jit(solution)/shard_map/pallas_call | solution.py:272
  34.4 3.0 collective-permute-start.2
  38.0 12.2 %shard_map.181 = (f32[96,2048]{1,0:T(8,128)}, f32[96,2048]{1,0:T(8,128)}, bf16[96,2048]{1,0:T(8,128)(2,1)S(1)}, bf16[96,2048]{1,0:T(8,128)(2,1)S(1)}) custom-call(s32[1]{0:T(128)} %bitcast.3.me_ref, s32[384,1]{1,0:T(8,128)S(1)} %broadcast_in_dim.56.seg_col_ref, s32[1,384]{1,0:T(1,128)S(1)} %broadcast_in_dim.47.seg_row_ref, ...), custom_call_target="tpu_custom_call" | custom-call | flops 2000000000 | bytes 100000 | tf_op jit(solution)/shard_map/pallas_call | solution.py:272
  54.7 9.8 %collective-permute-done.5.refs_1_ = bf16[96,2048]{1,0:T(8,128)(2,1)S(1)} collective-permute-done((bf16[96,2048]{1,0:T(8,128)(2,1)S(1)}, bf16[96,2048]{1,0:T(8,128)(2,1)S(1)}, u32[]{:S(2)}, u32[]{:S(2)}) %collective-permute-start.5) | collective-permute-done | bytes 393248 | tf_op jit(solution)/shard_map/ppermute | solution.py:736
  66.3 8.4 %collective-permute-done.6.refs_1_ = bf16[96,2048]{1,0:T(8,128)(2,1)S(1)} collective-permute-done((bf16[96,2048]{1,0:T(8,128)(2,1)S(1)}, bf16[96,2048]{1,0:T(8,128)(2,1)S(1)}, u32[]{:S(2)}, u32[]{:S(2)}) %collective-permute-start.6) | collective-permute-done | bytes 393248 | tf_op jit(solution)/shard_map/ppermute | solution.py:736
  76.5 11.1 %shard_map.184 = (f32[96,2048]{1,0:T(8,128)S(1)}, f32[96,2048]{1,0:T(8,128)S(1)}, bf16[96,2048]{1,0:T(8,128)(2,1)S(1)}, bf16[96,2048]{1,0:T(8,128)(2,1)S(1)}) custom-call(s32[1]{0:T(128)} %bitcast.3.me_ref, bf16[96,2048]{1,0:T(8,128)(2,1)S(1)} %get-tuple-element.338.refs_0_, bf16[96,2048]{1,0:T(8,128)(2,1)S(1)} %collective-permute-done.6.refs_1_, ...), custom_call_target="tpu_custom_call" | custom-call | flops 2000000000 | bytes 100000 | tf_op jit(solution)/shard_map/pallas_call | solution.py:272
  93.7 10.7 %shard_map.185 = (f32[96,2048]{1,0:T(8,128)S(1)}, f32[96,2048]{1,0:T(8,128)S(1)}, bf16[96,2048]{1,0:T(8,128)(2,1)S(1)}, bf16[96,2048]{1,0:T(8,128)(2,1)S(1)}) custom-call(s32[1]{0:T(128)} %bitcast.3.me_ref, bf16[96,2048]{1,0:T(8,128)(2,1)S(1)} %get-tuple-element.350.refs_0_, bf16[96,2048]{1,0:T(8,128)(2,1)S(1)} %collective-permute-done.7.refs_1_, ...), custom_call_target="tpu_custom_call" | custom-call | flops 2000000000 | bytes 100000 | tf_op jit(solution)/shard_map/pallas_call | solution.py:272
  105.6 3.4 collective-permute-start.18
  110.8 7.3 collective-permute-done.18
  122.3 3.7 collective-permute-start.19
  126.1 5.3 collective-permute-done.20.refs_1_
  136.9 16.4 %shard_map.188 = (f32[96,2048]{1,0:T(8,128)}, f32[96,2048]{1,0:T(8,128)}, bf16[96,2048]{1,0:T(8,128)(2,1)S(1)}, bf16[96,2048]{1,0:T(8,128)(2,1)}, bf16[384,2048]...) custom-call(s32[1]{0:T(128)} %bitcast.3.me_ref, ...), custom_call_target="tpu_custom_call" | custom-call | flops 2000000000 | bytes 100000 | tf_op jit(solution)/shard_map/pallas_call | solution.py:272
  159.7 16.6 %shard_map.189 = (f32[96,2048]{1,0:T(8,128)}, f32[96,2048]{1,0:T(8,128)}, bf16[96,2048]{1,0:T(8,128)(2,1)S(1)}, bf16[96,2048]{1,0:T(8,128)(2,1)}, bf16[384,2048]...) custom-call(s32[1]{0:T(128)} %bitcast.3.me_ref, ...), custom_call_target="tpu_custom_call" | custom-call | flops 2000000000 | bytes 100000 | tf_op jit(solution)/shard_map/pallas_call | solution.py:272
  184.1 9.2 %collective-permute-done.31.refs_1_ = bf16[96,2048]{1,0:T(8,128)(2,1)S(1)} collective-permute-done((bf16[96,2048]{1,0:T(8,128)(2,1)S(1)}, bf16[96,2048]{1,0:T(8,128)(2,1)S(1)}, u32[]{:S(2)}, u32[]{:S(2)}) %collective-permute-start.31) | collective-permute-done | bytes 393248 | tf_op jit(solution)/shard_map/ppermute | solution.py:736
  194.5 9.1 %collective-permute-done.32.refs_1_ = bf16[96,2048]{1,0:T(8,128)(2,1)S(1)} collective-permute-done((bf16[96,2048]{1,0:T(8,128)(2,1)S(1)}, bf16[96,2048]{1,0:T(8,128)(2,1)S(1)}, u32[]{:S(2)}, u32[]{:S(2)}) %collective-permute-start.32) | collective-permute-done | bytes 393248 | tf_op jit(solution)/shard_map/ppermute | solution.py:736
  205.8 10.4 %shard_map.192 = (bf16[384,2048]{1,0:T(8,128)(2,1)}, bf16[384,1408]{1,0:T(8,128)(2,1)}, bf16[384,1408]{1,0:T(8,128)(2,1)S(1)}, bf16[384,1408]{1,0:T(8,128)(2,1)}) custom-call(s32[1]{0:T(128)} %bitcast.3.me_ref, bf16[96,2048]{1,0:T(8,128)(2,1)S(1)} %get-tuple-element.415.refs_0_, bf16[96,2048]{1,0:T(8,128)(2,1)S(1)} %collective-permute-done.32.refs_1_, ...), custom_call_target="tpu_custom_call" | custom-call | flops 2000000000 | bytes 100000 | tf_op jit(solution)/shard_map/pallas_call | solution.py:272
  221.0 11.8 %shard_map.193 = (f32[96,2048]{1,0:T(8,128)S(1)}, f32[96,2048]{1,0:T(8,128)S(1)}, bf16[96,2048]{1,0:T(8,128)(2,1)S(1)}, bf16[96,2048]{1,0:T(8,128)(2,1)S(1)}, bf16[384,2816]{1,0:T(8,128)(2,1)}) custom-call(s32[1]{0:T(128)} %bitcast.3.me_ref, bf16[96,2048]{1,0:T(8,128)(2,1)S(1)} %get-tuple-element.657.refs_0_.base_ref, ...), custom_call_target="tpu_custom_call" | custom-call | flops 2000000000 | bytes 100000 | tf_op jit(solution)/shard_map/pallas_call | solution.py:272
  236.6 10.8 %shard_map.194 = (bf16[384,2048]{1,0:T(8,128)(2,1)}, bf16[384,1408]{1,0:T(8,128)(2,1)S(1)}, bf16[384,1408]{1,0:T(8,128)(2,1)S(1)}, bf16[384,1408]{1,0:T(8,128)(2,1)}) custom-call(s32[1]{0:T(128)} %bitcast.3.me_ref, bf16[96,2048]{1,0:T(8,128)(2,1)S(1)} %copy-done.19, bf16[96,2048]{1,0:T(8,128)(2,1)S(1)} %copy-done.21, ...), custom_call_target="tpu_custom_call" | custom-call | flops 2000000000 | bytes 100000 | tf_op jit(solution)/shard_map/pallas_call | solution.py:272
  249.4 11.8 %shard_map.195 = (f32[96,2048]{1,0:T(8,128)S(1)}, f32[96,2048]{1,0:T(8,128)S(1)}, bf16[96,2048]{1,0:T(8,128)(2,1)S(1)}, bf16[96,2048]{1,0:T(8,128)(2,1)S(1)}, bf16[384,2816]{1,0:T(8,128)(2,1)}) custom-call(s32[1]{0:T(128)} %bitcast.3.me_ref, bf16[96,2048]{1,0:T(8,128)(2,1)S(1)} %get-tuple-element.427.refs_0_.base_ref, ...), custom_call_target="tpu_custom_call" | custom-call | flops 2000000000 | bytes 100000 | tf_op jit(solution)/shard_map/pallas_call | solution.py:272
  265.6 8.8 %collective-permute-done.43.far_ref = bf16[96,2048]{1,0:T(8,128)(2,1)S(1)} collective-permute-done((bf16[96,2048]{1,0:T(8,128)(2,1)S(1)}, bf16[96,2048]{1,0:T(8,128)(2,1)S(1)}, u32[]{:S(2)}, u32[]{:S(2)}) %collective-permute-start.43) | collective-permute-done | bytes 393248 | tf_op jit(solution)/shard_map/ppermute | solution.py:736
  276.1 9.1 %collective-permute-done.44.refs_1_ = bf16[96,2048]{1,0:T(8,128)(2,1)} collective-permute-done((bf16[96,2048]{1,0:T(8,128)(2,1)}, bf16[96,2048]{1,0:T(8,128)(2,1)}, u32[]{:S(2)}, u32[]{:S(2)}) %collective-permute-start.44) | collective-permute-done | bytes 393248 | tf_op jit(solution)/shard_map/ppermute | solution.py:736
  289.0 19.8 %shard_map.198 = (f32[96,2048]{1,0:T(8,128)}, f32[96,2048]{1,0:T(8,128)}, bf16[96,2048]{1,0:T(8,128)(2,1)S(1)}, bf16[96,2048]{1,0:T(8,128)(2,1)S(1)}, f32[3,4,51...) custom-call(s32[1]{0:T(128)} %bitcast.3.me_ref, ...), custom_call_target="tpu_custom_call" | custom-call | flops 2000000000 | bytes 100000 | tf_op jit(solution)/shard_map/pallas_call | solution.py:272
  313.6 19.3 %shard_map.199 = (f32[96,2048]{1,0:T(8,128)}, f32[96,2048]{1,0:T(8,128)}, bf16[96,2048]{1,0:T(8,128)(2,1)S(1)}, bf16[96,2048]{1,0:T(8,128)(2,1)}, f32[3,4,512]{2...) custom-call(s32[1]{0:T(128)} %bitcast.3.me_ref, ...), custom_call_target="tpu_custom_call" | custom-call | flops 2000000000 | bytes 100000 | tf_op jit(solution)/shard_map/pallas_call | solution.py:272
  343.8 8.9 %collective-permute-done.56 = bf16[96,2048]{1,0:T(8,128)(2,1)S(1)} collective-permute-done((bf16[96,2048]{1,0:T(8,128)(2,1)S(1)}, bf16[96,2048]{1,0:T(8,128)(2,1)S(1)}, u32[]{:S(2)}, u32[]{:S(2)}) %collective-permute-start.56) | collective-permute-done | bytes 393248 | tf_op jit(solution)/shard_map/ppermute | solution.py:741
  357.5 6.2 collective-permute-done.58.refs_1_
  363.7 4.9 collective-permute-done.57
  369.3 11.8 %shard_map.202 = (f32[96,2048]{1,0:T(8,128)S(1)}, f32[96,2048]{1,0:T(8,128)S(1)}, bf16[96,2048]{1,0:T(8,128)(2,1)S(1)}, bf16[96,2048]{1,0:T(8,128)(2,1)S(1)}, bf16[384,2816]{1,0:T(8,128)(2,1)}) custom-call(s32[1]{0:T(128)} %bitcast.3.me_ref, bf16[96,2048]{1,0:T(8,128)(2,1)S(1)} %broadcast_select_fusion.refs_0_.base_ref, ...), custom_call_target="tpu_custom_call" | custom-call | flops 2000000000 | bytes 100000 | tf_op jit(solution)/shard_map/pallas_call | solution.py:272
  385.6 11.4 %all-gather.7.cloned.1.call-done = bf16[1536,1408]{1,0:T(8,128)(2,1)} async-done(((bf16[384,1408]{1,0:T(8,128)(2,1)}), bf16[1536,1408]{1,0:T(8,128)(2,1)}) %all-gather.7.cloned.1.call-update) | async-done | bytes 4325392 | tf_op jit(solution)/shard_map/all_gather | solution.py:955
  398.0 11.9 %shard_map.203 = (f32[96,2048]{1,0:T(8,128)S(1)}, f32[96,2048]{1,0:T(8,128)S(1)}, bf16[96,2048]{1,0:T(8,128)(2,1)S(1)}, bf16[96,2048]{1,0:T(8,128)(2,1)S(1)}, bf16[384,2816]{1,0:T(8,128)(2,1)}) custom-call(s32[1]{0:T(128)} %bitcast.3.me_ref, bf16[96,2048]{1,0:T(8,128)(2,1)S(1)} %broadcast_select_fusion.1.refs_0_.base_ref, ...), custom_call_target="tpu_custom_call" | custom-call | flops 2000000000 | bytes 100000 | tf_op jit(solution)/shard_map/pallas_call | solution.py:272
  413.3 13.9 %convolution_convert_fusion = bf16[2048,2816]{1,0:T(8,128)(2,1)} fusion(bf16[384,2816]{1,0:T(8,128)(2,1)} %get-tuple-element.536, bf16[384,2816]{1,0:T(8,128)(2,1)S(1)} %copy-done.104, bf16[384,2048]{1,0:T(8,128)(2,1)S(1)} %copy-done.106, bf16[384,2048]{1,0:T(8,128)(2,1)S(1)} %copy-done.105), kind=kOutput, calls=%fused_computation | convolution fusion | flops 8879079424 | bytes 19005440 | tf_op jit(solution)/shard_map/dot_general | solution.py:722
  429.7 9.4 %collective-permute-done.66.far_ref = bf16[96,2048]{1,0:T(8,128)(2,1)S(1)} collective-permute-done((bf16[96,2048]{1,0:T(8,128)(2,1)S(1)}, bf16[96,2048]{1,0:T(8,128)(2,1)S(1)}, u32[]{:S(2)}, u32[]{:S(2)}) %collective-permute-start.66) | collective-permute-done | bytes 393248 | tf_op jit(solution)/shard_map/ppermute | solution.py:736
  445.2 8.1 %collective-permute-done.69.far_ref = bf16[96,2048]{1,0:T(8,128)(2,1)S(1)} collective-permute-done((bf16[96,2048]{1,0:T(8,128)(2,1)S(1)}, bf16[96,2048]{1,0:T(8,128)(2,1)S(1)}, u32[]{:S(2)}, u32[]{:S(2)}) %collective-permute-start.69) | collective-permute-done | bytes 393248 | tf_op jit(solution)/shard_map/ppermute | solution.py:736
  455.3 8.5 %collective-permute-done.70.refs_1_ = bf16[96,2048]{1,0:T(8,128)(2,1)S(1)} collective-permute-done((bf16[96,2048]{1,0:T(8,128)(2,1)S(1)}, bf16[96,2048]{1,0:T(8,128)(2,1)S(1)}, u32[]{:S(2)}, u32[]{:S(2)}) %collective-permute-start.70) | collective-permute-done | bytes 393248 | tf_op jit(solution)/shard_map/ppermute | solution.py:736
  467.5 19.3 %shard_map.206 = (f32[96,2048]{1,0:T(8,128)}, f32[96,2048]{1,0:T(8,128)}, bf16[96,2048]{1,0:T(8,128)(2,1)}, bf16[96,2048]{1,0:T(8,128)(2,1)S(1)}, f32[3,4,512]{2...) custom-call(s32[1]{0:T(128)} %bitcast.3.me_ref, ...), custom_call_target="tpu_custom_call" | custom-call | flops 2000000000 | bytes 100000 | tf_op jit(solution)/shard_map/pallas_call | solution.py:272
  488.6 2.8 constant_dynamic-update-slice_fusion.1
  500.2 19.1 %shard_map.207 = (f32[96,2048]{1,0:T(8,128)}, f32[96,2048]{1,0:T(8,128)}, bf16[96,2048]{1,0:T(8,128)(2,1)S(1)}, bf16[96,2048]{1,0:T(8,128)(2,1)S(1)}, f32[3,4,51...) custom-call(s32[1]{0:T(128)} %bitcast.3.me_ref, ...), custom_call_target="tpu_custom_call" | custom-call | flops 2000000000 | bytes 100000 | tf_op jit(solution)/shard_map/pallas_call | solution.py:272
  520.8 25.2 %collective-permute-done.84 = bf16[4,96,512]{2,1,0:T(8,128)(2,1)} collective-permute-done((bf16[4,96,512]{2,1,0:T(8,128)(2,1)}, bf16[4,96,512]{2,1,0:T(8,128)(2,1)}, u32[]{:S(2)}, u32[]{:S(2)}) %collective-permute-start.84) | collective-permute-done | bytes 393248 | tf_op jit(solution)/shard_map/ppermute | solution.py:865
  557.4 5.4 collective-permute-done.81.far_ref
  567.6 28.9 %collective-permute-start.89 = (f32[14336]{0:T(1024)S(1)}, f32[14336]{0:T(1024)S(1)}, u32[]{:S(2)}, u32[]{:S(2)}) collective-permute-start(f32[14336]{0:T(1024)S(1)} %constant_dynamic-update-slice_fusion.3), channel_id=1, source_target_pairs={{0,4},{4,0},{8,12},{12,8},{1,5},{5,1},{9,13},{13,9},{2,6},{6,2},{1... | collective-permute-start | bytes 172040 | tf_op jit(solution)/shard_map/ppermute | solution.py:736
  603.2 2.6 collective-permute-start.90
  607.2 2.8 collective-permute-start.92
  610.9 4.1 collective-permute-start.82
  617.0 9.3 %convolution_convert_fusion.1 = bf16[2048,1536]{1,0:T(8,128)(2,1)} fusion(bf16[768,2048]{1,0:T(8,128)(2,1)} %constant_dynamic-update-slice_fusion, bf16[384,1536]{1,0:T(8,128)(2,1)} %get-tuple-element.570, bf16[384,1536]{1,0:T(8,128)(2,1)} %get-tuple-element.559), kind=kOutput, calls=%fused_computation.1 | convolution fusion | flops 4839702528 | bytes 11796480 | tf_op jit(solution)/shard_map/dot_general | solution.py:722
  634.5 3.5 pad_maximum_fusion
  645.2 4.1 convolution_add_fusion
  651.5 2.9 maximum_convert_fusion
  654.4 115.5 %reduce-scatter.5.cloned.1.call-done = bf16[512,1536]{1,0:T(8,128)(2,1)} async-done(((bf16[2048,1536]{1,0:T(8,128)(2,1)}), bf16[512,1536]{1,0:T(8,128)(2,1)}) %reduce-scatter.5.cloned.1.call-update) | async-done | bytes 1572880 | tf_op jit(solution)/shard_map/reduce_scatter | solution.py:985
  (529 shorter events, 179.1 us)
Async XLA Ops:
  7.2 378.4 %all-gather.9.cloned.1.call-start = ((), (), s32[]{:S(2)}) async-start(), calls=%async_computation.4 | async-start | bytes 1966080 | tf_op jit(solution)/shard_map/all_gather | solution.py:956
  34.4 15.8 %collective-permute-start.2 = (bf16[96,2048]{1,0:T(8,128)(2,1)S(1)}, bf16[96,2048]{1,0:T(8,128)(2,1)S(1)}, u32[]{:S(2)}, u32[]{:S(2)}) collective-permute-start(bf16[96,2048]{1,0:T(8,128)(2,1)S(1)} %convert_add_fusion.18), channel_id=1, source_target_pairs={{0,2},{1,3},{2,0},{3,1},{4,6},{5,7},{6,4},{7,5},{8,10},{9,11},{10,... | collective-permute-start | bytes 1179656 | tf_op jit(solution)/shard_map/ppermute | solution.py:736
  53.2 11.2 %collective-permute-start.5 = (bf16[96,2048]{1,0:T(8,128)(2,1)S(1)}, bf16[96,2048]{1,0:T(8,128)(2,1)S(1)}, u32[]{:S(2)}, u32[]{:S(2)}) collective-permute-start(bf16[96,2048]{1,0:T(8,128)(2,1)S(1)} %add_convert_fusion.8), channel_id=1, source_target_pairs={{0,2},{1,3},{2,0},{3,1},{4,6},{5,7},{6,4},{7,5},{8,10},{9,11},{10,... | collective-permute-start | bytes 1179656 | tf_op jit(solution)/shard_map/ppermute | solution.py:736
  75.2 12.4 %collective-permute-start.7 = (bf16[96,2048]{1,0:T(8,128)(2,1)S(1)}, bf16[96,2048]{1,0:T(8,128)(2,1)S(1)}, u32[]{:S(2)}, u32[]{:S(2)}) collective-permute-start(bf16[96,2048]{1,0:T(8,128)(2,1)S(1)} %get-tuple-element.350.refs_0_), channel_id=1, source_target_pairs={{0,2},{1,3},{2,0},{3,1},{4,6},{5,7},{6,4},{7,5},{8,10},{9,11},{10,... | collective-permute-start | bytes 1179656 | tf_op jit(solution)/shard_map/ppermute | solution.py:736
  91.9 12.5 %collective-permute-start.14 = (bf16[96,2048]{1,0:T(8,128)(2,1)}, bf16[96,2048]{1,0:T(8,128)(2,1)}, u32[]{:S(2)}, u32[]{:S(2)}) collective-permute-start(bf16[96,2048]{1,0:T(8,128)(2,1)} %convert_add_fusion.15), channel_id=1, source_target_pairs={{0,2},{1,3},{2,0},{3,1},{4,6},{5,7},{6,4},{7,5},{8,10},{9,11},{10,... | collective-permute-start | bytes 1179656 | tf_op jit(solution)/shard_map/ppermute | solution.py:736
  105.6 12.4 %collective-permute-start.18 = (bf16[96,2048]{1,0:T(8,128)(2,1)S(1)}, bf16[96,2048]{1,0:T(8,128)(2,1)S(1)}, u32[]{:S(2)}, u32[]{:S(2)}) collective-permute-start(bf16[96,2048]{1,0:T(8,128)(2,1)S(1)} %add_convert_fusion.6), channel_id=1, source_target_pairs={{0,16},{1,17},{2,18},{3,19},{4,20},{5,21},{6,22},{7,23},{8,24},{9,... | collective-permute-start | bytes 1179656 | tf_op jit(solution)/shard_map/ppermute | solution.py:741
  109.1 13.0 %collective-permute-start.15 = (bf16[96,2048]{1,0:T(8,128)(2,1)S(1)}, bf16[96,2048]{1,0:T(8,128)(2,1)S(1)}, u32[]{:S(2)}, u32[]{:S(2)}) collective-permute-start(bf16[96,2048]{1,0:T(8,128)(2,1)S(1)} %get-tuple-element.361), channel_id=1, source_target_pairs={{0,1},{1,0},{2,3},{3,2},{4,5},{5,4},{6,7},{7,6},{8,9},{9,8},{10,11... | collective-permute-start | bytes 1179656 | tf_op jit(solution)/shard_map/ppermute | solution.py:736
  109.5 11.4 %collective-permute-start.17 = (bf16[96,2048]{1,0:T(8,128)(2,1)S(1)}, bf16[96,2048]{1,0:T(8,128)(2,1)S(1)}, u32[]{:S(2)}, u32[]{:S(2)}) collective-permute-start(bf16[96,2048]{1,0:T(8,128)(2,1)S(1)} %add_convert_fusion.7), channel_id=1, source_target_pairs={{0,2},{1,3},{2,0},{3,1},{4,6},{5,7},{6,4},{7,5},{8,10},{9,11},{10,... | collective-permute-start | bytes 1179656 | tf_op jit(solution)/shard_map/ppermute | solution.py:736
  122.3 11.7 %collective-permute-start.19 = (bf16[96,2048]{1,0:T(8,128)(2,1)S(1)}, bf16[96,2048]{1,0:T(8,128)(2,1)S(1)}, u32[]{:S(2)}, u32[]{:S(2)}) collective-permute-start(bf16[96,2048]{1,0:T(8,128)(2,1)S(1)} %add_convert_fusion.5), channel_id=1, source_target_pairs={{0,16},{1,17},{2,18},{3,19},{4,20},{5,21},{6,22},{7,23},{8,24},{9,... | collective-permute-start | bytes 1179656 | tf_op jit(solution)/shard_map/ppermute | solution.py:741
  126.0 10.8 %collective-permute-start.22 = (bf16[96,2048]{1,0:T(8,128)(2,1)S(1)}, bf16[96,2048]{1,0:T(8,128)(2,1)S(1)}, u32[]{:S(2)}, u32[]{:S(2)}) collective-permute-start(bf16[96,2048]{1,0:T(8,128)(2,1)S(1)} %get-tuple-element.370.refs_0_), channel_id=1, source_target_pairs={{0,1},{1,0},{2,3},{3,2},{4,5},{5,4},{6,7},{7,6},{8,9},{9,8},{10,11... | collective-permute-start | bytes 1179656 | tf_op jit(solution)/shard_map/ppermute | solution.py:736
  136.1 17.9 %collective-permute-start.21 = (bf16[96,2048]{1,0:T(8,128)(2,1)S(1)}, bf16[96,2048]{1,0:T(8,128)(2,1)S(1)}, u32[]{:S(2)}, u32[]{:S(2)}) collective-permute-start(bf16[96,2048]{1,0:T(8,128)(2,1)S(1)} %get-tuple-element.392.refs_0_), channel_id=1, source_target_pairs={{0,2},{1,3},{2,0},{3,1},{4,6},{5,7},{6,4},{7,5},{8,10},{9,11},{10,... | collective-permute-start | bytes 1179656 | tf_op jit(solution)/shard_map/ppermute | solution.py:736
  154.0 231.6 %all-gather.11.cloned.1.call-start = ((), (), s32[]{:S(2)}) async-start(), calls=%async_computation.5 | async-start | bytes 1966080 | tf_op jit(solution)/shard_map/all_gather | solution.py:956
  157.5 20.3 %collective-permute-start.28 = (bf16[96,2048]{1,0:T(8,128)(2,1)S(1)}, bf16[96,2048]{1,0:T(8,128)(2,1)S(1)}, u32[]{:S(2)}, u32[]{:S(2)}) collective-permute-start(bf16[96,2048]{1,0:T(8,128)(2,1)S(1)} %convert_add_fusion.13), channel_id=1, source_target_pairs={{0,2},{1,3},{2,0},{3,1},{4,6},{5,7},{6,4},{7,5},{8,10},{9,11},{10,... | collective-permute-start | bytes 1179656 | tf_op jit(solution)/shard_map/ppermute | solution.py:736
  178.6 206.9 %all-gather.5.cloned.1.call-start = ((), (), s32[]{:S(2)}) async-start(), calls=%async_computation.2 | async-start | bytes 5406720 | tf_op jit(solution)/shard_map/all_gather | solution.py:955
  182.0 11.2 %collective-permute-start.31 = (bf16[96,2048]{1,0:T(8,128)(2,1)S(1)}, bf16[96,2048]{1,0:T(8,128)(2,1)S(1)}, u32[]{:S(2)}, u32[]{:S(2)}) collective-permute-start(bf16[96,2048]{1,0:T(8,128)(2,1)S(1)} %add_convert_fusion.4), channel_id=1, source_target_pairs={{0,2},{1,3},{2,0},{3,1},{4,6},{5,7},{6,4},{7,5},{8,10},{9,11},{10,... | collective-permute-start | bytes 1179656 | tf_op jit(solution)/shard_map/ppermute | solution.py:736
  194.0 11.8 %collective-permute-start.34 = (bf16[96,2048]{1,0:T(8,128)(2,1)S(1)}, bf16[96,2048]{1,0:T(8,128)(2,1)S(1)}, u32[]{:S(2)}, u32[]{:S(2)}) collective-permute-start(bf16[96,2048]{1,0:T(8,128)(2,1)S(1)} %get-tuple-element.415.refs_0_), channel_id=1, source_target_pairs={{0,1},{1,0},{2,3},{3,2},{4,5},{5,4},{6,7},{7,6},{8,9},{9,8},{10,11... | collective-permute-start | bytes 1179656 | tf_op jit(solution)/shard_map/ppermute | solution.py:736
  205.0 12.3 %collective-permute-start.33 = (bf16[96,2048]{1,0:T(8,128)(2,1)S(1)}, bf16[96,2048]{1,0:T(8,128)(2,1)S(1)}, u32[]{:S(2)}, u32[]{:S(2)}) collective-permute-start(bf16[96,2048]{1,0:T(8,128)(2,1)S(1)} %get-tuple-element.431.refs_0_), channel_id=1, source_target_pairs={{0,2},{1,3},{2,0},{3,1},{4,6},{5,7},{6,4},{7,5},{8,10},{9,11},{10,... | collective-permute-start | bytes 1179656 | tf_op jit(solution)/shard_map/ppermute | solution.py:736
  218.1 178.9 %all-gather.7.cloned.1.call-start = ((), (), s32[]{:S(2)}) async-start(), calls=%async_computation.3 | async-start | bytes 5406720 | tf_op jit(solution)/shard_map/all_gather | solution.py:955
  235.3 26.0 %collective-permute-start.40 = (bf16[96,2048]{1,0:T(8,128)(2,1)S(1)}, bf16[96,2048]{1,0:T(8,128)(2,1)S(1)}, u32[]{:S(2)}, u32[]{:S(2)}) collective-permute-start(bf16[96,2048]{1,0:T(8,128)(2,1)S(1)} %convert_add_fusion.10), channel_id=1, source_target_pairs={{0,2},{1,3},{2,0},{3,1},{4,6},{5,7},{6,4},{7,5},{8,10},{9,11},{10,... | collective-permute-start | bytes 1179656 | tf_op jit(solution)/shard_map/ppermute | solution.py:736
  263.2 11.2 %collective-permute-start.43 = (bf16[96,2048]{1,0:T(8,128)(2,1)S(1)}, bf16[96,2048]{1,0:T(8,128)(2,1)S(1)}, u32[]{:S(2)}, u32[]{:S(2)}) collective-permute-start(bf16[96,2048]{1,0:T(8,128)(2,1)S(1)} %add_convert_fusion.3), channel_id=1, source_target_pairs={{0,2},{1,3},{2,0},{3,1},{4,6},{5,7},{6,4},{7,5},{8,10},{9,11},{10,... | collective-permute-start | bytes 1179656 | tf_op jit(solution)/shard_map/ppermute | solution.py:736
  274.4 10.8 %collective-permute-start.44 = (bf16[96,2048]{1,0:T(8,128)(2,1)}, bf16[96,2048]{1,0:T(8,128)(2,1)}, u32[]{:S(2)}, u32[]{:S(2)}) collective-permute-start(bf16[96,2048]{1,0:T(8,128)(2,1)} %get-tuple-element.454.refs_0_), channel_id=1, source_target_pairs={{0,2},{1,3},{2,0},{3,1},{4,6},{5,7},{6,4},{7,5},{8,10},{9,11},{10,... | collective-permute-start | bytes 1179656 | tf_op jit(solution)/shard_map/ppermute | solution.py:736
  275.6 13.4 %collective-permute-start.46 = (bf16[96,2048]{1,0:T(8,128)(2,1)}, bf16[96,2048]{1,0:T(8,128)(2,1)}, u32[]{:S(2)}, u32[]{:S(2)}) collective-permute-start(bf16[96,2048]{1,0:T(8,128)(2,1)} %get-tuple-element.454.refs_0_), channel_id=1, source_target_pairs={{0,1},{1,0},{2,3},{3,2},{4,5},{5,4},{6,7},{7,6},{8,9},{9,8},{10,11... | collective-permute-start | bytes 1179656 | tf_op jit(solution)/shard_map/ppermute | solution.py:736
  287.5 21.3 %collective-permute-start.45 = (bf16[96,2048]{1,0:T(8,128)(2,1)}, bf16[96,2048]{1,0:T(8,128)(2,1)}, u32[]{:S(2)}, u32[]{:S(2)}) collective-permute-start(bf16[96,2048]{1,0:T(8,128)(2,1)} %get-tuple-element.473.refs_0_), channel_id=1, source_target_pairs={{0,2},{1,3},{2,0},{3,1},{4,6},{5,7},{6,4},{7,5},{8,10},{9,11},{10,... | collective-permute-start | bytes 1179656 | tf_op jit(solution)/shard_map/ppermute | solution.py:736
  288.9 360.5 %reduce-scatter.3.cloned.1.call-start = ((), (), s32[]{:S(2)}) async-start(), calls=%async_computation.6 | async-start | bytes 14417920 | tf_op jit(solution)/shard_map/reduce_scatter | solution.py:985
  312.9 20.7 %collective-permute-start.52 = (bf16[96,2048]{1,0:T(8,128)(2,1)S(1)}, bf16[96,2048]{1,0:T(8,128)(2,1)S(1)}, u32[]{:S(2)}, u32[]{:S(2)}) collective-permute-start(bf16[96,2048]{1,0:T(8,128)(2,1)S(1)} %convert_add_fusion.7), channel_id=1, source_target_pairs={{0,2},{1,3},{2,0},{3,1},{4,6},{5,7},{6,4},{7,5},{8,10},{9,11},{10,... | collective-permute-start | bytes 1179656 | tf_op jit(solution)/shard_map/ppermute | solution.py:736
  339.1 13.6 %collective-permute-start.56 = (bf16[96,2048]{1,0:T(8,128)(2,1)S(1)}, bf16[96,2048]{1,0:T(8,128)(2,1)S(1)}, u32[]{:S(2)}, u32[]{:S(2)}) collective-permute-start(bf16[96,2048]{1,0:T(8,128)(2,1)S(1)} %get-tuple-element.497), channel_id=1, source_target_pairs={{16,0},{17,1},{18,2},{19,3},{20,4},{21,5},{22,6},{23,7},{24,8},{25... | collective-permute-start | bytes 1179656 | tf_op jit(solution)/shard_map/ppermute | solution.py:741
  342.2 11.1 %collective-permute-start.55 = (bf16[96,2048]{1,0:T(8,128)(2,1)S(1)}, bf16[96,2048]{1,0:T(8,128)(2,1)S(1)}, u32[]{:S(2)}, u32[]{:S(2)}) collective-permute-start(bf16[96,2048]{1,0:T(8,128)(2,1)S(1)} %add_convert_fusion.2), channel_id=1, source_target_pairs={{0,2},{1,3},{2,0},{3,1},{4,6},{5,7},{6,4},{7,5},{8,10},{9,11},{10,... | collective-permute-start | bytes 1179656 | tf_op jit(solution)/shard_map/ppermute | solution.py:736
  356.2 12.4 %collective-permute-start.57 = (bf16[96,2048]{1,0:T(8,128)(2,1)S(1)}, bf16[96,2048]{1,0:T(8,128)(2,1)S(1)}, u32[]{:S(2)}, u32[]{:S(2)}) collective-permute-start(bf16[96,2048]{1,0:T(8,128)(2,1)S(1)} %get-tuple-element.499), channel_id=1, source_target_pairs={{16,0},{17,1},{18,2},{19,3},{20,4},{21,5},{22,6},{23,7},{24,8},{25... | collective-permute-start | bytes 1179656 | tf_op jit(solution)/shard_map/ppermute | solution.py:741
  357.5 11.9 %collective-permute-start.60 = (bf16[96,2048]{1,0:T(8,128)(2,1)S(1)}, bf16[96,2048]{1,0:T(8,128)(2,1)S(1)}, u32[]{:S(2)}, u32[]{:S(2)}) collective-permute-start(bf16[96,2048]{1,0:T(8,128)(2,1)S(1)} %broadcast_select_fusion.refs_0_.base_ref), channel_id=1, source_target_pairs={{0,1},{1,0},{2,3},{3,2},{4,5},{5,4},{6,7},{7,6},{8,9},{9,8},{10,11... | collective-permute-start | bytes 1179656 | tf_op jit(solution)/shard_map/ppermute | solution.py:736
  368.6 12.6 %collective-permute-start.59 = (bf16[96,2048]{1,0:T(8,128)(2,1)S(1)}, bf16[96,2048]{1,0:T(8,128)(2,1)S(1)}, u32[]{:S(2)}, u32[]{:S(2)}) collective-permute-start(bf16[96,2048]{1,0:T(8,128)(2,1)S(1)} %broadcast_select_fusion.1.refs_0_.base_ref), channel_id=1, source_target_pairs={{0,2},{1,3},{2,0},{3,1},{4,6},{5,7},{6,4},{7,5},{8,10},{9,11},{10,... | collective-permute-start | bytes 1179656 | tf_op jit(solution)/shard_map/ppermute | solution.py:736
  427.3 342.6 %reduce-scatter.5.cloned.1.call-start = ((), (), s32[]{:S(2)}) async-start(), calls=%async_computation.7 | async-start | bytes 7864320 | tf_op jit(solution)/shard_map/reduce_scatter | solution.py:985
  428.2 10.9 %collective-permute-start.66 = (bf16[96,2048]{1,0:T(8,128)(2,1)S(1)}, bf16[96,2048]{1,0:T(8,128)(2,1)S(1)}, u32[]{:S(2)}, u32[]{:S(2)}) collective-permute-start(bf16[96,2048]{1,0:T(8,128)(2,1)S(1)} %copy-done.102), channel_id=1, source_target_pairs={{0,2},{1,3},{2,0},{3,1},{4,6},{5,7},{6,4},{7,5},{8,10},{9,11},{10,... | collective-permute-start | bytes 1179656 | tf_op jit(solution)/shard_map/ppermute | solution.py:736
  442.1 11.2 %collective-permute-start.69 = (bf16[96,2048]{1,0:T(8,128)(2,1)S(1)}, bf16[96,2048]{1,0:T(8,128)(2,1)S(1)}, u32[]{:S(2)}, u32[]{:S(2)}) collective-permute-start(bf16[96,2048]{1,0:T(8,128)(2,1)S(1)} %add_convert_fusion.1), channel_id=1, source_target_pairs={{0,2},{1,3},{2,0},{3,1},{4,6},{5,7},{6,4},{7,5},{8,10},{9,11},{10,... | collective-permute-start | bytes 1179656 | tf_op jit(solution)/shard_map/ppermute | solution.py:736
  454.8 12.8 %collective-permute-start.72 = (bf16[96,2048]{1,0:T(8,128)(2,1)S(1)}, bf16[96,2048]{1,0:T(8,128)(2,1)S(1)}, u32[]{:S(2)}, u32[]{:S(2)}) collective-permute-start(bf16[96,2048]{1,0:T(8,128)(2,1)S(1)} %get-tuple-element.549.refs_0_), channel_id=1, source_target_pairs={{0,1},{1,0},{2,3},{3,2},{4,5},{5,4},{6,7},{7,6},{8,9},{9,8},{10,11... | collective-permute-start | bytes 1179656 | tf_op jit(solution)/shard_map/ppermute | solution.py:736
  466.1 21.5 %collective-permute-start.71 = (bf16[96,2048]{1,0:T(8,128)(2,1)S(1)}, bf16[96,2048]{1,0:T(8,128)(2,1)S(1)}, u32[]{:S(2)}, u32[]{:S(2)}) collective-permute-start(bf16[96,2048]{1,0:T(8,128)(2,1)S(1)} %get-tuple-element.566.refs_0_), channel_id=1, source_target_pairs={{0,2},{1,3},{2,0},{3,1},{4,6},{5,7},{6,4},{7,5},{8,10},{9,11},{10,... | collective-permute-start | bytes 1179656 | tf_op jit(solution)/shard_map/ppermute | solution.py:736
  494.3 25.0 %collective-permute-start.78 = (bf16[96,2048]{1,0:T(8,128)(2,1)S(1)}, bf16[96,2048]{1,0:T(8,128)(2,1)S(1)}, u32[]{:S(2)}, u32[]{:S(2)}) collective-permute-start(bf16[96,2048]{1,0:T(8,128)(2,1)S(1)} %convert_add_fusion.1), channel_id=1, source_target_pairs={{0,2},{1,3},{2,0},{3,1},{4,6},{5,7},{6,4},{7,5},{8,10},{9,11},{10,... | collective-permute-start | bytes 1179656 | tf_op jit(solution)/shard_map/ppermute | solution.py:736
  496.3 24.5 %collective-permute-start.83 = (bf16[4,96,512]{2,1,0:T(8,128)(2,1)}, bf16[4,96,512]{2,1,0:T(8,128)(2,1)}, u32[]{:S(2)}, u32[]{:S(2)}) collective-permute-start(bf16[4,96,512]{2,1,0:T(8,128)(2,1)} %get-tuple-element.653), channel_id=1, source_target_pairs={{0,4},{4,8},{8,12},{12,0},{1,5},{5,9},{9,13},{13,1},{2,6},{6,10},{... | collective-permute-start | bytes 1179656 | tf_op jit(solution)/shard_map/ppermute | solution.py:865
  496.3 49.8 %collective-permute-start.84 = (bf16[4,96,512]{2,1,0:T(8,128)(2,1)}, bf16[4,96,512]{2,1,0:T(8,128)(2,1)}, u32[]{:S(2)}, u32[]{:S(2)}) collective-permute-start(bf16[4,96,512]{2,1,0:T(8,128)(2,1)} %get-tuple-element.652), channel_id=1, source_target_pairs={{0,8},{4,12},{8,0},{12,4},{1,9},{5,13},{9,1},{13,5},{2,10},{6,14},... | collective-permute-start | bytes 1179656 | tf_op jit(solution)/shard_map/ppermute | solution.py:865
  497.6 50.4 %collective-permute-start.85 = (bf16[4,96,512]{2,1,0:T(8,128)(2,1)}, bf16[4,96,512]{2,1,0:T(8,128)(2,1)}, u32[]{:S(2)}, u32[]{:S(2)}) collective-permute-start(bf16[4,96,512]{2,1,0:T(8,128)(2,1)} %get-tuple-element.651), channel_id=1, source_target_pairs={{0,12},{4,0},{8,4},{12,8},{1,13},{5,1},{9,5},{13,9},{2,14},{6,2},{... | collective-permute-start | bytes 1179656 | tf_op jit(solution)/shard_map/ppermute | solution.py:865
  519.3 30.4 %collective-permute-start.80 = (bf16[96,2048]{1,0:T(8,128)(2,1)S(1)}, bf16[96,2048]{1,0:T(8,128)(2,1)}, u32[]{:S(2)}, u32[]{:S(2)}) collective-permute-start(bf16[96,2048]{1,0:T(8,128)(2,1)S(1)} %get-tuple-element.584), channel_id=1, source_target_pairs={{0,1},{1,0},{2,3},{3,2},{4,5},{5,4},{6,7},{7,6},{8,9},{9,8},{10,11... | collective-permute-start | bytes 1179656 | tf_op jit(solution)/shard_map/ppermute | solution.py:736
  562.7 53.8 %collective-permute-start.86 = (bf16[4,4,96,512]{3,2,0,1:T(8,128)(2,1)}, bf16[4,4,96,512]{3,2,0,1:T(8,128)(2,1)}, u32[]{:S(2)}, u32[]{:S(2)}) collective-permute-start(bf16[4,4,96,512]{3,2,0,1:T(8,128)(2,1)} %pad_maximum_fusion.3), channel_id=1, source_target_pairs={{0,2},{1,3},{2,0},{3,1},{4,6},{5,7},{6,4},{7,5},{8,10},{9,11},{10,... | collective-permute-start | bytes 4718600 | tf_op jit(solution)/shard_map/ppermute | solution.py:736
  567.5 31.5 %collective-permute-start.79 = (bf16[96,2048]{1,0:T(8,128)(2,1)S(1)}, bf16[96,2048]{1,0:T(8,128)(2,1)}, u32[]{:S(2)}, u32[]{:S(2)}) collective-permute-start(bf16[96,2048]{1,0:T(8,128)(2,1)S(1)} %copy-done.49), channel_id=1, source_target_pairs={{0,1},{1,0},{2,3},{3,2},{4,5},{5,4},{6,7},{7,6},{8,9},{9,8},{10,11... | collective-permute-start | bytes 1179656 | tf_op jit(solution)/shard_map/ppermute | solution.py:736
  567.6 35.6 %collective-permute-start.89 = (f32[14336]{0:T(1024)S(1)}, f32[14336]{0:T(1024)S(1)}, u32[]{:S(2)}, u32[]{:S(2)}) collective-permute-start(f32[14336]{0:T(1024)S(1)} %constant_dynamic-update-slice_fusion.3), channel_id=1, source_target_pairs={{0,4},{4,0},{8,12},{12,8},{1,5},{5,1},{9,13},{13,9},{2,6},{6,2},{1... | collective-permute-start | bytes 172040 | tf_op jit(solution)/shard_map/ppermute | solution.py:736
  602.9 31.5 %collective-permute-start.87 = (bf16[4,4,96,512]{3,2,0,1:T(8,128)(2,1)}, bf16[4,4,96,512]{3,2,0,1:T(8,128)(2,1)}, u32[]{:S(2)}, u32[]{:S(2)}) collective-permute-start(bf16[4,4,96,512]{3,2,0,1:T(8,128)(2,1)} %pad_maximum_fusion.3), channel_id=1, source_target_pairs={{0,1},{1,0},{2,3},{3,2},{4,5},{5,4},{6,7},{7,6},{8,9},{9,8},{10,11... | collective-permute-start | bytes 4718600 | tf_op jit(solution)/shard_map/ppermute | solution.py:736
  603.2 23.2 %collective-permute-start.90 = (f32[14336]{0:T(1024)S(1)}, f32[14336]{0:T(1024)S(1)}, u32[]{:S(2)}, u32[]{:S(2)}) collective-permute-start(f32[14336]{0:T(1024)S(1)} %add.294), channel_id=1, source_target_pairs={{0,8},{4,12},{8,0},{12,4},{1,9},{5,13},{9,1},{13,5},{2,10},{6,14},... | collective-permute-start | bytes 172040 | tf_op jit(solution)/shard_map/ppermute | solution.py:736
  610.9 21.6 %collective-permute-start.82 = (bf16[2,96,1024]{2,1,0:T(8,128)(2,1)}, bf16[2,96,1024]{2,1,0:T(8,128)(2,1)}, u32[]{:S(2)}, u32[]{:S(2)}) collective-permute-start(bf16[2,96,1024]{2,1,0:T(8,128)(2,1)} %fusion.11), channel_id=1, source_target_pairs={{0,16},{1,17},{2,18},{3,19},{4,20},{5,21},{6,22},{7,23},{8,24},{9,... | collective-permute-start | bytes 1179656 | tf_op jit(solution)/shard_map/ppermute | solution.py:741
  616.5 10.9 %collective-permute-start.93 = (f32[4224]{0:T(1024)S(1)}, f32[4224]{0:T(1024)S(1)}, u32[]{:S(2)}, u32[]{:S(2)}) collective-permute-start(f32[4224]{0:T(1024)S(1)} %add.301), channel_id=1, source_target_pairs={{0,1},{1,0},{2,3},{3,2},{4,5},{5,4},{6,7},{7,6},{8,9},{9,8},{10,11... | collective-permute-start | bytes 50696 | tf_op jit(solution)/shard_map/ppermute | solution.py:736
  616.5 17.9 %collective-permute-start.88 = (bf16[4,4,96,512]{3,2,0,1:T(8,128)(2,1)}, bf16[4,4,96,512]{3,2,0,1:T(8,128)(2,1)}, u32[]{:S(2)}, u32[]{:S(2)}) collective-permute-start(bf16[4,4,96,512]{3,2,0,1:T(8,128)(2,1)} %collective-permute-done.86), channel_id=1, source_target_pairs={{0,1},{1,0},{2,3},{3,2},{4,5},{5,4},{6,7},{7,6},{8,9},{9,8},{10,11... | collective-permute-start | bytes 4718600 | tf_op jit(solution)/shard_map/ppermute | solution.py:736
  (164 other events, 1108.2 us)
Sparse Core Ops, SparseCore 0:
  154.1 39.0 all-gather.8
  194.7 35.9 all-gather.10
  232.3 81.7 all-gather.4
  315.5 81.4 all-gather.6
  427.4 222.0 reduce-scatter.2
  651.6 118.2 reduce-scatter.4

commit v8 on v7

--- a/solution.py
+++ b/solution.py
@@ -21,6 +21,7 @@
 TILE = 256
 QUARTERS = 4
 ATTEND_KEPT = 9
+ROW_COPIES = 16
 VMEM_LIMIT = 50 * 1024 * 1024
 
 
@@ -130,6 +131,26 @@
             self.wait(QUARTERS * group + place)
 
 
+def load_rows(me_ref, shards, rows_ref, count, sems):
+    share = TOK_MB // count
+    if len(shards) == count:
+        for k in range(count):
+            rows_ref[k * share : (k + 1) * share, :] = shards[k][...]
+        return
+    copies = [
+        pltpu.make_async_copy(
+            shards[0].at[place_of(me_ref, difference, share), :],
+            rows_ref.at[k * share : (k + 1) * share, :],
+            sems.at[k],
+        )
+        for k, difference in enumerate(relative_order(count))
+    ]
+    for copy in copies:
+        copy.start()
+    for copy in copies:
+        copy.wait()
+
+
 class Push:
 
     def __init__(self, sems):
@@ -146,8 +167,9 @@
             copy.wait()
 
 
-def attend_kernel(heads, count, save, me_ref, seg_col_ref, seg_row_ref, masks_ref, taps_ref, gain_ref, *refs):
-    shards, refs = refs[:count], refs[count:]
+def attend_kernel(heads, count, save, held, me_ref, seg_col_ref, seg_row_ref, masks_ref, taps_ref, gain_ref, *refs):
+    *refs, row_sems = refs
+    shards, refs = refs[:held], refs[held:]
     project_hbm, beta_hbm, merge_hbm = refs[:3]
     partials, refs = refs[3 : 3 + count], refs[3 + count :]
     targets, refs = (refs[:ATTEND_KEPT], refs[ATTEND_KEPT:]) if save else ([], refs)
@@ -169,8 +191,7 @@
         sems,
         5,
     )
-    for k in range(count):
-        rows_ref[k * share : (k + 1) * share, :] = shards[k][...]
+    load_rows(me_ref, shards, rows_ref, count, row_sems)
     rows = rows_ref[...]
     ready(0)
 
@@ -266,30 +287,37 @@
     return [jax.ShapeDtypeStruct((share, width), F32 if k < count // 2 else BF16) for k in range(count)]
 
 
-def call(kernel, operands, hbm, out_shape, hbm_shape, scratch_shapes):
+def call(kernel, operands, rows, hbm, out_shape, hbm_shape, scratch_shapes, in_place=False):
     vmem = pl.BlockSpec(memory_space=pltpu.VMEM)
     far = pl.BlockSpec(memory_space=pltpu.HBM)
+    blocks = isinstance(rows, list)
+    rows = rows if blocks else [rows]
     return pl.pallas_call(
-        kernel,
-        in_specs=[pl.BlockSpec(memory_space=pltpu.SMEM)] + [vmem] * (len(operands) - 1) + [far] * len(hbm),
+        functools.partial(kernel, len(rows)),
+        in_specs=[pl.BlockSpec(memory_space=pltpu.SMEM)]
+        + [vmem] * (len(operands) - 1)
+        + [vmem if blocks else far] * len(rows)
+        + [far] * len(hbm),
         out_specs=[vmem] * len(out_shape) + [far] * len(hbm_shape),
         out_shape=out_shape + hbm_shape,
-        scratch_shapes=scratch_shapes,
+        input_output_aliases=(
+            {len(operands) + len(rows) + len(hbm) - 1: len(out_shape) + len(hbm_shape) - 1} if in_place else {}
+        ),
+        scratch_shapes=scratch_shapes + [pltpu.SemaphoreType.DMA((ROW_COPIES,))],
         compiler_params=pltpu.CompilerParams(vmem_limit_bytes=VMEM_LIMIT),
         cost_estimate=pl.CostEstimate(flops=2 * 10**9, bytes_accessed=10**5, transcendentals=0),
-    )(*operands, *hbm)
+    )(*operands, *rows, *hbm)
 
 
 def as_scratch(shapes):
     return [pltpu.VMEM(shape.shape, shape.dtype) for shape in shapes]
 
 
-def attend_forward(me, mine, shards, taps, gain, project, beta_weight, merge, save):
+def attend_forward(me, mine, count, rows, taps, gain, project, beta_weight, merge, save):
     masks, seg_col, seg_row = mine
     heads = merge.shape[1] // HEAD_DIM
     width = heads * HEAD_DIM
     model = merge.shape[2]
-    count = len(shards)
     kept = [
         jax.ShapeDtypeStruct((TOK_MB, model), BF16),
         jax.ShapeDtypeStruct((3, TOK_MB, width), F32),
@@ -303,7 +331,8 @@
     ]
     results = call(
         functools.partial(attend_kernel, heads, count, save),
-        (me, seg_col, seg_row, masks, taps, gain, *shards),
+        (me, seg_col, seg_row, masks, taps, gain),
+        rows,
         (project, beta_weight, merge),
         partial_shapes(count, model),
         kept if save else [],
@@ -320,8 +349,9 @@
     return results[count:], results[:count]
 
 
-def expand_kernel(count, save, me_ref, *refs):
-    shards, refs = refs[:count], refs[count:]
+def expand_kernel(count, save, held, me_ref, *refs):
+    *refs, row_sems = refs
+    shards, refs = refs[:held], refs[held:]
     share = TOK_MB // count
     if save:
         expand_hbm, *targets = refs[:5]
@@ -339,8 +369,7 @@
         sems,
         QUARTERS,
     )
-    for k in range(count):
-        rows_ref[k * share : (k + 1) * share, :] = shards[k][...]
+    load_rows(me_ref, shards, rows_ref, count, row_sems)
     if save:
         push.start(rows_ref, targets[0])
     fetch.wait_group(0)
@@ -365,13 +394,13 @@
         write_partials(partials, rows_ref.shape[1], share, lambda cols: mm(hidden_ref[...], contract_ref[:, cols]))
 
 
-def expand_forward(me, shards, expand, contract, save):
-    count = len(shards)
+def expand_forward(me, count, rows, expand, contract, save):
     model, units = expand.shape[2:]
     kept = [jax.ShapeDtypeStruct((TOK_MB, model), BF16)] + [jax.ShapeDtypeStruct((TOK_MB, units), BF16)] * 3
     results = call(
         functools.partial(expand_kernel, count, save),
-        (me, *shards),
+        (me,),
+        rows,
         (expand,) if save else (expand, contract),
         [] if save else partial_shapes(count, model),
         kept if save else [],
@@ -388,10 +417,13 @@
     return -(-units // LANES) * LANES
 
 
-def expand_back_kernel(count, me_ref, *refs):
-    shards, refs = refs[:count], refs[count:]
-    silu_hbm, slope_hbm, expand_hbm, contract_hbm = refs[:4]
-    partials, refs = refs[4 : 4 + count], refs[4 + count :]
+def expand_back_kernel(count, into, held, me_ref, *refs):
+    *refs, row_sems = refs
+    shards, refs = refs[:held], refs[held:]
+    silu_hbm, slope_hbm, expand_hbm, contract_hbm, *refs = refs
+    if into:
+        refs = refs[1:]
+    partials, refs = refs[:count], refs[count:]
     both_hbm, rows_ref, silu_ref, slope_ref, both_ref, expand_ref, contract_ref, sems, push_sems = refs
     push = Push(push_sems)
     share = TOK_MB // count
@@ -405,8 +437,7 @@
         sems,
         QUARTERS + 2,
     )
-    for k in range(count):
-        rows_ref[k * share : (k + 1) * share, :] = shards[k][...]
+    load_rows(me_ref, shards, rows_ref, count, row_sems)
     if second > units:
         both_ref[...] = jnp.zeros(both_ref.shape, BF16)
     fetch.wait_group(0)
@@ -418,7 +449,7 @@
         both_ref[:, second + t.start : second + t.stop] = (
             grad_hidden * silu_ref[:, t].astype(F32)
         ).astype(BF16)
-    push.start(both_ref, both_hbm)
+    push.start(both_ref, both_hbm.at[into * TOK_MB : (into + 1) * TOK_MB, :])
     for i, span in enumerate(spans):
         for j in range(2):
             fetch.wait(QUARTERS + 2 + 2 * i + j)
@@ -431,16 +462,16 @@
     push.wait()
 
 
-def expand_backward(me, shards, silu, slope, expand, contract):
-    count = len(shards)
+def expand_backward(me, count, rows, silu, slope, expand, contract, into, micro, joint):
     model, units = expand.shape[2:]
     both = jax.ShapeDtypeStruct((TOK_MB, 2 * padded(units)), BF16)
     results = call(
-        functools.partial(expand_back_kernel, count),
-        (me, *shards),
-        (silu, slope, expand, contract),
+        functools.partial(expand_back_kernel, count, into),
+        (me,),
+        rows,
+        (silu, slope, expand, contract) + ((joint,) if into else ()),
         partial_shapes(count, model),
-        [both],
+        [jax.ShapeDtypeStruct((micro * TOK_MB, both.shape[1]), BF16)],
         [pltpu.VMEM((TOK_MB, model), BF16)]
         + as_scratch([silu, slope, both])
         + [
@@ -449,6 +480,7 @@
             pltpu.SemaphoreType.DMA((QUARTERS + 2 + 2 * len(tiles_of(model, 2 * TILE)),)),
             pltpu.SemaphoreType.DMA((1,)),
         ],
+        into > 0,
     )
     return results[count], results[:count]
 
@@ -464,8 +496,9 @@
     return grad_x
 
 
-def attend_back_kernel(heads, count, me_ref, seg_col_ref, seg_row_ref, masks_ref, taps_ref, gain_ref, *refs):
-    shards, refs = refs[:count], refs[count:]
+def attend_back_kernel(heads, count, held, me_ref, seg_col_ref, seg_row_ref, masks_ref, taps_ref, gain_ref, *refs):
+    *refs, row_sems = refs
+    shards, refs = refs[:held], refs[held:]
     sources, refs = refs[: ATTEND_KEPT - 2], refs[ATTEND_KEPT - 2 :]
     project_hbm, beta_hbm, merge_hbm = refs[:3]
     partials, refs = refs[3 : 3 + count], refs[3 + count :]
@@ -487,8 +520,7 @@
         sems,
         ATTEND_KEPT,
     )
-    for k in range(count):
-        rows_ref[k * share : (k + 1) * share, :] = shards[k][...]
+    load_rows(me_ref, shards, rows_ref, count, row_sems)
     fetch.wait(0)
     for cols in tiles_of(heads * HEAD_DIM):
         value = mm_t(rows_ref[...], merge_ref[cols, :])
@@ -608,17 +640,17 @@
     push.wait()
 
 
-def attend_backward(me, mine, shards, kept, taps, gain, project, beta_weight, merge):
+def attend_backward(me, mine, count, rows, kept, taps, gain, project, beta_weight, merge):
     masks, seg_col, seg_row = mine
     heads = merge.shape[1] // HEAD_DIM
     width = heads * HEAD_DIM
     model = merge.shape[2]
-    count = len(shards)
     kept = kept[1:3] + kept[4:]
     grads = [jax.ShapeDtypeStruct((TOK_MB, 3 * width), BF16), jax.ShapeDtypeStruct((TOK_MB, LANES), BF16)]
     results = call(
         functools.partial(attend_back_kernel, heads, count),
-        (me, seg_col, seg_row, masks, taps, gain, *shards),
+        (me, seg_col, seg_row, masks, taps, gain),
+        rows,
         (*kept, project, beta_weight, merge),
         partial_shapes(count, model)
         + [
@@ -657,11 +689,16 @@
     )(*operands)
 
 
-def norm_kernel(gain_ref, x_ref, *refs):
-    *more, total_ref, normed_ref = refs
-    total = x_ref[...].astype(F32)
-    for ref in more:
+def total_of(refs):
+    total = refs[0][...].astype(F32)
+    for ref in refs[1:]:
         total = total + ref[...].astype(F32)
+    return total
+
+
+def norm_kernel(gain_ref, *refs):
+    *terms, total_ref, normed_ref = refs
+    total = total_of(terms)
     scale = lax.rsqrt(jnp.mean(total * total, axis=-1, keepdims=True) + EPS)
     total_ref[...] = total
     normed_ref[...] = (total * scale * gain_ref[...]).astype(BF16)
@@ -674,8 +711,35 @@
     )
 
 
-def norm_back_kernel(gain_ref, base_ref, x_ref, near_ref, far_ref, grad_ref, narrow_ref, gain_out):
-    grad_normed = near_ref[...].astype(F32) + far_ref[...].astype(F32)
+def first_norm_kernel(m, me_ref, gain_ref, tokens_hbm, normed_ref, own_ref, rows_ref, sem):
+    copy = pltpu.make_async_copy(tokens_hbm.at[m], rows_ref, sem)
+    copy.start()
+    copy.wait()
+    share = own_ref.shape[0]
+    own_ref[...] = rows_ref[place_of(me_ref, 0, share), :]
+    for rows in tiles_of(TOK_MB, BLOCK):
+        x = rows_ref[rows, :].astype(F32)
+        scale = lax.rsqrt(jnp.mean(x * x, axis=-1, keepdims=True) + EPS)
+        normed_ref[rows, :] = (x * scale * gain_ref[...]).astype(BF16)
+
+
+def first_norm(me, gain, tokens, m, share):
+    vmem = pl.BlockSpec(memory_space=pltpu.VMEM)
+    width = tokens.shape[2]
+    return pl.pallas_call(
+        functools.partial(first_norm_kernel, m),
+        in_specs=[pl.BlockSpec(memory_space=pltpu.SMEM), vmem, pl.BlockSpec(memory_space=pltpu.HBM)],
+        out_specs=[vmem, vmem],
+        out_shape=[jax.ShapeDtypeStruct((TOK_MB, width), BF16), jax.ShapeDtypeStruct((share, width), BF16)],
+        scratch_shapes=[pltpu.VMEM((TOK_MB, width), BF16), pltpu.SemaphoreType.DMA],
+        compiler_params=pltpu.CompilerParams(vmem_limit_bytes=16 * 1024 * 1024),
+        cost_estimate=pl.CostEstimate(flops=10**9, bytes_accessed=10**5, transcendentals=0),
+    )(me, gain, tokens)
+
+
+def norm_back_kernel(gain_ref, base_ref, x_ref, *refs):
+    *terms, grad_ref, narrow_ref, gain_out = refs
+    grad_normed = total_of(terms)
     x = x_ref[...].astype(F32)
     scale = lax.rsqrt(jnp.mean(x * x, axis=-1, keepdims=True) + EPS)
     unit = x * scale
@@ -689,11 +753,11 @@
     gain_out[...] = jnp.sum((grad_normed * unit).reshape(rows // 8, 8, width), axis=0)
 
 
-def norm_backward(gain, base, x, near, far):
+def norm_backward(gain, base, x, *terms):
     shape = x.shape
     return small_call(
         norm_back_kernel,
-        (gain, base, x, near, far),
+        (gain, base, x, *terms),
         [
             jax.ShapeDtypeStruct(shape, F32),
             jax.ShapeDtypeStruct(shape, BF16),
@@ -784,22 +848,21 @@
     return gather_near(gather_far(shard, order))
 
 
-def added(parts, arrived):
-    return [part.astype(F32) + other.astype(F32) for part, other in zip(parts, arrived)]
+def total(terms):
+    return sum(term.astype(F32) for term in terms)
 
 
 def scatter_near(parts):
     half = len(parts) // 2
-    return added(parts[:half], [flipped(part, "head", 1) for part in parts[half:]])
+    return [[part, flipped(other, "head", 1)] for part, other in zip(parts[:half], parts[half:])]
 
 
 def scatter_far(parts, order):
     for bit in bits_of("head")[1:]:
         half = len(parts) // 2
-        arrived = [order.flipped(narrow(part), bit) for part in parts[half:]]
-        if half == 1:
-            return parts[0], arrived[0]
-        parts = added(parts[:half], arrived)
+        arrived = [order.flipped(narrow(total(terms)), bit) for terms in parts[half:]]
+        parts = [terms + [other] for terms, other in zip(parts[:half], arrived)]
+    return parts[0]
 
 
 def after(values, earlier):
@@ -817,11 +880,14 @@
     for m in range(len(rows or fars)):
         parts = gather_near(fars[m]) if rows is None else rows[m]
         if near is not None:
-            parts, near = together(parts, near)
+            half = len(near) // 2
+            sent_on = [[total(terms)] for terms in near[half:]]
+            parts, sent_on = together(parts, sent_on)
+            near = near[:half] + sent_on
             sums.append(scatter_far(near, order))
         keep, partials = kernel(m, parts)
         if sums:
-            partials = after(partials, sums[-1][1])
+            partials = after(partials, sums[-1][-1])
         if rows is None and m + 1 < len(fars):
             fars[m + 1], keep, partials = together(fars[m + 1], keep, partials)
         kept.append(keep)
@@ -837,19 +903,19 @@
 
 def in_order(sums, finish):
     results = []
-    for m, (near, far) in enumerate(sums):
+    for m, (*terms, far) in enumerate(sums):
         if results:
             far, results[-1] = together(far, results[-1])
-        results.append(finish(m, near, far))
+        results.append(finish(m, *terms, far))
     return results
 
 
 def sent(distance, sums, finish):
     arrived = []
-    for m, (near, far) in enumerate(sums):
+    for m, (*terms, far) in enumerate(sums):
         if arrived:
             far = after(far, arrived[-1])
-        arrived.append(shifted(finish(m, near, far), "section", distance))
+        arrived.append(shifted(finish(m, *terms, far), "section", distance))
     return arrived
 
 
@@ -896,44 +962,47 @@
     segments = [segment_ids(lengths[m], TOK_MB) for m in every]
     masks = [(tap_masks(s), s[:, None], s[None, :]) for s in segments]
     order = Order()
-    relative = relative_order(lax.axis_size("head"))
-
-    def blocks(values):
-        return [lax.dynamic_slice_in_dim(values, (member ^ k) * share, share, 0) for k in relative]
-
-    tokens_own = [blocks(tokens[m])[0] for m in every]
-    cotangent_own = [blocks(cotangent[m])[0] for m in every]
+    groups = lax.axis_size("head")
+    cotangent_own = [
+        lax.dynamic_slice(cotangent, (m, member * share, 0), (1, share, width))[0] for m in every
+    ]
     gain_in, gain_mid = gains[0:1], gains[1:2]
 
     def forward_turn(inputs, save, shards=None, rows=None):
         kept, sums = in_turn(
             lambda m, rows: attend_forward(
-                me, masks[m], rows, conv_weight, o_gain, attn_in, beta_wide, attn_out, save
+                me, masks[m], groups, rows, conv_weight, o_gain, attn_in, beta_wide, attn_out, save
             ),
             order,
             shards,
             rows,
         )
-        middles = in_order(sums, lambda m, near, far: norm_of_sum(gain_mid, inputs[m], near, far))
+        middles = in_order(sums, lambda m, *terms: norm_of_sum(gain_mid, inputs[m], *terms))
         kept_mid, sums = in_turn(
-            lambda m, rows: expand_forward(me, rows, mlp_in, mlp_out, save),
+            lambda m, rows: expand_forward(me, groups, rows, mlp_in, mlp_out, save),
             order,
             [values[1] for values in middles],
         )
         if save:
             return kept, [values[0] for values in middles], kept_mid
-        return sent(1, sums, lambda m, near, far: narrow(middles[m][0] + near + far.astype(F32)))
+        return sent(1, sums, lambda m, *terms: narrow(total([middles[m][0], *terms])))
 
     def backward_expand(incoming, slopes, shards=None, rows=None, finish=None):
-        grads, sums = in_turn(
-            lambda m, rows: expand_backward(me, rows, *slopes[m], mlp_in, mlp_out), order, shards, rows, finish
-        )
+        joint = [None]
+
+        def kernel(m, rows):
+            joint[0], partials = expand_backward(
+                me, groups, rows, *slopes[m], mlp_in, mlp_out, m, micro, joint[0]
+            )
+            return joint[0], partials
+
+        grads, sums = in_turn(kernel, order, shards, rows, finish)
         return grads, in_order(sums, lambda m, *terms: norm_backward(gain_mid, incoming[m], middles[m], *terms))
 
     def backward_attend(grad_middles):
         return in_turn(
             lambda m, rows: attend_backward(
-                me, masks[m], rows, kept[m], conv_weight, o_gain, attn_in, beta_wide, attn_out
+                me, masks[m], groups, rows, kept[m], conv_weight, o_gain, attn_in, beta_wide, attn_out
             ),
             order,
             [values[1] for values in grad_middles],
@@ -943,8 +1012,8 @@
         return jnp.concatenate(values, axis=0)
 
     last = sections - 1
-    inputs = tokens_own
-    normed_own, normed = None, [blocks(norm_of_sum(gain_in, tokens[m])[1]) for m in every]
+    normed, tokens_own = zip(*(first_norm(me, gain_in, tokens, m, share) for m in every))
+    inputs, normed_own = tokens_own, None
     for turn in range(last):
         arrived = forward_turn(inputs, False, normed_own, normed)
         inputs = [jnp.where(section == 0, tokens_own[m], arrived[m]) for m in every]
@@ -957,7 +1026,7 @@
 
     slopes = [values[2:] for values in kept_mid]
     incoming = cotangent_own
-    rows = [blocks(cotangent[m]) for m in every]
+    rows = [cotangent[m] for m in every]
     for turn in range(last):
         _, grad_middles = backward_expand(incoming, slopes, incoming, rows)
         _, sums = backward_attend(grad_middles)
@@ -967,10 +1036,15 @@
         incoming = [jnp.where(section == last, cotangent_own[m], arrived[m]) for m in every]
         rows = None
     normed_mid = all_rows([values[0] for values in kept_mid])
-    slopes[-1], hidden_rows, mixed_rows = together(slopes[-1], hidden_rows, mixed_rows)
-    expands, grad_middles = backward_expand(
-        incoming, slopes, incoming, rows, lambda grads: narrow(product_left(normed_mid, all_rows(grads)))
-    )
+
+
+    def expand_terms(grads):
+        nonlocal hidden_rows, mixed_rows
+        both, hidden_rows, mixed_rows = together(grads[-1], hidden_rows, mixed_rows)
+        columns = swapped(after(incoming, both))
+        return together(narrow(product_left(normed_mid, both)), columns)
+
+    (expands, columns_out), grad_middles = backward_expand(incoming, slopes, incoming, rows, expand_terms)
     grads, sums = backward_attend(grad_middles)
     finals = [norm_backward(gain_in, grad_middles[m][0], inputs[m], *sums[m]) for m in every]
     gain_one, gain_two = (
@@ -991,9 +1065,13 @@
     grad_taps, grad_head_gain = (sum(grad[place] for grad in grads) for place in (2, 3))
     grad_head_gain = jnp.sum(grad_head_gain, axis=0)
 
-    columns = swapped(after(incoming, expands) + [values[1] for values in grad_middles])
-    columns = jnp.concatenate(gather(columns, order), axis=2)
-    columns = [part.reshape(-1, part.shape[-1]) for part in columns]
+    grad_project, early, middles_out = together(grad_project, early, [values[1] for values in grad_middles])
+    grad_project, columns_mid = together(grad_project, swapped(middles_out))
+    columns = [
+        part.reshape(-1, part.shape[-1])
+        for arrived in (columns_out, columns_mid)
+        for part in jnp.concatenate(gather(arrived, order), axis=2)
+    ]
     grad_contract = sum(product_left(left, right) for left, right in zip(hidden_rows, columns[:micro]))
     grad_merge = sum(product_left(left, right) for left, right in zip(mixed_rows, columns[micro:]))
     flat = jnp.concatenate([gain_one, gain_two, grad_head_gain])
@@ -1003,9 +1081,6 @@
     grad_taps, grad_beta = flat[: grad_taps.size].reshape(grad_taps.shape), flat[grad_taps.size :]
     rows = width // lax.axis_size("dp")
     grad_beta = lax.dynamic_slice_in_dim(grad_beta.reshape(width, heads), lax.axis_index("dp") * rows, rows, 0)
-    done = (grad_tokens, grad_contract, grad_merge, grad_beta, grad_taps, grad_head_gain, grad_gains, early)
-    grad_project, done = lax.optimization_barrier((grad_project, done))
-    grad_tokens, grad_contract, grad_merge, grad_beta, grad_taps, grad_head_gain, grad_gains, early = done
     units = mlp_in.shape[3]
     grad_expand = jnp.stack([part[:, :units] for part in jnp.split(early, 2, axis=1)]).astype(F32)
     grad_project = jnp.stack(jnp.split(spread(grad_project, 0), 3, axis=1)).astype(F32)

time: 790 us -> 778 us (0.985)
  starting transfers between devices: 96.4 us -> 78.1 us
  Pallas kernels: 242 us -> 253 us
  other arithmetic: 35.9 us -> 27 us
    ppermute x87 -> x90, starting transfers between devices: 77.9 us -> 54.1 us  [flipped(): lax.ppermute(values, axis, [(i, i ^ bit) for i in range(lax.axis_size(axi...]
    ppermute x87 -> x90, waiting for transfers between devices: 114 us -> 138 us  [flipped(): lax.ppermute(values, axis, [(i, i ^ bit) for i in range(lax.axis_size(axi...]
    ppermute x3 -> x6, waiting for transfers between devices: 27.2 us -> 10.7 us  [swapped(): lax.ppermute(block, 'dp', [(i, (i + distance) % count) for i in range(cou...]
    all_gather x2, waiting for transfers between devices: 11.4 us -> 0.01 us  [per_device(): lax.all_gather(values[1], 'dp', axis=0, tiled=True)]
    pallas_call x16 -> x18, Pallas kernels: 225 us -> 235 us  [the longest x16 233 us: call(): pl.pallas_call(functools.partial(kernel, len(rows)), in_specs=[pl.BlockSp...]
    ppermute x3 -> x6, starting transfers between devices: 3.9 us -> 12 us  [swapped(): lax.ppermute(block, 'dp', [(i, (i + distance) % count) for i in range(cou...]
    unnamed x227 -> x216, local copies, waits for them, and re-layouts: 39.7 us -> 46.8 us
    pallas_call x16 -> x14, Pallas kernels: 16.8 us -> 18.4 us  [small_call(): pl.pallas_call(kernel, in_specs=[vmem] * len(operands), out_specs=[vmem]...]
  transfers between devices with their start and end apart: 101 -> 107, of which waited for: 38 -> 41; matrix products, arithmetic and copies ran while one was open for 9% -> 10% of each run, Pallas kernels for 28% -> 31%
where the time goes in v8:
time: 778 us; the launch traced here: 768 us
  waiting for transfers between devices  290 us (37%)
  Pallas kernels  253 us (33%)
  starting transfers between devices  78.1 us (10%)
  local copies, waits for them, and re-layouts  68.3 us (9%)
  matrix products  35 us (4%)
  other arithmetic  27 us (3%)
  between operations  16.2 us (2%)
    pallas_call x16, Pallas kernels, call(): pl.pallas_call(functools.partial(kernel, len(rows)), in_specs=[pl.BlockSp...  233 us
    ppermute x90, waiting for transfers between devices, flipped(): lax.ppermute(values, axis, [(i, i ^ bit) for i in range(lax.axis_size(axi...  138 us
    reduce_scatter x2, waiting for transfers between devices, spread(): return lax.psum_scatter(value, 'dp', scatter_dimension=axis, tiled=True)  120 us
    ppermute x90, starting transfers between devices, flipped(): lax.ppermute(values, axis, [(i, i ^ bit) for i in range(lax.axis_size(axi...  54.1 us
    unnamed x216, local copies, waits for them, and re-layouts  46.8 us
    dot_general x7, matrix products, product_left(): lax.dot_general(left, right, (((0,), (0,)), ((), ())), preferred_element_...  35 us
    ppermute x5, waiting for transfers between devices, shifted(): lax.ppermute(values, axis, [(i, i + distance) for i in devices if i + dis...  21.4 us
    pallas_call x14, Pallas kernels, small_call(): pl.pallas_call(kernel, in_specs=[vmem] * len(operands), out_specs=[vmem]...  18.4 us
  transfers between devices with their start and end apart: 107, of which 41 were waited for; matrix products, arithmetic and copies ran while one was open for 10% of the time, Pallas kernels for 31%

profile of v8, /device:TPU:0, one launch (start us, length us, event | category | flops | bytes accessed | tf_op | source)
XLA Modules:
  0.0 768.2 jit_solution(3648909166416578270)
XLA Ops:
  15.1 13.7 %shard_map.180 = (f32[96,2048]{1,0:T(8,128)S(1)}, f32[96,2048]{1,0:T(8,128)S(1)}, bf16[96,2048]{1,0:T(8,128)(2,1)S(1)}, bf16[96,2048]{1,0:T(8,128)(2,1)S(1)}) custom-call(s32[1]{0:T(128)} %bitcast.1.me_ref, s32[384,1]{1,0:T(8,128)S(1)} %broadcast_in_dim.49.seg_col_ref, s32[1,384]{1,0:T(1,128)S(1)} %broadcast_in_dim.43.seg_row_ref, ...), custom_call_target="tpu_custom_call" | custom-call | flops 2000000000 | bytes 100000 | tf_op jit(solution)/shard_map/pallas_call | solution.py:295
  30.7 2.9 collective-permute-start.1
  34.2 13.7 %shard_map.181 = (f32[96,2048]{1,0:T(8,128)S(1)}, f32[96,2048]{1,0:T(8,128)S(1)}, bf16[96,2048]{1,0:T(8,128)(2,1)S(1)}, bf16[96,2048]{1,0:T(8,128)(2,1)S(1)}) custom-call(s32[1]{0:T(128)} %bitcast.1.me_ref, s32[384,1]{1,0:T(8,128)S(1)} %broadcast_in_dim.48.seg_col_ref, s32[1,384]{1,0:T(1,128)S(1)} %broadcast_in_dim.20.seg_row_ref, ...), custom_call_target="tpu_custom_call" | custom-call | flops 2000000000 | bytes 100000 | tf_op jit(solution)/shard_map/pallas_call | solution.py:295
  50.7 10.4 %collective-permute-done.4.refs_3_ = bf16[96,2048]{1,0:T(8,128)(2,1)S(1)} collective-permute-done((bf16[96,2048]{1,0:T(8,128)(2,1)S(1)}, bf16[96,2048]{1,0:T(8,128)(2,1)S(1)}, u32[]{:S(2)}, u32[]{:S(2)}) %collective-permute-start.4) | collective-permute-done | bytes 393248 | tf_op jit(solution)/shard_map/ppermute | solution.py:800
  61.9 9.5 %collective-permute-done.6.refs_1_ = bf16[96,2048]{1,0:T(8,128)(2,1)S(1)} collective-permute-done((bf16[96,2048]{1,0:T(8,128)(2,1)S(1)}, bf16[96,2048]{1,0:T(8,128)(2,1)S(1)}, u32[]{:S(2)}, u32[]{:S(2)}) %collective-permute-start.6) | collective-permute-done | bytes 393248 | tf_op jit(solution)/shard_map/ppermute | solution.py:800
  73.1 11.9 %shard_map.184 = (f32[96,2048]{1,0:T(8,128)S(1)}, f32[96,2048]{1,0:T(8,128)S(1)}, bf16[96,2048]{1,0:T(8,128)(2,1)}, bf16[96,2048]{1,0:T(8,128)(2,1)S(1)}) custom-call(s32[1]{0:T(128)} %bitcast.1.me_ref, bf16[96,2048]{1,0:T(8,128)(2,1)S(1)} %get-tuple-element.324.refs_0_, bf16[96,2048]{1,0:T(8,128)(2,1)S(1)} %collective-permute-done.6.refs_1_, ...), custom_call_target="tpu_custom_call" | custom-call | flops 2000000000 | bytes 100000 | tf_op jit(solution)/shard_map/pallas_call | solution.py:295
  94.0 10.8 %shard_map.185 = (f32[96,2048]{1,0:T(8,128)S(1)}, f32[96,2048]{1,0:T(8,128)S(1)}, bf16[96,2048]{1,0:T(8,128)(2,1)S(1)}, bf16[96,2048]{1,0:T(8,128)(2,1)S(1)}) custom-call(s32[1]{0:T(128)} %bitcast.1.me_ref, bf16[96,2048]{1,0:T(8,128)(2,1)S(1)} %copy-done.31, bf16[96,2048]{1,0:T(8,128)(2,1)S(1)} %copy-done.33, bf16[96,2048]{1,0:T(8,128)(2,1)S(1)} %copy-done.35, ...), custom_call_target="tpu_custom_call" | custom-call | flops 2000000000 | bytes 100000 | tf_op jit(solution)/shard_map/pallas_call | solution.py:295
  106.7 3.4 collective-permute-start.18
  111.7 7.0 collective-permute-done.18
  125.7 7.0 collective-permute-done.20.refs_1_
  135.0 16.4 %shard_map.188 = (f32[96,2048]{1,0:T(8,128)}, f32[96,2048]{1,0:T(8,128)}, bf16[96,2048]{1,0:T(8,128)(2,1)S(1)}, bf16[96,2048]{1,0:T(8,128)(2,1)S(1)}, bf16[384,2...) custom-call(s32[1]{0:T(128)} %bitcast.1.me_ref, ...), custom_call_target="tpu_custom_call" | custom-call | flops 2000000000 | bytes 100000 | tf_op jit(solution)/shard_map/pallas_call | solution.py:295
  157.1 16.4 %shard_map.189 = (f32[96,2048]{1,0:T(8,128)}, f32[96,2048]{1,0:T(8,128)}, bf16[96,2048]{1,0:T(8,128)(2,1)S(1)}, bf16[96,2048]{1,0:T(8,128)(2,1)S(1)}, bf16[384,2...) custom-call(s32[1]{0:T(128)} %bitcast.1.me_ref, ...), custom_call_target="tpu_custom_call" | custom-call | flops 2000000000 | bytes 100000 | tf_op jit(solution)/shard_map/pallas_call | solution.py:295
  183.2 7.8 %collective-permute-done.30.refs_3_ = bf16[96,2048]{1,0:T(8,128)(2,1)S(1)} collective-permute-done((bf16[96,2048]{1,0:T(8,128)(2,1)S(1)}, bf16[96,2048]{1,0:T(8,128)(2,1)S(1)}, u32[]{:S(2)}, u32[]{:S(2)}) %collective-permute-start.30) | collective-permute-done | bytes 393248 | tf_op jit(solution)/shard_map/ppermute | solution.py:800
  192.4 9.0 %collective-permute-done.32.refs_1_ = bf16[96,2048]{1,0:T(8,128)(2,1)S(1)} collective-permute-done((bf16[96,2048]{1,0:T(8,128)(2,1)S(1)}, bf16[96,2048]{1,0:T(8,128)(2,1)S(1)}, u32[]{:S(2)}, u32[]{:S(2)}) %collective-permute-start.32) | collective-permute-done | bytes 393248 | tf_op jit(solution)/shard_map/ppermute | solution.py:800
  203.1 10.5 %shard_map.192 = (bf16[384,2048]{1,0:T(8,128)(2,1)}, bf16[384,1408]{1,0:T(8,128)(2,1)}, bf16[384,1408]{1,0:T(8,128)(2,1)S(1)}, bf16[384,1408]{1,0:T(8,128)(2,1)}) custom-call(s32[1]{0:T(128)} %bitcast.1.me_ref, bf16[96,2048]{1,0:T(8,128)(2,1)S(1)} %get-tuple-element.397.refs_0_, bf16[96,2048]{1,0:T(8,128)(2,1)S(1)} %collective-permute-done.32.refs_1_, ...), custom_call_target="tpu_custom_call" | custom-call | flops 2000000000 | bytes 100000 | tf_op jit(solution)/shard_map/pallas_call | solution.py:295
  213.7 4.4 slice_bitcast_fusion
  218.1 13.0 %shard_map.193 = (f32[96,2048]{1,0:T(8,128)S(1)}, f32[96,2048]{1,0:T(8,128)S(1)}, bf16[96,2048]{1,0:T(8,128)(2,1)}, bf16[96,2048]{1,0:T(8,128)(2,1)S(1)}, bf16[768,2816]{1,0:T(8,128)(2,1)}) custom-call(s32[1]{0:T(128)} %bitcast.1.me_ref, bf16[384,2048]{1,0:T(8,128)(2,1)} %get-tuple-element.595.refs_0_, ...), custom_call_target="tpu_custom_call" | custom-call | flops 2000000000 | bytes 100000 | tf_op jit(solution)/shard_map/pallas_call | solution.py:295
  234.0 10.8 %shard_map.194 = (bf16[384,2048]{1,0:T(8,128)(2,1)}, bf16[384,1408]{1,0:T(8,128)(2,1)}, bf16[384,1408]{1,0:T(8,128)(2,1)S(1)}, bf16[384,1408]{1,0:T(8,128)(2,1)}) custom-call(s32[1]{0:T(128)} %bitcast.1.me_ref, bf16[96,2048]{1,0:T(8,128)(2,1)S(1)} %get-tuple-element.408.refs_0_, bf16[96,2048]{1,0:T(8,128)(2,1)S(1)} %collective-permute-done.33.refs_1_, ...), custom_call_target="tpu_custom_call" | custom-call | flops 2000000000 | bytes 100000 | tf_op jit(solution)/shard_map/pallas_call | solution.py:295
  244.8 13.2 %shard_map.195 = (f32[96,2048]{1,0:T(8,128)S(1)}, f32[96,2048]{1,0:T(8,128)S(1)}, bf16[96,2048]{1,0:T(8,128)(2,1)S(1)}, bf16[96,2048]{1,0:T(8,128)(2,1)}, bf16[768,2816]{1,0:T(8,128)(2,1)}) custom-call(s32[1]{0:T(128)} %bitcast.1.me_ref, bf16[384,2048]{1,0:T(8,128)(2,1)} %get-tuple-element.407.refs_0_, ...), custom_call_target="tpu_custom_call", output_to_operand_aliasing={{4}: (6, {})} | custom-call | flops 2000000000 | bytes 100000 | tf_op jit(solution)/shard_map/pallas_call | solution.py:295
  270.6 3.5 collective-permute-done.42.refs_2_
  275.5 9.0 %collective-permute-done.44.refs_1_ = bf16[96,2048]{1,0:T(8,128)(2,1)S(1)} collective-permute-done((bf16[96,2048]{1,0:T(8,128)(2,1)S(1)}, bf16[96,2048]{1,0:T(8,128)(2,1)S(1)}, u32[]{:S(2)}, u32[]{:S(2)}) %collective-permute-start.44) | collective-permute-done | bytes 393248 | tf_op jit(solution)/shard_map/ppermute | solution.py:800
  287.7 19.6 %shard_map.198 = (f32[96,2048]{1,0:T(8,128)}, f32[96,2048]{1,0:T(8,128)}, bf16[96,2048]{1,0:T(8,128)(2,1)}, bf16[96,2048]{1,0:T(8,128)(2,1)S(1)}, f32[3,4,512]{2...) custom-call(s32[1]{0:T(128)} %bitcast.1.me_ref, ...), custom_call_target="tpu_custom_call" | custom-call | flops 2000000000 | bytes 100000 | tf_op jit(solution)/shard_map/pallas_call | solution.py:295
  311.6 19.2 %shard_map.199 = (f32[96,2048]{1,0:T(8,128)}, f32[96,2048]{1,0:T(8,128)}, bf16[96,2048]{1,0:T(8,128)(2,1)}, bf16[96,2048]{1,0:T(8,128)(2,1)S(1)}, f32[3,4,512]{2...) custom-call(s32[1]{0:T(128)} %bitcast.1.me_ref, ...), custom_call_target="tpu_custom_call" | custom-call | flops 2000000000 | bytes 100000 | tf_op jit(solution)/shard_map/pallas_call | solution.py:295
  341.5 9.6 %collective-permute-done.56 = bf16[96,2048]{1,0:T(8,128)(2,1)S(1)} collective-permute-done((bf16[96,2048]{1,0:T(8,128)(2,1)S(1)}, bf16[96,2048]{1,0:T(8,128)(2,1)S(1)}, u32[]{:S(2)}, u32[]{:S(2)}) %collective-permute-start.56) | collective-permute-done | bytes 393248 | tf_op jit(solution)/shard_map/ppermute | solution.py:805
  355.9 7.0 collective-permute-done.58.refs_1_
  363.0 4.3 collective-permute-done.57
  368.6 12.7 %shard_map.202 = (f32[96,2048]{1,0:T(8,128)S(1)}, f32[96,2048]{1,0:T(8,128)S(1)}, bf16[96,2048]{1,0:T(8,128)(2,1)S(1)}, bf16[96,2048]{1,0:T(8,128)(2,1)}, bf16[768,2816]{1,0:T(8,128)(2,1)}) custom-call(s32[1]{0:T(128)} %bitcast.1.me_ref, bf16[96,2048]{1,0:T(8,128)(2,1)S(1)} %broadcast_select_fusion.2.refs_0_.base_ref, ...), custom_call_target="tpu_custom_call" | custom-call | flops 2000000000 | bytes 100000 | tf_op jit(solution)/shard_map/pallas_call | solution.py:295
  387.4 12.9 %shard_map.203 = (f32[96,2048]{1,0:T(8,128)S(1)}, f32[96,2048]{1,0:T(8,128)S(1)}, bf16[96,2048]{1,0:T(8,128)(2,1)S(1)}, bf16[96,2048]{1,0:T(8,128)(2,1)S(1)}, bf16[768,2816]{1,0:T(8,128)(2,1)}) custom-call(s32[1]{0:T(128)} %bitcast.1.me_ref, bf16[96,2048]{1,0:T(8,128)(2,1)S(1)} %broadcast_select_fusion.3.refs_0_.base_ref, ...), custom_call_target="tpu_custom_call", output_to_operand_aliasing={{4}: (9, {})} | custom-call | flops 2000000000 | bytes 100000 | tf_op jit(solution)/shard_map/pallas_call | solution.py:295
  409.2 14.6 %convolution_convert_fusion = bf16[2048,2816]{1,0:T(8,128)(2,1)} fusion(bf16[768,2816]{1,0:T(8,128)(2,1)} %get-tuple-element.510, bf16[384,2048]{1,0:T(8,128)(2,1)} %get-tuple-element.504, bf16[384,2048]{1,0:T(8,128)(2,1)} %get-tuple-element.503), kind=kOutput, calls=%fused_computation | convolution fusion | flops 8870428672 | bytes 19005440 | tf_op jit(solution)/shard_map/dot_general | solution.py:786
  427.3 9.5 %collective-permute-done.65.refs_2_ = bf16[96,2048]{1,0:T(8,128)(2,1)S(1)} collective-permute-done((bf16[96,2048]{1,0:T(8,128)(2,1)}, bf16[96,2048]{1,0:T(8,128)(2,1)S(1)}, u32[]{:S(2)}, u32[]{:S(2)}) %collective-permute-start.65) | collective-permute-done | bytes 393248 | tf_op jit(solution)/shard_map/ppermute | solution.py:800
  443.8 6.3 collective-permute-done.70.refs_2_
  451.6 8.9 %collective-permute-done.73.refs_1_ = bf16[96,2048]{1,0:T(8,128)(2,1)S(1)} collective-permute-done((bf16[96,2048]{1,0:T(8,128)(2,1)S(1)}, bf16[96,2048]{1,0:T(8,128)(2,1)S(1)}, u32[]{:S(2)}, u32[]{:S(2)}) %collective-permute-start.73) | collective-permute-done | bytes 393248 | tf_op jit(solution)/shard_map/ppermute | solution.py:800
  462.3 19.3 %shard_map.206 = (f32[96,2048]{1,0:T(8,128)}, f32[96,2048]{1,0:T(8,128)}, bf16[96,2048]{1,0:T(8,128)(2,1)S(1)}, bf16[96,2048]{1,0:T(8,128)(2,1)S(1)}, f32[3,4,51...) custom-call(s32[1]{0:T(128)} %bitcast.1.me_ref, ...), custom_call_target="tpu_custom_call" | custom-call | flops 2000000000 | bytes 100000 | tf_op jit(solution)/shard_map/pallas_call | solution.py:295
  485.6 19.4 %shard_map.208 = (f32[96,2048]{1,0:T(8,128)}, f32[96,2048]{1,0:T(8,128)}, bf16[96,2048]{1,0:T(8,128)(2,1)}, bf16[96,2048]{1,0:T(8,128)(2,1)S(1)}, f32[3,4,512]{2...) custom-call(s32[1]{0:T(128)} %bitcast.1.me_ref, ...), custom_call_target="tpu_custom_call" | custom-call | flops 2000000000 | bytes 100000 | tf_op jit(solution)/shard_map/pallas_call | solution.py:295
  505.7 8.3 %convolution_convert_fusion.1 = bf16[2048,1536]{1,0:T(8,128)(2,1)} fusion(bf16[768,2048]{1,0:T(8,128)(2,1)S(1)} %constant_dynamic-update-slice_fusion, bf16[384,1536]{1,0:T(8,128)(2,1)} %get-tuple-element.566, bf16[384,1536]{1,0:T(8,128)(2,1)S(1)} %copy-done.98), kind=kOutput, calls=%fused_computation.1 | convolution fusion | flops 4839702528 | bytes 11796480 | tf_op jit(solution)/shard_map/dot_general | solution.py:786
  514.0 106.7 %reduce-scatter.3.cloned.1.call-done = bf16[512,2816]{1,0:T(8,128)(2,1)} async-done(((bf16[2048,2816]{1,0:T(8,128)(2,1)}), bf16[512,2816]{1,0:T(8,128)(2,1)}) %reduce-scatter.3.cloned.1.call-update) | async-done | bytes 2883600 | tf_op jit(solution)/shard_map/reduce_scatter | solution.py:1059
  624.5 2.7 collective-permute-start.88
  627.2 3.3 collective-permute-done.86
  630.5 7.3 collective-permute-done.87
  641.5 9.5 %collective-permute-done.81.refs_2_ = bf16[96,2048]{1,0:T(8,128)(2,1)S(1)} collective-permute-done((bf16[96,2048]{1,0:T(8,128)(2,1)S(1)}, bf16[96,2048]{1,0:T(8,128)(2,1)S(1)}, u32[]{:S(2)}, u32[]{:S(2)}) %collective-permute-start.81) | collective-permute-done | bytes 393248 | tf_op jit(solution)/shard_map/ppermute | solution.py:800
  660.8 4.8 collective-permute-start.89
  678.7 4.8 collective-permute-start.91
  688.4 3.5 collective-permute-start.85
  691.9 5.7 collective-permute-done.92
  718.1 4.2 fusion
  722.5 14.1 %collective-permute-done.96 = bf16[2,4,96,512]{3,2,0,1:T(8,128)(2,1)S(1)} collective-permute-done((bf16[2,4,96,512]{3,2,0,1:T(8,128)(2,1)S(1)}, bf16[2,4,96,512]{3,2,0,1:T(8,128)(2,1)S(1)}, u32[]{:S(2)}, u32[]{:S(2)}) %collective-permute-start.96) | collective-permute-done | bytes 786464 | tf_op jit(solution)/shard_map/ppermute | solution.py:800
  736.6 2.9 maximum_convert_fusion
  744.3 13.2 %reduce-scatter.5.cloned.1.call-done = bf16[512,1536]{1,0:T(8,128)(2,1)} async-done(((bf16[2048,1536]{1,0:T(8,128)(2,1)}), bf16[512,1536]{1,0:T(8,128)(2,1)}) %reduce-scatter.5.cloned.1.call-update) | async-done | bytes 1572880 | tf_op jit(solution)/shard_map/reduce_scatter | solution.py:1059
  (517 shorter events, 193.0 us)
Async XLA Ops:
  7.2 395.5 %all-gather.9.cloned.1.call-start = ((), (), s32[]{:S(2)}) async-start(), calls=%async_computation.4 | async-start | bytes 1966080 | tf_op jit(solution)/shard_map/all_gather | solution.py:1025
  30.7 17.3 %collective-permute-start.1 = (bf16[96,2048]{1,0:T(8,128)(2,1)S(1)}, bf16[96,2048]{1,0:T(8,128)(2,1)S(1)}, u32[]{:S(2)}, u32[]{:S(2)}) collective-permute-start(bf16[96,2048]{1,0:T(8,128)(2,1)S(1)} %convert_add_fusion.6), channel_id=1, source_target_pairs={{0,2},{1,3},{2,0},{3,1},{4,6},{5,7},{6,4},{7,5},{8,10},{9,11},{10,... | collective-permute-start | bytes 1179656 | tf_op jit(solution)/shard_map/ppermute | solution.py:800
  49.8 11.2 %collective-permute-start.4 = (bf16[96,2048]{1,0:T(8,128)(2,1)S(1)}, bf16[96,2048]{1,0:T(8,128)(2,1)S(1)}, u32[]{:S(2)}, u32[]{:S(2)}) collective-permute-start(bf16[96,2048]{1,0:T(8,128)(2,1)S(1)} %add_convert_fusion.8), channel_id=1, source_target_pairs={{0,2},{1,3},{2,0},{3,1},{4,6},{5,7},{6,4},{7,5},{8,10},{9,11},{10,... | collective-permute-start | bytes 1179656 | tf_op jit(solution)/shard_map/ppermute | solution.py:800
  71.8 13.3 %collective-permute-start.7 = (bf16[96,2048]{1,0:T(8,128)(2,1)S(1)}, bf16[96,2048]{1,0:T(8,128)(2,1)S(1)}, u32[]{:S(2)}, u32[]{:S(2)}) collective-permute-start(bf16[96,2048]{1,0:T(8,128)(2,1)S(1)} %get-tuple-element.334.refs_0_), channel_id=1, source_target_pairs={{0,2},{1,3},{2,0},{3,1},{4,6},{5,7},{6,4},{7,5},{8,10},{9,11},{10,... | collective-permute-start | bytes 1179656 | tf_op jit(solution)/shard_map/ppermute | solution.py:800
  89.2 15.6 %collective-permute-start.13 = (bf16[96,2048]{1,0:T(8,128)(2,1)}, bf16[96,2048]{1,0:T(8,128)(2,1)}, u32[]{:S(2)}, u32[]{:S(2)}) collective-permute-start(bf16[96,2048]{1,0:T(8,128)(2,1)} %convert_add_fusion.5), channel_id=1, source_target_pairs={{0,2},{1,3},{2,0},{3,1},{4,6},{5,7},{6,4},{7,5},{8,10},{9,11},{10,... | collective-permute-start | bytes 1179656 | tf_op jit(solution)/shard_map/ppermute | solution.py:800
  90.0 15.4 %collective-permute-start.17 = (bf16[96,2048]{1,0:T(8,128)(2,1)}, bf16[96,2048]{1,0:T(8,128)(2,1)}, u32[]{:S(2)}, u32[]{:S(2)}) collective-permute-start(bf16[96,2048]{1,0:T(8,128)(2,1)} %get-tuple-element.351), channel_id=1, source_target_pairs={{0,1},{1,0},{2,3},{3,2},{4,5},{5,4},{6,7},{7,6},{8,9},{9,8},{10,11... | collective-permute-start | bytes 1179656 | tf_op jit(solution)/shard_map/ppermute | solution.py:800
  106.7 12.0 %collective-permute-start.18 = (bf16[96,2048]{1,0:T(8,128)(2,1)S(1)}, bf16[96,2048]{1,0:T(8,128)(2,1)S(1)}, u32[]{:S(2)}, u32[]{:S(2)}) collective-permute-start(bf16[96,2048]{1,0:T(8,128)(2,1)S(1)} %add_convert_fusion.6), channel_id=1, source_target_pairs={{0,16},{1,17},{2,18},{3,19},{4,20},{5,21},{6,22},{7,23},{8,24},{9,... | collective-permute-start | bytes 1179656 | tf_op jit(solution)/shard_map/ppermute | solution.py:805
  110.2 13.0 %collective-permute-start.14 = (bf16[96,2048]{1,0:T(8,128)(2,1)S(1)}, bf16[96,2048]{1,0:T(8,128)(2,1)S(1)}, u32[]{:S(2)}, u32[]{:S(2)}) collective-permute-start(bf16[96,2048]{1,0:T(8,128)(2,1)S(1)} %get-tuple-element.345), channel_id=1, source_target_pairs={{0,1},{1,0},{2,3},{3,2},{4,5},{5,4},{6,7},{7,6},{8,9},{9,8},{10,11... | collective-permute-start | bytes 1179656 | tf_op jit(solution)/shard_map/ppermute | solution.py:800
  110.3 11.6 %collective-permute-start.16 = (bf16[96,2048]{1,0:T(8,128)(2,1)S(1)}, bf16[96,2048]{1,0:T(8,128)(2,1)S(1)}, u32[]{:S(2)}, u32[]{:S(2)}) collective-permute-start(bf16[96,2048]{1,0:T(8,128)(2,1)S(1)} %add_convert_fusion.7), channel_id=1, source_target_pairs={{0,2},{1,3},{2,0},{3,1},{4,6},{5,7},{6,4},{7,5},{8,10},{9,11},{10,... | collective-permute-start | bytes 1179656 | tf_op jit(solution)/shard_map/ppermute | solution.py:800
  134.1 18.0 %collective-permute-start.21 = (bf16[96,2048]{1,0:T(8,128)(2,1)S(1)}, bf16[96,2048]{1,0:T(8,128)(2,1)S(1)}, u32[]{:S(2)}, u32[]{:S(2)}) collective-permute-start(bf16[96,2048]{1,0:T(8,128)(2,1)S(1)} %get-tuple-element.374.refs_0_), channel_id=1, source_target_pairs={{0,2},{1,3},{2,0},{3,1},{4,6},{5,7},{6,4},{7,5},{8,10},{9,11},{10,... | collective-permute-start | bytes 1179656 | tf_op jit(solution)/shard_map/ppermute | solution.py:800
  152.1 250.6 %all-gather.11.cloned.1.call-start = ((), (), s32[]{:S(2)}) async-start(), calls=%async_computation.5 | async-start | bytes 1966080 | tf_op jit(solution)/shard_map/all_gather | solution.py:1025
  155.9 20.6 %collective-permute-start.27 = (bf16[96,2048]{1,0:T(8,128)(2,1)}, bf16[96,2048]{1,0:T(8,128)(2,1)}, u32[]{:S(2)}, u32[]{:S(2)}) collective-permute-start(bf16[96,2048]{1,0:T(8,128)(2,1)} %convert_add_fusion.4), channel_id=1, source_target_pairs={{0,2},{1,3},{2,0},{3,1},{4,6},{5,7},{6,4},{7,5},{8,10},{9,11},{10,... | collective-permute-start | bytes 1179656 | tf_op jit(solution)/shard_map/ppermute | solution.py:800
  176.5 226.2 %all-gather.5.cloned.1.call-start = ((), (), s32[]{:S(2)}) async-start(), calls=%async_computation.2 | async-start | bytes 5406720 | tf_op jit(solution)/shard_map/all_gather | solution.py:1024
  179.8 11.2 %collective-permute-start.30 = (bf16[96,2048]{1,0:T(8,128)(2,1)S(1)}, bf16[96,2048]{1,0:T(8,128)(2,1)S(1)}, u32[]{:S(2)}, u32[]{:S(2)}) collective-permute-start(bf16[96,2048]{1,0:T(8,128)(2,1)S(1)} %add_convert_fusion.4), channel_id=1, source_target_pairs={{0,2},{1,3},{2,0},{3,1},{4,6},{5,7},{6,4},{7,5},{8,10},{9,11},{10,... | collective-permute-start | bytes 1179656 | tf_op jit(solution)/shard_map/ppermute | solution.py:800
  201.8 11.8 %collective-permute-start.33 = (bf16[96,2048]{1,0:T(8,128)(2,1)S(1)}, bf16[96,2048]{1,0:T(8,128)(2,1)S(1)}, u32[]{:S(2)}, u32[]{:S(2)}) collective-permute-start(bf16[96,2048]{1,0:T(8,128)(2,1)S(1)} %get-tuple-element.408.refs_0_), channel_id=1, source_target_pairs={{0,2},{1,3},{2,0},{3,1},{4,6},{5,7},{6,4},{7,5},{8,10},{9,11},{10,... | collective-permute-start | bytes 1179656 | tf_op jit(solution)/shard_map/ppermute | solution.py:800
  213.7 189.0 %all-gather.7.cloned.1.call-start = ((), (), s32[]{:S(2)}) async-start(), calls=%async_computation.3 | async-start | bytes 5406720 | tf_op jit(solution)/shard_map/all_gather | solution.py:1024
  232.9 25.1 %collective-permute-start.39 = (bf16[96,2048]{1,0:T(8,128)(2,1)S(1)}, bf16[96,2048]{1,0:T(8,128)(2,1)S(1)}, u32[]{:S(2)}, u32[]{:S(2)}) collective-permute-start(bf16[96,2048]{1,0:T(8,128)(2,1)S(1)} %convert_add_fusion.3), channel_id=1, source_target_pairs={{0,2},{1,3},{2,0},{3,1},{4,6},{5,7},{6,4},{7,5},{8,10},{9,11},{10,... | collective-permute-start | bytes 1179656 | tf_op jit(solution)/shard_map/ppermute | solution.py:800
  259.4 361.3 %reduce-scatter.3.cloned.1.call-start = ((), (), s32[]{:S(2)}) async-start(), calls=%async_computation.6 | async-start | bytes 14417920 | tf_op jit(solution)/shard_map/reduce_scatter | solution.py:1059
  262.8 11.4 %collective-permute-start.42 = (bf16[96,2048]{1,0:T(8,128)(2,1)}, bf16[96,2048]{1,0:T(8,128)(2,1)S(1)}, u32[]{:S(2)}, u32[]{:S(2)}) collective-permute-start(bf16[96,2048]{1,0:T(8,128)(2,1)} %add_convert_fusion.3), channel_id=1, source_target_pairs={{0,2},{1,3},{2,0},{3,1},{4,6},{5,7},{6,4},{7,5},{8,10},{9,11},{10,... | collective-permute-start | bytes 1179656 | tf_op jit(solution)/shard_map/ppermute | solution.py:800
  275.0 12.7 %collective-permute-start.46 = (bf16[96,2048]{1,0:T(8,128)(2,1)S(1)}, bf16[96,2048]{1,0:T(8,128)(2,1)S(1)}, u32[]{:S(2)}, u32[]{:S(2)}) collective-permute-start(bf16[96,2048]{1,0:T(8,128)(2,1)S(1)} %get-tuple-element.433.refs_0_), channel_id=1, source_target_pairs={{0,1},{1,0},{2,3},{3,2},{4,5},{5,4},{6,7},{7,6},{8,9},{9,8},{10,11... | collective-permute-start | bytes 1179656 | tf_op jit(solution)/shard_map/ppermute | solution.py:800
  286.8 20.5 %collective-permute-start.45 = (bf16[96,2048]{1,0:T(8,128)(2,1)S(1)}, bf16[96,2048]{1,0:T(8,128)(2,1)S(1)}, u32[]{:S(2)}, u32[]{:S(2)}) collective-permute-start(bf16[96,2048]{1,0:T(8,128)(2,1)S(1)} %get-tuple-element.450.refs_0_), channel_id=1, source_target_pairs={{0,2},{1,3},{2,0},{3,1},{4,6},{5,7},{6,4},{7,5},{8,10},{9,11},{10,... | collective-permute-start | bytes 1179656 | tf_op jit(solution)/shard_map/ppermute | solution.py:800
  310.4 20.5 %collective-permute-start.51 = (bf16[96,2048]{1,0:T(8,128)(2,1)S(1)}, bf16[96,2048]{1,0:T(8,128)(2,1)S(1)}, u32[]{:S(2)}, u32[]{:S(2)}) collective-permute-start(bf16[96,2048]{1,0:T(8,128)(2,1)S(1)} %convert_add_fusion.2), channel_id=1, source_target_pairs={{0,2},{1,3},{2,0},{3,1},{4,6},{5,7},{6,4},{7,5},{8,10},{9,11},{10,... | collective-permute-start | bytes 1179656 | tf_op jit(solution)/shard_map/ppermute | solution.py:800
  311.6 20.5 %collective-permute-start.55 = (bf16[96,2048]{1,0:T(8,128)(2,1)}, bf16[96,2048]{1,0:T(8,128)(2,1)}, u32[]{:S(2)}, u32[]{:S(2)}) collective-permute-start(bf16[96,2048]{1,0:T(8,128)(2,1)} %get-tuple-element.474), channel_id=1, source_target_pairs={{0,1},{1,0},{2,3},{3,2},{4,5},{5,4},{6,7},{7,6},{8,9},{9,8},{10,11... | collective-permute-start | bytes 1179656 | tf_op jit(solution)/shard_map/ppermute | solution.py:800
  338.1 13.1 %collective-permute-start.56 = (bf16[96,2048]{1,0:T(8,128)(2,1)S(1)}, bf16[96,2048]{1,0:T(8,128)(2,1)S(1)}, u32[]{:S(2)}, u32[]{:S(2)}) collective-permute-start(bf16[96,2048]{1,0:T(8,128)(2,1)S(1)} %get-tuple-element.475), channel_id=1, source_target_pairs={{16,0},{17,1},{18,2},{19,3},{20,4},{21,5},{22,6},{23,7},{24,8},{25... | collective-permute-start | bytes 1179656 | tf_op jit(solution)/shard_map/ppermute | solution.py:805
  339.4 13.7 %collective-permute-start.52 = (bf16[96,2048]{1,0:T(8,128)(2,1)}, bf16[96,2048]{1,0:T(8,128)(2,1)S(1)}, u32[]{:S(2)}, u32[]{:S(2)}) collective-permute-start(bf16[96,2048]{1,0:T(8,128)(2,1)} %get-tuple-element.468), channel_id=1, source_target_pairs={{0,1},{1,0},{2,3},{3,2},{4,5},{5,4},{6,7},{7,6},{8,9},{9,8},{10,11... | collective-permute-start | bytes 1179656 | tf_op jit(solution)/shard_map/ppermute | solution.py:800
  340.6 11.6 %collective-permute-start.54 = (bf16[96,2048]{1,0:T(8,128)(2,1)S(1)}, bf16[96,2048]{1,0:T(8,128)(2,1)S(1)}, u32[]{:S(2)}, u32[]{:S(2)}) collective-permute-start(bf16[96,2048]{1,0:T(8,128)(2,1)S(1)} %add_convert_fusion.2), channel_id=1, source_target_pairs={{0,2},{1,3},{2,0},{3,1},{4,6},{5,7},{6,4},{7,5},{8,10},{9,11},{10,... | collective-permute-start | bytes 1179656 | tf_op jit(solution)/shard_map/ppermute | solution.py:800
  354.6 12.7 %collective-permute-start.57 = (bf16[96,2048]{1,0:T(8,128)(2,1)S(1)}, bf16[96,2048]{1,0:T(8,128)(2,1)S(1)}, u32[]{:S(2)}, u32[]{:S(2)}) collective-permute-start(bf16[96,2048]{1,0:T(8,128)(2,1)S(1)} %get-tuple-element.477), channel_id=1, source_target_pairs={{16,0},{17,1},{18,2},{19,3},{20,4},{21,5},{22,6},{23,7},{24,8},{25... | collective-permute-start | bytes 1179656 | tf_op jit(solution)/shard_map/ppermute | solution.py:805
  355.9 12.7 %collective-permute-start.60 = (bf16[96,2048]{1,0:T(8,128)(2,1)S(1)}, bf16[96,2048]{1,0:T(8,128)(2,1)S(1)}, u32[]{:S(2)}, u32[]{:S(2)}) collective-permute-start(bf16[96,2048]{1,0:T(8,128)(2,1)S(1)} %broadcast_select_fusion.2.refs_0_.base_ref), channel_id=1, source_target_pairs={{0,1},{1,0},{2,3},{3,2},{4,5},{5,4},{6,7},{7,6},{8,9},{9,8},{10,11... | collective-permute-start | bytes 1179656 | tf_op jit(solution)/shard_map/ppermute | solution.py:800
  367.3 14.8 %collective-permute-start.59 = (bf16[96,2048]{1,0:T(8,128)(2,1)S(1)}, bf16[96,2048]{1,0:T(8,128)(2,1)}, u32[]{:S(2)}, u32[]{:S(2)}) collective-permute-start(bf16[96,2048]{1,0:T(8,128)(2,1)S(1)} %broadcast_select_fusion.3.refs_0_.base_ref), channel_id=1, source_target_pairs={{0,2},{1,3},{2,0},{3,1},{4,6},{5,7},{6,4},{7,5},{8,10},{9,11},{10,... | collective-permute-start | bytes 1179656 | tf_op jit(solution)/shard_map/ppermute | solution.py:800
  403.6 20.2 %collective-permute-start.66 = (bf16[2,96,512]{2,1,0:T(8,128)(2,1)}, bf16[2,96,512]{2,1,0:T(8,128)(2,1)}, u32[]{:S(2)}, u32[]{:S(2)}) collective-permute-start(bf16[2,96,512]{2,1,0:T(8,128)(2,1)} %get-tuple-element.615), channel_id=1, source_target_pairs={{0,4},{4,8},{8,12},{12,0},{1,5},{5,9},{9,13},{13,1},{2,6},{6,10},{... | collective-permute-start | bytes 589832 | tf_op jit(solution)/shard_map/ppermute | solution.py:931
  405.2 18.6 %collective-permute-start.67 = (bf16[2,96,512]{2,1,0:T(8,128)(2,1)}, bf16[2,96,512]{2,1,0:T(8,128)(2,1)}, u32[]{:S(2)}, u32[]{:S(2)}) collective-permute-start(bf16[2,96,512]{2,1,0:T(8,128)(2,1)} %get-tuple-element.616), channel_id=1, source_target_pairs={{0,8},{4,12},{8,0},{12,4},{1,9},{5,13},{9,1},{13,5},{2,10},{6,14},... | collective-permute-start | bytes 589832 | tf_op jit(solution)/shard_map/ppermute | solution.py:931
  407.9 15.9 %collective-permute-start.68 = (bf16[2,96,512]{2,1,0:T(8,128)(2,1)}, bf16[2,96,512]{2,1,0:T(8,128)(2,1)}, u32[]{:S(2)}, u32[]{:S(2)}) collective-permute-start(bf16[2,96,512]{2,1,0:T(8,128)(2,1)} %get-tuple-element.617), channel_id=1, source_target_pairs={{0,12},{4,0},{8,4},{12,8},{1,13},{5,1},{9,5},{13,9},{2,14},{6,2},{... | collective-permute-start | bytes 589832 | tf_op jit(solution)/shard_map/ppermute | solution.py:931
  426.2 331.3 %reduce-scatter.5.cloned.1.call-start = ((), (), s32[]{:S(2)}) async-start(), calls=%async_computation.7 | async-start | bytes 7864320 | tf_op jit(solution)/shard_map/reduce_scatter | solution.py:1059
  438.9 11.2 %collective-permute-start.70 = (bf16[96,2048]{1,0:T(8,128)(2,1)S(1)}, bf16[96,2048]{1,0:T(8,128)(2,1)S(1)}, u32[]{:S(2)}, u32[]{:S(2)}) collective-permute-start(bf16[96,2048]{1,0:T(8,128)(2,1)S(1)} %add_convert_fusion.1), channel_id=1, source_target_pairs={{0,2},{1,3},{2,0},{3,1},{4,6},{5,7},{6,4},{7,5},{8,10},{9,11},{10,... | collective-permute-start | bytes 1179656 | tf_op jit(solution)/shard_map/ppermute | solution.py:800
  451.1 11.2 %collective-permute-start.75 = (bf16[96,2048]{1,0:T(8,128)(2,1)S(1)}, bf16[96,2048]{1,0:T(8,128)(2,1)S(1)}, u32[]{:S(2)}, u32[]{:S(2)}) collective-permute-start(bf16[96,2048]{1,0:T(8,128)(2,1)S(1)} %get-tuple-element.568.refs_0_), channel_id=1, source_target_pairs={{0,1},{1,0},{2,3},{3,2},{4,5},{5,4},{6,7},{7,6},{8,9},{9,8},{10,11... | collective-permute-start | bytes 1179656 | tf_op jit(solution)/shard_map/ppermute | solution.py:800
  461.3 20.4 %collective-permute-start.74 = (bf16[96,2048]{1,0:T(8,128)(2,1)S(1)}, bf16[96,2048]{1,0:T(8,128)(2,1)S(1)}, u32[]{:S(2)}, u32[]{:S(2)}) collective-permute-start(bf16[96,2048]{1,0:T(8,128)(2,1)S(1)} %get-tuple-element.569.refs_0_), channel_id=1, source_target_pairs={{0,2},{1,3},{2,0},{3,1},{4,6},{5,7},{6,4},{7,5},{8,10},{9,11},{10,... | collective-permute-start | bytes 1179656 | tf_op jit(solution)/shard_map/ppermute | solution.py:800
  622.3 15.6 %collective-permute-start.87 = (bf16[2,96,512]{2,1,0:T(8,128)(2,1)S(1)}, bf16[2,96,512]{2,1,0:T(8,128)(2,1)S(1)}, u32[]{:S(2)}, u32[]{:S(2)}) collective-permute-start(bf16[2,96,512]{2,1,0:T(8,128)(2,1)S(1)} %get-tuple-element.608), channel_id=1, source_target_pairs={{0,8},{4,12},{8,0},{12,4},{1,9},{5,13},{9,1},{13,5},{2,10},{6,14},... | collective-permute-start | bytes 589832 | tf_op jit(solution)/shard_map/ppermute | solution.py:931
  624.5 13.4 %collective-permute-start.88 = (bf16[2,96,512]{2,1,0:T(8,128)(2,1)S(1)}, bf16[2,96,512]{2,1,0:T(8,128)(2,1)S(1)}, u32[]{:S(2)}, u32[]{:S(2)}) collective-permute-start(bf16[2,96,512]{2,1,0:T(8,128)(2,1)S(1)} %get-tuple-element.609), channel_id=1, source_target_pairs={{0,12},{4,0},{8,4},{12,8},{1,13},{5,1},{9,5},{13,9},{2,14},{6,2},{... | collective-permute-start | bytes 589832 | tf_op jit(solution)/shard_map/ppermute | solution.py:931
  651.8 17.5 %collective-permute-start.77 = (bf16[96,2048]{1,0:T(8,128)(2,1)S(1)}, bf16[96,2048]{1,0:T(8,128)(2,1)}, u32[]{:S(2)}, u32[]{:S(2)}) collective-permute-start(bf16[96,2048]{1,0:T(8,128)(2,1)S(1)} %get-tuple-element.540), channel_id=1, source_target_pairs={{0,1},{1,0},{2,3},{3,2},{4,5},{5,4},{6,7},{7,6},{8,9},{9,8},{10,11... | collective-permute-start | bytes 1179656 | tf_op jit(solution)/shard_map/ppermute | solution.py:800
  660.7 13.2 %collective-permute-start.82 = (bf16[96,2048]{1,0:T(8,128)(2,1)}, bf16[96,2048]{1,0:T(8,128)(2,1)}, u32[]{:S(2)}, u32[]{:S(2)}) collective-permute-start(bf16[96,2048]{1,0:T(8,128)(2,1)} %get-tuple-element.558), channel_id=1, source_target_pairs={{0,1},{1,0},{2,3},{3,2},{4,5},{5,4},{6,7},{7,6},{8,9},{9,8},{10,11... | collective-permute-start | bytes 1179656 | tf_op jit(solution)/shard_map/ppermute | solution.py:800
  660.8 22.7 %collective-permute-start.89 = (f32[14336]{0:T(1024)S(1)}, f32[14336]{0:T(1024)}, u32[]{:S(2)}, u32[]{:S(2)}) collective-permute-start(f32[14336]{0:T(1024)S(1)} %constant_dynamic-update-slice_fusion.11), channel_id=1, source_target_pairs={{0,4},{4,0},{8,12},{12,8},{1,5},{5,1},{9,13},{13,9},{2,6},{6,2},{1... | collective-permute-start | bytes 172040 | tf_op jit(solution)/shard_map/ppermute | solution.py:800
  667.8 32.5 %collective-permute-start.95 = (bf16[2,4,96,512]{3,2,0,1:T(8,128)(2,1)}, bf16[2,4,96,512]{3,2,0,1:T(8,128)(2,1)}, u32[]{:S(2)}, u32[]{:S(2)}) collective-permute-start(bf16[2,4,96,512]{3,2,0,1:T(8,128)(2,1)} %pad_maximum_fusion.2), channel_id=1, source_target_pairs={{0,2},{1,3},{2,0},{3,1},{4,6},{5,7},{6,4},{7,5},{8,10},{9,11},{10,... | collective-permute-start | bytes 2359304 | tf_op jit(solution)/shard_map/ppermute | solution.py:800
  683.5 24.8 %collective-permute-start.99 = (bf16[2,4,96,512]{3,2,0,1:T(8,128)(2,1)}, bf16[2,4,96,512]{3,2,0,1:T(8,128)(2,1)}, u32[]{:S(2)}, u32[]{:S(2)}) collective-permute-start(bf16[2,4,96,512]{3,2,0,1:T(8,128)(2,1)} %pad_maximum_fusion.2), channel_id=1, source_target_pairs={{0,1},{1,0},{2,3},{3,2},{4,5},{5,4},{6,7},{7,6},{8,9},{9,8},{10,11... | collective-permute-start | bytes 2359304 | tf_op jit(solution)/shard_map/ppermute | solution.py:800
  684.3 14.3 %collective-permute-start.90 = (f32[14336]{0:T(1024)S(1)}, f32[14336]{0:T(1024)S(1)}, u32[]{:S(2)}, u32[]{:S(2)}) collective-permute-start(f32[14336]{0:T(1024)S(1)} %add.236), channel_id=1, source_target_pairs={{0,8},{4,12},{8,0},{12,4},{1,9},{5,13},{9,1},{13,5},{2,10},{6,14},... | collective-permute-start | bytes 172040 | tf_op jit(solution)/shard_map/ppermute | solution.py:800
  685.9 11.7 %collective-permute-start.92 = (f32[4224]{0:T(1024)S(1)}, f32[4224]{0:T(1024)S(1)}, u32[]{:S(2)}, u32[]{:S(2)}) collective-permute-start(f32[4224]{0:T(1024)S(1)} %fusion.34), channel_id=1, source_target_pairs={{0,8},{4,12},{8,0},{12,4},{1,9},{5,13},{9,1},{13,5},{2,10},{6,14},... | collective-permute-start | bytes 50696 | tf_op jit(solution)/shard_map/ppermute | solution.py:800
  688.4 16.4 %collective-permute-start.85 = (bf16[2,96,1024]{2,1,0:T(8,128)(2,1)}, bf16[2,96,1024]{2,1,0:T(8,128)(2,1)S(1)}, u32[]{:S(2)}, u32[]{:S(2)}) collective-permute-start(bf16[2,96,1024]{2,1,0:T(8,128)(2,1)} %fusion.10), channel_id=1, source_target_pairs={{0,16},{1,17},{2,18},{3,19},{4,20},{5,21},{6,22},{7,23},{8,24},{9,... | collective-permute-start | bytes 1179656 | tf_op jit(solution)/shard_map/ppermute | solution.py:805
  717.3 19.3 %collective-permute-start.96 = (bf16[2,4,96,512]{3,2,0,1:T(8,128)(2,1)S(1)}, bf16[2,4,96,512]{3,2,0,1:T(8,128)(2,1)S(1)}, u32[]{:S(2)}, u32[]{:S(2)}) collective-permute-start(bf16[2,4,96,512]{3,2,0,1:T(8,128)(2,1)S(1)} %copy-done.88), channel_id=1, source_target_pairs={{0,2},{1,3},{2,0},{3,1},{4,6},{5,7},{6,4},{7,5},{8,10},{9,11},{10,... | collective-permute-start | bytes 2359304 | tf_op jit(solution)/shard_map/ppermute | solution.py:800
  722.3 17.3 %collective-permute-start.97 = (bf16[2,4,96,512]{3,2,0,1:T(8,128)(2,1)S(1)}, bf16[2,4,96,512]{3,2,0,1:T(8,128)(2,1)S(1)}, u32[]{:S(2)}, u32[]{:S(2)}) collective-permute-start(bf16[2,4,96,512]{3,2,0,1:T(8,128)(2,1)S(1)} %copy-done.88), channel_id=1, source_target_pairs={{0,1},{1,0},{2,3},{3,2},{4,5},{5,4},{6,7},{7,6},{8,9},{9,8},{10,11... | collective-permute-start | bytes 2359304 | tf_op jit(solution)/shard_map/ppermute | solution.py:800
  (162 other events, 1457.9 us)
Sparse Core Ops, SparseCore 0:
  152.2 38.9 all-gather.8
  192.8 35.9 all-gather.10
  230.3 81.8 all-gather.4
  313.7 81.4 all-gather.6
  426.3 194.3 reduce-scatter.2
  639.2 118.2 reduce-scatter.4

commit v9 on v8

--- a/solution.py
+++ b/solution.py
@@ -22,7 +22,7 @@
 QUARTERS = 4
 ATTEND_KEPT = 9
 ROW_COPIES = 16
-VMEM_LIMIT = 50 * 1024 * 1024
+KEEP_GRANT, PASS_GRANT, EXPAND_BACK_GRANT, ATTEND_BACK_GRANT = 50, 47, 50, 50
 
 
 def mm(left, right):
@@ -287,7 +287,7 @@
     return [jax.ShapeDtypeStruct((share, width), F32 if k < count // 2 else BF16) for k in range(count)]
 
 
-def call(kernel, operands, rows, hbm, out_shape, hbm_shape, scratch_shapes, in_place=False):
+def call(kernel, operands, rows, hbm, out_shape, hbm_shape, scratch_shapes, grant, in_place=False):
     vmem = pl.BlockSpec(memory_space=pltpu.VMEM)
     far = pl.BlockSpec(memory_space=pltpu.HBM)
     blocks = isinstance(rows, list)
@@ -304,7 +304,7 @@
             {len(operands) + len(rows) + len(hbm) - 1: len(out_shape) + len(hbm_shape) - 1} if in_place else {}
         ),
         scratch_shapes=scratch_shapes + [pltpu.SemaphoreType.DMA((ROW_COPIES,))],
-        compiler_params=pltpu.CompilerParams(vmem_limit_bytes=VMEM_LIMIT),
+        compiler_params=pltpu.CompilerParams(vmem_limit_bytes=grant * 1024 * 1024),
         cost_estimate=pl.CostEstimate(flops=2 * 10**9, bytes_accessed=10**5, transcendentals=0),
     )(*operands, *rows, *hbm)
 
@@ -345,6 +345,7 @@
             pltpu.SemaphoreType.DMA((5,)),
             pltpu.SemaphoreType.DMA((ATTEND_KEPT,)),
         ],
+        KEEP_GRANT if save else PASS_GRANT,
     )
     return results[count:], results[:count]
 
@@ -409,6 +410,7 @@
         + ([] if save else [pltpu.VMEM(contract.shape[1:], BF16)])
         + [pltpu.SemaphoreType.DMA(((2 if save else 3) * QUARTERS,))]
         + ([pltpu.SemaphoreType.DMA((4,))] if save else []),
+        KEEP_GRANT if save else PASS_GRANT,
     )
     return (results, None) if save else (None, results)
 
@@ -480,6 +482,7 @@
             pltpu.SemaphoreType.DMA((QUARTERS + 2 + 2 * len(tiles_of(model, 2 * TILE)),)),
             pltpu.SemaphoreType.DMA((1,)),
         ],
+        EXPAND_BACK_GRANT,
         into > 0,
     )
     return results[count], results[:count]
@@ -673,6 +676,7 @@
             pltpu.SemaphoreType.DMA((ATTEND_KEPT + 3,)),
             pltpu.SemaphoreType.DMA((2,)),
         ],
+        ATTEND_BACK_GRANT,
     )
     return results[count + 2 :] + results[count : count + 2], results[:count]
 

time: 778 us -> 772 us (level)
    unnamed x216 -> x212, local copies, waits for them, and re-layouts: 46.8 us -> 45.6 us
where the time goes in v9:
time: 772 us; the launch traced here: 762 us
  waiting for transfers between devices  290 us (38%)
  Pallas kernels  249 us (32%)
  starting transfers between devices  78 us (10%)
  local copies, waits for them, and re-layouts  67.1 us (9%)
  matrix products  35 us (5%)
  other arithmetic  27 us (3%)
  between operations  16.2 us (2%)
    pallas_call x16, Pallas kernels, call(): pl.pallas_call(functools.partial(kernel, len(rows)), in_specs=[pl.BlockSp...  229 us
    ppermute x90, waiting for transfers between devices, flipped(): lax.ppermute(values, axis, [(i, i ^ bit) for i in range(lax.axis_size(axi...  138 us
    reduce_scatter x2, waiting for transfers between devices, spread(): return lax.psum_scatter(value, 'dp', scatter_dimension=axis, tiled=True)  120 us
    ppermute x90, starting transfers between devices, flipped(): lax.ppermute(values, axis, [(i, i ^ bit) for i in range(lax.axis_size(axi...  54 us
    unnamed x212, local copies, waits for them, and re-layouts  45.6 us
    dot_general x7, matrix products, product_left(): lax.dot_general(left, right, (((0,), (0,)), ((), ())), preferred_element_...  35 us
    ppermute x5, waiting for transfers between devices, shifted(): lax.ppermute(values, axis, [(i, i + distance) for i in devices if i + dis...  21.4 us
    pallas_call x14, Pallas kernels, small_call(): pl.pallas_call(kernel, in_specs=[vmem] * len(operands), out_specs=[vmem]...  18.5 us
  transfers between devices with their start and end apart: 107, of which 41 were waited for; matrix products, arithmetic and copies ran while one was open for 10% of the time, Pallas kernels for 31%

profile of v9, /device:TPU:0, one launch (start us, length us, event | category | flops | bytes accessed | tf_op | source)
XLA Modules:
  0.0 762.4 jit_solution(5970735097621984632)
XLA Ops:
  13.9 11.3 %shard_map.180 = (f32[96,2048]{1,0:T(8,128)S(1)}, f32[96,2048]{1,0:T(8,128)S(1)}, bf16[96,2048]{1,0:T(8,128)(2,1)S(1)}, bf16[96,2048]{1,0:T(8,128)(2,1)S(1)}) custom-call(s32[1]{0:T(128)} %bitcast.1.me_ref, s32[384,1]{1,0:T(8,128)S(1)} %broadcast_in_dim.49.seg_col_ref, s32[1,384]{1,0:T(1,128)S(1)} %broadcast_in_dim.43.seg_row_ref, ...), custom_call_target="tpu_custom_call" | custom-call | flops 2000000000 | bytes 100000 | tf_op jit(solution)/shard_map/pallas_call | solution.py:295
  27.2 2.9 collective-permute-start.1
  30.8 11.4 %shard_map.181 = (f32[96,2048]{1,0:T(8,128)S(1)}, f32[96,2048]{1,0:T(8,128)S(1)}, bf16[96,2048]{1,0:T(8,128)(2,1)S(1)}, bf16[96,2048]{1,0:T(8,128)(2,1)S(1)}) custom-call(s32[1]{0:T(128)} %bitcast.1.me_ref, s32[384,1]{1,0:T(8,128)S(1)} %broadcast_in_dim.48.seg_col_ref, s32[1,384]{1,0:T(1,128)S(1)} %broadcast_in_dim.20.seg_row_ref, ...), custom_call_target="tpu_custom_call" | custom-call | flops 2000000000 | bytes 100000 | tf_op jit(solution)/shard_map/pallas_call | solution.py:295
  44.9 10.4 %collective-permute-done.4.refs_3_ = bf16[96,2048]{1,0:T(8,128)(2,1)S(1)} collective-permute-done((bf16[96,2048]{1,0:T(8,128)(2,1)S(1)}, bf16[96,2048]{1,0:T(8,128)(2,1)S(1)}, u32[]{:S(2)}, u32[]{:S(2)}) %collective-permute-start.4) | collective-permute-done | bytes 393248 | tf_op jit(solution)/shard_map/ppermute | solution.py:804
  56.1 9.5 %collective-permute-done.6.refs_1_ = bf16[96,2048]{1,0:T(8,128)(2,1)S(1)} collective-permute-done((bf16[96,2048]{1,0:T(8,128)(2,1)S(1)}, bf16[96,2048]{1,0:T(8,128)(2,1)S(1)}, u32[]{:S(2)}, u32[]{:S(2)}) %collective-permute-start.6) | collective-permute-done | bytes 393248 | tf_op jit(solution)/shard_map/ppermute | solution.py:804
  67.4 11.9 %shard_map.184 = (f32[96,2048]{1,0:T(8,128)S(1)}, f32[96,2048]{1,0:T(8,128)S(1)}, bf16[96,2048]{1,0:T(8,128)(2,1)}, bf16[96,2048]{1,0:T(8,128)(2,1)S(1)}) custom-call(s32[1]{0:T(128)} %bitcast.1.me_ref, bf16[96,2048]{1,0:T(8,128)(2,1)S(1)} %get-tuple-element.324.refs_0_, bf16[96,2048]{1,0:T(8,128)(2,1)S(1)} %collective-permute-done.6.refs_1_, ...), custom_call_target="tpu_custom_call" | custom-call | flops 2000000000 | bytes 100000 | tf_op jit(solution)/shard_map/pallas_call | solution.py:295
  88.2 10.8 %shard_map.185 = (f32[96,2048]{1,0:T(8,128)S(1)}, f32[96,2048]{1,0:T(8,128)S(1)}, bf16[96,2048]{1,0:T(8,128)(2,1)S(1)}, bf16[96,2048]{1,0:T(8,128)(2,1)S(1)}) custom-call(s32[1]{0:T(128)} %bitcast.1.me_ref, bf16[96,2048]{1,0:T(8,128)(2,1)S(1)} %copy-done.29, bf16[96,2048]{1,0:T(8,128)(2,1)S(1)} %copy-done.31, bf16[96,2048]{1,0:T(8,128)(2,1)S(1)} %copy-done.33, ...), custom_call_target="tpu_custom_call" | custom-call | flops 2000000000 | bytes 100000 | tf_op jit(solution)/shard_map/pallas_call | solution.py:295
  100.9 3.4 collective-permute-start.18
  105.9 7.1 collective-permute-done.18
  119.9 7.0 collective-permute-done.20.refs_1_
  129.2 16.4 %shard_map.188 = (f32[96,2048]{1,0:T(8,128)}, f32[96,2048]{1,0:T(8,128)}, bf16[96,2048]{1,0:T(8,128)(2,1)S(1)}, bf16[96,2048]{1,0:T(8,128)(2,1)S(1)}, bf16[384,2...) custom-call(s32[1]{0:T(128)} %bitcast.1.me_ref, ...), custom_call_target="tpu_custom_call" | custom-call | flops 2000000000 | bytes 100000 | tf_op jit(solution)/shard_map/pallas_call | solution.py:295
  151.3 16.4 %shard_map.189 = (f32[96,2048]{1,0:T(8,128)}, f32[96,2048]{1,0:T(8,128)}, bf16[96,2048]{1,0:T(8,128)(2,1)S(1)}, bf16[96,2048]{1,0:T(8,128)(2,1)S(1)}, bf16[384,2...) custom-call(s32[1]{0:T(128)} %bitcast.1.me_ref, ...), custom_call_target="tpu_custom_call" | custom-call | flops 2000000000 | bytes 100000 | tf_op jit(solution)/shard_map/pallas_call | solution.py:295
  177.4 7.8 %collective-permute-done.30.refs_3_ = bf16[96,2048]{1,0:T(8,128)(2,1)S(1)} collective-permute-done((bf16[96,2048]{1,0:T(8,128)(2,1)S(1)}, bf16[96,2048]{1,0:T(8,128)(2,1)S(1)}, u32[]{:S(2)}, u32[]{:S(2)}) %collective-permute-start.30) | collective-permute-done | bytes 393248 | tf_op jit(solution)/shard_map/ppermute | solution.py:804
  186.6 9.1 %collective-permute-done.32.refs_1_ = bf16[96,2048]{1,0:T(8,128)(2,1)S(1)} collective-permute-done((bf16[96,2048]{1,0:T(8,128)(2,1)S(1)}, bf16[96,2048]{1,0:T(8,128)(2,1)S(1)}, u32[]{:S(2)}, u32[]{:S(2)}) %collective-permute-start.32) | collective-permute-done | bytes 393248 | tf_op jit(solution)/shard_map/ppermute | solution.py:804
  197.4 10.5 %shard_map.192 = (bf16[384,2048]{1,0:T(8,128)(2,1)}, bf16[384,1408]{1,0:T(8,128)(2,1)}, bf16[384,1408]{1,0:T(8,128)(2,1)S(1)}, bf16[384,1408]{1,0:T(8,128)(2,1)}) custom-call(s32[1]{0:T(128)} %bitcast.1.me_ref, bf16[96,2048]{1,0:T(8,128)(2,1)S(1)} %get-tuple-element.397.refs_0_, bf16[96,2048]{1,0:T(8,128)(2,1)S(1)} %collective-permute-done.32.refs_1_, ...), custom_call_target="tpu_custom_call" | custom-call | flops 2000000000 | bytes 100000 | tf_op jit(solution)/shard_map/pallas_call | solution.py:295
  208.0 4.3 slice_bitcast_fusion
  212.3 12.9 %shard_map.193 = (f32[96,2048]{1,0:T(8,128)S(1)}, f32[96,2048]{1,0:T(8,128)S(1)}, bf16[96,2048]{1,0:T(8,128)(2,1)}, bf16[96,2048]{1,0:T(8,128)(2,1)S(1)}, bf16[768,2816]{1,0:T(8,128)(2,1)}) custom-call(s32[1]{0:T(128)} %bitcast.1.me_ref, bf16[384,2048]{1,0:T(8,128)(2,1)} %get-tuple-element.595.refs_0_, ...), custom_call_target="tpu_custom_call" | custom-call | flops 2000000000 | bytes 100000 | tf_op jit(solution)/shard_map/pallas_call | solution.py:295
  228.2 10.9 %shard_map.194 = (bf16[384,2048]{1,0:T(8,128)(2,1)}, bf16[384,1408]{1,0:T(8,128)(2,1)}, bf16[384,1408]{1,0:T(8,128)(2,1)S(1)}, bf16[384,1408]{1,0:T(8,128)(2,1)}) custom-call(s32[1]{0:T(128)} %bitcast.1.me_ref, bf16[96,2048]{1,0:T(8,128)(2,1)S(1)} %get-tuple-element.408.refs_0_, bf16[96,2048]{1,0:T(8,128)(2,1)S(1)} %collective-permute-done.33.refs_1_, ...), custom_call_target="tpu_custom_call" | custom-call | flops 2000000000 | bytes 100000 | tf_op jit(solution)/shard_map/pallas_call | solution.py:295
  239.1 13.2 %shard_map.195 = (f32[96,2048]{1,0:T(8,128)S(1)}, f32[96,2048]{1,0:T(8,128)S(1)}, bf16[96,2048]{1,0:T(8,128)(2,1)S(1)}, bf16[96,2048]{1,0:T(8,128)(2,1)}, bf16[768,2816]{1,0:T(8,128)(2,1)}) custom-call(s32[1]{0:T(128)} %bitcast.1.me_ref, bf16[384,2048]{1,0:T(8,128)(2,1)} %get-tuple-element.407.refs_0_, ...), custom_call_target="tpu_custom_call", output_to_operand_aliasing={{4}: (6, {})} | custom-call | flops 2000000000 | bytes 100000 | tf_op jit(solution)/shard_map/pallas_call | solution.py:295
  264.9 3.5 collective-permute-done.42.refs_2_
  269.8 9.0 %collective-permute-done.44.refs_1_ = bf16[96,2048]{1,0:T(8,128)(2,1)S(1)} collective-permute-done((bf16[96,2048]{1,0:T(8,128)(2,1)S(1)}, bf16[96,2048]{1,0:T(8,128)(2,1)S(1)}, u32[]{:S(2)}, u32[]{:S(2)}) %collective-permute-start.44) | collective-permute-done | bytes 393248 | tf_op jit(solution)/shard_map/ppermute | solution.py:804
  282.1 19.6 %shard_map.198 = (f32[96,2048]{1,0:T(8,128)}, f32[96,2048]{1,0:T(8,128)}, bf16[96,2048]{1,0:T(8,128)(2,1)}, bf16[96,2048]{1,0:T(8,128)(2,1)S(1)}, f32[3,4,512]{2...) custom-call(s32[1]{0:T(128)} %bitcast.1.me_ref, ...), custom_call_target="tpu_custom_call" | custom-call | flops 2000000000 | bytes 100000 | tf_op jit(solution)/shard_map/pallas_call | solution.py:295
  305.9 19.2 %shard_map.199 = (f32[96,2048]{1,0:T(8,128)}, f32[96,2048]{1,0:T(8,128)}, bf16[96,2048]{1,0:T(8,128)(2,1)}, bf16[96,2048]{1,0:T(8,128)(2,1)S(1)}, f32[3,4,512]{2...) custom-call(s32[1]{0:T(128)} %bitcast.1.me_ref, ...), custom_call_target="tpu_custom_call" | custom-call | flops 2000000000 | bytes 100000 | tf_op jit(solution)/shard_map/pallas_call | solution.py:295
  335.9 9.6 %collective-permute-done.56 = bf16[96,2048]{1,0:T(8,128)(2,1)S(1)} collective-permute-done((bf16[96,2048]{1,0:T(8,128)(2,1)S(1)}, bf16[96,2048]{1,0:T(8,128)(2,1)S(1)}, u32[]{:S(2)}, u32[]{:S(2)}) %collective-permute-start.56) | collective-permute-done | bytes 393248 | tf_op jit(solution)/shard_map/ppermute | solution.py:809
  350.3 7.0 collective-permute-done.58.refs_1_
  357.3 4.3 collective-permute-done.57
  362.9 12.7 %shard_map.202 = (f32[96,2048]{1,0:T(8,128)S(1)}, f32[96,2048]{1,0:T(8,128)S(1)}, bf16[96,2048]{1,0:T(8,128)(2,1)S(1)}, bf16[96,2048]{1,0:T(8,128)(2,1)}, bf16[768,2816]{1,0:T(8,128)(2,1)}) custom-call(s32[1]{0:T(128)} %bitcast.1.me_ref, bf16[96,2048]{1,0:T(8,128)(2,1)S(1)} %broadcast_select_fusion.2.refs_0_.base_ref, ...), custom_call_target="tpu_custom_call" | custom-call | flops 2000000000 | bytes 100000 | tf_op jit(solution)/shard_map/pallas_call | solution.py:295
  381.7 12.9 %shard_map.203 = (f32[96,2048]{1,0:T(8,128)S(1)}, f32[96,2048]{1,0:T(8,128)S(1)}, bf16[96,2048]{1,0:T(8,128)(2,1)S(1)}, bf16[96,2048]{1,0:T(8,128)(2,1)S(1)}, bf16[768,2816]{1,0:T(8,128)(2,1)}) custom-call(s32[1]{0:T(128)} %bitcast.1.me_ref, bf16[96,2048]{1,0:T(8,128)(2,1)S(1)} %broadcast_select_fusion.3.refs_0_.base_ref, ...), custom_call_target="tpu_custom_call", output_to_operand_aliasing={{4}: (9, {})} | custom-call | flops 2000000000 | bytes 100000 | tf_op jit(solution)/shard_map/pallas_call | solution.py:295
  403.5 14.6 %convolution_convert_fusion = bf16[2048,2816]{1,0:T(8,128)(2,1)} fusion(bf16[768,2816]{1,0:T(8,128)(2,1)} %get-tuple-element.510, bf16[384,2048]{1,0:T(8,128)(2,1)} %get-tuple-element.504, bf16[384,2048]{1,0:T(8,128)(2,1)} %get-tuple-element.503), kind=kOutput, calls=%fused_computation | convolution fusion | flops 8870428672 | bytes 19005440 | tf_op jit(solution)/shard_map/dot_general | solution.py:790
  421.6 9.6 %collective-permute-done.65.refs_2_ = bf16[96,2048]{1,0:T(8,128)(2,1)S(1)} collective-permute-done((bf16[96,2048]{1,0:T(8,128)(2,1)}, bf16[96,2048]{1,0:T(8,128)(2,1)S(1)}, u32[]{:S(2)}, u32[]{:S(2)}) %collective-permute-start.65) | collective-permute-done | bytes 393248 | tf_op jit(solution)/shard_map/ppermute | solution.py:804
  438.0 6.3 collective-permute-done.70.refs_2_
  445.8 9.0 %collective-permute-done.73.refs_1_ = bf16[96,2048]{1,0:T(8,128)(2,1)S(1)} collective-permute-done((bf16[96,2048]{1,0:T(8,128)(2,1)S(1)}, bf16[96,2048]{1,0:T(8,128)(2,1)S(1)}, u32[]{:S(2)}, u32[]{:S(2)}) %collective-permute-start.73) | collective-permute-done | bytes 393248 | tf_op jit(solution)/shard_map/ppermute | solution.py:804
  456.6 19.3 %shard_map.206 = (f32[96,2048]{1,0:T(8,128)}, f32[96,2048]{1,0:T(8,128)}, bf16[96,2048]{1,0:T(8,128)(2,1)S(1)}, bf16[96,2048]{1,0:T(8,128)(2,1)S(1)}, f32[3,4,51...) custom-call(s32[1]{0:T(128)} %bitcast.1.me_ref, ...), custom_call_target="tpu_custom_call" | custom-call | flops 2000000000 | bytes 100000 | tf_op jit(solution)/shard_map/pallas_call | solution.py:295
  479.8 19.4 %shard_map.208 = (f32[96,2048]{1,0:T(8,128)}, f32[96,2048]{1,0:T(8,128)}, bf16[96,2048]{1,0:T(8,128)(2,1)}, bf16[96,2048]{1,0:T(8,128)(2,1)S(1)}, f32[3,4,512]{2...) custom-call(s32[1]{0:T(128)} %bitcast.1.me_ref, ...), custom_call_target="tpu_custom_call" | custom-call | flops 2000000000 | bytes 100000 | tf_op jit(solution)/shard_map/pallas_call | solution.py:295
  500.0 8.3 %convolution_convert_fusion.1 = bf16[2048,1536]{1,0:T(8,128)(2,1)} fusion(bf16[768,2048]{1,0:T(8,128)(2,1)S(1)} %constant_dynamic-update-slice_fusion, bf16[384,1536]{1,0:T(8,128)(2,1)} %get-tuple-element.566, bf16[384,1536]{1,0:T(8,128)(2,1)S(1)} %copy-done.96), kind=kOutput, calls=%fused_computation.1 | convolution fusion | flops 4839702528 | bytes 11796480 | tf_op jit(solution)/shard_map/dot_general | solution.py:790
  508.2 106.7 %reduce-scatter.3.cloned.1.call-done = bf16[512,2816]{1,0:T(8,128)(2,1)} async-done(((bf16[2048,2816]{1,0:T(8,128)(2,1)}), bf16[512,2816]{1,0:T(8,128)(2,1)}) %reduce-scatter.3.cloned.1.call-update) | async-done | bytes 2883600 | tf_op jit(solution)/shard_map/reduce_scatter | solution.py:1063
  618.7 2.7 collective-permute-start.88
  621.4 3.3 collective-permute-done.86
  624.8 7.3 collective-permute-done.87
  635.7 9.5 %collective-permute-done.81.refs_2_ = bf16[96,2048]{1,0:T(8,128)(2,1)S(1)} collective-permute-done((bf16[96,2048]{1,0:T(8,128)(2,1)S(1)}, bf16[96,2048]{1,0:T(8,128)(2,1)S(1)}, u32[]{:S(2)}, u32[]{:S(2)}) %collective-permute-start.81) | collective-permute-done | bytes 393248 | tf_op jit(solution)/shard_map/ppermute | solution.py:804
  655.1 4.8 collective-permute-start.89
  672.9 4.8 collective-permute-start.91
  682.6 3.5 collective-permute-start.85
  686.2 5.7 collective-permute-done.92
  712.3 4.2 fusion
  716.7 14.1 %collective-permute-done.96 = bf16[2,4,96,512]{3,2,0,1:T(8,128)(2,1)S(1)} collective-permute-done((bf16[2,4,96,512]{3,2,0,1:T(8,128)(2,1)S(1)}, bf16[2,4,96,512]{3,2,0,1:T(8,128)(2,1)S(1)}, u32[]{:S(2)}, u32[]{:S(2)}) %collective-permute-start.96) | collective-permute-done | bytes 786464 | tf_op jit(solution)/shard_map/ppermute | solution.py:804
  730.8 2.9 maximum_convert_fusion
  738.5 13.3 %reduce-scatter.5.cloned.1.call-done = bf16[512,1536]{1,0:T(8,128)(2,1)} async-done(((bf16[2048,1536]{1,0:T(8,128)(2,1)}), bf16[512,1536]{1,0:T(8,128)(2,1)}) %reduce-scatter.5.cloned.1.call-update) | async-done | bytes 1572880 | tf_op jit(solution)/shard_map/reduce_scatter | solution.py:1063
  (513 shorter events, 191.8 us)
Async XLA Ops:
  7.2 389.8 %all-gather.9.cloned.1.call-start = ((), (), s32[]{:S(2)}) async-start(), calls=%async_computation.4 | async-start | bytes 1966080 | tf_op jit(solution)/shard_map/all_gather | solution.py:1029
  27.2 15.0 %collective-permute-start.1 = (bf16[96,2048]{1,0:T(8,128)(2,1)S(1)}, bf16[96,2048]{1,0:T(8,128)(2,1)S(1)}, u32[]{:S(2)}, u32[]{:S(2)}) collective-permute-start(bf16[96,2048]{1,0:T(8,128)(2,1)S(1)} %convert_add_fusion.6), channel_id=1, source_target_pairs={{0,2},{1,3},{2,0},{3,1},{4,6},{5,7},{6,4},{7,5},{8,10},{9,11},{10,... | collective-permute-start | bytes 1179656 | tf_op jit(solution)/shard_map/ppermute | solution.py:804
  44.1 11.2 %collective-permute-start.4 = (bf16[96,2048]{1,0:T(8,128)(2,1)S(1)}, bf16[96,2048]{1,0:T(8,128)(2,1)S(1)}, u32[]{:S(2)}, u32[]{:S(2)}) collective-permute-start(bf16[96,2048]{1,0:T(8,128)(2,1)S(1)} %add_convert_fusion.8), channel_id=1, source_target_pairs={{0,2},{1,3},{2,0},{3,1},{4,6},{5,7},{6,4},{7,5},{8,10},{9,11},{10,... | collective-permute-start | bytes 1179656 | tf_op jit(solution)/shard_map/ppermute | solution.py:804
  66.0 13.3 %collective-permute-start.7 = (bf16[96,2048]{1,0:T(8,128)(2,1)S(1)}, bf16[96,2048]{1,0:T(8,128)(2,1)S(1)}, u32[]{:S(2)}, u32[]{:S(2)}) collective-permute-start(bf16[96,2048]{1,0:T(8,128)(2,1)S(1)} %get-tuple-element.334.refs_0_), channel_id=1, source_target_pairs={{0,2},{1,3},{2,0},{3,1},{4,6},{5,7},{6,4},{7,5},{8,10},{9,11},{10,... | collective-permute-start | bytes 1179656 | tf_op jit(solution)/shard_map/ppermute | solution.py:804
  83.5 15.6 %collective-permute-start.13 = (bf16[96,2048]{1,0:T(8,128)(2,1)}, bf16[96,2048]{1,0:T(8,128)(2,1)}, u32[]{:S(2)}, u32[]{:S(2)}) collective-permute-start(bf16[96,2048]{1,0:T(8,128)(2,1)} %convert_add_fusion.5), channel_id=1, source_target_pairs={{0,2},{1,3},{2,0},{3,1},{4,6},{5,7},{6,4},{7,5},{8,10},{9,11},{10,... | collective-permute-start | bytes 1179656 | tf_op jit(solution)/shard_map/ppermute | solution.py:804
  84.2 15.4 %collective-permute-start.17 = (bf16[96,2048]{1,0:T(8,128)(2,1)}, bf16[96,2048]{1,0:T(8,128)(2,1)}, u32[]{:S(2)}, u32[]{:S(2)}) collective-permute-start(bf16[96,2048]{1,0:T(8,128)(2,1)} %get-tuple-element.351), channel_id=1, source_target_pairs={{0,1},{1,0},{2,3},{3,2},{4,5},{5,4},{6,7},{7,6},{8,9},{9,8},{10,11... | collective-permute-start | bytes 1179656 | tf_op jit(solution)/shard_map/ppermute | solution.py:804
  100.9 12.0 %collective-permute-start.18 = (bf16[96,2048]{1,0:T(8,128)(2,1)S(1)}, bf16[96,2048]{1,0:T(8,128)(2,1)S(1)}, u32[]{:S(2)}, u32[]{:S(2)}) collective-permute-start(bf16[96,2048]{1,0:T(8,128)(2,1)S(1)} %add_convert_fusion.6), channel_id=1, source_target_pairs={{0,16},{1,17},{2,18},{3,19},{4,20},{5,21},{6,22},{7,23},{8,24},{9,... | collective-permute-start | bytes 1179656 | tf_op jit(solution)/shard_map/ppermute | solution.py:809
  104.4 13.0 %collective-permute-start.14 = (bf16[96,2048]{1,0:T(8,128)(2,1)S(1)}, bf16[96,2048]{1,0:T(8,128)(2,1)S(1)}, u32[]{:S(2)}, u32[]{:S(2)}) collective-permute-start(bf16[96,2048]{1,0:T(8,128)(2,1)S(1)} %get-tuple-element.345), channel_id=1, source_target_pairs={{0,1},{1,0},{2,3},{3,2},{4,5},{5,4},{6,7},{7,6},{8,9},{9,8},{10,11... | collective-permute-start | bytes 1179656 | tf_op jit(solution)/shard_map/ppermute | solution.py:804
  104.6 11.6 %collective-permute-start.16 = (bf16[96,2048]{1,0:T(8,128)(2,1)S(1)}, bf16[96,2048]{1,0:T(8,128)(2,1)S(1)}, u32[]{:S(2)}, u32[]{:S(2)}) collective-permute-start(bf16[96,2048]{1,0:T(8,128)(2,1)S(1)} %add_convert_fusion.7), channel_id=1, source_target_pairs={{0,2},{1,3},{2,0},{3,1},{4,6},{5,7},{6,4},{7,5},{8,10},{9,11},{10,... | collective-permute-start | bytes 1179656 | tf_op jit(solution)/shard_map/ppermute | solution.py:804
  128.3 18.0 %collective-permute-start.21 = (bf16[96,2048]{1,0:T(8,128)(2,1)S(1)}, bf16[96,2048]{1,0:T(8,128)(2,1)S(1)}, u32[]{:S(2)}, u32[]{:S(2)}) collective-permute-start(bf16[96,2048]{1,0:T(8,128)(2,1)S(1)} %get-tuple-element.374.refs_0_), channel_id=1, source_target_pairs={{0,2},{1,3},{2,0},{3,1},{4,6},{5,7},{6,4},{7,5},{8,10},{9,11},{10,... | collective-permute-start | bytes 1179656 | tf_op jit(solution)/shard_map/ppermute | solution.py:804
  146.3 250.7 %all-gather.11.cloned.1.call-start = ((), (), s32[]{:S(2)}) async-start(), calls=%async_computation.5 | async-start | bytes 1966080 | tf_op jit(solution)/shard_map/all_gather | solution.py:1029
  150.2 20.6 %collective-permute-start.27 = (bf16[96,2048]{1,0:T(8,128)(2,1)}, bf16[96,2048]{1,0:T(8,128)(2,1)}, u32[]{:S(2)}, u32[]{:S(2)}) collective-permute-start(bf16[96,2048]{1,0:T(8,128)(2,1)} %convert_add_fusion.4), channel_id=1, source_target_pairs={{0,2},{1,3},{2,0},{3,1},{4,6},{5,7},{6,4},{7,5},{8,10},{9,11},{10,... | collective-permute-start | bytes 1179656 | tf_op jit(solution)/shard_map/ppermute | solution.py:804
  170.7 226.3 %all-gather.5.cloned.1.call-start = ((), (), s32[]{:S(2)}) async-start(), calls=%async_computation.2 | async-start | bytes 5406720 | tf_op jit(solution)/shard_map/all_gather | solution.py:1028
  174.0 11.2 %collective-permute-start.30 = (bf16[96,2048]{1,0:T(8,128)(2,1)S(1)}, bf16[96,2048]{1,0:T(8,128)(2,1)S(1)}, u32[]{:S(2)}, u32[]{:S(2)}) collective-permute-start(bf16[96,2048]{1,0:T(8,128)(2,1)S(1)} %add_convert_fusion.4), channel_id=1, source_target_pairs={{0,2},{1,3},{2,0},{3,1},{4,6},{5,7},{6,4},{7,5},{8,10},{9,11},{10,... | collective-permute-start | bytes 1179656 | tf_op jit(solution)/shard_map/ppermute | solution.py:804
  196.1 11.8 %collective-permute-start.33 = (bf16[96,2048]{1,0:T(8,128)(2,1)S(1)}, bf16[96,2048]{1,0:T(8,128)(2,1)S(1)}, u32[]{:S(2)}, u32[]{:S(2)}) collective-permute-start(bf16[96,2048]{1,0:T(8,128)(2,1)S(1)} %get-tuple-element.408.refs_0_), channel_id=1, source_target_pairs={{0,2},{1,3},{2,0},{3,1},{4,6},{5,7},{6,4},{7,5},{8,10},{9,11},{10,... | collective-permute-start | bytes 1179656 | tf_op jit(solution)/shard_map/ppermute | solution.py:804
  207.9 189.1 %all-gather.7.cloned.1.call-start = ((), (), s32[]{:S(2)}) async-start(), calls=%async_computation.3 | async-start | bytes 5406720 | tf_op jit(solution)/shard_map/all_gather | solution.py:1028
  227.2 25.2 %collective-permute-start.39 = (bf16[96,2048]{1,0:T(8,128)(2,1)S(1)}, bf16[96,2048]{1,0:T(8,128)(2,1)S(1)}, u32[]{:S(2)}, u32[]{:S(2)}) collective-permute-start(bf16[96,2048]{1,0:T(8,128)(2,1)S(1)} %convert_add_fusion.3), channel_id=1, source_target_pairs={{0,2},{1,3},{2,0},{3,1},{4,6},{5,7},{6,4},{7,5},{8,10},{9,11},{10,... | collective-permute-start | bytes 1179656 | tf_op jit(solution)/shard_map/ppermute | solution.py:804
  253.7 361.2 %reduce-scatter.3.cloned.1.call-start = ((), (), s32[]{:S(2)}) async-start(), calls=%async_computation.6 | async-start | bytes 14417920 | tf_op jit(solution)/shard_map/reduce_scatter | solution.py:1063
  257.1 11.4 %collective-permute-start.42 = (bf16[96,2048]{1,0:T(8,128)(2,1)}, bf16[96,2048]{1,0:T(8,128)(2,1)S(1)}, u32[]{:S(2)}, u32[]{:S(2)}) collective-permute-start(bf16[96,2048]{1,0:T(8,128)(2,1)} %add_convert_fusion.3), channel_id=1, source_target_pairs={{0,2},{1,3},{2,0},{3,1},{4,6},{5,7},{6,4},{7,5},{8,10},{9,11},{10,... | collective-permute-start | bytes 1179656 | tf_op jit(solution)/shard_map/ppermute | solution.py:804
  269.3 12.7 %collective-permute-start.46 = (bf16[96,2048]{1,0:T(8,128)(2,1)S(1)}, bf16[96,2048]{1,0:T(8,128)(2,1)S(1)}, u32[]{:S(2)}, u32[]{:S(2)}) collective-permute-start(bf16[96,2048]{1,0:T(8,128)(2,1)S(1)} %get-tuple-element.433.refs_0_), channel_id=1, source_target_pairs={{0,1},{1,0},{2,3},{3,2},{4,5},{5,4},{6,7},{7,6},{8,9},{9,8},{10,11... | collective-permute-start | bytes 1179656 | tf_op jit(solution)/shard_map/ppermute | solution.py:804
  281.1 20.5 %collective-permute-start.45 = (bf16[96,2048]{1,0:T(8,128)(2,1)S(1)}, bf16[96,2048]{1,0:T(8,128)(2,1)S(1)}, u32[]{:S(2)}, u32[]{:S(2)}) collective-permute-start(bf16[96,2048]{1,0:T(8,128)(2,1)S(1)} %get-tuple-element.450.refs_0_), channel_id=1, source_target_pairs={{0,2},{1,3},{2,0},{3,1},{4,6},{5,7},{6,4},{7,5},{8,10},{9,11},{10,... | collective-permute-start | bytes 1179656 | tf_op jit(solution)/shard_map/ppermute | solution.py:804
  304.7 20.5 %collective-permute-start.51 = (bf16[96,2048]{1,0:T(8,128)(2,1)S(1)}, bf16[96,2048]{1,0:T(8,128)(2,1)S(1)}, u32[]{:S(2)}, u32[]{:S(2)}) collective-permute-start(bf16[96,2048]{1,0:T(8,128)(2,1)S(1)} %convert_add_fusion.2), channel_id=1, source_target_pairs={{0,2},{1,3},{2,0},{3,1},{4,6},{5,7},{6,4},{7,5},{8,10},{9,11},{10,... | collective-permute-start | bytes 1179656 | tf_op jit(solution)/shard_map/ppermute | solution.py:804
  305.9 20.6 %collective-permute-start.55 = (bf16[96,2048]{1,0:T(8,128)(2,1)}, bf16[96,2048]{1,0:T(8,128)(2,1)}, u32[]{:S(2)}, u32[]{:S(2)}) collective-permute-start(bf16[96,2048]{1,0:T(8,128)(2,1)} %get-tuple-element.474), channel_id=1, source_target_pairs={{0,1},{1,0},{2,3},{3,2},{4,5},{5,4},{6,7},{7,6},{8,9},{9,8},{10,11... | collective-permute-start | bytes 1179656 | tf_op jit(solution)/shard_map/ppermute | solution.py:804
  332.4 13.0 %collective-permute-start.56 = (bf16[96,2048]{1,0:T(8,128)(2,1)S(1)}, bf16[96,2048]{1,0:T(8,128)(2,1)S(1)}, u32[]{:S(2)}, u32[]{:S(2)}) collective-permute-start(bf16[96,2048]{1,0:T(8,128)(2,1)S(1)} %get-tuple-element.475), channel_id=1, source_target_pairs={{16,0},{17,1},{18,2},{19,3},{20,4},{21,5},{22,6},{23,7},{24,8},{25... | collective-permute-start | bytes 1179656 | tf_op jit(solution)/shard_map/ppermute | solution.py:809
  333.7 13.7 %collective-permute-start.52 = (bf16[96,2048]{1,0:T(8,128)(2,1)}, bf16[96,2048]{1,0:T(8,128)(2,1)S(1)}, u32[]{:S(2)}, u32[]{:S(2)}) collective-permute-start(bf16[96,2048]{1,0:T(8,128)(2,1)} %get-tuple-element.468), channel_id=1, source_target_pairs={{0,1},{1,0},{2,3},{3,2},{4,5},{5,4},{6,7},{7,6},{8,9},{9,8},{10,11... | collective-permute-start | bytes 1179656 | tf_op jit(solution)/shard_map/ppermute | solution.py:804
  334.9 11.6 %collective-permute-start.54 = (bf16[96,2048]{1,0:T(8,128)(2,1)S(1)}, bf16[96,2048]{1,0:T(8,128)(2,1)S(1)}, u32[]{:S(2)}, u32[]{:S(2)}) collective-permute-start(bf16[96,2048]{1,0:T(8,128)(2,1)S(1)} %add_convert_fusion.2), channel_id=1, source_target_pairs={{0,2},{1,3},{2,0},{3,1},{4,6},{5,7},{6,4},{7,5},{8,10},{9,11},{10,... | collective-permute-start | bytes 1179656 | tf_op jit(solution)/shard_map/ppermute | solution.py:804
  348.9 12.7 %collective-permute-start.57 = (bf16[96,2048]{1,0:T(8,128)(2,1)S(1)}, bf16[96,2048]{1,0:T(8,128)(2,1)S(1)}, u32[]{:S(2)}, u32[]{:S(2)}) collective-permute-start(bf16[96,2048]{1,0:T(8,128)(2,1)S(1)} %get-tuple-element.477), channel_id=1, source_target_pairs={{16,0},{17,1},{18,2},{19,3},{20,4},{21,5},{22,6},{23,7},{24,8},{25... | collective-permute-start | bytes 1179656 | tf_op jit(solution)/shard_map/ppermute | solution.py:809
  350.2 12.7 %collective-permute-start.60 = (bf16[96,2048]{1,0:T(8,128)(2,1)S(1)}, bf16[96,2048]{1,0:T(8,128)(2,1)S(1)}, u32[]{:S(2)}, u32[]{:S(2)}) collective-permute-start(bf16[96,2048]{1,0:T(8,128)(2,1)S(1)} %broadcast_select_fusion.2.refs_0_.base_ref), channel_id=1, source_target_pairs={{0,1},{1,0},{2,3},{3,2},{4,5},{5,4},{6,7},{7,6},{8,9},{9,8},{10,11... | collective-permute-start | bytes 1179656 | tf_op jit(solution)/shard_map/ppermute | solution.py:804
  361.7 14.8 %collective-permute-start.59 = (bf16[96,2048]{1,0:T(8,128)(2,1)S(1)}, bf16[96,2048]{1,0:T(8,128)(2,1)}, u32[]{:S(2)}, u32[]{:S(2)}) collective-permute-start(bf16[96,2048]{1,0:T(8,128)(2,1)S(1)} %broadcast_select_fusion.3.refs_0_.base_ref), channel_id=1, source_target_pairs={{0,2},{1,3},{2,0},{3,1},{4,6},{5,7},{6,4},{7,5},{8,10},{9,11},{10,... | collective-permute-start | bytes 1179656 | tf_op jit(solution)/shard_map/ppermute | solution.py:804
  397.9 20.2 %collective-permute-start.66 = (bf16[2,96,512]{2,1,0:T(8,128)(2,1)}, bf16[2,96,512]{2,1,0:T(8,128)(2,1)}, u32[]{:S(2)}, u32[]{:S(2)}) collective-permute-start(bf16[2,96,512]{2,1,0:T(8,128)(2,1)} %get-tuple-element.615), channel_id=1, source_target_pairs={{0,4},{4,8},{8,12},{12,0},{1,5},{5,9},{9,13},{13,1},{2,6},{6,10},{... | collective-permute-start | bytes 589832 | tf_op jit(solution)/shard_map/ppermute | solution.py:935
  399.5 18.6 %collective-permute-start.67 = (bf16[2,96,512]{2,1,0:T(8,128)(2,1)}, bf16[2,96,512]{2,1,0:T(8,128)(2,1)}, u32[]{:S(2)}, u32[]{:S(2)}) collective-permute-start(bf16[2,96,512]{2,1,0:T(8,128)(2,1)} %get-tuple-element.616), channel_id=1, source_target_pairs={{0,8},{4,12},{8,0},{12,4},{1,9},{5,13},{9,1},{13,5},{2,10},{6,14},... | collective-permute-start | bytes 589832 | tf_op jit(solution)/shard_map/ppermute | solution.py:935
  402.2 15.9 %collective-permute-start.68 = (bf16[2,96,512]{2,1,0:T(8,128)(2,1)}, bf16[2,96,512]{2,1,0:T(8,128)(2,1)}, u32[]{:S(2)}, u32[]{:S(2)}) collective-permute-start(bf16[2,96,512]{2,1,0:T(8,128)(2,1)} %get-tuple-element.617), channel_id=1, source_target_pairs={{0,12},{4,0},{8,4},{12,8},{1,13},{5,1},{9,5},{13,9},{2,14},{6,2},{... | collective-permute-start | bytes 589832 | tf_op jit(solution)/shard_map/ppermute | solution.py:935
  420.5 331.3 %reduce-scatter.5.cloned.1.call-start = ((), (), s32[]{:S(2)}) async-start(), calls=%async_computation.7 | async-start | bytes 7864320 | tf_op jit(solution)/shard_map/reduce_scatter | solution.py:1063
  433.1 11.2 %collective-permute-start.70 = (bf16[96,2048]{1,0:T(8,128)(2,1)S(1)}, bf16[96,2048]{1,0:T(8,128)(2,1)S(1)}, u32[]{:S(2)}, u32[]{:S(2)}) collective-permute-start(bf16[96,2048]{1,0:T(8,128)(2,1)S(1)} %add_convert_fusion.1), channel_id=1, source_target_pairs={{0,2},{1,3},{2,0},{3,1},{4,6},{5,7},{6,4},{7,5},{8,10},{9,11},{10,... | collective-permute-start | bytes 1179656 | tf_op jit(solution)/shard_map/ppermute | solution.py:804
  445.3 11.2 %collective-permute-start.75 = (bf16[96,2048]{1,0:T(8,128)(2,1)S(1)}, bf16[96,2048]{1,0:T(8,128)(2,1)S(1)}, u32[]{:S(2)}, u32[]{:S(2)}) collective-permute-start(bf16[96,2048]{1,0:T(8,128)(2,1)S(1)} %get-tuple-element.568.refs_0_), channel_id=1, source_target_pairs={{0,1},{1,0},{2,3},{3,2},{4,5},{5,4},{6,7},{7,6},{8,9},{9,8},{10,11... | collective-permute-start | bytes 1179656 | tf_op jit(solution)/shard_map/ppermute | solution.py:804
  455.6 20.3 %collective-permute-start.74 = (bf16[96,2048]{1,0:T(8,128)(2,1)S(1)}, bf16[96,2048]{1,0:T(8,128)(2,1)S(1)}, u32[]{:S(2)}, u32[]{:S(2)}) collective-permute-start(bf16[96,2048]{1,0:T(8,128)(2,1)S(1)} %get-tuple-element.569.refs_0_), channel_id=1, source_target_pairs={{0,2},{1,3},{2,0},{3,1},{4,6},{5,7},{6,4},{7,5},{8,10},{9,11},{10,... | collective-permute-start | bytes 1179656 | tf_op jit(solution)/shard_map/ppermute | solution.py:804
  616.5 15.6 %collective-permute-start.87 = (bf16[2,96,512]{2,1,0:T(8,128)(2,1)S(1)}, bf16[2,96,512]{2,1,0:T(8,128)(2,1)S(1)}, u32[]{:S(2)}, u32[]{:S(2)}) collective-permute-start(bf16[2,96,512]{2,1,0:T(8,128)(2,1)S(1)} %get-tuple-element.608), channel_id=1, source_target_pairs={{0,8},{4,12},{8,0},{12,4},{1,9},{5,13},{9,1},{13,5},{2,10},{6,14},... | collective-permute-start | bytes 589832 | tf_op jit(solution)/shard_map/ppermute | solution.py:935
  618.7 13.4 %collective-permute-start.88 = (bf16[2,96,512]{2,1,0:T(8,128)(2,1)S(1)}, bf16[2,96,512]{2,1,0:T(8,128)(2,1)S(1)}, u32[]{:S(2)}, u32[]{:S(2)}) collective-permute-start(bf16[2,96,512]{2,1,0:T(8,128)(2,1)S(1)} %get-tuple-element.609), channel_id=1, source_target_pairs={{0,12},{4,0},{8,4},{12,8},{1,13},{5,1},{9,5},{13,9},{2,14},{6,2},{... | collective-permute-start | bytes 589832 | tf_op jit(solution)/shard_map/ppermute | solution.py:935
  646.0 17.5 %collective-permute-start.77 = (bf16[96,2048]{1,0:T(8,128)(2,1)S(1)}, bf16[96,2048]{1,0:T(8,128)(2,1)}, u32[]{:S(2)}, u32[]{:S(2)}) collective-permute-start(bf16[96,2048]{1,0:T(8,128)(2,1)S(1)} %get-tuple-element.540), channel_id=1, source_target_pairs={{0,1},{1,0},{2,3},{3,2},{4,5},{5,4},{6,7},{7,6},{8,9},{9,8},{10,11... | collective-permute-start | bytes 1179656 | tf_op jit(solution)/shard_map/ppermute | solution.py:804
  655.0 13.2 %collective-permute-start.82 = (bf16[96,2048]{1,0:T(8,128)(2,1)}, bf16[96,2048]{1,0:T(8,128)(2,1)}, u32[]{:S(2)}, u32[]{:S(2)}) collective-permute-start(bf16[96,2048]{1,0:T(8,128)(2,1)} %get-tuple-element.558), channel_id=1, source_target_pairs={{0,1},{1,0},{2,3},{3,2},{4,5},{5,4},{6,7},{7,6},{8,9},{9,8},{10,11... | collective-permute-start | bytes 1179656 | tf_op jit(solution)/shard_map/ppermute | solution.py:804
  655.1 22.7 %collective-permute-start.89 = (f32[14336]{0:T(1024)S(1)}, f32[14336]{0:T(1024)}, u32[]{:S(2)}, u32[]{:S(2)}) collective-permute-start(f32[14336]{0:T(1024)S(1)} %constant_dynamic-update-slice_fusion.11), channel_id=1, source_target_pairs={{0,4},{4,0},{8,12},{12,8},{1,5},{5,1},{9,13},{13,9},{2,6},{6,2},{1... | collective-permute-start | bytes 172040 | tf_op jit(solution)/shard_map/ppermute | solution.py:804
  662.1 32.5 %collective-permute-start.95 = (bf16[2,4,96,512]{3,2,0,1:T(8,128)(2,1)}, bf16[2,4,96,512]{3,2,0,1:T(8,128)(2,1)}, u32[]{:S(2)}, u32[]{:S(2)}) collective-permute-start(bf16[2,4,96,512]{3,2,0,1:T(8,128)(2,1)} %pad_maximum_fusion.2), channel_id=1, source_target_pairs={{0,2},{1,3},{2,0},{3,1},{4,6},{5,7},{6,4},{7,5},{8,10},{9,11},{10,... | collective-permute-start | bytes 2359304 | tf_op jit(solution)/shard_map/ppermute | solution.py:804
  677.8 24.9 %collective-permute-start.99 = (bf16[2,4,96,512]{3,2,0,1:T(8,128)(2,1)}, bf16[2,4,96,512]{3,2,0,1:T(8,128)(2,1)}, u32[]{:S(2)}, u32[]{:S(2)}) collective-permute-start(bf16[2,4,96,512]{3,2,0,1:T(8,128)(2,1)} %pad_maximum_fusion.2), channel_id=1, source_target_pairs={{0,1},{1,0},{2,3},{3,2},{4,5},{5,4},{6,7},{7,6},{8,9},{9,8},{10,11... | collective-permute-start | bytes 2359304 | tf_op jit(solution)/shard_map/ppermute | solution.py:804
  678.6 14.3 %collective-permute-start.90 = (f32[14336]{0:T(1024)S(1)}, f32[14336]{0:T(1024)S(1)}, u32[]{:S(2)}, u32[]{:S(2)}) collective-permute-start(f32[14336]{0:T(1024)S(1)} %add.236), channel_id=1, source_target_pairs={{0,8},{4,12},{8,0},{12,4},{1,9},{5,13},{9,1},{13,5},{2,10},{6,14},... | collective-permute-start | bytes 172040 | tf_op jit(solution)/shard_map/ppermute | solution.py:804
  680.2 11.7 %collective-permute-start.92 = (f32[4224]{0:T(1024)S(1)}, f32[4224]{0:T(1024)S(1)}, u32[]{:S(2)}, u32[]{:S(2)}) collective-permute-start(f32[4224]{0:T(1024)S(1)} %fusion.34), channel_id=1, source_target_pairs={{0,8},{4,12},{8,0},{12,4},{1,9},{5,13},{9,1},{13,5},{2,10},{6,14},... | collective-permute-start | bytes 50696 | tf_op jit(solution)/shard_map/ppermute | solution.py:804
  682.6 16.4 %collective-permute-start.85 = (bf16[2,96,1024]{2,1,0:T(8,128)(2,1)}, bf16[2,96,1024]{2,1,0:T(8,128)(2,1)S(1)}, u32[]{:S(2)}, u32[]{:S(2)}) collective-permute-start(bf16[2,96,1024]{2,1,0:T(8,128)(2,1)} %fusion.10), channel_id=1, source_target_pairs={{0,16},{1,17},{2,18},{3,19},{4,20},{5,21},{6,22},{7,23},{8,24},{9,... | collective-permute-start | bytes 1179656 | tf_op jit(solution)/shard_map/ppermute | solution.py:809
  711.6 19.3 %collective-permute-start.96 = (bf16[2,4,96,512]{3,2,0,1:T(8,128)(2,1)S(1)}, bf16[2,4,96,512]{3,2,0,1:T(8,128)(2,1)S(1)}, u32[]{:S(2)}, u32[]{:S(2)}) collective-permute-start(bf16[2,4,96,512]{3,2,0,1:T(8,128)(2,1)S(1)} %copy-done.86), channel_id=1, source_target_pairs={{0,2},{1,3},{2,0},{3,1},{4,6},{5,7},{6,4},{7,5},{8,10},{9,11},{10,... | collective-permute-start | bytes 2359304 | tf_op jit(solution)/shard_map/ppermute | solution.py:804
  716.5 17.3 %collective-permute-start.97 = (bf16[2,4,96,512]{3,2,0,1:T(8,128)(2,1)S(1)}, bf16[2,4,96,512]{3,2,0,1:T(8,128)(2,1)S(1)}, u32[]{:S(2)}, u32[]{:S(2)}) collective-permute-start(bf16[2,4,96,512]{3,2,0,1:T(8,128)(2,1)S(1)} %copy-done.86), channel_id=1, source_target_pairs={{0,1},{1,0},{2,3},{3,2},{4,5},{5,4},{6,7},{7,6},{8,9},{9,8},{10,11... | collective-permute-start | bytes 2359304 | tf_op jit(solution)/shard_map/ppermute | solution.py:804
  (160 other events, 1432.2 us)
Sparse Core Ops, SparseCore 0:
  146.5 38.9 all-gather.8
  187.0 35.9 all-gather.10
  224.6 81.8 all-gather.4
  307.9 81.4 all-gather.6
  420.6 194.3 reduce-scatter.2
  633.4 118.3 reduce-scatter.4

commit v10 on v9

--- a/solution.py
+++ b/solution.py
@@ -929,13 +929,17 @@
     values = jnp.stack(shards)
     wide = values.shape[-1] // count
     arrived = []
-    for distance in range(count):
-        block = lax.dynamic_slice_in_dim(values, ((me + distance) % count) * wide, wide, 2)
-        if distance:
-            block = lax.ppermute(block, "dp", [(i, (i + distance) % count) for i in range(count)])
-        arrived.append(block)
+    for pair in range(count):
+        block = lax.dynamic_slice_in_dim(values, (me ^ pair) * wide, wide, 2)
+        arrived.append(flipped(block, "dp", pair) if pair else block)
+    return arrived
+
+
+def in_dp_order(arrived):
+    me = lax.axis_index("dp")
+    count = len(arrived)
     arrived = jnp.stack(arrived)
-    ordered = [lax.dynamic_index_in_dim(arrived, (me - q) % count, 0, keepdims=False) for q in range(count)]
+    ordered = [lax.dynamic_index_in_dim(arrived, me ^ q, 0, keepdims=False) for q in range(count)]
     return jnp.stack(ordered, axis=1)
 
 
@@ -1074,7 +1078,7 @@
     columns = [
         part.reshape(-1, part.shape[-1])
         for arrived in (columns_out, columns_mid)
-        for part in jnp.concatenate(gather(arrived, order), axis=2)
+        for part in jnp.concatenate(gather(in_dp_order(arrived), order), axis=2)
     ]
     grad_contract = sum(product_left(left, right) for left, right in zip(hidden_rows, columns[:micro]))
     grad_merge = sum(product_left(left, right) for left, right in zip(mixed_rows, columns[micro:]))

time: 772 us -> 772 us (level)
  starting transfers between devices: 78 us -> 67.3 us
  waiting for transfers between devices: 290 us -> 299 us
    ppermute x90 -> x96, waiting for transfers between devices: 138 us -> 161 us  [flipped(): lax.ppermute(values, axis, [(i, i ^ bit) for i in range(lax.axis_size(axi...]
    ppermute x6 -> x0, starting transfers between devices: 12 us -> none  [swapped(): lax.ppermute(block, 'dp', [(i, (i + distance) % count) for i in range(cou...]
    ppermute x6 -> x0, waiting for transfers between devices: 10.7 us -> none  [swapped(): lax.ppermute(block, 'dp', [(i, (i + distance) % count) for i in range(cou...]
    unnamed x212 -> x236, local copies, waits for them, and re-layouts: 45.6 us -> 50.8 us
    ppermute x90 -> x96, starting transfers between devices: 54 us -> 54.6 us  [flipped(): lax.ppermute(values, axis, [(i, i ^ bit) for i in range(lax.axis_size(axi...]
  transfers between devices with their start and end apart: 107 -> 107, of which waited for: 41 -> 45; matrix products, arithmetic and copies ran while one was open for 10% -> 10% of each run, Pallas kernels for 31% -> 31%
where the time goes in v10:
time: 772 us; the launch traced here: 763 us
  waiting for transfers between devices  299 us (39%)
  Pallas kernels  246 us (32%)
  local copies, waits for them, and re-layouts  69.3 us (9%)
  starting transfers between devices  67.3 us (9%)
  matrix products  35.2 us (5%)
  other arithmetic  30 us (4%)
  between operations  16.2 us (2%)
    pallas_call x16, Pallas kernels, call(): pl.pallas_call(functools.partial(kernel, len(rows)), in_specs=[pl.BlockSp...  227 us
    ppermute x96, waiting for transfers between devices, flipped(): lax.ppermute(values, axis, [(i, i ^ bit) for i in range(lax.axis_size(axi...  161 us
    reduce_scatter x2, waiting for transfers between devices, spread(): return lax.psum_scatter(value, 'dp', scatter_dimension=axis, tiled=True)  116 us
    ppermute x96, starting transfers between devices, flipped(): lax.ppermute(values, axis, [(i, i ^ bit) for i in range(lax.axis_size(axi...  54.6 us
    unnamed x236, local copies, waits for them, and re-layouts  50.8 us
    dot_general x7, matrix products, product_left(): lax.dot_general(left, right, (((0,), (0,)), ((), ())), preferred_element_...  35.2 us
    ppermute x5, waiting for transfers between devices, shifted(): lax.ppermute(values, axis, [(i, i + distance) for i in devices if i + dis...  21.3 us
    pallas_call x14, Pallas kernels, small_call(): pl.pallas_call(kernel, in_specs=[vmem] * len(operands), out_specs=[vmem]...  17.3 us
  transfers between devices with their start and end apart: 107, of which 45 were waited for; matrix products, arithmetic and copies ran while one was open for 10% of the time, Pallas kernels for 31%

profile of v10, /device:TPU:0, one launch (start us, length us, event | category | flops | bytes accessed | tf_op | source)
XLA Modules:
  0.0 762.7 jit_solution(381063225656074436)
XLA Ops:
  14.0 11.4 %shard_map.180 = (f32[96,2048]{1,0:T(8,128)S(1)}, f32[96,2048]{1,0:T(8,128)S(1)}, bf16[96,2048]{1,0:T(8,128)(2,1)S(1)}, bf16[96,2048]{1,0:T(8,128)(2,1)S(1)}) custom-call(s32[1]{0:T(128)} %bitcast.1.me_ref, s32[384,1]{1,0:T(8,128)S(1)} %broadcast_in_dim.49.seg_col_ref, s32[1,384]{1,0:T(1,128)S(1)} %broadcast_in_dim.43.seg_row_ref, ...), custom_call_target="tpu_custom_call" | custom-call | flops 2000000000 | bytes 100000 | tf_op jit(solution)/shard_map/pallas_call | solution.py:295
  27.3 2.9 collective-permute-start.1
  30.8 11.4 %shard_map.181 = (f32[96,2048]{1,0:T(8,128)S(1)}, f32[96,2048]{1,0:T(8,128)S(1)}, bf16[96,2048]{1,0:T(8,128)(2,1)S(1)}, bf16[96,2048]{1,0:T(8,128)(2,1)S(1)}) custom-call(s32[1]{0:T(128)} %bitcast.1.me_ref, s32[384,1]{1,0:T(8,128)S(1)} %broadcast_in_dim.48.seg_col_ref, s32[1,384]{1,0:T(1,128)S(1)} %broadcast_in_dim.20.seg_row_ref, ...), custom_call_target="tpu_custom_call" | custom-call | flops 2000000000 | bytes 100000 | tf_op jit(solution)/shard_map/pallas_call | solution.py:295
  45.0 10.4 %collective-permute-done.4.refs_3_ = bf16[96,2048]{1,0:T(8,128)(2,1)S(1)} collective-permute-done((bf16[96,2048]{1,0:T(8,128)(2,1)S(1)}, bf16[96,2048]{1,0:T(8,128)(2,1)S(1)}, u32[]{:S(2)}, u32[]{:S(2)}) %collective-permute-start.4) | collective-permute-done | bytes 393248 | tf_op jit(solution)/shard_map/ppermute | solution.py:804
  56.1 9.5 %collective-permute-done.6.refs_1_ = bf16[96,2048]{1,0:T(8,128)(2,1)S(1)} collective-permute-done((bf16[96,2048]{1,0:T(8,128)(2,1)S(1)}, bf16[96,2048]{1,0:T(8,128)(2,1)S(1)}, u32[]{:S(2)}, u32[]{:S(2)}) %collective-permute-start.6) | collective-permute-done | bytes 393248 | tf_op jit(solution)/shard_map/ppermute | solution.py:804
  67.4 11.9 %shard_map.184 = (f32[96,2048]{1,0:T(8,128)S(1)}, f32[96,2048]{1,0:T(8,128)S(1)}, bf16[96,2048]{1,0:T(8,128)(2,1)}, bf16[96,2048]{1,0:T(8,128)(2,1)S(1)}) custom-call(s32[1]{0:T(128)} %bitcast.1.me_ref, bf16[96,2048]{1,0:T(8,128)(2,1)S(1)} %get-tuple-element.330.refs_0_, bf16[96,2048]{1,0:T(8,128)(2,1)S(1)} %collective-permute-done.6.refs_1_, ...), custom_call_target="tpu_custom_call" | custom-call | flops 2000000000 | bytes 100000 | tf_op jit(solution)/shard_map/pallas_call | solution.py:295
  87.2 10.8 %shard_map.185 = (f32[96,2048]{1,0:T(8,128)S(1)}, f32[96,2048]{1,0:T(8,128)S(1)}, bf16[96,2048]{1,0:T(8,128)(2,1)S(1)}, bf16[96,2048]{1,0:T(8,128)(2,1)S(1)}) custom-call(s32[1]{0:T(128)} %bitcast.1.me_ref, bf16[96,2048]{1,0:T(8,128)(2,1)S(1)} %get-tuple-element.340.refs_0_, bf16[96,2048]{1,0:T(8,128)(2,1)S(1)} %copy-done.33, ...), custom_call_target="tpu_custom_call" | custom-call | flops 2000000000 | bytes 100000 | tf_op jit(solution)/shard_map/pallas_call | solution.py:295
  99.9 3.4 collective-permute-start.18
  104.9 7.0 collective-permute-done.18
  118.9 6.9 collective-permute-done.20.refs_1_
  128.2 16.4 %shard_map.188 = (f32[96,2048]{1,0:T(8,128)}, f32[96,2048]{1,0:T(8,128)}, bf16[96,2048]{1,0:T(8,128)(2,1)S(1)}, bf16[96,2048]{1,0:T(8,128)(2,1)S(1)}, bf16[384,2...) custom-call(s32[1]{0:T(128)} %bitcast.1.me_ref, ...), custom_call_target="tpu_custom_call" | custom-call | flops 2000000000 | bytes 100000 | tf_op jit(solution)/shard_map/pallas_call | solution.py:295
  150.3 16.4 %shard_map.189 = (f32[96,2048]{1,0:T(8,128)}, f32[96,2048]{1,0:T(8,128)}, bf16[96,2048]{1,0:T(8,128)(2,1)S(1)}, bf16[96,2048]{1,0:T(8,128)(2,1)S(1)}, bf16[384,2...) custom-call(s32[1]{0:T(128)} %bitcast.1.me_ref, ...), custom_call_target="tpu_custom_call" | custom-call | flops 2000000000 | bytes 100000 | tf_op jit(solution)/shard_map/pallas_call | solution.py:295
  177.3 6.9 collective-permute-done.30.refs_3_
  185.6 9.1 %collective-permute-done.32.refs_1_ = bf16[96,2048]{1,0:T(8,128)(2,1)S(1)} collective-permute-done((bf16[96,2048]{1,0:T(8,128)(2,1)S(1)}, bf16[96,2048]{1,0:T(8,128)(2,1)S(1)}, u32[]{:S(2)}, u32[]{:S(2)}) %collective-permute-start.32) | collective-permute-done | bytes 393248 | tf_op jit(solution)/shard_map/ppermute | solution.py:804
  196.8 10.4 %shard_map.192 = (bf16[384,2048]{1,0:T(8,128)(2,1)}, bf16[384,1408]{1,0:T(8,128)(2,1)}, bf16[384,1408]{1,0:T(8,128)(2,1)S(1)}, bf16[384,1408]{1,0:T(8,128)(2,1)}) custom-call(s32[1]{0:T(128)} %bitcast.1.me_ref, bf16[96,2048]{1,0:T(8,128)(2,1)S(1)} %get-tuple-element.403.refs_0_, bf16[96,2048]{1,0:T(8,128)(2,1)S(1)} %collective-permute-done.32.refs_1_, ...), custom_call_target="tpu_custom_call" | custom-call | flops 2000000000 | bytes 100000 | tf_op jit(solution)/shard_map/pallas_call | solution.py:295
  208.5 4.0 slice_bitcast_fusion
  212.4 12.2 %shard_map.193 = (f32[96,2048]{1,0:T(8,128)S(1)}, f32[96,2048]{1,0:T(8,128)S(1)}, bf16[96,2048]{1,0:T(8,128)(2,1)S(1)}, bf16[96,2048]{1,0:T(8,128)(2,1)S(1)}, bf16[768,2816]{1,0:T(8,128)(2,1)}) custom-call(s32[1]{0:T(128)} %bitcast.1.me_ref, bf16[384,2048]{1,0:T(8,128)(2,1)} %get-tuple-element.607.refs_0_, ...), custom_call_target="tpu_custom_call" | custom-call | flops 2000000000 | bytes 100000 | tf_op jit(solution)/shard_map/pallas_call | solution.py:295
  228.4 10.9 %shard_map.194 = (bf16[384,2048]{1,0:T(8,128)(2,1)}, bf16[384,1408]{1,0:T(8,128)(2,1)}, bf16[384,1408]{1,0:T(8,128)(2,1)S(1)}, bf16[384,1408]{1,0:T(8,128)(2,1)}) custom-call(s32[1]{0:T(128)} %bitcast.1.me_ref, bf16[96,2048]{1,0:T(8,128)(2,1)S(1)} %get-tuple-element.414.refs_0_, bf16[96,2048]{1,0:T(8,128)(2,1)S(1)} %copy-done.18, ...), custom_call_target="tpu_custom_call" | custom-call | flops 2000000000 | bytes 100000 | tf_op jit(solution)/shard_map/pallas_call | solution.py:295
  239.3 12.5 %shard_map.195 = (f32[96,2048]{1,0:T(8,128)S(1)}, f32[96,2048]{1,0:T(8,128)S(1)}, bf16[96,2048]{1,0:T(8,128)(2,1)S(1)}, bf16[96,2048]{1,0:T(8,128)(2,1)S(1)}, bf16[768,2816]{1,0:T(8,128)(2,1)}) custom-call(s32[1]{0:T(128)} %bitcast.1.me_ref, bf16[384,2048]{1,0:T(8,128)(2,1)} %get-tuple-element.413.refs_0_, ...), custom_call_target="tpu_custom_call", output_to_operand_aliasing={{4}: (6, {})} | custom-call | flops 2000000000 | bytes 100000 | tf_op jit(solution)/shard_map/pallas_call | solution.py:295
  269.4 8.8 %collective-permute-done.44.refs_1_ = bf16[96,2048]{1,0:T(8,128)(2,1)S(1)} collective-permute-done((bf16[96,2048]{1,0:T(8,128)(2,1)S(1)}, bf16[96,2048]{1,0:T(8,128)(2,1)S(1)}, u32[]{:S(2)}, u32[]{:S(2)}) %collective-permute-start.44) | collective-permute-done | bytes 393248 | tf_op jit(solution)/shard_map/ppermute | solution.py:804
  283.7 19.7 %shard_map.198 = (f32[96,2048]{1,0:T(8,128)}, f32[96,2048]{1,0:T(8,128)}, bf16[96,2048]{1,0:T(8,128)(2,1)}, bf16[96,2048]{1,0:T(8,128)(2,1)S(1)}, f32[3,4,512]{2...) custom-call(s32[1]{0:T(128)} %bitcast.1.me_ref, ...), custom_call_target="tpu_custom_call" | custom-call | flops 2000000000 | bytes 100000 | tf_op jit(solution)/shard_map/pallas_call | solution.py:295
  307.6 19.4 %shard_map.199 = (f32[96,2048]{1,0:T(8,128)}, f32[96,2048]{1,0:T(8,128)}, bf16[96,2048]{1,0:T(8,128)(2,1)S(1)}, bf16[96,2048]{1,0:T(8,128)(2,1)}, f32[3,4,512]{2...) custom-call(s32[1]{0:T(128)} %bitcast.1.me_ref, ...), custom_call_target="tpu_custom_call" | custom-call | flops 2000000000 | bytes 100000 | tf_op jit(solution)/shard_map/pallas_call | solution.py:295
  338.5 9.6 %collective-permute-done.56 = bf16[96,2048]{1,0:T(8,128)(2,1)S(1)} collective-permute-done((bf16[96,2048]{1,0:T(8,128)(2,1)S(1)}, bf16[96,2048]{1,0:T(8,128)(2,1)S(1)}, u32[]{:S(2)}, u32[]{:S(2)}) %collective-permute-start.56) | collective-permute-done | bytes 393248 | tf_op jit(solution)/shard_map/ppermute | solution.py:809
  352.9 7.1 collective-permute-done.58.refs_1_
  359.9 4.3 collective-permute-done.57
  365.5 12.7 %shard_map.202 = (f32[96,2048]{1,0:T(8,128)S(1)}, f32[96,2048]{1,0:T(8,128)S(1)}, bf16[96,2048]{1,0:T(8,128)(2,1)S(1)}, bf16[96,2048]{1,0:T(8,128)(2,1)}, bf16[768,2816]{1,0:T(8,128)(2,1)}) custom-call(s32[1]{0:T(128)} %bitcast.1.me_ref, bf16[96,2048]{1,0:T(8,128)(2,1)S(1)} %broadcast_select_fusion.2.refs_0_.base_ref, ...), custom_call_target="tpu_custom_call" | custom-call | flops 2000000000 | bytes 100000 | tf_op jit(solution)/shard_map/pallas_call | solution.py:295
  386.1 11.9 %shard_map.203 = (f32[96,2048]{1,0:T(8,128)S(1)}, f32[96,2048]{1,0:T(8,128)S(1)}, bf16[96,2048]{1,0:T(8,128)(2,1)S(1)}, bf16[96,2048]{1,0:T(8,128)(2,1)S(1)}, bf16[768,2816]{1,0:T(8,128)(2,1)}) custom-call(s32[1]{0:T(128)} %bitcast.1.me_ref, bf16[96,2048]{1,0:T(8,128)(2,1)S(1)} %broadcast_select_fusion.3.refs_0_.base_ref, ...), custom_call_target="tpu_custom_call", output_to_operand_aliasing={{4}: (9, {})} | custom-call | flops 2000000000 | bytes 100000 | tf_op jit(solution)/shard_map/pallas_call | solution.py:295
  401.4 3.3 collective-permute-start.68
  406.0 14.7 %convolution_convert_fusion = bf16[2048,2816]{1,0:T(8,128)(2,1)} fusion(bf16[768,2816]{1,0:T(8,128)(2,1)} %get-tuple-element.516, bf16[384,2048]{1,0:T(8,128)(2,1)} %get-tuple-element.510, bf16[384,2048]{1,0:T(8,128)(2,1)} %get-tuple-element.509), kind=kOutput, calls=%fused_computation | convolution fusion | flops 8870428672 | bytes 19005440 | tf_op jit(solution)/shard_map/dot_general | solution.py:790
  423.1 9.5 %collective-permute-done.65.refs_2_ = bf16[96,2048]{1,0:T(8,128)(2,1)S(1)} collective-permute-done((bf16[96,2048]{1,0:T(8,128)(2,1)}, bf16[96,2048]{1,0:T(8,128)(2,1)S(1)}, u32[]{:S(2)}, u32[]{:S(2)}) %collective-permute-start.65) | collective-permute-done | bytes 393248 | tf_op jit(solution)/shard_map/ppermute | solution.py:804
  439.6 6.3 collective-permute-done.70.refs_2_
  447.4 8.9 %collective-permute-done.73.refs_1_ = bf16[96,2048]{1,0:T(8,128)(2,1)S(1)} collective-permute-done((bf16[96,2048]{1,0:T(8,128)(2,1)S(1)}, bf16[96,2048]{1,0:T(8,128)(2,1)S(1)}, u32[]{:S(2)}, u32[]{:S(2)}) %collective-permute-start.73) | collective-permute-done | bytes 393248 | tf_op jit(solution)/shard_map/ppermute | solution.py:804
  458.9 19.4 %shard_map.206 = (f32[96,2048]{1,0:T(8,128)}, f32[96,2048]{1,0:T(8,128)}, bf16[96,2048]{1,0:T(8,128)(2,1)S(1)}, bf16[96,2048]{1,0:T(8,128)(2,1)S(1)}, f32[3,4,51...) custom-call(s32[1]{0:T(128)} %bitcast.1.me_ref, ...), custom_call_target="tpu_custom_call" | custom-call | flops 2000000000 | bytes 100000 | tf_op jit(solution)/shard_map/pallas_call | solution.py:295
  483.1 19.6 %shard_map.208 = (f32[96,2048]{1,0:T(8,128)}, f32[96,2048]{1,0:T(8,128)}, bf16[96,2048]{1,0:T(8,128)(2,1)}, bf16[96,2048]{1,0:T(8,128)(2,1)}, f32[3,4,512]{2,1,0...) custom-call(s32[1]{0:T(128)} %bitcast.1.me_ref, ...), custom_call_target="tpu_custom_call" | custom-call | flops 2000000000 | bytes 100000 | tf_op jit(solution)/shard_map/pallas_call | solution.py:295
  502.7 8.3 %convolution_convert_fusion.1 = bf16[2048,1536]{1,0:T(8,128)(2,1)} fusion(bf16[768,2048]{1,0:T(8,128)(2,1)S(1)} %constant_dynamic-update-slice_fusion, bf16[384,1536]{1,0:T(8,128)(2,1)} %get-tuple-element.575, bf16[384,1536]{1,0:T(8,128)(2,1)S(1)} %copy-done.111), kind=kOutput, calls=%fused_computation.1 | convolution fusion | flops 4839702528 | bytes 11796480 | tf_op jit(solution)/shard_map/dot_general | solution.py:790
  511.1 104.7 %reduce-scatter.3.cloned.1.call-done = bf16[512,2816]{1,0:T(8,128)(2,1)} async-done(((bf16[2048,2816]{1,0:T(8,128)(2,1)}), bf16[512,2816]{1,0:T(8,128)(2,1)}) %reduce-scatter.3.cloned.1.call-update) | async-done | bytes 2883600 | tf_op jit(solution)/shard_map/reduce_scatter | solution.py:1067
  616.5 3.1 collective-permute-start.88
  620.9 5.2 collective-permute-done.88
  626.1 3.2 collective-permute-done.86
  629.3 8.3 %collective-permute-done.87 = bf16[2,96,512]{2,1,0:T(8,128)(2,1)S(1)} collective-permute-done((bf16[2,96,512]{2,1,0:T(8,128)(2,1)S(1)}, bf16[2,96,512]{2,1,0:T(8,128)(2,1)S(1)}, u32[]{:S(2)}, u32[]{:S(2)}) %collective-permute-start.87) | collective-permute-done | bytes 196640 | tf_op jit(solution)/shard_map/ppermute | solution.py:804
  639.7 9.5 %collective-permute-done.81.refs_2_ = bf16[96,2048]{1,0:T(8,128)(2,1)S(1)} collective-permute-done((bf16[96,2048]{1,0:T(8,128)(2,1)S(1)}, bf16[96,2048]{1,0:T(8,128)(2,1)S(1)}, u32[]{:S(2)}, u32[]{:S(2)}) %collective-permute-start.81) | collective-permute-done | bytes 393248 | tf_op jit(solution)/shard_map/ppermute | solution.py:804
  658.4 5.4 collective-permute-done.84.refs_2_
  668.7 6.0 collective-permute-done.89
  688.8 4.2 collective-permute-start.85
  693.7 5.1 collective-permute-done.92
  716.4 4.2 fusion
  720.5 12.1 %collective-permute-done.96 = bf16[2,4,96,512]{3,2,0,1:T(8,128)(2,1)S(1)} collective-permute-done((bf16[2,4,96,512]{3,2,0,1:T(8,128)(2,1)S(1)}, bf16[2,4,96,512]{3,2,0,1:T(8,128)(2,1)S(1)}, u32[]{:S(2)}, u32[]{:S(2)}) %collective-permute-start.96) | collective-permute-done | bytes 786464 | tf_op jit(solution)/shard_map/ppermute | solution.py:804
  740.4 11.6 %reduce-scatter.5.cloned.1.call-done = bf16[512,1536]{1,0:T(8,128)(2,1)} async-done(((bf16[2048,1536]{1,0:T(8,128)(2,1)}), bf16[512,1536]{1,0:T(8,128)(2,1)}) %reduce-scatter.5.cloned.1.call-update) | async-done | bytes 1572880 | tf_op jit(solution)/shard_map/reduce_scatter | solution.py:1067
  (537 shorter events, 195.9 us)
Async XLA Ops:
  7.2 393.3 %all-gather.9.cloned.1.call-start = ((), (), s32[]{:S(2)}) async-start(), calls=%async_computation.4 | async-start | bytes 1966080 | tf_op jit(solution)/shard_map/all_gather | solution.py:1033
  27.3 15.0 %collective-permute-start.1 = (bf16[96,2048]{1,0:T(8,128)(2,1)S(1)}, bf16[96,2048]{1,0:T(8,128)(2,1)S(1)}, u32[]{:S(2)}, u32[]{:S(2)}) collective-permute-start(bf16[96,2048]{1,0:T(8,128)(2,1)S(1)} %convert_add_fusion.6), channel_id=1, source_target_pairs={{0,2},{1,3},{2,0},{3,1},{4,6},{5,7},{6,4},{7,5},{8,10},{9,11},{10,... | collective-permute-start | bytes 1179656 | tf_op jit(solution)/shard_map/ppermute | solution.py:804
  44.1 11.2 %collective-permute-start.4 = (bf16[96,2048]{1,0:T(8,128)(2,1)S(1)}, bf16[96,2048]{1,0:T(8,128)(2,1)S(1)}, u32[]{:S(2)}, u32[]{:S(2)}) collective-permute-start(bf16[96,2048]{1,0:T(8,128)(2,1)S(1)} %add_convert_fusion.8), channel_id=1, source_target_pairs={{0,2},{1,3},{2,0},{3,1},{4,6},{5,7},{6,4},{7,5},{8,10},{9,11},{10,... | collective-permute-start | bytes 1179656 | tf_op jit(solution)/shard_map/ppermute | solution.py:804
  66.0 13.3 %collective-permute-start.7 = (bf16[96,2048]{1,0:T(8,128)(2,1)S(1)}, bf16[96,2048]{1,0:T(8,128)(2,1)S(1)}, u32[]{:S(2)}, u32[]{:S(2)}) collective-permute-start(bf16[96,2048]{1,0:T(8,128)(2,1)S(1)} %get-tuple-element.340.refs_0_), channel_id=1, source_target_pairs={{0,2},{1,3},{2,0},{3,1},{4,6},{5,7},{6,4},{7,5},{8,10},{9,11},{10,... | collective-permute-start | bytes 1179656 | tf_op jit(solution)/shard_map/ppermute | solution.py:804
  83.5 14.5 %collective-permute-start.13 = (bf16[96,2048]{1,0:T(8,128)(2,1)}, bf16[96,2048]{1,0:T(8,128)(2,1)}, u32[]{:S(2)}, u32[]{:S(2)}) collective-permute-start(bf16[96,2048]{1,0:T(8,128)(2,1)} %convert_add_fusion.5), channel_id=1, source_target_pairs={{0,2},{1,3},{2,0},{3,1},{4,6},{5,7},{6,4},{7,5},{8,10},{9,11},{10,... | collective-permute-start | bytes 1179656 | tf_op jit(solution)/shard_map/ppermute | solution.py:804
  84.2 14.4 %collective-permute-start.17 = (bf16[96,2048]{1,0:T(8,128)(2,1)}, bf16[96,2048]{1,0:T(8,128)(2,1)}, u32[]{:S(2)}, u32[]{:S(2)}) collective-permute-start(bf16[96,2048]{1,0:T(8,128)(2,1)} %get-tuple-element.357), channel_id=1, source_target_pairs={{0,1},{1,0},{2,3},{3,2},{4,5},{5,4},{6,7},{7,6},{8,9},{9,8},{10,11... | collective-permute-start | bytes 1179656 | tf_op jit(solution)/shard_map/ppermute | solution.py:804
  99.9 12.0 %collective-permute-start.18 = (bf16[96,2048]{1,0:T(8,128)(2,1)S(1)}, bf16[96,2048]{1,0:T(8,128)(2,1)S(1)}, u32[]{:S(2)}, u32[]{:S(2)}) collective-permute-start(bf16[96,2048]{1,0:T(8,128)(2,1)S(1)} %add_convert_fusion.6), channel_id=1, source_target_pairs={{0,16},{1,17},{2,18},{3,19},{4,20},{5,21},{6,22},{7,23},{8,24},{9,... | collective-permute-start | bytes 1179656 | tf_op jit(solution)/shard_map/ppermute | solution.py:809
  103.4 13.0 %collective-permute-start.14 = (bf16[96,2048]{1,0:T(8,128)(2,1)S(1)}, bf16[96,2048]{1,0:T(8,128)(2,1)S(1)}, u32[]{:S(2)}, u32[]{:S(2)}) collective-permute-start(bf16[96,2048]{1,0:T(8,128)(2,1)S(1)} %get-tuple-element.351), channel_id=1, source_target_pairs={{0,1},{1,0},{2,3},{3,2},{4,5},{5,4},{6,7},{7,6},{8,9},{9,8},{10,11... | collective-permute-start | bytes 1179656 | tf_op jit(solution)/shard_map/ppermute | solution.py:804
  103.5 11.6 %collective-permute-start.16 = (bf16[96,2048]{1,0:T(8,128)(2,1)S(1)}, bf16[96,2048]{1,0:T(8,128)(2,1)S(1)}, u32[]{:S(2)}, u32[]{:S(2)}) collective-permute-start(bf16[96,2048]{1,0:T(8,128)(2,1)S(1)} %add_convert_fusion.7), channel_id=1, source_target_pairs={{0,2},{1,3},{2,0},{3,1},{4,6},{5,7},{6,4},{7,5},{8,10},{9,11},{10,... | collective-permute-start | bytes 1179656 | tf_op jit(solution)/shard_map/ppermute | solution.py:804
  127.3 18.0 %collective-permute-start.21 = (bf16[96,2048]{1,0:T(8,128)(2,1)S(1)}, bf16[96,2048]{1,0:T(8,128)(2,1)S(1)}, u32[]{:S(2)}, u32[]{:S(2)}) collective-permute-start(bf16[96,2048]{1,0:T(8,128)(2,1)S(1)} %get-tuple-element.380.refs_0_), channel_id=1, source_target_pairs={{0,2},{1,3},{2,0},{3,1},{4,6},{5,7},{6,4},{7,5},{8,10},{9,11},{10,... | collective-permute-start | bytes 1179656 | tf_op jit(solution)/shard_map/ppermute | solution.py:804
  145.3 255.2 %all-gather.11.cloned.1.call-start = ((), (), s32[]{:S(2)}) async-start(), calls=%async_computation.5 | async-start | bytes 1966080 | tf_op jit(solution)/shard_map/all_gather | solution.py:1033
  149.2 20.6 %collective-permute-start.27 = (bf16[96,2048]{1,0:T(8,128)(2,1)}, bf16[96,2048]{1,0:T(8,128)(2,1)}, u32[]{:S(2)}, u32[]{:S(2)}) collective-permute-start(bf16[96,2048]{1,0:T(8,128)(2,1)} %convert_add_fusion.4), channel_id=1, source_target_pairs={{0,2},{1,3},{2,0},{3,1},{4,6},{5,7},{6,4},{7,5},{8,10},{9,11},{10,... | collective-permute-start | bytes 1179656 | tf_op jit(solution)/shard_map/ppermute | solution.py:804
  169.7 230.8 %all-gather.5.cloned.1.call-start = ((), (), s32[]{:S(2)}) async-start(), calls=%async_computation.2 | async-start | bytes 5406720 | tf_op jit(solution)/shard_map/all_gather | solution.py:1032
  173.0 11.2 %collective-permute-start.30 = (bf16[96,2048]{1,0:T(8,128)(2,1)S(1)}, bf16[96,2048]{1,0:T(8,128)(2,1)S(1)}, u32[]{:S(2)}, u32[]{:S(2)}) collective-permute-start(bf16[96,2048]{1,0:T(8,128)(2,1)S(1)} %add_convert_fusion.4), channel_id=1, source_target_pairs={{0,2},{1,3},{2,0},{3,1},{4,6},{5,7},{6,4},{7,5},{8,10},{9,11},{10,... | collective-permute-start | bytes 1179656 | tf_op jit(solution)/shard_map/ppermute | solution.py:804
  185.1 11.7 %collective-permute-start.34 = (bf16[96,2048]{1,0:T(8,128)(2,1)S(1)}, bf16[96,2048]{1,0:T(8,128)(2,1)S(1)}, u32[]{:S(2)}, u32[]{:S(2)}) collective-permute-start(bf16[96,2048]{1,0:T(8,128)(2,1)S(1)} %get-tuple-element.403.refs_0_), channel_id=1, source_target_pairs={{0,1},{1,0},{2,3},{3,2},{4,5},{5,4},{6,7},{7,6},{8,9},{9,8},{10,11... | collective-permute-start | bytes 1179656 | tf_op jit(solution)/shard_map/ppermute | solution.py:804
  195.9 11.5 %collective-permute-start.33 = (bf16[96,2048]{1,0:T(8,128)(2,1)S(1)}, bf16[96,2048]{1,0:T(8,128)(2,1)S(1)}, u32[]{:S(2)}, u32[]{:S(2)}) collective-permute-start(bf16[96,2048]{1,0:T(8,128)(2,1)S(1)} %get-tuple-element.414.refs_0_), channel_id=1, source_target_pairs={{0,2},{1,3},{2,0},{3,1},{4,6},{5,7},{6,4},{7,5},{8,10},{9,11},{10,... | collective-permute-start | bytes 1179656 | tf_op jit(solution)/shard_map/ppermute | solution.py:804
  208.4 192.1 %all-gather.7.cloned.1.call-start = ((), (), s32[]{:S(2)}) async-start(), calls=%async_computation.3 | async-start | bytes 5406720 | tf_op jit(solution)/shard_map/all_gather | solution.py:1032
  227.4 25.3 %collective-permute-start.39 = (bf16[96,2048]{1,0:T(8,128)(2,1)S(1)}, bf16[96,2048]{1,0:T(8,128)(2,1)S(1)}, u32[]{:S(2)}, u32[]{:S(2)}) collective-permute-start(bf16[96,2048]{1,0:T(8,128)(2,1)S(1)} %convert_add_fusion.3), channel_id=1, source_target_pairs={{0,2},{1,3},{2,0},{3,1},{4,6},{5,7},{6,4},{7,5},{8,10},{9,11},{10,... | collective-permute-start | bytes 1179656 | tf_op jit(solution)/shard_map/ppermute | solution.py:804
  253.4 362.3 %reduce-scatter.3.cloned.1.call-start = ((), (), s32[]{:S(2)}) async-start(), calls=%async_computation.6 | async-start | bytes 14417920 | tf_op jit(solution)/shard_map/reduce_scatter | solution.py:1067
  256.4 11.5 %collective-permute-start.42 = (bf16[96,2048]{1,0:T(8,128)(2,1)}, bf16[96,2048]{1,0:T(8,128)(2,1)}, u32[]{:S(2)}, u32[]{:S(2)}) collective-permute-start(bf16[96,2048]{1,0:T(8,128)(2,1)} %add_convert_fusion.3), channel_id=1, source_target_pairs={{0,2},{1,3},{2,0},{3,1},{4,6},{5,7},{6,4},{7,5},{8,10},{9,11},{10,... | collective-permute-start | bytes 1179656 | tf_op jit(solution)/shard_map/ppermute | solution.py:804
  268.9 14.7 %collective-permute-start.46 = (bf16[96,2048]{1,0:T(8,128)(2,1)S(1)}, bf16[96,2048]{1,0:T(8,128)(2,1)S(1)}, u32[]{:S(2)}, u32[]{:S(2)}) collective-permute-start(bf16[96,2048]{1,0:T(8,128)(2,1)S(1)} %get-tuple-element.439.refs_0_), channel_id=1, source_target_pairs={{0,1},{1,0},{2,3},{3,2},{4,5},{5,4},{6,7},{7,6},{8,9},{9,8},{10,11... | collective-permute-start | bytes 1179656 | tf_op jit(solution)/shard_map/ppermute | solution.py:804
  282.6 20.7 %collective-permute-start.45 = (bf16[96,2048]{1,0:T(8,128)(2,1)S(1)}, bf16[96,2048]{1,0:T(8,128)(2,1)S(1)}, u32[]{:S(2)}, u32[]{:S(2)}) collective-permute-start(bf16[96,2048]{1,0:T(8,128)(2,1)S(1)} %get-tuple-element.456.refs_0_), channel_id=1, source_target_pairs={{0,2},{1,3},{2,0},{3,1},{4,6},{5,7},{6,4},{7,5},{8,10},{9,11},{10,... | collective-permute-start | bytes 1179656 | tf_op jit(solution)/shard_map/ppermute | solution.py:804
  306.4 21.4 %collective-permute-start.51 = (bf16[96,2048]{1,0:T(8,128)(2,1)S(1)}, bf16[96,2048]{1,0:T(8,128)(2,1)S(1)}, u32[]{:S(2)}, u32[]{:S(2)}) collective-permute-start(bf16[96,2048]{1,0:T(8,128)(2,1)S(1)} %convert_add_fusion.2), channel_id=1, source_target_pairs={{0,2},{1,3},{2,0},{3,1},{4,6},{5,7},{6,4},{7,5},{8,10},{9,11},{10,... | collective-permute-start | bytes 1179656 | tf_op jit(solution)/shard_map/ppermute | solution.py:804
  307.5 21.5 %collective-permute-start.55 = (bf16[96,2048]{1,0:T(8,128)(2,1)}, bf16[96,2048]{1,0:T(8,128)(2,1)}, u32[]{:S(2)}, u32[]{:S(2)}) collective-permute-start(bf16[96,2048]{1,0:T(8,128)(2,1)} %get-tuple-element.480), channel_id=1, source_target_pairs={{0,1},{1,0},{2,3},{3,2},{4,5},{5,4},{6,7},{7,6},{8,9},{9,8},{10,11... | collective-permute-start | bytes 1179656 | tf_op jit(solution)/shard_map/ppermute | solution.py:804
  335.0 13.0 %collective-permute-start.56 = (bf16[96,2048]{1,0:T(8,128)(2,1)S(1)}, bf16[96,2048]{1,0:T(8,128)(2,1)S(1)}, u32[]{:S(2)}, u32[]{:S(2)}) collective-permute-start(bf16[96,2048]{1,0:T(8,128)(2,1)S(1)} %get-tuple-element.481), channel_id=1, source_target_pairs={{16,0},{17,1},{18,2},{19,3},{20,4},{21,5},{22,6},{23,7},{24,8},{25... | collective-permute-start | bytes 1179656 | tf_op jit(solution)/shard_map/ppermute | solution.py:809
  336.3 13.6 %collective-permute-start.52 = (bf16[96,2048]{1,0:T(8,128)(2,1)S(1)}, bf16[96,2048]{1,0:T(8,128)(2,1)S(1)}, u32[]{:S(2)}, u32[]{:S(2)}) collective-permute-start(bf16[96,2048]{1,0:T(8,128)(2,1)S(1)} %copy-done.67), channel_id=1, source_target_pairs={{0,1},{1,0},{2,3},{3,2},{4,5},{5,4},{6,7},{7,6},{8,9},{9,8},{10,11... | collective-permute-start | bytes 1179656 | tf_op jit(solution)/shard_map/ppermute | solution.py:804
  337.5 11.6 %collective-permute-start.54 = (bf16[96,2048]{1,0:T(8,128)(2,1)S(1)}, bf16[96,2048]{1,0:T(8,128)(2,1)S(1)}, u32[]{:S(2)}, u32[]{:S(2)}) collective-permute-start(bf16[96,2048]{1,0:T(8,128)(2,1)S(1)} %add_convert_fusion.2), channel_id=1, source_target_pairs={{0,2},{1,3},{2,0},{3,1},{4,6},{5,7},{6,4},{7,5},{8,10},{9,11},{10,... | collective-permute-start | bytes 1179656 | tf_op jit(solution)/shard_map/ppermute | solution.py:804
  351.5 12.7 %collective-permute-start.57 = (bf16[96,2048]{1,0:T(8,128)(2,1)S(1)}, bf16[96,2048]{1,0:T(8,128)(2,1)S(1)}, u32[]{:S(2)}, u32[]{:S(2)}) collective-permute-start(bf16[96,2048]{1,0:T(8,128)(2,1)S(1)} %get-tuple-element.483), channel_id=1, source_target_pairs={{16,0},{17,1},{18,2},{19,3},{20,4},{21,5},{22,6},{23,7},{24,8},{25... | collective-permute-start | bytes 1179656 | tf_op jit(solution)/shard_map/ppermute | solution.py:809
  352.8 12.7 %collective-permute-start.60 = (bf16[96,2048]{1,0:T(8,128)(2,1)S(1)}, bf16[96,2048]{1,0:T(8,128)(2,1)S(1)}, u32[]{:S(2)}, u32[]{:S(2)}) collective-permute-start(bf16[96,2048]{1,0:T(8,128)(2,1)S(1)} %broadcast_select_fusion.2.refs_0_.base_ref), channel_id=1, source_target_pairs={{0,1},{1,0},{2,3},{3,2},{4,5},{5,4},{6,7},{7,6},{8,9},{9,8},{10,11... | collective-permute-start | bytes 1179656 | tf_op jit(solution)/shard_map/ppermute | solution.py:804
  364.3 15.6 %collective-permute-start.59 = (bf16[96,2048]{1,0:T(8,128)(2,1)S(1)}, bf16[96,2048]{1,0:T(8,128)(2,1)S(1)}, u32[]{:S(2)}, u32[]{:S(2)}) collective-permute-start(bf16[96,2048]{1,0:T(8,128)(2,1)S(1)} %broadcast_select_fusion.3.refs_0_.base_ref), channel_id=1, source_target_pairs={{0,2},{1,3},{2,0},{3,1},{4,6},{5,7},{6,4},{7,5},{8,10},{9,11},{10,... | collective-permute-start | bytes 1179656 | tf_op jit(solution)/shard_map/ppermute | solution.py:804
  401.4 19.3 %collective-permute-start.68 = (bf16[2,96,512]{2,1,0:T(8,128)(2,1)}, bf16[2,96,512]{2,1,0:T(8,128)(2,1)}, u32[]{:S(2)}, u32[]{:S(2)}) collective-permute-start(bf16[2,96,512]{2,1,0:T(8,128)(2,1)} %get-tuple-element.626), channel_id=1, source_target_pairs={{0,12},{4,8},{8,4},{12,0},{1,13},{5,9},{9,5},{13,1},{2,14},{6,10},... | collective-permute-start | bytes 589832 | tf_op jit(solution)/shard_map/ppermute | solution.py:804
  404.7 16.1 %collective-permute-start.66 = (bf16[2,96,512]{2,1,0:T(8,128)(2,1)}, bf16[2,96,512]{2,1,0:T(8,128)(2,1)}, u32[]{:S(2)}, u32[]{:S(2)}) collective-permute-start(bf16[2,96,512]{2,1,0:T(8,128)(2,1)} %get-tuple-element.628), channel_id=1, source_target_pairs={{0,4},{4,0},{8,12},{12,8},{1,5},{5,1},{9,13},{13,9},{2,6},{6,2},{1... | collective-permute-start | bytes 589832 | tf_op jit(solution)/shard_map/ppermute | solution.py:804
  404.7 17.2 %collective-permute-start.67 = (bf16[2,96,512]{2,1,0:T(8,128)(2,1)}, bf16[2,96,512]{2,1,0:T(8,128)(2,1)}, u32[]{:S(2)}, u32[]{:S(2)}) collective-permute-start(bf16[2,96,512]{2,1,0:T(8,128)(2,1)} %get-tuple-element.629), channel_id=1, source_target_pairs={{0,8},{4,12},{8,0},{12,4},{1,9},{5,13},{9,1},{13,5},{2,10},{6,14},... | collective-permute-start | bytes 589832 | tf_op jit(solution)/shard_map/ppermute | solution.py:804
  421.9 330.1 %reduce-scatter.5.cloned.1.call-start = ((), (), s32[]{:S(2)}) async-start(), calls=%async_computation.7 | async-start | bytes 7864320 | tf_op jit(solution)/shard_map/reduce_scatter | solution.py:1067
  434.6 11.2 %collective-permute-start.70 = (bf16[96,2048]{1,0:T(8,128)(2,1)S(1)}, bf16[96,2048]{1,0:T(8,128)(2,1)S(1)}, u32[]{:S(2)}, u32[]{:S(2)}) collective-permute-start(bf16[96,2048]{1,0:T(8,128)(2,1)S(1)} %add_convert_fusion.1), channel_id=1, source_target_pairs={{0,2},{1,3},{2,0},{3,1},{4,6},{5,7},{6,4},{7,5},{8,10},{9,11},{10,... | collective-permute-start | bytes 1179656 | tf_op jit(solution)/shard_map/ppermute | solution.py:804
  446.9 12.0 %collective-permute-start.75 = (bf16[96,2048]{1,0:T(8,128)(2,1)S(1)}, bf16[96,2048]{1,0:T(8,128)(2,1)S(1)}, u32[]{:S(2)}, u32[]{:S(2)}) collective-permute-start(bf16[96,2048]{1,0:T(8,128)(2,1)S(1)} %get-tuple-element.577.refs_0_), channel_id=1, source_target_pairs={{0,1},{1,0},{2,3},{3,2},{4,5},{5,4},{6,7},{7,6},{8,9},{9,8},{10,11... | collective-permute-start | bytes 1179656 | tf_op jit(solution)/shard_map/ppermute | solution.py:804
  457.9 21.3 %collective-permute-start.74 = (bf16[96,2048]{1,0:T(8,128)(2,1)S(1)}, bf16[96,2048]{1,0:T(8,128)(2,1)S(1)}, u32[]{:S(2)}, u32[]{:S(2)}) collective-permute-start(bf16[96,2048]{1,0:T(8,128)(2,1)S(1)} %get-tuple-element.578.refs_0_), channel_id=1, source_target_pairs={{0,2},{1,3},{2,0},{3,1},{4,6},{5,7},{6,4},{7,5},{8,10},{9,11},{10,... | collective-permute-start | bytes 1179656 | tf_op jit(solution)/shard_map/ppermute | solution.py:804
  620.5 17.0 %collective-permute-start.87 = (bf16[2,96,512]{2,1,0:T(8,128)(2,1)S(1)}, bf16[2,96,512]{2,1,0:T(8,128)(2,1)S(1)}, u32[]{:S(2)}, u32[]{:S(2)}) collective-permute-start(bf16[2,96,512]{2,1,0:T(8,128)(2,1)S(1)} %get-tuple-element.625), channel_id=1, source_target_pairs={{0,8},{4,12},{8,0},{12,4},{1,9},{5,13},{9,1},{13,5},{2,10},{6,14},... | collective-permute-start | bytes 589832 | tf_op jit(solution)/shard_map/ppermute | solution.py:804
  652.6 11.2 %collective-permute-start.84 = (bf16[96,2048]{1,0:T(8,128)(2,1)S(1)}, bf16[96,2048]{1,0:T(8,128)(2,1)S(1)}, u32[]{:S(2)}, u32[]{:S(2)}) collective-permute-start(bf16[96,2048]{1,0:T(8,128)(2,1)S(1)} %add_convert_fusion), channel_id=1, source_target_pairs={{0,2},{1,3},{2,0},{3,1},{4,6},{5,7},{6,4},{7,5},{8,10},{9,11},{10,... | collective-permute-start | bytes 1179656 | tf_op jit(solution)/shard_map/ppermute | solution.py:804
  655.1 54.2 %collective-permute-start.99 = (bf16[2,4,96,512]{3,2,0,1:T(8,128)(2,1)}, bf16[2,4,96,512]{3,2,0,1:T(8,128)(2,1)}, u32[]{:S(2)}, u32[]{:S(2)}) collective-permute-start(bf16[2,4,96,512]{3,2,0,1:T(8,128)(2,1)} %pad_maximum_fusion.6), channel_id=1, source_target_pairs={{0,1},{1,0},{2,3},{3,2},{4,5},{5,4},{6,7},{7,6},{8,9},{9,8},{10,11... | collective-permute-start | bytes 2359304 | tf_op jit(solution)/shard_map/ppermute | solution.py:804
  655.2 19.9 %collective-permute-start.77 = (bf16[96,2048]{1,0:T(8,128)(2,1)S(1)}, bf16[96,2048]{1,0:T(8,128)(2,1)S(1)}, u32[]{:S(2)}, u32[]{:S(2)}) collective-permute-start(bf16[96,2048]{1,0:T(8,128)(2,1)S(1)} %copy-done.56), channel_id=1, source_target_pairs={{0,1},{1,0},{2,3},{3,2},{4,5},{5,4},{6,7},{7,6},{8,9},{9,8},{10,11... | collective-permute-start | bytes 1179656 | tf_op jit(solution)/shard_map/ppermute | solution.py:804
  663.8 29.2 %collective-permute-start.95 = (bf16[2,4,96,512]{3,2,0,1:T(8,128)(2,1)}, bf16[2,4,96,512]{3,2,0,1:T(8,128)(2,1)}, u32[]{:S(2)}, u32[]{:S(2)}) collective-permute-start(bf16[2,4,96,512]{3,2,0,1:T(8,128)(2,1)} %pad_maximum_fusion.6), channel_id=1, source_target_pairs={{0,2},{1,3},{2,0},{3,1},{4,6},{5,7},{6,4},{7,5},{8,10},{9,11},{10,... | collective-permute-start | bytes 2359304 | tf_op jit(solution)/shard_map/ppermute | solution.py:804
  668.5 12.0 %collective-permute-start.82 = (bf16[96,2048]{1,0:T(8,128)(2,1)}, bf16[96,2048]{1,0:T(8,128)(2,1)S(1)}, u32[]{:S(2)}, u32[]{:S(2)}) collective-permute-start(bf16[96,2048]{1,0:T(8,128)(2,1)} %get-tuple-element.567), channel_id=1, source_target_pairs={{0,1},{1,0},{2,3},{3,2},{4,5},{5,4},{6,7},{7,6},{8,9},{9,8},{10,11... | collective-permute-start | bytes 1179656 | tf_op jit(solution)/shard_map/ppermute | solution.py:804
  674.8 24.2 %collective-permute-start.90 = (f32[14336]{0:T(1024)S(1)}, f32[14336]{0:T(1024)}, u32[]{:S(2)}, u32[]{:S(2)}) collective-permute-start(f32[14336]{0:T(1024)S(1)} %add.174), channel_id=1, source_target_pairs={{0,8},{4,12},{8,0},{12,4},{1,9},{5,13},{9,1},{13,5},{2,10},{6,14},... | collective-permute-start | bytes 172040 | tf_op jit(solution)/shard_map/ppermute | solution.py:804
  688.8 18.5 %collective-permute-start.85 = (bf16[2,96,1024]{2,1,0:T(8,128)(2,1)}, bf16[2,96,1024]{2,1,0:T(8,128)(2,1)}, u32[]{:S(2)}, u32[]{:S(2)}) collective-permute-start(bf16[2,96,1024]{2,1,0:T(8,128)(2,1)} %fusion.10), channel_id=1, source_target_pairs={{0,16},{1,17},{2,18},{3,19},{4,20},{5,21},{6,22},{7,23},{8,24},{9,... | collective-permute-start | bytes 1179656 | tf_op jit(solution)/shard_map/ppermute | solution.py:809
  693.0 16.3 %collective-permute-start.100 = (bf16[2,4,96,512]{3,2,0,1:T(8,128)(2,1)}, bf16[2,4,96,512]{3,2,0,1:T(8,128)(2,1)}, u32[]{:S(2)}, u32[]{:S(2)}) collective-permute-start(bf16[2,4,96,512]{3,2,0,1:T(8,128)(2,1)} %collective-permute-done.95), channel_id=1, source_target_pairs={{0,1},{1,0},{2,3},{3,2},{4,5},{5,4},{6,7},{7,6},{8,9},{9,8},{10,11... | collective-permute-start | bytes 2359304 | tf_op jit(solution)/shard_map/ppermute | solution.py:804
  713.0 19.6 %collective-permute-start.96 = (bf16[2,4,96,512]{3,2,0,1:T(8,128)(2,1)S(1)}, bf16[2,4,96,512]{3,2,0,1:T(8,128)(2,1)S(1)}, u32[]{:S(2)}, u32[]{:S(2)}) collective-permute-start(bf16[2,4,96,512]{3,2,0,1:T(8,128)(2,1)S(1)} %pad_maximum_fusion.4), channel_id=1, source_target_pairs={{0,2},{1,3},{2,0},{3,1},{4,6},{5,7},{6,4},{7,5},{8,10},{9,11},{10,... | collective-permute-start | bytes 2359304 | tf_op jit(solution)/shard_map/ppermute | solution.py:804
  720.5 15.2 %collective-permute-start.97 = (bf16[2,4,96,512]{3,2,0,1:T(8,128)(2,1)S(1)}, bf16[2,4,96,512]{3,2,0,1:T(8,128)(2,1)S(1)}, u32[]{:S(2)}, u32[]{:S(2)}) collective-permute-start(bf16[2,4,96,512]{3,2,0,1:T(8,128)(2,1)S(1)} %pad_maximum_fusion.4), channel_id=1, source_target_pairs={{0,1},{1,0},{2,3},{3,2},{4,5},{5,4},{6,7},{7,6},{8,9},{9,8},{10,11... | collective-permute-start | bytes 2359304 | tf_op jit(solution)/shard_map/ppermute | solution.py:804
  (175 other events, 1428.5 us)
Sparse Core Ops, SparseCore 0:
  145.4 38.9 all-gather.8
  186.0 35.9 all-gather.10
  223.6 81.7 all-gather.4
  306.8 81.4 all-gather.6
  422.0 193.6 reduce-scatter.2
  637.7 114.2 reduce-scatter.4
